TPU v7x, 32 devices: a whole 2x2x4 slice. The times are simulated.
32 devices in a mesh: dp: 8 (over z, x), expert: 4 (over y, core).
Axes of the slice: x: 2, y: 2, z: 4, core: 2. Of those that a mesh axis runs over, the one named last changes fastest.
Arguments:
- tokens: bfloat16 [8192, 1536], P(('dp', 'expert')), may hold values from -6 to 6
- cotangent: bfloat16 [8192, 1536], P(('dp', 'expert')), may hold values from -6 to 6
- routes: int32 [8192, 8], P(('dp', 'expert')), may hold values from 0 to 19, all different within a row; in each aligned block of 256 rows (0 to 255, 256 to 511, ...) at most 153 rows name the same one
- segments: int32 [32, 256], P(('dp', 'expert')), may hold values from 0 to 1, never falling along the last dimension, each value on 1 to 192 neighbouring positions
- w_qkv: bfloat16 [1536, 2560], P(('dp', 'expert')), may hold values from -0.21875 to 0.21875
- w_out: bfloat16 [1536, 1536], P(('dp', 'expert')), may hold values from -0.4375 to 0.4375
- router: bfloat16 [1536, 20], P(('dp', 'expert')), may hold values from -0.078125 to 0.078125
- gain_attn: bfloat16 [1536], P(('dp', 'expert')), may hold values from 0.099609375 to 1.8984375
- gain_mlp: bfloat16 [1536], P(('dp', 'expert')), may hold values from 0.099609375 to 1.8984375
- expert_in: bfloat16 [20, 1536, 1024], P('expert'), may hold values from -0.15625 to 0.15625
- expert_out: bfloat16 [20, 512, 1536], P('expert'), may hold values from -1 to 1
Outputs:
- activations: bfloat16 [8192, 1536], P(('dp', 'expert'))
- d_tokens: float32 [8192, 1536], P(('dp', 'expert'))
- d_w_qkv: float32 [1536, 2560], P(('dp', 'expert'))
- d_w_out: float32 [1536, 1536], P(('dp', 'expert'))
- d_router: float32 [1536, 20], P(('dp', 'expert'))
- d_gain_attn: float32 [1536], P(('dp', 'expert'))
- d_gain_mlp: float32 [1536], P(('dp', 'expert'))
- d_expert_in: float32 [20, 1536, 1024], P('expert', 'dp')
- d_expert_out: float32 [20, 512, 1536], P('expert', 'dp')
Inputs may be any that keep to these rules, and one draw needn't show every extreme that they name: `routes`: each row names 8 different experts. In the rows of one device (aligned blocks of 256 rows) no expert is named by more than 153 rows, a bound that some block reaches. `segments`: within a row the numbers never fall; each row holds two documents, each one run of a number of 64 to 192 positions.
All inputs are finite; a program needn't handle non-finite values.
Results may differ from a plain program's by a relative error of at most 0.017.
The roundings to bfloat16 on the way count: a program that leaves them out, or rounds other values in their place, can miss the bound.
Values may be sent and summed in bfloat16 or wider, within the bound.
No kernel may reach another device: no remote copies, remote signals or barrier semaphores. Data moves between devices by JAX's collectives and lax.ppermute only.
A program may use at most 320 MiB of HBM per device.

v0:
```python
import jax
import jax.numpy as jnp
from jax import lax
from jax.sharding import PartitionSpec as P

H = 24
KV = 8
HD = 64
FE = 512
TOP = 8


EPSILON = 1e-06
THETA = 10000.0
NEGATIVE = -1e30


def rope_tables(length, head_size):
    half_size = head_size // 2
    frequency = THETA ** (-(jnp.arange(half_size, dtype=jnp.float32) * 2.0) / head_size)
    angles = jnp.arange(length, dtype=jnp.float32)[:, None] * frequency[None, :]
    return (jnp.cos(angles)[:, None, :], jnp.sin(angles)[:, None, :])


def rotate(values_in, cos_table, sin_table):
    half_size = values_in.shape[-1] // 2
    first_half = values_in[..., :half_size]
    second_half = values_in[..., half_size:]
    return jnp.concatenate(
        [
            first_half * cos_table - second_half * sin_table,
            second_half * cos_table + first_half * sin_table,
        ],
        axis=-1,
    )


def slot_tables(routes_dev, experts_all, capacity):
    flat_routes = routes_dev.reshape(-1)
    choose = routes_dev.shape[1]
    onehot = (flat_routes[:, None] == jnp.arange(experts_all, dtype=jnp.int32)[None, :]).astype(
        jnp.int32
    )
    slot_rank = jnp.sum((jnp.cumsum(onehot, axis=0) - onehot) * onehot, axis=1)
    slot_index = flat_routes * capacity + slot_rank
    token_of = jnp.arange(flat_routes.shape[0], dtype=jnp.int32) // choose
    slot_token = jnp.zeros((experts_all * capacity,), jnp.int32).at[slot_index].set(token_of)
    slot_used = jnp.zeros((experts_all * capacity,), jnp.int32).at[slot_index].set(1)
    return (slot_index.reshape(routes_dev.shape), slot_token, slot_used)


def norm_back(grad_normed, normed_plain, recip_row, gain_row):
    scaled = grad_normed * gain_row
    gain_grad = jnp.sum(grad_normed * normed_plain, axis=0)
    back_part = recip_row * (
        scaled - normed_plain * jnp.mean(scaled * normed_plain, axis=-1, keepdims=True)
    )
    return (back_part, gain_grad)


def contract_rows(left_side, right_side):
    return lax.dot_general(
        left_side, right_side, (((0,), (0,)), ((), ())), preferred_element_type=jnp.float32
    )


def on_device(
    tokens,
    cotangent,
    routes,
    segments,
    w_qkv,
    w_out,
    router,
    gain_attn,
    gain_mlp,
    expert_in,
    expert_out,
):
    qkv_full, out_full, router_full, gain_first, gain_second = (
        lax.all_gather(w_qkv, ("dp", "expert"), axis=0, tiled=True),
        lax.all_gather(w_out, ("dp", "expert"), axis=0, tiled=True),
        lax.all_gather(router, ("dp", "expert"), axis=0, tiled=True),
        lax.all_gather(gain_attn, ("dp", "expert"), axis=0, tiled=True),
        lax.all_gather(gain_mlp, ("dp", "expert"), axis=0, tiled=True),
    )
    length, width = tokens.shape
    group_size = H // KV
    score_scale = HD ** (-0.5)
    owner_count = lax.axis_size("expert")
    local_count = expert_in.shape[0]
    experts_all = local_count * owner_count
    capacity = 3 * length * TOP // (2 * experts_all)
    slot_index, slot_token, slot_used = slot_tables(routes, experts_all, capacity)
    flat_slots = slot_index.reshape(-1)
    inputs = tokens.astype(jnp.float32)
    gain_one = gain_first.astype(jnp.float32)
    gain_two = gain_second.astype(jnp.float32)
    recip_one = lax.rsqrt(jnp.mean(inputs * inputs, axis=-1, keepdims=True) + EPSILON)
    plain_one = inputs * recip_one
    normed = (plain_one * gain_one).astype(jnp.bfloat16)
    project = jnp.dot(normed, qkv_full, preferred_element_type=jnp.float32)
    cos_table, sin_table = rope_tables(length, HD)
    queries = rotate(project[:, : H * HD].reshape(length, H, HD), cos_table, sin_table).astype(
        jnp.bfloat16
    )
    queries = queries.reshape(length, KV, group_size, HD)
    key_rows = rotate(
        project[:, H * HD : (H + KV) * HD].reshape(length, KV, HD), cos_table, sin_table
    ).astype(jnp.bfloat16)
    values = project[:, (H + KV) * HD :].reshape(length, KV, HD).astype(jnp.bfloat16)
    segment_row = segments[0]
    places = jnp.arange(length)
    block_rows = min(length, 512)
    starts = jnp.arange(length // block_rows) * block_rows

    def block_scores(block_start):
        raw_scores = (
            jnp.einsum("tkgd,skd->kgts", queries, key_rows, preferred_element_type=jnp.float32)
            * score_scale
        )
        rows_here = block_start + jnp.arange(block_rows)
        allowed = (rows_here[:, None] >= places[None, :]) & (
            segment_row[:, None] == segment_row[None, :]
        )
        return jnp.where(allowed, raw_scores, NEGATIVE)

    def attend(block_start):
        masked = block_scores(block_start)
        row_peak = jnp.max(masked, axis=-1, keepdims=True)
        exponent = jnp.exp(masked - row_peak)
        row_total = jnp.sum(exponent, axis=-1, keepdims=True)
        probability = (exponent / row_total).astype(jnp.bfloat16)
        block_out = jnp.einsum(
            "kgts,skd->tkgd", probability, values, preferred_element_type=jnp.float32
        )
        return (block_out, row_peak + jnp.log(row_total))

    block_outs, log_totals = lax.map(attend, starts)
    mixed_heads = block_outs.reshape(length, H * HD).astype(jnp.bfloat16)
    hidden_state = inputs + jnp.dot(mixed_heads, out_full, preferred_element_type=jnp.float32)
    recip_two = lax.rsqrt(jnp.mean(hidden_state * hidden_state, axis=-1, keepdims=True) + EPSILON)
    plain_two = hidden_state * recip_two
    normed_two = (plain_two * gain_two).astype(jnp.bfloat16)
    logits = jnp.dot(normed_two, router_full, preferred_element_type=jnp.float32)
    chosen = jnp.take_along_axis(logits, routes, axis=1)
    top_logit = jnp.max(chosen, axis=-1, keepdims=True)
    gate_exp = jnp.exp(chosen - top_logit)
    gate_float = gate_exp / jnp.sum(gate_exp, axis=-1, keepdims=True)
    gate_values = gate_float.astype(jnp.bfloat16)
    slot_gate = (
        jnp.zeros((experts_all * capacity,), jnp.bfloat16)
        .at[flat_slots]
        .set(gate_values.reshape(-1))
    )
    slot_gate = slot_gate.reshape(experts_all, capacity)
    dispatch = jnp.where(
        slot_used[:, None] > 0, normed_two[slot_token], jnp.zeros((), jnp.bfloat16)
    )
    dispatch = dispatch.reshape(experts_all, capacity, width)
    arrived = lax.all_to_all(dispatch, "expert", split_axis=0, concat_axis=1, tiled=True)
    pre_act = jnp.einsum("erd,edf->erf", arrived, expert_in, preferred_element_type=jnp.float32)
    gate_part = pre_act[..., :FE]
    up_part = pre_act[..., FE:]
    sigmoid_gate = jax.nn.sigmoid(gate_part)
    silu_gate = gate_part * sigmoid_gate
    activated = (silu_gate * up_part).astype(jnp.bfloat16)
    result_rows = jnp.einsum(
        "erf,efd->erd", activated, expert_out, preferred_element_type=jnp.float32
    ).astype(jnp.bfloat16)
    upstream_grad = cotangent.astype(jnp.float32)
    back_rows = lax.all_to_all(result_rows, "expert", split_axis=1, concat_axis=0, tiled=True)
    picked_low = back_rows.reshape(experts_all * capacity, width)[slot_index]
    picked = picked_low.astype(jnp.float32)
    mixture = jnp.sum(gate_values.astype(jnp.float32)[:, :, None] * picked, axis=1)
    activations = (hidden_state + mixture).astype(jnp.bfloat16)
    gate_grads = jnp.einsum("td,tjd->tj", cotangent, picked_low, preferred_element_type=jnp.float32)
    gate_grads = gate_grads.astype(jnp.bfloat16).astype(jnp.float32)
    slot_upstream = slot_gate.reshape(-1).astype(jnp.float32)[:, None] * upstream_grad[slot_token]
    grad_slots = slot_upstream.astype(jnp.bfloat16).reshape(experts_all, capacity, width)
    grad_rows = lax.all_to_all(grad_slots, "expert", split_axis=0, concat_axis=1, tiled=True)
    grad_act = jnp.einsum("erd,efd->erf", grad_rows, expert_out, preferred_element_type=jnp.float32)
    grad_gate = grad_act * up_part * sigmoid_gate * (1.0 + gate_part * (1.0 - sigmoid_gate))
    grad_up = grad_act * silu_gate
    grad_pre = jnp.concatenate([grad_gate, grad_up], axis=-1).astype(jnp.bfloat16)
    grad_out_weight = jnp.einsum(
        "erf,erd->efd", activated, grad_rows, preferred_element_type=jnp.float32
    )
    grad_in_weight = jnp.einsum(
        "erd,erf->edf", arrived, grad_pre, preferred_element_type=jnp.float32
    )
    grad_inputs = jnp.einsum(
        "erf,edf->erd", grad_pre, expert_in, preferred_element_type=jnp.float32
    )
    d_expert_in_local, d_expert_out_local, grad_inputs = (
        grad_in_weight,
        grad_out_weight,
        grad_inputs.astype(jnp.bfloat16),
    )
    returned = lax.all_to_all(grad_inputs, "expert", split_axis=1, concat_axis=0, tiled=True)
    grad_normed_two = jnp.sum(
        returned.reshape(experts_all * capacity, width)[slot_index].astype(jnp.float32), axis=1
    )
    centered = gate_grads - jnp.sum(gate_float * gate_grads, axis=-1, keepdims=True)
    chosen_grad = gate_float * centered
    expert_ids = jnp.arange(experts_all, dtype=jnp.int32)
    logit_grad = jnp.sum(
        chosen_grad[:, :, None] * (routes[:, :, None] == expert_ids[None, None, :]), axis=1
    )
    logit_grad = logit_grad.astype(jnp.bfloat16)
    d_router_local = contract_rows(normed_two, logit_grad)
    grad_normed_two = grad_normed_two + jnp.dot(
        logit_grad, router_full.T, preferred_element_type=jnp.float32
    )
    back_two, d_gain_second = norm_back(grad_normed_two, plain_two, recip_two, gain_two)
    grad_hidden = upstream_grad + back_two
    grad_branch = grad_hidden.astype(jnp.bfloat16)
    d_out_local = contract_rows(mixed_heads, grad_branch)
    grad_mixed = jnp.dot(grad_branch, out_full.T, preferred_element_type=jnp.float32).astype(
        jnp.bfloat16
    )
    grad_mixed = grad_mixed.reshape(length, KV, group_size, HD)

    def back_block(carried, pieces):
        key_sum, value_sum = carried
        block_start, log_total = pieces
        probability = jnp.exp(block_scores(block_start) - log_total)
        value_sum = value_sum + jnp.einsum(
            "kgts,tkgd->skd",
            probability.astype(jnp.bfloat16),
            grad_mixed,
            preferred_element_type=jnp.float32,
        )
        grad_probs = jnp.einsum(
            "tkgd,skd->kgts", grad_mixed, values, preferred_element_type=jnp.float32
        )
        delta_row = jnp.sum(probability * grad_probs, axis=-1, keepdims=True)
        grad_scores = (probability * (grad_probs - delta_row)).astype(jnp.bfloat16)
        grad_query = (
            jnp.einsum("kgts,skd->tkgd", grad_scores, key_rows, preferred_element_type=jnp.float32)
            * score_scale
        )
        key_sum = (
            key_sum
            + jnp.einsum("kgts,tkgd->skd", grad_scores, queries, preferred_element_type=jnp.float32)
            * score_scale
        )
        return ((key_sum, value_sum), grad_query)

    zero_heads = jnp.zeros((length, KV, HD), jnp.float32)
    (grad_keys, grad_values), grad_queries = lax.scan(
        back_block, (zero_heads, zero_heads), (starts, log_totals)
    )
    grad_queries = rotate(grad_queries.reshape(length, H, HD), cos_table, -sin_table)
    grad_keys = rotate(grad_keys, cos_table, -sin_table)
    grad_project = jnp.concatenate(
        [
            grad_queries.reshape(length, H * HD),
            grad_keys.reshape(length, KV * HD),
            grad_values.reshape(length, KV * HD),
        ],
        axis=1,
    ).astype(jnp.bfloat16)
    d_qkv_local = contract_rows(normed, grad_project)
    grad_normed = jnp.dot(grad_project, qkv_full.T, preferred_element_type=jnp.float32)
    back_one, d_gain_first = norm_back(grad_normed, plain_one, recip_one, gain_one)
    grad_tokens = grad_hidden + back_one
    d_qkv, d_out, d_router, d_gain_attn, d_gain_mlp = (
        lax.psum_scatter(d_qkv_local, ("dp", "expert"), scatter_dimension=0, tiled=True),
        lax.psum_scatter(d_out_local, ("dp", "expert"), scatter_dimension=0, tiled=True),
        lax.psum_scatter(d_router_local, ("dp", "expert"), scatter_dimension=0, tiled=True),
        lax.psum_scatter(d_gain_first, ("dp", "expert"), scatter_dimension=0, tiled=True),
        lax.psum_scatter(d_gain_second, ("dp", "expert"), scatter_dimension=0, tiled=True),
    )
    d_expert_in, d_expert_out = (
        lax.psum_scatter(
            d_expert_in_local.astype(jnp.bfloat16), "dp", scatter_dimension=1, tiled=True
        ).astype(jnp.float32),
        lax.psum_scatter(
            d_expert_out_local.astype(jnp.bfloat16), "dp", scatter_dimension=1, tiled=True
        ).astype(jnp.float32),
    )
    return (
        activations,
        grad_tokens,
        d_qkv,
        d_out,
        d_router,
        d_gain_attn,
        d_gain_mlp,
        d_expert_in,
        d_expert_out,
    )


def solution(mesh):
    placed = (
        P(("dp", "expert"), None),
        P(("dp", "expert"), None),
        P(("dp", "expert"), None),
        P(("dp", "expert"), None),
        P(("dp", "expert"), None),
        P(("dp", "expert"), None),
        P(("dp", "expert"), None),
        P(("dp", "expert")),
        P(("dp", "expert")),
        P("expert", None, None),
        P("expert", None, None),
    )
    return jax.shard_map(
        on_device,
        mesh=mesh,
        in_specs=placed,
        out_specs=(
            P(("dp", "expert"), None),
            P(("dp", "expert"), None),
            P(("dp", "expert"), None),
            P(("dp", "expert"), None),
            P(("dp", "expert"), None),
            P(("dp", "expert")),
            P(("dp", "expert")),
            P("expert", "dp", None),
            P("expert", "dp", None),
        ),
        check_vma=False,
    )
```

profile of v0, /device:TPU:0, one launch (start us, length us, event | category | flops | bytes accessed | tf_op | source)
XLA Modules:
  0.0 1560.7 jit_solution(10960854324735903917)
XLA Ops:
  11.4 42.8 %all-reduce.5 = (bf16[1536]{0:T(1024)(128)(2,1)S(1)}, bf16[1536]{0:T(1024)(128)(2,1)S(1)}) all-reduce(bf16[1536]{0:T(1024)(128)(2,1)S(1)} %dynamic-update-slice, bf16[1536]{0:T(1024)(128)(2,1)S(1)} %dynamic-update-slice.1), channel_id=1, replica_groups=mesh['dp'=8,'expert'=4] {'dp','expert'}, use_global_device_ids=true, to_apply=%add | all-reduce | flops 3072 | bytes 12288
  54.9 41.8 %all-gather = bf16[32,48,20]{1,2,0:T(8,128)(2,1)S(1)} all-gather(bf16[1,48,20]{1,2,0:T(8,128)(2,1)} %bitcast.163), channel_id=1, replica_groups=mesh['dp'=8,'expert'=4] {'dp','expert'}, dimensions={0}, use_global_device_ids=true | all-gather | bytes 63360 | tf_op jit(solution)/shard_map/all_gather | solution.py:83
  108.1 8.2 scatter_custom_fusion.1
  116.3 15.9 %gather_fusion.2 = f32[3060,1536]{1,0:T(8,128)} fusion(f32[256,1536]{1,0:T(8,128)S(1)} %convert_element_type.135, s32[3072]{0:T(1024)S(1)} %pad_clamp_fusion), kind=kCustom, calls=%fused_computation.2 | custom fusion | bytes 37613520 | tf_op jit(solution)/shard_map/gather | solution.py:179
  132.3 19.0 %gather.25 = f32[20,153,1536]{2,1,0:T(8,128)} reshape(f32[3060,1536]{1,0:T(8,128)} %gather_fusion.2) | data formatting | bytes 37601280 | tf_op jit(solution)/shard_map/gather | solution.py:179
  153.1 5.8 fusion.40
  176.8 16.8 %gather_fusion.4 = f32[2048]{0:T(1024)S(1)} fusion(f32[256,20]{0,1:T(8,128)S(1)} %fusion.74, s32[2048]{0:T(1024)S(1)} %reshape.316), kind=kCustom, calls=%fused_computation.4 | custom fusion | bytes 32768 | tf_op jit(solution)/shard_map/jit(take_along_axis)/gather | solution.py:146
  194.7 14.9 scatter_custom_fusion.2
  209.7 11.7 multiply_convert_fusion
  221.4 5.9 all-to-all-start.2
  227.3 8.2 scatter_custom_fusion
  235.7 14.7 gather_fusion
  250.4 7.9 gather.22
  258.3 8.3 broadcast_select_fusion
  266.6 69.3 %all-to-all-done.2 = bf16[20,153,1536]{2,1,0:T(8,128)(2,1)} async-done(((bf16[20,153,1536]{2,1,0:T(8,128)(2,1)}), bf16[20,153,1536]{2,1,0:T(8,128)(2,1)}, u32[]{:S(2)}, u32[]{:S(2)}) %all-to-all-start.2) | async-done | bytes 9400352 | tf_op jit(solution)/shard_map/all_to_all | solution.py:181
  335.9 6.3 all-to-all-start
  342.2 8.3 copy.144
  350.5 10.2 all_to_all.58
  360.8 90.1 %all-to-all-done = bf16[20,153,1536]{2,1,0:T(8,128)(2,1)} async-done(((bf16[20,153,1536]{2,1,0:T(8,128)(2,1)}), bf16[20,153,1536]{2,1,0:T(8,128)(2,1)}, u32[]{:S(2)}, u32[]{:S(2)}) %all-to-all-start) | async-done | bytes 9400352 | tf_op jit(solution)/shard_map/all_to_all | solution.py:161
  450.8 8.4 copy.137
  459.3 10.2 all_to_all.51
  469.5 18.9 %fusion.75 = f32[5,612,1024]{2,1,0:T(8,128)} fusion(bf16[5,612,1536]{2,1,0:T(8,128)(2,1)} %all_to_all.51, bf16[5,1536,1024]{2,1,0:T(8,128)(2,1)} %param.20), kind=kOutput, calls=%fused_computation.154 | convolution fusion | flops 9625927680 | bytes 37662720 | tf_op jit(solution)/shard_map/erd,edf->erf/dot_general | solution.py:162
  488.4 16.3 %multiply_convert_fusion.2 = (bf16[5,612,512]{2,1,0:T(8,128)(2,1)}, bf16[5,612,512]{2,1,0:T(8,128)(2,1)}, bf16[5,612,512]{2,1,0:T(8,128)(2,1)}) fusion(f32[5,612,1024]{2,1,0:T(8,128)} %fusion.75, bf16[5,612,1536]{2,1,0:T(8,128)(2,1)} %all_to_all.58, bf16[5,512,1536]{2,1,0:T(8,128)(2,1)} %param.21), kind=kOutput, calls=%fused_computation.17 | convolution fusion | flops 4836464640 | bytes 39198720 | tf_op jit(solution)/shard_map/erd,efd->erf/dot_general | solution.py:182
  504.6 8.4 convolution_convert_fusion.2
  513.0 14.7 copy.138
  527.6 6.9 all-to-all-start.1
  534.8 164.1 %all-to-all-done.1 = bf16[5,612,1536]{2,0,1:T(8,128)(2,1)} async-done(((bf16[5,612,1536]{2,0,1:T(8,128)(2,1)}), bf16[5,612,1536]{2,0,1:T(8,128)(2,1)}, u32[]{:S(2)}, u32[]{:S(2)}) %all-to-all-start.1) | async-done | bytes 9400352 | tf_op jit(solution)/shard_map/all_to_all | solution.py:172
  698.9 13.0 copy.140
  711.9 8.0 reshape.276
  719.9 18.3 %gather_fusion.1 = bf16[2048,1536]{1,0:T(8,128)(2,1)} fusion(bf16[3060,1536]{1,0:T(8,128)(2,1)} %reshape.276, s32[2048]{0:T(1024)S(1)} %broadcast_clamp_fusion), kind=kCustom, calls=%fused_computation.1 | custom fusion | bytes 12591104 | tf_op jit(solution)/shard_map/gather | solution.py:173
  738.3 6.2 fusion.4
  746.1 13.1 convolution_convert_fusion.3
  759.3 19.1 %convolution_convert_fusion = bf16[5,1536,1024]{2,1,0:T(8,128)(2,1)} fusion(bf16[5,612,1536]{2,1,0:T(8,128)(2,1)} %all_to_all.51, bf16[5,612,512]{2,1,0:T(8,128)(2,1)} %get-tuple-element.77, bf16[5,612,512]{2,1,0:T(8,128)(2,1)} %get-tuple-element.76), kind=kOutput, calls=%fused_computation.9 | convolution fusion | flops 9646325760 | bytes 31395840 | tf_op jit(solution)/shard_map/erd,erf->edf/dot_general | solution.py:189
  778.4 16.7 %convolution_convert_fusion.1 = bf16[5,612,1536]{2,1,0:T(8,128)(2,1)} fusion(bf16[5,1536,1024]{2,1,0:T(8,128)(2,1)} %param.20, bf16[5,612,512]{2,1,0:T(8,128)(2,1)} %get-tuple-element.77, bf16[5,612,512]{2,1,0:T(8,128)(2,1)} %get-tuple-element.76), kind=kOutput, calls=%fused_computation.13 | convolution fusion | flops 9643161600 | bytes 31395840 | tf_op jit(solution)/shard_map/erf,edf->erd/dot_general | solution.py:192
  795.1 22.1 %copy.145 = bf16[5,612,1536]{2,0,1:T(8,128)(2,1)} copy(bf16[5,612,1536]{2,1,0:T(8,128)(2,1)} %convolution_convert_fusion.1) | data formatting | bytes 18800640 | tf_op jit(solution)/shard_map/convert_element_type | solution.py:198
  817.2 6.9 all-to-all-start.3
  824.2 164.4 %all-to-all-done.3 = bf16[5,612,1536]{2,0,1:T(8,128)(2,1)} async-done(((bf16[5,612,1536]{2,0,1:T(8,128)(2,1)}), bf16[5,612,1536]{2,0,1:T(8,128)(2,1)}, u32[]{:S(2)}, u32[]{:S(2)}) %all-to-all-start.3) | async-done | bytes 9400352 | tf_op jit(solution)/shard_map/all_to_all | solution.py:200
  988.6 12.9 copy.147
  1001.5 8.0 reshape.277
  1009.6 18.2 %gather_fusion.3 = bf16[2048,1536]{1,0:T(8,128)(2,1)} fusion(bf16[3060,1536]{1,0:T(8,128)(2,1)} %reshape.277, s32[2048]{0:T(1024)S(1)} %broadcast_clamp_fusion), kind=kCustom, calls=%fused_computation.3 | custom fusion | bytes 12591104 | tf_op jit(solution)/shard_map/gather | solution.py:202
  1027.8 7.2 convert_reduce_fusion
  1035.8 9.0 multiply_reduce_fusion
  1070.0 8.0 fusion.33
  1078.0 7.2 fusion.21
  1085.1 42.9 %all-reduce.4 = (f32[1536]{0:T(1024)S(1)}, f32[1536]{0:T(1024)S(1)}) all-reduce(f32[1536]{0:T(1024)S(1)} %get-tuple-element.57, f32[1536]{0:T(1024)S(1)} %get-tuple-element.55), channel_id=5, replica_groups=mesh['dp'=8,'expert'=4] {'dp','expert'}, use_global_device_ids=true, to_apply=%region_23.24.clone | all-reduce | flops 3072 | bytes 24576
  1136.3 99.0 %reduce-scatter.12.cloned.1.call-done = bf16[5,192,1024]{2,1,0:T(8,128)(2,1)} async-done(((bf16[5,1536,1024]{2,1,0:T(8,128)(2,1)}), bf16[5,192,1024]{2,1,0:T(8,128)(2,1)}) %reduce-scatter.12.cloned.1.call-update) | async-done | bytes 1966096 | tf_op jit(solution)/shard_map/reduce_scatter | solution.py:276
  1239.2 137.0 %reduce-scatter.10.cloned.1.call-done = f32[48,1536]{1,0:T(8,128)} async-done(((f32[1536,1536]{1,0:T(8,128)}), f32[48,1536]{1,0:T(8,128)}) %reduce-scatter.10.cloned.1.call-update) | async-done | bytes 294928 | tf_op jit(solution)/shard_map/reduce_scatter | solution.py:270
  1376.3 177.3 %reduce-scatter.8.cloned.1.call-done = f32[48,2560]{1,0:T(8,128)} async-done(((f32[1536,2560]{1,0:T(8,128)}), f32[48,2560]{1,0:T(8,128)}) %reduce-scatter.8.cloned.1.call-update) | async-done | bytes 491536 | tf_op jit(solution)/shard_map/reduce_scatter | solution.py:269
  (229 shorter events, 76.7 us)
Async XLA Ops:
  7.2 145.9 %all-gather.4.cloned.1.call-start = ((), (), s32[]{:S(2)}) async-start(), calls=%async_computation.9 | async-start | bytes 8110080 | tf_op jit(solution)/shard_map/all_gather | solution.py:81
  7.9 163.1 %all-gather.6.cloned.1.call-start = ((), (), s32[]{:S(2)}) async-start(), calls=%async_computation.10 | async-start | bytes 4866048 | tf_op jit(solution)/shard_map/all_gather | solution.py:82
  54.3 98.8 %copy-start.28 = (f32[1536]{0:T(1024)}, f32[1536]{0:T(1024)S(1)}, u32[]{:S(2)}) copy-start(f32[1536]{0:T(1024)S(1)} %convert_element_type.118) | copy-start | bytes 18436
  96.9 79.6 %copy-start.21 = (bf16[1536,20]{0,1:T(8,128)(2,1)}, bf16[1536,20]{0,1:T(8,128)(2,1)S(1)}, u32[]{:S(2)}) copy-start(bf16[1536,20]{0,1:T(8,128)(2,1)S(1)} %reshape.363) | copy-start | bytes 184324
  116.3 15.9 %copy-start.40 = (s32[3072]{0:T(1024)}, s32[3072]{0:T(1024)S(1)}, u32[]{:S(2)}) copy-start(s32[3072]{0:T(1024)S(1)} %pad_clamp_fusion) | copy-start | bytes 36868
  132.2 19.0 %copy-start.3 = (bf16[256,1536]{1,0:T(8,128)(2,1)S(1)}, bf16[256,1536]{1,0:T(8,128)(2,1)}, u32[]{:S(2)}) copy-start(bf16[256,1536]{1,0:T(8,128)(2,1)} %param.11) | copy-start | bytes 2359300
  132.2 19.3 %copy-start.54 = (s32[1,256]{1,0:T(1,128)S(1)}, s32[1,256]{1,0:T(1,128)}, u32[]{:S(2)}) copy-start(s32[1,256]{1,0:T(1,128)} %param.14) | copy-start | bytes 3076
  151.5 7.3 copy-start.45
  153.1 11.1 copy-start.19
  164.1 4.3 copy-start.17
  164.2 4.2 copy-start.23
  164.2 4.2 copy-start.25
  167.2 3.8 copy-start.36
  171.0 4.2 copy-start.7
  171.0 5.3 copy-start.34
  176.8 17.0 %copy-start.32 = (s32[256,8]{0,1:T(8,128)S(1)}, s32[256,8]{0,1:T(8,128)}, u32[]{:S(2)}) copy-start(s32[256,8]{0,1:T(8,128)} %param.13) | copy-start | bytes 24580
  194.4 27.0 %copy-start.51 = (f32[256]{0:T(256)}, f32[256]{0:T(256)S(1)}, u32[]{:S(2)}) copy-start(f32[256]{0:T(256)S(1)} %fusion.54) | copy-start | bytes 3076
  194.4 27.0 %copy-start.42 = (bf16[256,8]{0,1:T(8,128)(2,1)}, bf16[256,8]{0,1:T(8,128)(2,1)S(1)}, u32[]{:S(2)}) copy-start(bf16[256,8]{0,1:T(8,128)(2,1)S(1)} %fusion.71) | copy-start | bytes 12292
  221.4 14.3 copy-start.41
  221.4 114.5 %all-to-all-start.2 = ((bf16[20,153,1536]{2,1,0:T(8,128)(2,1)}), bf16[20,153,1536]{2,1,0:T(8,128)(2,1)}, u32[]{:S(2)}, u32[]{:S(2)}) async-start(bf16[20,153,1536]{2,1,0:T(8,128)(2,1)} %multiply_convert_fusion), calls=%async_computation.2 | async-start | bytes 19660800 | tf_op jit(solution)/shard_map/all_to_all | solution.py:181
  335.9 114.9 %all-to-all-start = ((bf16[20,153,1536]{2,1,0:T(8,128)(2,1)}), bf16[20,153,1536]{2,1,0:T(8,128)(2,1)}, u32[]{:S(2)}, u32[]{:S(2)}) async-start(bf16[20,153,1536]{2,1,0:T(8,128)(2,1)} %broadcast_select_fusion), calls=%async_computation | async-start | bytes 19660800 | tf_op jit(solution)/shard_map/all_to_all | solution.py:161
  527.6 6.9 copy-start.44
  527.6 171.3 %all-to-all-start.1 = ((bf16[5,612,1536]{2,0,1:T(8,128)(2,1)}), bf16[5,612,1536]{2,0,1:T(8,128)(2,1)}, u32[]{:S(2)}, u32[]{:S(2)}) async-start(bf16[5,612,1536]{2,0,1:T(8,128)(2,1)} %copy.138), calls=%async_computation.1 | async-start | bytes 30081024 | tf_op jit(solution)/shard_map/all_to_all | solution.py:172
  534.5 597.6 %reduce-scatter.16.cloned.1.call-start = ((), (), s32[]{:S(2)}) async-start(), calls=%async_computation.15 | async-start | bytes 811008
  719.9 18.3 %copy-start.12 = (bf16[256,1536]{1,0:T(8,128)(2,1)S(1)}, bf16[256,1536]{1,0:T(8,128)(2,1)}, u32[]{:S(2)}) copy-start(bf16[256,1536]{1,0:T(8,128)(2,1)} %param.12) | copy-start | bytes 2359300
  738.3 6.3 copy-start.31
  738.3 6.3 copy-start.48
  738.3 6.3 copy-start.52
  738.3 6.4 copy-start.33
  746.1 387.5 %reduce-scatter.14.cloned.1.call-start = ((), (), s32[]{:S(2)}) async-start(), calls=%async_computation.14 | async-start | bytes 8847360 | tf_op jit(solution)/shard_map/reduce_scatter | solution.py:279
  759.2 476.1 %reduce-scatter.12.cloned.1.call-start = ((), (), s32[]{:S(2)}) async-start(), calls=%async_computation.13 | async-start | bytes 17694720 | tf_op jit(solution)/shard_map/reduce_scatter | solution.py:276
  817.2 6.9 copy-start.43
  817.2 171.4 %all-to-all-start.3 = ((bf16[5,612,1536]{2,0,1:T(8,128)(2,1)}), bf16[5,612,1536]{2,0,1:T(8,128)(2,1)}, u32[]{:S(2)}, u32[]{:S(2)}) async-start(bf16[5,612,1536]{2,0,1:T(8,128)(2,1)} %copy.145), calls=%async_computation.3 | async-start | bytes 30081024 | tf_op jit(solution)/shard_map/all_to_all | solution.py:200
  824.0 552.3 %reduce-scatter.10.cloned.1.call-start = ((), (), s32[]{:S(2)}) async-start(), calls=%async_computation.12 | async-start | bytes 9732096 | tf_op jit(solution)/shard_map/reduce_scatter | solution.py:270
  1027.8 7.2 copy-start.2
  1027.8 7.2 copy-start.22
  1027.8 7.2 copy-start.35
  1027.8 7.2 copy-start.50
  1035.8 11.7 copy-start.8
  1052.6 7.7 copy-start.18
  1052.6 501.0 %reduce-scatter.8.cloned.1.call-start = ((), (), s32[]{:S(2)}) async-start(), calls=%async_computation.11 | async-start | bytes 16220160 | tf_op jit(solution)/shard_map/reduce_scatter | solution.py:269
  1053.4 11.4 slice-start
  1060.3 4.5 copy-start.9
  1060.3 4.5 slice-start.1
  1064.8 2.8 copy-start.20
  1064.9 2.9 copy-start.24
  1064.9 2.9 copy-start.26
  1078.0 51.2 %copy-start.6 = (f32[256,1536]{1,0:T(8,128)S(1)}, f32[256,1536]{1,0:T(8,128)}, u32[]{:S(2)}) copy-start(f32[256,1536]{1,0:T(8,128)} %copy-done.5) | copy-start | bytes 4718596
  (20 other events, 27.4 us)
Sparse Core Ops, SparseCore 0:
  10.9 79.4 all-gather.3
  93.3 62.4 all-gather.5
  746.2 91.7 reduce-scatter.15
  841.4 138.9 reduce-scatter.13
  983.9 251.3 reduce-scatter.11
  1241.7 134.5 reduce-scatter.9
  1383.9 169.6 reduce-scatter.7
where the time goes:
time: 1570 us; the launch traced here: 1560 us
  waiting for transfers between devices  903 us (58%)
  local copies, waits for them, and re-layouts  279 us (18%)
  matrix products  147 us (9%)
  blocking collectives  127 us (8%)
  other arithmetic  63 us (4%)
  starting transfers between devices  26.2 us (2%)
    reduce_scatter x1, waiting for transfers between devices, on_device(): lax.psum_scatter(d_qkv_local, ('dp', 'expert'), scatter_dimension=0, tile...  177 us
    all_to_all x1, waiting for transfers between devices, on_device(): lax.all_to_all(grad_inputs, 'expert', split_axis=1, concat_axis=0, tiled=...  164 us
    all_to_all x1, waiting for transfers between devices, on_device(): lax.all_to_all(result_rows, 'expert', split_axis=1, concat_axis=0, tiled=...  164 us
    reduce_scatter x1, waiting for transfers between devices, on_device(): lax.psum_scatter(d_out_local, ('dp', 'expert'), scatter_dimension=0, tile...  137 us
    reduce_scatter x1, waiting for transfers between devices, on_device(): lax.psum_scatter(d_expert_in_local.astype(jnp.bfloat16), 'dp', scatter_di...  99 us
    all_to_all x1, waiting for transfers between devices, on_device(): lax.all_to_all(dispatch, 'expert', split_axis=0, concat_axis=1, tiled=True)  90.1 us
    unnamed x2, blocking collectives  85.7 us
    all_to_all x1, waiting for transfers between devices, on_device(): lax.all_to_all(grad_slots, 'expert', split_axis=0, concat_axis=1, tiled=T...  69.3 us
  transfers between devices with their start and end apart: 11, of which 7 were waited for; matrix products, arithmetic and copies ran while one was open for 19% of the time, Pallas kernels for 0%

commit v1 on v0

v1 whole, which is shorter than its diff:
```python
import jax
import jax.numpy as jnp
from jax import lax
from jax.sharding import PartitionSpec as P

H = 24
KV = 8
HD = 64
FE = 512
TOP = 8

EPSILON = 1e-06
THETA = 10000.0
NEGATIVE = -1e30
AXES = ("dp", "expert")
CORE, WIDE = 1, 2
LANES = 128

F32 = jnp.float32
BF16 = jnp.bfloat16


def rope_tables(length, head_size):
    half_size = head_size // 2
    frequency = THETA ** (-(jnp.arange(half_size, dtype=jnp.float32) * 2.0) / head_size)
    angles = jnp.arange(length, dtype=jnp.float32)[:, None] * frequency[None, :]
    return (jnp.cos(angles)[:, None, :], jnp.sin(angles)[:, None, :])


def rotate(values_in, cos_table, sin_table):
    half_size = values_in.shape[-1] // 2
    first_half = values_in[..., :half_size]
    second_half = values_in[..., half_size:]
    return jnp.concatenate(
        [
            first_half * cos_table - second_half * sin_table,
            second_half * cos_table + first_half * sin_table,
        ],
        axis=-1,
    )


def norm_back(grad_normed, normed_plain, recip_row, gain_row):
    scaled = grad_normed * gain_row
    gain_grad = jnp.sum(grad_normed * normed_plain, axis=0)
    back_part = recip_row * (
        scaled - normed_plain * jnp.mean(scaled * normed_plain, axis=-1, keepdims=True)
    )
    return (back_part, gain_grad)


def dot(left, right, dims):
    return lax.dot_general(left, right, (dims, ((), ())), preferred_element_type=F32)


class Net:
    def __init__(self):
        self.nd = lax.axis_size("dp")
        self.ne = lax.axis_size("expert")
        self.p = lax.axis_index("dp")
        self.e = lax.axis_index("expert")
        self.r = self.place_of(self.p)
        order = list(range(0, self.nd, 2)) + list(range(1, self.nd, 2))[::-1]
        nd, ne = self.nd, self.ne
        self.ring = {
            way: [
                (order[i] * ne + e, order[(i + way) % nd] * ne + e)
                for i in range(nd)
                for e in range(ne)
            ]
            for way in (1, -1)
        }
        self.pair = {
            bit: [(p * ne + e, p * ne + (e ^ bit)) for p in range(nd) for e in range(ne)]
            for bit in (CORE, WIDE)
        }

    def place_of(self, p):
        return jnp.where(p % 2 == 0, p // 2, self.nd - 1 - p // 2)

    def dp_of(self, r):
        r = r % self.nd
        return jnp.where(r < self.nd // 2, 2 * r, 2 * (self.nd - 1 - r) + 1)

    def step(self, value, way):
        return lax.ppermute(value, AXES, self.ring[way])

    def swap(self, value, bit):
        return lax.ppermute(value, AXES, self.pair[bit])


def gather_weight(net, block):
    rows, columns = block.shape
    half = net.nd // 2
    own = jnp.stack([block, net.swap(block, WIDE)])
    parts = {0: own}
    ahead, back = own, own
    for s in range(1, half):
        ahead = net.step(ahead, 1)
        back = net.step(back, -1)
        parts[-s] = ahead
        parts[s] = back
    parts[half] = jnp.stack([net.step(ahead[0], 1), net.step(back[1], -1)])
    full = jnp.zeros((net.nd, net.ne, rows, columns), block.dtype)
    core, wide = net.e % 2, net.e // 2
    for offset, mine in parts.items():
        other = net.swap(mine, CORE)
        low = jnp.where(core == 0, mine, other)
        high = jnp.where(core == 0, other, mine)
        both = jnp.stack([low, high], axis=1)
        both = jnp.where(wide == 0, both, both[::-1]).reshape(net.ne, rows, columns)
        full = lax.dynamic_update_slice(full, both[None], (net.dp_of(net.r + offset), 0, 0, 0))
    return full.reshape(net.nd * net.ne * rows, columns)


def gather_rows(net, value):
    across = net.swap(value, WIDE)
    return jnp.concatenate([value, net.swap(value, CORE), across, net.swap(across, CORE)], axis=0)


def return_rows(net, partial):
    own, beside, across, corner = jnp.split(partial, 4, axis=0)
    sent = jnp.concatenate([beside, corner], axis=0).astype(BF16)
    came_beside, came_corner = jnp.split(net.swap(sent, CORE), 2, axis=0)
    onward = (across + came_corner.astype(F32)).astype(BF16)
    came = net.swap(onward, WIDE)
    return own + came_beside.astype(F32) + came.astype(F32)


def ring_sum(net, make, way):
    came = None
    for s in range(net.nd - 1):
        came = net.step(make(net.dp_of(net.r - way * (1 + s)), came).astype(BF16), way)
    return make(net.p, came)


def plus(value, came):
    return value if came is None else value + came.astype(F32)


def scatter_weight(net, left, right):
    depth = left.shape[1]
    rows = depth // (net.nd * net.ne)
    columns = right.shape[1]
    core, wide = net.e % 2, net.e // 2
    blocks = left.T.reshape(net.nd, net.ne // 2, 2, rows, left.shape[0])

    def product(which):
        some = lax.dynamic_index_in_dim(blocks, which, 2, keepdims=False)
        some = some.reshape(depth // 2, left.shape[0])
        return dot(some, right, ((1,), (0,)))

    came = net.swap(product(1 - core).astype(BF16), CORE)
    first = (product(core) + came.astype(F32)).reshape(net.nd, 2, rows, columns)
    sent = lax.dynamic_index_in_dim(first, 1 - wide, 1, keepdims=False).astype(BF16)
    kept = lax.dynamic_index_in_dim(first, wide, 1, keepdims=False)
    second = kept + net.swap(sent, WIDE).astype(F32)
    half = columns // 2

    def way_sum(way, low, high):
        def make(place, came):
            mine = lax.dynamic_index_in_dim(second[:, :, low:high], place, 0, keepdims=False)
            return plus(mine, came)

        return ring_sum(net, make, way)

    return jnp.concatenate([way_sum(1, 0, half), way_sum(-1, half, columns)], axis=1)


def on_device(
    tokens,
    cotangent,
    routes,
    segments,
    w_qkv,
    w_out,
    router,
    gain_attn,
    gain_mlp,
    expert_in,
    expert_out,
):
    net = Net()
    length, width = tokens.shape
    local_count = expert_in.shape[0]
    experts_all = local_count * net.ne
    group_size = H // KV
    score_scale = HD ** (-0.5)
    wide_qkv = w_qkv.shape[1]

    small = jnp.concatenate([router, gain_attn[:, None], gain_mlp[:, None]], axis=1)
    small = jnp.pad(small, ((0, 0), (0, LANES - small.shape[1])))
    first_full = gather_weight(net, jnp.concatenate([w_qkv, small], axis=1))
    out_full = gather_weight(net, w_out)
    qkv_full = first_full[:, :wide_qkv]
    router_full = first_full[:, wide_qkv : wide_qkv + experts_all]
    gains = first_full[:, wide_qkv + experts_all : wide_qkv + experts_all + 2].T.astype(F32)
    gain_one, gain_two = gains[0], gains[1]

    upstream_all = gather_rows(net, cotangent)
    grad_act_plain = jnp.einsum("td,efd->etf", upstream_all, expert_out, preferred_element_type=F32)

    inputs = tokens.astype(F32)
    recip_one = lax.rsqrt(jnp.mean(inputs * inputs, axis=-1, keepdims=True) + EPSILON)
    plain_one = inputs * recip_one
    normed = (plain_one * gain_one).astype(BF16)
    project = jnp.dot(normed, qkv_full, preferred_element_type=F32)
    cos_table, sin_table = rope_tables(length, HD)
    queries = rotate(project[:, : H * HD].reshape(length, H, HD), cos_table, sin_table).astype(BF16)
    queries = queries.reshape(length, KV, group_size, HD)
    key_rows = rotate(
        project[:, H * HD : (H + KV) * HD].reshape(length, KV, HD), cos_table, sin_table
    ).astype(BF16)
    values = project[:, (H + KV) * HD :].reshape(length, KV, HD).astype(BF16)
    segment_row = segments[0]
    places = jnp.arange(length)
    allowed = (places[:, None] >= places[None, :]) & (segment_row[:, None] == segment_row[None, :])

    raw_scores = (
        jnp.einsum("tkgd,skd->kgts", queries, key_rows, preferred_element_type=F32) * score_scale
    )
    masked = jnp.where(allowed, raw_scores, NEGATIVE)
    row_peak = jnp.max(masked, axis=-1, keepdims=True)
    exponent = jnp.exp(masked - row_peak)
    prob_float = exponent / jnp.sum(exponent, axis=-1, keepdims=True)
    probability = prob_float.astype(BF16)
    mixed_heads = jnp.einsum("kgts,skd->tkgd", probability, values, preferred_element_type=F32)
    mixed_heads = mixed_heads.reshape(length, H * HD).astype(BF16)
    hidden_state = inputs + jnp.dot(mixed_heads, out_full, preferred_element_type=F32)
    recip_two = lax.rsqrt(jnp.mean(hidden_state * hidden_state, axis=-1, keepdims=True) + EPSILON)
    plain_two = hidden_state * recip_two
    normed_two = (plain_two * gain_two).astype(BF16)
    logits = jnp.dot(normed_two, router_full, preferred_element_type=F32)
    expert_ids = jnp.arange(experts_all, dtype=jnp.int32)
    chosen = jnp.any(routes[:, :, None] == expert_ids[None, None, :], axis=1)
    picked = jnp.where(chosen, logits, NEGATIVE)
    gate_exp = jnp.where(chosen, jnp.exp(picked - jnp.max(picked, axis=-1, keepdims=True)), 0.0)
    gate_float = gate_exp / jnp.sum(gate_exp, axis=-1, keepdims=True)
    gate_values = gate_float.astype(BF16)

    sent = jnp.concatenate(
        [normed_two, jnp.pad(gate_values, ((0, 0), (0, LANES - experts_all)))], axis=1
    )
    arrived = gather_rows(net, sent)
    rows_all = arrived[:, :width]
    gates = lax.dynamic_slice_in_dim(
        arrived[:, width : width + experts_all], net.e * local_count, local_count, axis=1
    )
    gates = gates.T.astype(F32)[:, :, None]
    gate_part = jnp.einsum("td,edf->etf", rows_all, expert_in[..., :FE], preferred_element_type=F32)
    up_part = jnp.einsum("td,edf->etf", rows_all, expert_in[..., FE:], preferred_element_type=F32)
    sigmoid_gate = jax.nn.sigmoid(gate_part)
    silu_gate = gate_part * sigmoid_gate
    act_float = silu_gate * up_part
    activated = (act_float * gates).astype(BF16)
    gate_grads = jnp.sum(act_float * grad_act_plain, axis=-1).T
    grad_act = grad_act_plain * gates
    grad_pre = jnp.concatenate(
        [
            grad_act * up_part * sigmoid_gate * (1.0 + gate_part * (1.0 - sigmoid_gate)),
            grad_act * silu_gate,
        ],
        axis=-1,
    ).astype(BF16)

    rows_turned = rows_all.T
    act_turned = jnp.swapaxes(activated, 1, 2)
    slice_in = width // net.nd
    slice_out = FE // net.nd
    tokens_all = rows_all.shape[0]

    def in_share(low, high):
        def make(place, came):
            some = lax.dynamic_slice_in_dim(rows_turned, place * slice_in, slice_in, axis=0)
            return plus(
                jnp.einsum("dt,etf->edf", some, grad_pre[..., low:high], preferred_element_type=F32),
                came,
            )

        return make

    def out_share(low, high):
        def make(place, came):
            some = lax.dynamic_slice_in_dim(act_turned, place * slice_out, slice_out, axis=1)
            some = some.reshape(local_count * slice_out, tokens_all)
            return plus(
                dot(some, upstream_all[:, low:high], ((1,), (0,))),
                came,
            )

        return make

    d_expert_out = jnp.concatenate(
        [
            ring_sum(net, out_share(0, width // 2), 1),
            ring_sum(net, out_share(width // 2, width), -1),
        ],
        axis=-1,
    ).reshape(local_count, slice_out, width)
    d_expert_in = jnp.concatenate(
        [ring_sum(net, in_share(0, FE), 1), ring_sum(net, in_share(FE, 2 * FE), -1)], axis=-1
    )

    grad_rows = jnp.einsum("etf,edf->td", grad_pre, expert_in, preferred_element_type=F32)
    spread = jnp.zeros((tokens_all, LANES), F32)
    spread = lax.dynamic_update_slice(spread, gate_grads, (0, net.e * local_count))
    returned = return_rows(net, jnp.concatenate([grad_rows, spread], axis=1))
    mixture = return_rows(
        net, jnp.einsum("etf,efd->td", activated, expert_out, preferred_element_type=F32)
    )
    activations = (hidden_state + mixture).astype(BF16)

    upstream_grad = cotangent.astype(F32)
    grad_normed_two = returned[:, :width]
    gate_grads = returned[:, width : width + experts_all].astype(BF16).astype(F32)
    centered = gate_grads - jnp.sum(gate_float * gate_grads, axis=-1, keepdims=True)
    logit_grad = (gate_float * centered).astype(BF16)
    grad_normed_two = grad_normed_two + dot(logit_grad, router_full, ((1,), (1,)))
    back_two, d_gain_second = norm_back(grad_normed_two, plain_two, recip_two, gain_two)
    grad_hidden = upstream_grad + back_two
    grad_branch = grad_hidden.astype(BF16)
    grad_mixed = dot(grad_branch, out_full, ((1,), (1,))).astype(BF16)
    grad_mixed = grad_mixed.reshape(length, KV, group_size, HD)

    grad_values = jnp.einsum("kgts,tkgd->skd", probability, grad_mixed, preferred_element_type=F32)
    grad_probs = jnp.einsum("tkgd,skd->kgts", grad_mixed, values, preferred_element_type=F32)
    delta_row = jnp.sum(prob_float * grad_probs, axis=-1, keepdims=True)
    grad_scores = (prob_float * (grad_probs - delta_row)).astype(BF16)
    grad_queries = (
        jnp.einsum("kgts,skd->tkgd", grad_scores, key_rows, preferred_element_type=F32)
        * score_scale
    )
    grad_keys = (
        jnp.einsum("kgts,tkgd->skd", grad_scores, queries, preferred_element_type=F32) * score_scale
    )
    grad_queries = rotate(grad_queries.reshape(length, H, HD), cos_table, -sin_table)
    grad_keys = rotate(grad_keys, cos_table, -sin_table)
    grad_project = jnp.concatenate(
        [
            grad_queries.reshape(length, H * HD),
            grad_keys.reshape(length, KV * HD),
            grad_values.reshape(length, KV * HD),
        ],
        axis=1,
    ).astype(BF16)
    grad_normed = dot(grad_project, qkv_full, ((1,), (1,)))
    back_one, d_gain_first = norm_back(grad_normed, plain_one, recip_one, gain_one)
    grad_tokens = grad_hidden + back_one

    d_qkv = scatter_weight(net, normed, grad_project)
    d_out = scatter_weight(net, mixed_heads, grad_branch)
    d_small_local = jnp.concatenate(
        [dot(normed_two, logit_grad, ((0,), (0,))), d_gain_first[:, None], d_gain_second[:, None]],
        axis=1,
    )
    d_small = lax.psum_scatter(d_small_local, AXES, scatter_dimension=0, tiled=True)
    return (
        activations,
        grad_tokens,
        d_qkv,
        d_out,
        d_small[:, :experts_all],
        d_small[:, experts_all],
        d_small[:, experts_all + 1],
        d_expert_in,
        d_expert_out,
    )


def solution(mesh):
    rows = P(AXES, None)
    return jax.shard_map(
        on_device,
        mesh=mesh,
        in_specs=(rows,) * 7
        + (P(AXES), P(AXES), P("expert", None, None), P("expert", None, None)),
        out_specs=(rows,) * 5
        + (P(AXES), P(AXES), P("expert", "dp", None), P("expert", "dp", None)),
        check_vma=False,
    )
```

time: 1570 us -> 745 us (0.47)
  waiting for transfers between devices: 903 us -> 332 us
  local copies, waits for them, and re-layouts: 279 us -> 48.5 us
  blocking collectives: 127 us -> 0 us
  starting transfers between devices: 26.2 us -> 90.4 us
  matrix products: 147 us -> 202 us
  other arithmetic: 63 us -> 46.9 us
    all_to_all x4 -> x0, waiting for transfers between devices: 488 us -> none  [the longest x1 164 us: on_device(): lax.all_to_all(grad_inputs, 'expert', split_axis=1, concat_axis=0, tiled=...]
    reduce_scatter x4 -> x0, waiting for transfers between devices: 413 us -> none  [the longest x1 177 us: on_device(): lax.psum_scatter(d_qkv_local, ('dp', 'expert'), scatter_dimension=0, tile...]
    ppermute x0 -> x104, waiting for transfers between devices: none -> 251 us  [the longest x72 203 us: step(): return lax.ppermute(value, AXES, self.ring[way])]
    gather x11 -> x0, local copies, waits for them, and re-layouts: 111 us -> none  [the longest x2 34.9 us: on_device(): upstream_grad[slot_token]]
    ppermute x0 -> x104, starting transfers between devices: none -> 90.3 us  [the longest x72 77.6 us: step(): return lax.ppermute(value, AXES, self.ring[way])]
    unnamed x2 -> x0, blocking collectives: 85.7 us -> none
    unnamed x8 -> x2, waiting for transfers between devices: 1.46 us -> 80.5 us
    all_to_all x6 -> x0, local copies, waits for them, and re-layouts: 63.1 us -> none  [the longest x2 18.6 us: on_device(): lax.all_to_all(dispatch, 'expert', split_axis=0, concat_axis=1, tiled=True)]
  transfers between devices with their start and end apart: 11 -> 105, of which waited for: 7 -> 52; matrix products, arithmetic and copies ran while one was open for 19% -> 28% of each run, Pallas kernels for 0% -> 0%
where the time goes in v1:
time: 745 us; the launch traced here: 736 us
  waiting for transfers between devices  332 us (45%)
  matrix products  202 us (27%)
  starting transfers between devices  90.4 us (12%)
  local copies, waits for them, and re-layouts  48.5 us (7%)
  other arithmetic  46.9 us (6%)
  between operations  17 us (2%)
    ppermute x72, waiting for transfers between devices, step(): return lax.ppermute(value, AXES, self.ring[way])  203 us
    unnamed x2, waiting for transfers between devices  80.5 us
    ppermute x72, starting transfers between devices, step(): return lax.ppermute(value, AXES, self.ring[way])  77.6 us
    dot_general x16, matrix products, make(): jnp.einsum('dt,etf->edf', some, grad_pre[..., low:high], preferred_elemen...  48.5 us
    ppermute x32, waiting for transfers between devices, swap(): return lax.ppermute(value, AXES, self.pair[bit])  48.5 us
    dot_general x24, matrix products, dot(): lax.dot_general(left, right, (dims, ((), ())), preferred_element_type=F32)  40.3 us
    dot_general x1, matrix products, on_device(): jnp.einsum('etf,edf->td', grad_pre, expert_in, preferred_element_type=F32)  23.8 us
    dot_general x1, matrix products, on_device(): jnp.einsum('td,efd->etf', upstream_all, expert_out, preferred_element_typ...  22.8 us
  transfers between devices with their start and end apart: 105, of which 52 were waited for; matrix products, arithmetic and copies ran while one was open for 28% of the time, Pallas kernels for 0%

profile of v1, /device:TPU:0, one launch (start us, length us, event | category | flops | bytes accessed | tf_op | source)
XLA Modules:
  0.0 736.4 jit_solution(11140883897863116124)
XLA Ops:
  7.2 3.0 collective-permute-start.17
  25.6 5.9 collective-permute-done.19
  36.4 12.0 %collective-permute-done.23 = bf16[2,48,1536]{2,1,0:T(8,128)(2,1)S(1)} collective-permute-done((bf16[2,48,1536]{2,1,0:T(8,128)(2,1)S(1)}, bf16[2,48,1536]{2,1,0:T(8,128)(2,1)S(1)}, u32[]{:S(2)}, u32[]{:S(2)}) %collective-permute-start.23) | collective-permute-done | bytes 294944 | tf_op jit(solution)/shard_map/ppermute | solution.py:86
  51.2 5.8 collective-permute-done.25
  59.4 5.3 collective-permute-done.27
  64.7 3.7 collective-permute-done.29
  77.5 7.4 %collective-permute-done.6 = bf16[2,48,2688]{2,1,0:T(8,128)(2,1)S(1)} collective-permute-done((bf16[2,48,2688]{2,1,0:T(8,128)(2,1)S(1)}, bf16[2,48,2688]{2,1,0:T(8,128)(2,1)S(1)}, u32[]{:S(2)}, u32[]{:S(2)}) %collective-permute-start.6) | collective-permute-done | bytes 516128 | tf_op jit(solution)/shard_map/ppermute | solution.py:86
  85.8 3.4 collective-permute-done.8
  94.5 8.0 %collective-permute-done.10 = bf16[2,48,2688]{2,1,0:T(8,128)(2,1)S(1)} collective-permute-done((bf16[2,48,2688]{2,1,0:T(8,128)(2,1)S(1)}, bf16[2,48,2688]{2,1,0:T(8,128)(2,1)S(1)}, u32[]{:S(2)}, u32[]{:S(2)}) %collective-permute-start.10) | collective-permute-done | bytes 516128 | tf_op jit(solution)/shard_map/ppermute | solution.py:86
  109.3 4.1 collective-permute-done.15
  126.1 6.0 fusion.242
  132.1 3.6 fusion.74
  144.6 18.6 %collective-permute-done.35 = bf16[256,1664]{1,0:T(8,128)(2,1)S(1)} collective-permute-done((bf16[256,1664]{1,0:T(8,128)(2,1)}, bf16[256,1664]{1,0:T(8,128)(2,1)S(1)}, u32[]{:S(2)}, u32[]{:S(2)}) %collective-permute-start.35) | collective-permute-done | bytes 852000 | tf_op jit(solution)/shard_map/ppermute | solution.py:89
  168.2 6.3 pad_maximum_fusion.2
  174.5 13.2 %fusion.13 = f32[1024,5,512]{0,2,1:T(8,128)} fusion(bf16[5,1536,1024]{2,1,0:T(8,128)(2,1)} %param.20, bf16[1024,1664]{1,0:T(8,128)(2,1)S(1)} %pad_maximum_fusion.2), kind=kOutput, calls=%fused_computation.26 | convolution fusion | flops 8053063680 | bytes 21495808 | tf_op jit(solution)/shard_map/td,edf->etf/dot_general | solution.py:251
  187.7 13.3 %fusion.15 = f32[1024,5,512]{0,2,1:T(8,128)} fusion(bf16[5,1536,1024]{2,1,0:T(8,128)(2,1)} %param.20, bf16[1024,1664]{1,0:T(8,128)(2,1)S(1)} %pad_maximum_fusion.2), kind=kOutput, calls=%fused_computation.28 | convolution fusion | flops 8053063680 | bytes 21495808 | tf_op jit(solution)/shard_map/td,edf->etf/dot_general | solution.py:250
  204.8 22.8 %fusion.5 = (f32[5,1024]{1,0:T(8,128)S(1)}, bf16[5,1024,512]{1,2,0:T(8,128)(2,1)}, bf16[5,1024,512]{1,2,0:T(8,128)(2,1)}, bf16[5,1024,512]{1,2,0:T(8,128)(2,1)}) fusion(f32[1024,5,512]{0,2,1:T(8,128)} %fusion.13, f32[1024,5,512]{0,2,1:T(8,128)} %fusion.15, f32[5,1024]{1,0:T(8,128)S(1)} %copy.333, bf16[5,512,1536]{2,1,0:T(8,128)(2,1)} %param.21, ...), kind=kOutput, calls=%fused_computation.10 | convolution fusion | flops 8102865920 | bytes 47751168 | tf_op jit(solution)/shard_map/td,efd->etf/dot_general | solution.py:201
  227.6 15.2 %fusion.244 = (bf16[1024,1536]{1,0:T(8,128)(2,1)}, f32[1024,1536]{1,0:T(8,128)}) fusion(bf16[5,1024,512]{1,2,0:T(8,128)(2,1)} %get-tuple-element.17, bf16[5,512,1536]{2,1,0:T(8,128)(2,1)} %param.21), kind=kOutput, calls=%fused_computation.491 | convolution fusion | flops 8054636544 | bytes 22544384 | tf_op jit(solution)/shard_map/etf,efd->td/dot_general | solution.py:309
  242.9 3.8 constant_dynamic-slice_fusion.7
  256.3 23.8 %fusion.26 = f32[1024,1536]{1,0:T(8,128)} fusion(bf16[5,1536,1024]{2,1,0:T(8,128)(2,1)} %param.20, bf16[5,1024,512]{1,2,0:T(8,128)(2,1)} %get-tuple-element.18, bf16[5,1024,512]{1,2,0:T(8,128)(2,1)} %get-tuple-element.16), kind=kOutput, calls=%fused_computation.48 | convolution fusion | flops 16127098880 | bytes 32505856 | tf_op jit(solution)/shard_map/etf,edf->td/dot_general | solution.py:304
  280.1 5.4 fusion.78
  287.8 3.2 dynamic_update_slice.67
  291.0 3.4 fusion.21
  303.2 8.6 %collective-permute-done.91 = bf16[320,768]{1,0:T(8,128)(2,1)S(1)} collective-permute-done((bf16[320,768]{1,0:T(8,128)(2,1)S(1)}, bf16[320,768]{1,0:T(8,128)(2,1)S(1)}, u32[]{:S(2)}, u32[]{:S(2)}) %collective-permute-start.91) | collective-permute-done | bytes 491552 | tf_op jit(solution)/shard_map/ppermute | solution.py:86
  312.5 6.7 collective-permute-done.98
  322.8 3.3 fusion.47
  327.6 4.3 fusion.41
  342.1 20.3 %collective-permute-done.93 = bf16[320,768]{1,0:T(8,128)(2,1)S(1)} collective-permute-done((bf16[320,768]{1,0:T(8,128)(2,1)S(1)}, bf16[320,768]{1,0:T(8,128)(2,1)S(1)}, u32[]{:S(2)}, u32[]{:S(2)}) %collective-permute-start.93) | collective-permute-done | bytes 491552 | tf_op jit(solution)/shard_map/ppermute | solution.py:86
  368.7 4.1 fusion.48
  373.4 4.4 fusion.42
  389.0 3.1 multiply_add_fusion
  393.9 6.6 fusion.22
  400.6 4.3 fusion.24
  416.5 3.1 convolution_convert_fusion.1
  424.0 3.2 fusion.63
  427.2 3.1 convolution_convert_fusion
  430.3 80.5 %reduce-scatter.4.cloned.1.call-done = f32[48,22]{1,0:T(8,128)} async-done(((f32[1536,22]{1,0:T(8,128)}), f32[48,22]{1,0:T(8,128)}) %reduce-scatter.4.cloned.1.call-update) | async-done | bytes 4240
  514.4 5.0 fusion.49
  520.9 3.3 fusion.43
  529.9 14.1 %collective-permute-done.79 = bf16[5,192,512]{2,1,0:T(8,128)(2,1)S(1)} collective-permute-done((bf16[5,192,512]{2,1,0:T(8,128)(2,1)S(1)}, bf16[5,192,512]{2,1,0:T(8,128)(2,1)S(1)}, u32[]{:S(2)}, u32[]{:S(2)}) %collective-permute-start.79) | collective-permute-done | bytes 983072 | tf_op jit(solution)/shard_map/ppermute | solution.py:86
  560.2 14.9 %collective-permute-done.80 = bf16[5,192,512]{2,1,0:T(8,128)(2,1)S(1)} collective-permute-done((bf16[5,192,512]{2,1,0:T(8,128)(2,1)S(1)}, bf16[5,192,512]{2,1,0:T(8,128)(2,1)S(1)}, u32[]{:S(2)}, u32[]{:S(2)}) %collective-permute-start.80) | collective-permute-done | bytes 983072 | tf_op jit(solution)/shard_map/ppermute | solution.py:86
  587.9 12.4 %collective-permute-done.81 = bf16[5,192,512]{2,1,0:T(8,128)(2,1)S(1)} collective-permute-done((bf16[5,192,512]{2,1,0:T(8,128)(2,1)S(1)}, bf16[5,192,512]{2,1,0:T(8,128)(2,1)S(1)}, u32[]{:S(2)}, u32[]{:S(2)}) %collective-permute-start.81) | collective-permute-done | bytes 983072 | tf_op jit(solution)/shard_map/ppermute | solution.py:86
  607.0 4.6 collective-permute-done.61
  614.4 11.7 %collective-permute-done.62 = bf16[48,768]{1,0:T(8,128)(2,1)S(1)} collective-permute-done((bf16[48,768]{1,0:T(8,128)(2,1)S(1)}, bf16[48,768]{1,0:T(8,128)(2,1)S(1)}, u32[]{:S(2)}, u32[]{:S(2)}) %collective-permute-start.62) | collective-permute-done | bytes 73760 | tf_op jit(solution)/shard_map/ppermute | solution.py:86
  665.8 22.8 %collective-permute-done.45 = bf16[8,48,2560]{2,1,0:T(8,128)(2,1)S(1)} collective-permute-done((bf16[8,48,2560]{2,1,0:T(8,128)(2,1)S(1)}, bf16[8,48,2560]{2,1,0:T(8,128)(2,1)S(1)}, u32[]{:S(2)}, u32[]{:S(2)}) %collective-permute-start.45) | collective-permute-done | bytes 1966112 | tf_op jit(solution)/shard_map/ppermute | solution.py:89
  691.8 3.2 collective-permute-done.46
  702.2 3.1 collective-permute-done.48
  707.5 4.0 collective-permute-done.49
  (623 shorter events, 267.3 us)
Async XLA Ops:
  7.2 503.6 %reduce-scatter.4.cloned.1.call-start = ((), (), s32[]{:S(2)}) async-start(), calls=%async_computation.1 | async-start | bytes 811008
  13.7 128.8 %collective-permute-start.40 = (bf16[256,1536]{1,0:T(8,128)(2,1)}, bf16[256,1536]{1,0:T(8,128)(2,1)}, u32[]{:S(2)}, u32[]{:S(2)}) collective-permute-start(bf16[256,1536]{1,0:T(8,128)(2,1)} %param.12), channel_id=1, source_target_pairs={{0,2},{1,3},{2,0},{3,1},{4,6},{5,7},{6,4},{7,5},{8,10},{9,11},{10,... | collective-permute-start | bytes 2359304 | tf_op jit(solution)/shard_map/ppermute | solution.py:89
  23.8 26.1 %collective-permute-start.1 = (bf16[2,48,2688]{2,1,0:T(8,128)(2,1)S(1)}, bf16[2,48,2688]{2,1,0:T(8,128)(2,1)S(1)}, u32[]{:S(2)}, u32[]{:S(2)}) collective-permute-start(bf16[2,48,2688]{2,1,0:T(8,128)(2,1)S(1)} %pad_maximum_fusion.26), channel_id=1, source_target_pairs={{0,1},{1,0},{2,3},{3,2},{4,5},{5,4},{6,7},{7,6},{8,9},{9,8},{10,11... | collective-permute-start | bytes 1548296 | tf_op jit(solution)/shard_map/ppermute | solution.py:89
  23.9 35.0 %collective-permute-start.2 = (bf16[2,48,2688]{2,1,0:T(8,128)(2,1)S(1)}, bf16[2,48,2688]{2,1,0:T(8,128)(2,1)S(1)}, u32[]{:S(2)}, u32[]{:S(2)}) collective-permute-start(bf16[2,48,2688]{2,1,0:T(8,128)(2,1)S(1)} %pad_maximum_fusion.26), channel_id=1, source_target_pairs={{0,8},{1,9},{2,10},{3,11},{8,16},{9,17},{10,18},{11,19},{16,24},{1... | collective-permute-start | bytes 1548296 | tf_op jit(solution)/shard_map/ppermute | solution.py:86
  32.3 38.5 %collective-permute-start.4 = (bf16[2,48,2688]{2,1,0:T(8,128)(2,1)S(1)}, bf16[2,48,2688]{2,1,0:T(8,128)(2,1)S(1)}, u32[]{:S(2)}, u32[]{:S(2)}) collective-permute-start(bf16[2,48,2688]{2,1,0:T(8,128)(2,1)S(1)} %pad_maximum_fusion.26), channel_id=1, source_target_pairs={{0,4},{1,5},{2,6},{3,7},{8,0},{9,1},{10,2},{11,3},{16,8},{17,9},{1... | collective-permute-start | bytes 1548296 | tf_op jit(solution)/shard_map/ppermute | solution.py:86
  70.8 14.1 %collective-permute-start.6 = (bf16[2,48,2688]{2,1,0:T(8,128)(2,1)S(1)}, bf16[2,48,2688]{2,1,0:T(8,128)(2,1)S(1)}, u32[]{:S(2)}, u32[]{:S(2)}) collective-permute-start(bf16[2,48,2688]{2,1,0:T(8,128)(2,1)S(1)} %collective-permute-done.2), channel_id=1, source_target_pairs={{0,8},{1,9},{2,10},{3,11},{8,16},{9,17},{10,18},{11,19},{16,24},{1... | collective-permute-start | bytes 1548296 | tf_op jit(solution)/shard_map/ppermute | solution.py:86
  75.2 14.0 %collective-permute-start.8 = (bf16[2,48,2688]{2,1,0:T(8,128)(2,1)S(1)}, bf16[2,48,2688]{2,1,0:T(8,128)(2,1)S(1)}, u32[]{:S(2)}, u32[]{:S(2)}) collective-permute-start(bf16[2,48,2688]{2,1,0:T(8,128)(2,1)S(1)} %collective-permute-done.4), channel_id=1, source_target_pairs={{0,4},{1,5},{2,6},{3,7},{8,0},{9,1},{10,2},{11,3},{16,8},{17,9},{1... | collective-permute-start | bytes 1548296 | tf_op jit(solution)/shard_map/ppermute | solution.py:86
  90.8 15.6 %collective-permute-start.9 = (bf16[2,48,2688]{2,1,0:T(8,128)(2,1)S(1)}, bf16[2,48,2688]{2,1,0:T(8,128)(2,1)S(1)}, u32[]{:S(2)}, u32[]{:S(2)}) collective-permute-start(bf16[2,48,2688]{2,1,0:T(8,128)(2,1)S(1)} %collective-permute-done.8), channel_id=1, source_target_pairs={{0,1},{1,0},{2,3},{3,2},{4,5},{5,4},{6,7},{7,6},{8,9},{9,8},{10,11... | collective-permute-start | bytes 1548296 | tf_op jit(solution)/shard_map/ppermute | solution.py:89
  91.1 14.2 %collective-permute-start.12 = (bf16[2,48,2688]{2,1,0:T(8,128)(2,1)S(1)}, bf16[2,48,2688]{2,1,0:T(8,128)(2,1)S(1)}, u32[]{:S(2)}, u32[]{:S(2)}) collective-permute-start(bf16[2,48,2688]{2,1,0:T(8,128)(2,1)S(1)} %collective-permute-done.8), channel_id=1, source_target_pairs={{0,4},{1,5},{2,6},{3,7},{8,0},{9,1},{10,2},{11,3},{16,8},{17,9},{1... | collective-permute-start | bytes 1548296 | tf_op jit(solution)/shard_map/ppermute | solution.py:86
  142.0 21.2 %collective-permute-start.35 = (bf16[256,1664]{1,0:T(8,128)(2,1)}, bf16[256,1664]{1,0:T(8,128)(2,1)S(1)}, u32[]{:S(2)}, u32[]{:S(2)}) collective-permute-start(bf16[256,1664]{1,0:T(8,128)(2,1)} %pad_maximum_fusion.15), channel_id=1, source_target_pairs={{0,2},{1,3},{2,0},{3,1},{4,6},{5,7},{6,4},{7,5},{8,10},{9,11},{10,... | collective-permute-start | bytes 2555912 | tf_op jit(solution)/shard_map/ppermute | solution.py:89
  142.5 20.7 %collective-permute-start.39 = (bf16[256,1536]{1,0:T(8,128)(2,1)}, bf16[256,1536]{1,0:T(8,128)(2,1)}, u32[]{:S(2)}, u32[]{:S(2)}) collective-permute-start(bf16[256,1536]{1,0:T(8,128)(2,1)} %param.12), channel_id=1, source_target_pairs={{0,1},{1,0},{2,3},{3,2},{4,5},{5,4},{6,7},{7,6},{8,9},{9,8},{10,11... | collective-permute-start | bytes 2359304 | tf_op jit(solution)/shard_map/ppermute | solution.py:89
  142.5 23.4 %collective-permute-start.41 = (bf16[256,1536]{1,0:T(8,128)(2,1)}, bf16[256,1536]{1,0:T(8,128)(2,1)}, u32[]{:S(2)}, u32[]{:S(2)}) collective-permute-start(bf16[256,1536]{1,0:T(8,128)(2,1)} %collective-permute-done.40), channel_id=1, source_target_pairs={{0,1},{1,0},{2,3},{3,2},{4,5},{5,4},{6,7},{7,6},{8,9},{9,8},{10,11... | collective-permute-start | bytes 2359304 | tf_op jit(solution)/shard_map/ppermute | solution.py:89
  144.2 24.0 %collective-permute-start.34 = (bf16[256,1664]{1,0:T(8,128)(2,1)}, bf16[256,1664]{1,0:T(8,128)(2,1)S(1)}, u32[]{:S(2)}, u32[]{:S(2)}) collective-permute-start(bf16[256,1664]{1,0:T(8,128)(2,1)} %pad_maximum_fusion.15), channel_id=1, source_target_pairs={{0,1},{1,0},{2,3},{3,2},{4,5},{5,4},{6,7},{7,6},{8,9},{9,8},{10,11... | collective-permute-start | bytes 2555912 | tf_op jit(solution)/shard_map/ppermute | solution.py:89
  248.2 48.1 %collective-permute-start.90 = (bf16[320,768]{1,0:T(8,128)(2,1)}, bf16[320,768]{1,0:T(8,128)(2,1)}, u32[]{:S(2)}, u32[]{:S(2)}) collective-permute-start(bf16[320,768]{1,0:T(8,128)(2,1)} %convolution_convert_fusion.6), channel_id=1, source_target_pairs={{0,8},{1,9},{2,10},{3,11},{8,16},{9,17},{10,18},{11,19},{16,24},{1... | collective-permute-start | bytes 1474568 | tf_op jit(solution)/shard_map/ppermute | solution.py:86
  251.3 49.5 %collective-permute-start.97 = (bf16[320,768]{1,0:T(8,128)(2,1)}, bf16[320,768]{1,0:T(8,128)(2,1)}, u32[]{:S(2)}, u32[]{:S(2)}) collective-permute-start(bf16[320,768]{1,0:T(8,128)(2,1)} %convolution_convert_fusion.5), channel_id=1, source_target_pairs={{0,4},{1,5},{2,6},{3,7},{8,0},{9,1},{10,2},{11,3},{16,8},{17,9},{1... | collective-permute-start | bytes 1474568 | tf_op jit(solution)/shard_map/ppermute | solution.py:86
  254.7 67.5 %collective-permute-start.76 = (bf16[5,192,512]{2,1,0:T(8,128)(2,1)}, bf16[5,192,512]{2,1,0:T(8,128)(2,1)}, u32[]{:S(2)}, u32[]{:S(2)}) collective-permute-start(bf16[5,192,512]{2,1,0:T(8,128)(2,1)} %fusion.77), channel_id=1, source_target_pairs={{0,8},{1,9},{2,10},{3,11},{8,16},{9,17},{10,18},{11,19},{16,24},{1... | collective-permute-start | bytes 2949128 | tf_op jit(solution)/shard_map/ppermute | solution.py:86
  285.5 40.6 %collective-permute-start.83 = (bf16[5,192,512]{2,1,0:T(8,128)(2,1)}, bf16[5,192,512]{2,1,0:T(8,128)(2,1)}, u32[]{:S(2)}, u32[]{:S(2)}) collective-permute-start(bf16[5,192,512]{2,1,0:T(8,128)(2,1)} %fusion.78), channel_id=1, source_target_pairs={{0,4},{1,5},{2,6},{3,7},{8,0},{9,1},{10,2},{11,3},{16,8},{17,9},{1... | collective-permute-start | bytes 2949128 | tf_op jit(solution)/shard_map/ppermute | solution.py:86
  294.7 46.7 %collective-permute-start.42 = (bf16[512,1664]{1,0:T(8,128)(2,1)S(1)}, bf16[512,1664]{1,0:T(8,128)(2,1)S(1)}, u32[]{:S(2)}, u32[]{:S(2)}) collective-permute-start(bf16[512,1664]{1,0:T(8,128)(2,1)S(1)} %pad_maximum_fusion.4), channel_id=1, source_target_pairs={{0,1},{1,0},{2,3},{3,2},{4,5},{5,4},{6,7},{7,6},{8,9},{9,8},{10,11... | collective-permute-start | bytes 5111816 | tf_op jit(solution)/shard_map/ppermute | solution.py:89
  302.6 16.6 %collective-permute-start.98 = (bf16[320,768]{1,0:T(8,128)(2,1)S(1)}, bf16[320,768]{1,0:T(8,128)(2,1)S(1)}, u32[]{:S(2)}, u32[]{:S(2)}) collective-permute-start(bf16[320,768]{1,0:T(8,128)(2,1)S(1)} %fusion.90), channel_id=1, source_target_pairs={{0,4},{1,5},{2,6},{3,7},{8,0},{9,1},{10,2},{11,3},{16,8},{17,9},{1... | collective-permute-start | bytes 1474568 | tf_op jit(solution)/shard_map/ppermute | solution.py:86
  311.8 27.9 %collective-permute-start.37 = (bf16[512,1536]{1,0:T(8,128)(2,1)S(1)}, bf16[512,1536]{1,0:T(8,128)(2,1)S(1)}, u32[]{:S(2)}, u32[]{:S(2)}) collective-permute-start(bf16[512,1536]{1,0:T(8,128)(2,1)S(1)} %pad_maximum_fusion.5), channel_id=1, source_target_pairs={{0,1},{1,0},{2,3},{3,2},{4,5},{5,4},{6,7},{7,6},{8,9},{9,8},{10,11... | collective-permute-start | bytes 4718600 | tf_op jit(solution)/shard_map/ppermute | solution.py:89
  319.2 14.2 %collective-permute-start.92 = (bf16[320,768]{1,0:T(8,128)(2,1)S(1)}, bf16[320,768]{1,0:T(8,128)(2,1)S(1)}, u32[]{:S(2)}, u32[]{:S(2)}) collective-permute-start(bf16[320,768]{1,0:T(8,128)(2,1)S(1)} %fusion.83), channel_id=1, source_target_pairs={{0,8},{1,9},{2,10},{3,11},{8,16},{9,17},{10,18},{11,19},{16,24},{1... | collective-permute-start | bytes 1474568 | tf_op jit(solution)/shard_map/ppermute | solution.py:86
  322.2 14.1 %collective-permute-start.99 = (bf16[320,768]{1,0:T(8,128)(2,1)}, bf16[320,768]{1,0:T(8,128)(2,1)}, u32[]{:S(2)}, u32[]{:S(2)}) collective-permute-start(bf16[320,768]{1,0:T(8,128)(2,1)} %fusion.89), channel_id=1, source_target_pairs={{0,4},{1,5},{2,6},{3,7},{8,0},{9,1},{10,2},{11,3},{16,8},{17,9},{1... | collective-permute-start | bytes 1474568 | tf_op jit(solution)/shard_map/ppermute | solution.py:86
  326.1 41.0 %collective-permute-start.77 = (bf16[5,192,512]{2,1,0:T(8,128)(2,1)S(1)}, bf16[5,192,512]{2,1,0:T(8,128)(2,1)}, u32[]{:S(2)}, u32[]{:S(2)}) collective-permute-start(bf16[5,192,512]{2,1,0:T(8,128)(2,1)S(1)} %fusion.47), channel_id=1, source_target_pairs={{0,8},{1,9},{2,10},{3,11},{8,16},{9,17},{10,18},{11,19},{16,24},{1... | collective-permute-start | bytes 2949128 | tf_op jit(solution)/shard_map/ppermute | solution.py:86
  333.4 39.5 %collective-permute-start.84 = (bf16[5,192,512]{2,1,0:T(8,128)(2,1)}, bf16[5,192,512]{2,1,0:T(8,128)(2,1)}, u32[]{:S(2)}, u32[]{:S(2)}) collective-permute-start(bf16[5,192,512]{2,1,0:T(8,128)(2,1)} %fusion.41), channel_id=1, source_target_pairs={{0,4},{1,5},{2,6},{3,7},{8,0},{9,1},{10,2},{11,3},{16,8},{17,9},{1... | collective-permute-start | bytes 2949128 | tf_op jit(solution)/shard_map/ppermute | solution.py:86
  336.3 26.1 %collective-permute-start.93 = (bf16[320,768]{1,0:T(8,128)(2,1)S(1)}, bf16[320,768]{1,0:T(8,128)(2,1)S(1)}, u32[]{:S(2)}, u32[]{:S(2)}) collective-permute-start(bf16[320,768]{1,0:T(8,128)(2,1)S(1)} %fusion.82), channel_id=1, source_target_pairs={{0,8},{1,9},{2,10},{3,11},{8,16},{9,17},{10,18},{11,19},{16,24},{1... | collective-permute-start | bytes 1474568 | tf_op jit(solution)/shard_map/ppermute | solution.py:86
  339.8 25.5 %collective-permute-start.100 = (bf16[320,768]{1,0:T(8,128)(2,1)S(1)}, bf16[320,768]{1,0:T(8,128)(2,1)S(1)}, u32[]{:S(2)}, u32[]{:S(2)}) collective-permute-start(bf16[320,768]{1,0:T(8,128)(2,1)S(1)} %fusion.88), channel_id=1, source_target_pairs={{0,4},{1,5},{2,6},{3,7},{8,0},{9,1},{10,2},{11,3},{16,8},{17,9},{1... | collective-permute-start | bytes 1474568 | tf_op jit(solution)/shard_map/ppermute | solution.py:86
  341.3 47.7 %collective-permute-start.38 = (bf16[256,1536]{1,0:T(8,128)(2,1)}, bf16[256,1536]{1,0:T(8,128)(2,1)}, u32[]{:S(2)}, u32[]{:S(2)}) collective-permute-start(bf16[256,1536]{1,0:T(8,128)(2,1)} %fusion.66), channel_id=1, source_target_pairs={{0,2},{1,3},{2,0},{3,1},{4,6},{5,7},{6,4},{7,5},{8,10},{9,11},{10,... | collective-permute-start | bytes 2359304 | tf_op jit(solution)/shard_map/ppermute | solution.py:89
  362.4 21.8 %collective-permute-start.43 = (bf16[256,1664]{1,0:T(8,128)(2,1)S(1)}, bf16[256,1664]{1,0:T(8,128)(2,1)S(1)}, u32[]{:S(2)}, u32[]{:S(2)}) collective-permute-start(bf16[256,1664]{1,0:T(8,128)(2,1)S(1)} %fusion.58), channel_id=1, source_target_pairs={{0,2},{1,3},{2,0},{3,1},{4,6},{5,7},{6,4},{7,5},{8,10},{9,11},{10,... | collective-permute-start | bytes 2555912 | tf_op jit(solution)/shard_map/ppermute | solution.py:89
  367.2 14.4 %collective-permute-start.101 = (bf16[320,768]{1,0:T(8,128)(2,1)}, bf16[320,768]{1,0:T(8,128)(2,1)S(1)}, u32[]{:S(2)}, u32[]{:S(2)}) collective-permute-start(bf16[320,768]{1,0:T(8,128)(2,1)} %fusion.87), channel_id=1, source_target_pairs={{0,4},{1,5},{2,6},{3,7},{8,0},{9,1},{10,2},{11,3},{16,8},{17,9},{1... | collective-permute-start | bytes 1474568 | tf_op jit(solution)/shard_map/ppermute | solution.py:86
  372.9 141.4 %collective-permute-start.78 = (bf16[5,192,512]{2,1,0:T(8,128)(2,1)}, bf16[5,192,512]{2,1,0:T(8,128)(2,1)}, u32[]{:S(2)}, u32[]{:S(2)}) collective-permute-start(bf16[5,192,512]{2,1,0:T(8,128)(2,1)} %fusion.48), channel_id=1, source_target_pairs={{0,8},{1,9},{2,10},{3,11},{8,16},{9,17},{10,18},{11,19},{16,24},{1... | collective-permute-start | bytes 2949128 | tf_op jit(solution)/shard_map/ppermute | solution.py:86
  378.1 141.3 %collective-permute-start.85 = (bf16[5,192,512]{2,1,0:T(8,128)(2,1)}, bf16[5,192,512]{2,1,0:T(8,128)(2,1)}, u32[]{:S(2)}, u32[]{:S(2)}) collective-permute-start(bf16[5,192,512]{2,1,0:T(8,128)(2,1)} %fusion.42), channel_id=1, source_target_pairs={{0,4},{1,5},{2,6},{3,7},{8,0},{9,1},{10,2},{11,3},{16,8},{17,9},{1... | collective-permute-start | bytes 2949128 | tf_op jit(solution)/shard_map/ppermute | solution.py:86
  381.6 142.7 %collective-permute-start.95 = (bf16[320,768]{1,0:T(8,128)(2,1)}, bf16[320,768]{1,0:T(8,128)(2,1)}, u32[]{:S(2)}, u32[]{:S(2)}) collective-permute-start(bf16[320,768]{1,0:T(8,128)(2,1)} %fusion.80), channel_id=1, source_target_pairs={{0,8},{1,9},{2,10},{3,11},{8,16},{9,17},{10,18},{11,19},{16,24},{1... | collective-permute-start | bytes 1474568 | tf_op jit(solution)/shard_map/ppermute | solution.py:86
  384.2 142.6 %collective-permute-start.102 = (bf16[320,768]{1,0:T(8,128)(2,1)}, bf16[320,768]{1,0:T(8,128)(2,1)}, u32[]{:S(2)}, u32[]{:S(2)}) collective-permute-start(bf16[320,768]{1,0:T(8,128)(2,1)} %fusion.86), channel_id=1, source_target_pairs={{0,4},{1,5},{2,6},{3,7},{8,0},{9,1},{10,2},{11,3},{16,8},{17,9},{1... | collective-permute-start | bytes 1474568 | tf_op jit(solution)/shard_map/ppermute | solution.py:86
  419.7 162.6 %collective-permute-start.60 = (bf16[768,1536]{1,0:T(8,128)(2,1)}, bf16[768,1536]{1,0:T(8,128)(2,1)}, u32[]{:S(2)}, u32[]{:S(2)}) collective-permute-start(bf16[768,1536]{1,0:T(8,128)(2,1)} %convolution_convert_fusion.1), channel_id=1, source_target_pairs={{0,1},{1,0},{2,3},{3,2},{4,5},{5,4},{6,7},{7,6},{8,9},{9,8},{10,11... | collective-permute-start | bytes 7077896 | tf_op jit(solution)/shard_map/ppermute | solution.py:89
  514.3 134.9 %collective-permute-start.44 = (bf16[768,2560]{1,0:T(8,128)(2,1)}, bf16[768,2560]{1,0:T(8,128)(2,1)S(1)}, u32[]{:S(2)}, u32[]{:S(2)}) collective-permute-start(bf16[768,2560]{1,0:T(8,128)(2,1)} %convolution_convert_fusion), channel_id=1, source_target_pairs={{0,1},{1,0},{2,3},{3,2},{4,5},{5,4},{6,7},{7,6},{8,9},{9,8},{10,11... | collective-permute-start | bytes 11796488 | tf_op jit(solution)/shard_map/ppermute | solution.py:89
  519.4 24.6 %collective-permute-start.79 = (bf16[5,192,512]{2,1,0:T(8,128)(2,1)S(1)}, bf16[5,192,512]{2,1,0:T(8,128)(2,1)S(1)}, u32[]{:S(2)}, u32[]{:S(2)}) collective-permute-start(bf16[5,192,512]{2,1,0:T(8,128)(2,1)S(1)} %fusion.49), channel_id=1, source_target_pairs={{0,8},{1,9},{2,10},{3,11},{8,16},{9,17},{10,18},{11,19},{16,24},{1... | collective-permute-start | bytes 2949128 | tf_op jit(solution)/shard_map/ppermute | solution.py:86
  524.3 24.7 %collective-permute-start.86 = (bf16[5,192,512]{2,1,0:T(8,128)(2,1)S(1)}, bf16[5,192,512]{2,1,0:T(8,128)(2,1)S(1)}, u32[]{:S(2)}, u32[]{:S(2)}) collective-permute-start(bf16[5,192,512]{2,1,0:T(8,128)(2,1)S(1)} %fusion.43), channel_id=1, source_target_pairs={{0,4},{1,5},{2,6},{3,7},{8,0},{9,1},{10,2},{11,3},{16,8},{17,9},{1... | collective-permute-start | bytes 2949128 | tf_op jit(solution)/shard_map/ppermute | solution.py:86
  526.8 27.7 %collective-permute-start.96 = (bf16[320,768]{1,0:T(8,128)(2,1)S(1)}, bf16[320,768]{1,0:T(8,128)(2,1)S(1)}, u32[]{:S(2)}, u32[]{:S(2)}) collective-permute-start(bf16[320,768]{1,0:T(8,128)(2,1)S(1)} %fusion.79), channel_id=1, source_target_pairs={{0,8},{1,9},{2,10},{3,11},{8,16},{9,17},{10,18},{11,19},{16,24},{1... | collective-permute-start | bytes 1474568 | tf_op jit(solution)/shard_map/ppermute | solution.py:86
  544.0 15.4 %collective-permute-start.103 = (bf16[320,768]{1,0:T(8,128)(2,1)S(1)}, bf16[320,768]{1,0:T(8,128)(2,1)S(1)}, u32[]{:S(2)}, u32[]{:S(2)}) collective-permute-start(bf16[320,768]{1,0:T(8,128)(2,1)S(1)} %fusion.85), channel_id=1, source_target_pairs={{0,4},{1,5},{2,6},{3,7},{8,0},{9,1},{10,2},{11,3},{16,8},{17,9},{1... | collective-permute-start | bytes 1474568 | tf_op jit(solution)/shard_map/ppermute | solution.py:86
  548.9 26.1 %collective-permute-start.80 = (bf16[5,192,512]{2,1,0:T(8,128)(2,1)S(1)}, bf16[5,192,512]{2,1,0:T(8,128)(2,1)S(1)}, u32[]{:S(2)}, u32[]{:S(2)}) collective-permute-start(bf16[5,192,512]{2,1,0:T(8,128)(2,1)S(1)} %fusion.50), channel_id=1, source_target_pairs={{0,8},{1,9},{2,10},{3,11},{8,16},{9,17},{10,18},{11,19},{16,24},{1... | collective-permute-start | bytes 2949128 | tf_op jit(solution)/shard_map/ppermute | solution.py:86
  554.6 25.1 %collective-permute-start.87 = (bf16[5,192,512]{2,1,0:T(8,128)(2,1)S(1)}, bf16[5,192,512]{2,1,0:T(8,128)(2,1)S(1)}, u32[]{:S(2)}, u32[]{:S(2)}) collective-permute-start(bf16[5,192,512]{2,1,0:T(8,128)(2,1)S(1)} %fusion.44), channel_id=1, source_target_pairs={{0,4},{1,5},{2,6},{3,7},{8,0},{9,1},{10,2},{11,3},{16,8},{17,9},{1... | collective-permute-start | bytes 2949128 | tf_op jit(solution)/shard_map/ppermute | solution.py:86
  577.0 23.2 %collective-permute-start.81 = (bf16[5,192,512]{2,1,0:T(8,128)(2,1)S(1)}, bf16[5,192,512]{2,1,0:T(8,128)(2,1)S(1)}, u32[]{:S(2)}, u32[]{:S(2)}) collective-permute-start(bf16[5,192,512]{2,1,0:T(8,128)(2,1)S(1)} %fusion.51), channel_id=1, source_target_pairs={{0,8},{1,9},{2,10},{3,11},{8,16},{9,17},{10,18},{11,19},{16,24},{1... | collective-permute-start | bytes 2949128 | tf_op jit(solution)/shard_map/ppermute | solution.py:86
  581.6 22.9 %collective-permute-start.88 = (bf16[5,192,512]{2,1,0:T(8,128)(2,1)S(1)}, bf16[5,192,512]{2,1,0:T(8,128)(2,1)S(1)}, u32[]{:S(2)}, u32[]{:S(2)}) collective-permute-start(bf16[5,192,512]{2,1,0:T(8,128)(2,1)S(1)} %fusion.45), channel_id=1, source_target_pairs={{0,4},{1,5},{2,6},{3,7},{8,0},{9,1},{10,2},{11,3},{16,8},{17,9},{1... | collective-permute-start | bytes 2949128 | tf_op jit(solution)/shard_map/ppermute | solution.py:86
  584.9 26.8 %collective-permute-start.61 = (bf16[8,48,1536]{2,1,0:T(8,128)(2,1)S(1)}, bf16[8,48,1536]{2,1,0:T(8,128)(2,1)S(1)}, u32[]{:S(2)}, u32[]{:S(2)}) collective-permute-start(bf16[8,48,1536]{2,1,0:T(8,128)(2,1)S(1)} %fusion.99), channel_id=1, source_target_pairs={{0,2},{1,3},{2,0},{3,1},{4,6},{5,7},{6,4},{7,5},{8,10},{9,11},{10,... | collective-permute-start | bytes 3538952 | tf_op jit(solution)/shard_map/ppermute | solution.py:89
  602.3 57.3 %collective-permute-start.82 = (bf16[5,192,512]{2,1,0:T(8,128)(2,1)S(1)}, bf16[5,192,512]{2,1,0:T(8,128)(2,1)S(1)}, u32[]{:S(2)}, u32[]{:S(2)}) collective-permute-start(bf16[5,192,512]{2,1,0:T(8,128)(2,1)S(1)} %fusion.52), channel_id=1, source_target_pairs={{0,8},{1,9},{2,10},{3,11},{8,16},{9,17},{10,18},{11,19},{16,24},{1... | collective-permute-start | bytes 2949128 | tf_op jit(solution)/shard_map/ppermute | solution.py:86
  606.5 55.0 %collective-permute-start.89 = (bf16[5,192,512]{2,1,0:T(8,128)(2,1)S(1)}, bf16[5,192,512]{2,1,0:T(8,128)(2,1)S(1)}, u32[]{:S(2)}, u32[]{:S(2)}) collective-permute-start(bf16[5,192,512]{2,1,0:T(8,128)(2,1)S(1)} %fusion.46), channel_id=1, source_target_pairs={{0,4},{1,5},{2,6},{3,7},{8,0},{9,1},{10,2},{11,3},{16,8},{17,9},{1... | collective-permute-start | bytes 2949128 | tf_op jit(solution)/shard_map/ppermute | solution.py:86
  613.9 16.2 %collective-permute-start.69 = (bf16[48,768]{1,0:T(8,128)(2,1)S(1)}, bf16[48,768]{1,0:T(8,128)(2,1)S(1)}, u32[]{:S(2)}, u32[]{:S(2)}) collective-permute-start(bf16[48,768]{1,0:T(8,128)(2,1)S(1)} %fusion.192), channel_id=1, source_target_pairs={{0,4},{1,5},{2,6},{3,7},{8,0},{9,1},{10,2},{11,3},{16,8},{17,9},{1... | collective-permute-start | bytes 221192 | tf_op jit(solution)/shard_map/ppermute | solution.py:86
  650.7 37.9 %collective-permute-start.45 = (bf16[8,48,2560]{2,1,0:T(8,128)(2,1)S(1)}, bf16[8,48,2560]{2,1,0:T(8,128)(2,1)S(1)}, u32[]{:S(2)}, u32[]{:S(2)}) collective-permute-start(bf16[8,48,2560]{2,1,0:T(8,128)(2,1)S(1)} %fusion.40), channel_id=1, source_target_pairs={{0,2},{1,3},{2,0},{3,1},{4,6},{5,7},{6,4},{7,5},{8,10},{9,11},{10,... | collective-permute-start | bytes 5898248 | tf_op jit(solution)/shard_map/ppermute | solution.py:89
  (158 other events, 1749.3 us)
Sparse Core Ops, SparseCore 0:
  416.6 94.1 reduce-scatter.3

commit v2 on v1

v2 whole, which is shorter than its diff:
```python
import functools

import jax
import jax.numpy as jnp
from jax import lax
from jax.experimental import pallas as pl
from jax.experimental.pallas import tpu as pltpu
from jax.sharding import PartitionSpec as P

H = 24
KV = 8
HD = 64
FE = 512
TOP = 8

EPSILON = 1e-06
THETA = 10000.0
NEGATIVE = -1e30
AXES = ("dp", "expert")
CORE, WIDE = 1, 2
LANES = 128

F32 = jnp.float32
BF16 = jnp.bfloat16


def rope_tables(length):
    half_size = HD // 2
    frequency = THETA ** (-(jnp.arange(half_size, dtype=F32) * 2.0) / HD)
    angles = jnp.arange(length, dtype=F32)[:, None] * frequency[None, :]
    cos, sin = jnp.cos(angles), jnp.sin(angles)
    return (
        jnp.concatenate([cos] * (LANES // half_size), axis=1),
        jnp.concatenate([-sin, sin] * (LANES // HD), axis=1),
    )


def rotate_tile(tile, cos, sin):
    half_size = HD // 2
    lane = lax.broadcasted_iota(jnp.int32, tile.shape, 1)
    ahead = pltpu.roll(tile, LANES - half_size, 1)
    back = pltpu.roll(tile, half_size, 1)
    return tile * cos + jnp.where(lane % HD < half_size, ahead, back) * sin


def dot(left, right, dims=((1,), (0,))):
    return lax.dot_general(left, right, (dims, ((), ())), preferred_element_type=F32)


NT = ((1,), (1,))


def spread_row(row, lane, count):
    at = lax.broadcasted_iota(jnp.int32, (count, row.shape[1]), 0) == lane
    return jnp.where(at, jnp.broadcast_to(row, at.shape), 0.0).T


def call(kernel, out_shape, scratch=(), limit=40, name=None, specs=None, aliases=None):
    vmem = pl.BlockSpec(memory_space=pltpu.VMEM)
    return pl.pallas_call(
        kernel,
        out_shape=out_shape,
        in_specs=specs,
        out_specs=jax.tree.map(lambda _: vmem, out_shape),
        scratch_shapes=scratch,
        compiler_params=pltpu.CompilerParams(vmem_limit_bytes=limit * 2**20),
        cost_estimate=pl.CostEstimate(flops=1024, bytes_accessed=1024, transcendentals=0),
        name=name,
    )


VMEM_SPEC = pl.BlockSpec(memory_space=pltpu.VMEM)
ANY_SPEC = pl.BlockSpec(memory_space=pl.ANY)


def heads_of(array, group):
    size = H // KV
    first = group * size
    return jnp.concatenate(
        [array[:, h * HD : (h + 1) * HD] for h in range(first, first + size)], axis=0
    )


def group_softmax(queries, keys, bias):
    scores = dot(keys, queries, NT) * HD ** (-0.5)
    scores = jnp.where(bias > 0.0, scores, NEGATIVE)
    exponent = jnp.exp(scores - jnp.max(scores, axis=0, keepdims=True))
    return exponent * (1.0 / jnp.sum(exponent, axis=0, keepdims=True))


def attend_kernel(
    experts_all,
    tokens,
    bias,
    cos,
    sin,
    weight,
    normed,
    normed_turned,
    queries,
    key_rows,
    values,
    mixed,
    gains,
    project,
    held,
    sems,
):
    columns = weight.shape[1]
    wide = columns - LANES
    tile = held.shape[1] // sems.shape[0]
    copies = [
        pltpu.make_async_copy(
            weight.at[:, pl.ds(c * tile, tile)], held.at[:, pl.ds(c * tile, tile)], sems.at[c]
        )
        for c in range(sems.shape[0])
    ]
    for copy in copies[::-1]:
        copy.start()
    x = tokens[...].astype(F32)
    plain = x * lax.rsqrt(jnp.mean(x * x, axis=-1, keepdims=True) + EPSILON)
    copies[-1].wait()
    turned = held[:, wide:].astype(F32).T
    gains[...] = turned[experts_all // 8 * 8 : experts_all // 8 * 8 + 16]
    row = experts_all
    low = (plain * turned[row : row + 1]).astype(BF16)
    normed[...] = low
    normed_turned[...] = low.T
    for c in range(sems.shape[0] - 1, -1, -1):
        if c < sems.shape[0] - 1:
            copies[c].wait()
        at = slice(c * tile, (c + 1) * tile)
        project[:, at] = dot(low, held[:, at])
    c, s = cos[...], sin[...]
    for t in range(H * HD // LANES):
        at = slice(t * LANES, (t + 1) * LANES)
        queries[:, at] = rotate_tile(project[:, at], c, s).astype(BF16)
    for t in range(KV * HD // LANES):
        at = slice(t * LANES, (t + 1) * LANES)
        from_ = slice(H * HD + t * LANES, H * HD + (t + 1) * LANES)
        key_rows[:, at] = rotate_tile(project[:, from_], c, s).astype(BF16)
    values[...] = project[:, (H + KV) * HD : (H + 2 * KV) * HD].astype(BF16)
    size = H // KV
    length = tokens.shape[0]
    wide_bias = jnp.concatenate([bias[...]] * size, axis=1)
    for g in range(KV):
        at = slice(g * HD, (g + 1) * HD)
        probs = group_softmax(heads_of(queries, g), key_rows[:, at], wide_bias).astype(BF16)
        out = dot(values[:, at].T, probs)
        for j in range(size):
            h = g * size + j
            mixed[:, h * HD : (h + 1) * HD] = (
                out[:, j * length : (j + 1) * length].T.astype(BF16)
            )


def attend(experts_all, tokens, bias, cos, sin, weight):
    length, width = tokens.shape
    columns = weight.shape[1]
    shape = lambda *dims, kind=BF16: jax.ShapeDtypeStruct(dims, kind)
    out_shape = [
        shape(length, width),
        shape(width, length),
        shape(length, H * HD),
        shape(length, KV * HD),
        shape(length, KV * HD),
        shape(length, H * HD),
        shape(16, width, kind=F32),
    ]
    scratch = [
        pltpu.VMEM((length, columns), F32),
        pltpu.VMEM((width, columns), BF16),
        pltpu.SemaphoreType.DMA((7,)),
    ]
    return call(
        functools.partial(attend_kernel, experts_all),
        out_shape,
        scratch,
        limit=30,
        name="attend",
        specs=[VMEM_SPEC] * 4 + [ANY_SPEC],
    )(tokens, bias, cos, sin, weight)


def branch_kernel(
    gain_row,
    tokens,
    mixed,
    weight,
    small,
    gains,
    routes,
    hidden,
    sent,
    normed_turned,
    gate_float,
):
    width = tokens.shape[1]
    state = tokens[...].astype(F32) + dot(mixed[...], weight[...])
    hidden[...] = state
    recip = lax.rsqrt(jnp.mean(state * state, axis=-1, keepdims=True) + EPSILON)
    low = (state * recip * gains[gain_row : gain_row + 1, :]).astype(BF16)
    sent[:, :width] = low
    normed_turned[...] = low.T
    logits = dot(low, small[...])
    lanes = lax.broadcasted_iota(jnp.int32, logits.shape, 1)
    chosen = lanes < 0
    for j in range(routes.shape[1]):
        chosen = chosen | (lanes == routes[:, j : j + 1])
    picked = jnp.where(chosen, logits, NEGATIVE)
    exponent = jnp.where(chosen, jnp.exp(picked - jnp.max(picked, axis=-1, keepdims=True)), 0.0)
    gate = exponent / jnp.sum(exponent, axis=-1, keepdims=True)
    gate_float[...] = gate
    sent[:, width:] = gate.astype(BF16)


def branch(gain_row, tokens, mixed, weight, small, gains, routes):
    length, width = tokens.shape
    shape = lambda *dims, kind=BF16: jax.ShapeDtypeStruct(dims, kind)
    return call(
        functools.partial(branch_kernel, gain_row),
        [
            shape(length, width, kind=F32),
            shape(length, width + LANES),
            shape(width, length),
            shape(length, LANES, kind=F32),
        ],
        limit=20,
        name="branch",
        specs=[VMEM_SPEC] * 6,
    )(tokens, mixed, weight, small, gains, routes)


def owner_rows_kernel(extra_given, blocks, *refs):
    refs = refs[1:]
    left, weight = refs[:blocks], refs[blocks]
    extra = refs[blocks + 1 : 2 * blocks + 1] if extra_given else None
    out, total = refs[-2:]
    expert = pl.program_id(0)
    count = left[0].shape[1]
    width = total.shape[1]
    dims = NT if extra_given else ((1,), (0,))
    share = dot(jnp.concatenate([a[0] for a in left], axis=0), weight[0], dims)

    @pl.when(expert == 0)
    def _():
        total[...] = share

    @pl.when(expert > 0)
    def _():
        total[...] += share

    @pl.when(expert == pl.num_programs(0) - 1)
    def _():
        out[:, :width] = total[...].astype(BF16)
        if extra_given:
            for i in range(blocks):
                out[i * count : (i + 1) * count, width:] = extra[i][...].astype(BF16)


def owner_rows(devices, left, weight, extra=None):
    blocks = devices.shape[0]
    local, rows, inner = left.shape
    width = weight.shape[1] if extra is not None else weight.shape[2]
    columns = width if extra is None else width + LANES
    count = rows // 4
    out_shape = jax.ShapeDtypeStruct((blocks * count, columns), BF16)
    piece = lambda k: pl.BlockSpec((1, count, inner), lambda i, d: (i, d[k], 0))
    in_specs = [piece(k) for k in range(blocks)]
    in_specs.append(pl.BlockSpec((1,) + weight.shape[1:], lambda i, d: (i, 0, 0)))
    operands = [left] * blocks + [weight]
    if extra is not None:
        more = lambda k: pl.BlockSpec((count, LANES), lambda i, d: (d[k], 0))
        in_specs += [more(k) for k in range(blocks)]
        operands += [extra] * blocks
    return pl.pallas_call(
        functools.partial(owner_rows_kernel, extra is not None, blocks),
        out_shape=out_shape,
        grid_spec=pltpu.PrefetchScalarGridSpec(
            num_scalar_prefetch=1,
            grid=(local,),
            in_specs=in_specs,
            out_specs=pl.BlockSpec(out_shape.shape, lambda i, d: (0, 0)),
            scratch_shapes=[pltpu.VMEM((blocks * count, width), F32)],
        ),
        compiler_params=pltpu.CompilerParams(vmem_limit_bytes=30 * 2**20),
        cost_estimate=pl.CostEstimate(flops=1024, bytes_accessed=1024, transcendentals=0),
        name="owner_rows",
    )(devices.astype(jnp.int32), *operands)


def middle_kernel(
    experts_all,
    gain_row,
    kept,
    beside,
    came,
    cotangent,
    hidden,
    gate_float,
    normed_turned,
    gains,
    small,
    weight,
    grad_hidden,
    grad_branch,
    grad_mixed,
    extra,
):
    count, width = cotangent.shape
    total = kept[:count].astype(F32) + beside[:count].astype(F32) + came[...].astype(F32)
    gate = gate_float[...]
    gate_grad = total[:, width:].astype(BF16).astype(F32)
    centered = gate_grad - jnp.sum(gate * gate_grad, axis=-1, keepdims=True)
    logit_grad = (gate * centered).astype(BF16)
    grad_normed = total[:, :width] + dot(logit_grad, small[...], NT)
    state = hidden[...]
    recip = lax.rsqrt(jnp.mean(state * state, axis=-1, keepdims=True) + EPSILON)
    plain = state * recip
    scaled = grad_normed * gains[gain_row : gain_row + 1, :]
    gain_grad = jnp.sum(grad_normed * plain, axis=0, keepdims=True)
    back = recip * (scaled - plain * jnp.mean(scaled * plain, axis=-1, keepdims=True))
    grad = cotangent[...].astype(F32) + back
    grad_hidden[...] = grad
    low = grad.astype(BF16)
    grad_branch[...] = low
    grad_mixed[...] = dot(low, weight[...], NT).astype(BF16)
    extra[...] = dot(normed_turned[...], logit_grad) + spread_row(gain_grad, experts_all, LANES)


def attend_back_kernel(
    gain_row,
    tokens,
    queries,
    key_rows,
    values,
    grad_mixed,
    bias,
    cos,
    sin,
    gains,
    grad_hidden,
    weight,
    grad_project,
    grad_tokens,
    extra,
    project,
    held,
    sem,
):
    columns = grad_project.shape[1]
    copy = pltpu.make_async_copy(weight.at[:, pl.ds(0, columns)], held, sem)
    copy.start()
    size = H // KV
    length = tokens.shape[0]
    scale = HD ** (-0.5)
    wide_bias = jnp.concatenate([bias[...]] * size, axis=1)
    for g in range(KV):
        at = slice(g * HD, (g + 1) * HD)
        q, k, v = heads_of(queries, g), key_rows[:, at], values[:, at]
        upstream = heads_of(grad_mixed, g)
        weights = group_softmax(q, k, wide_bias)
        grad_values = dot(weights.astype(BF16), upstream)
        grad_probs = dot(v, upstream, NT)
        delta = jnp.sum(weights * grad_probs, axis=0, keepdims=True)
        grad_scores = (weights * (grad_probs - delta)).astype(BF16)
        grad_keys = dot(grad_scores, q) * scale
        grad_queries = dot(k.T, grad_scores) * scale
        for j in range(size):
            h = g * size + j
            project[:, h * HD : (h + 1) * HD] = grad_queries[:, j * length : (j + 1) * length].T
        project[:, (H + g) * HD : (H + g + 1) * HD] = grad_keys
        project[:, (H + KV + g) * HD : (H + KV + g + 1) * HD] = grad_values
    c, s = cos[...], -sin[...]
    turns = (H + KV) * HD // LANES
    for t in range(turns):
        at = slice(t * LANES, (t + 1) * LANES)
        grad_project[:, at] = rotate_tile(project[:, at], c, s).astype(BF16)
    rest = slice(turns * LANES, columns)
    grad_project[:, rest] = project[:, rest].astype(BF16)
    copy.wait()
    grad_normed = dot(grad_project[...], held[...], NT)
    x = tokens[...].astype(F32)
    recip = lax.rsqrt(jnp.mean(x * x, axis=-1, keepdims=True) + EPSILON)
    plain = x * recip
    scaled = grad_normed * gains[gain_row : gain_row + 1, :]
    gain_grad = jnp.sum(grad_normed * plain, axis=0, keepdims=True)
    back = recip * (scaled - plain * jnp.mean(scaled * plain, axis=-1, keepdims=True))
    grad_tokens[...] = grad_hidden[...] + back
    extra[...] = spread_row(gain_grad, 0, LANES)


def middle(experts_all, gain_row, *operands):
    count, width = operands[3].shape
    shape = lambda *dims, kind=BF16: jax.ShapeDtypeStruct(dims, kind)
    return call(
        functools.partial(middle_kernel, experts_all, gain_row),
        [
            shape(count, width, kind=F32),
            shape(count, width),
            shape(count, width),
            shape(width, LANES, kind=F32),
        ],
        limit=24,
        name="middle",
        specs=[VMEM_SPEC] * 10,
    )(*operands)


def attend_back(gain_row, *operands):
    length, width = operands[0].shape
    columns = (H + 2 * KV) * HD
    shape = lambda *dims, kind=BF16: jax.ShapeDtypeStruct(dims, kind)
    return call(
        functools.partial(attend_back_kernel, gain_row),
        [
            shape(length, columns),
            shape(length, width, kind=F32),
            shape(width, LANES, kind=F32),
        ],
        [
            pltpu.VMEM((length, columns), F32),
            pltpu.VMEM((width, columns), BF16),
            pltpu.SemaphoreType.DMA,
        ],
        limit=32,
        name="attend_back",
        specs=[VMEM_SPEC] * 10 + [ANY_SPEC],
    )(*operands)


def after(value, *earlier):
    return lax.optimization_barrier((value, earlier))[0]


class Net:
    def __init__(self):
        self.nd = lax.axis_size("dp")
        self.ne = lax.axis_size("expert")
        self.p = lax.axis_index("dp")
        self.e = lax.axis_index("expert")
        self.r = self.place_of(self.p)
        order = list(range(0, self.nd, 2)) + list(range(1, self.nd, 2))[::-1]
        nd, ne = self.nd, self.ne
        self.ring = {
            way: [
                (order[i] * ne + e, order[(i + way) % nd] * ne + e)
                for i in range(nd)
                for e in range(ne)
            ]
            for way in (1, -1)
        }
        self.devices = nd * ne

    def place_of(self, p):
        return jnp.where(p % 2 == 0, p // 2, self.nd - 1 - p // 2)

    def dp_of(self, r):
        r = r % self.nd
        return jnp.where(r < self.nd // 2, 2 * r, 2 * (self.nd - 1 - r) + 1)

    def step(self, value, way):
        return lax.ppermute(value, AXES, self.ring[way])

    def exchange(self, value, bit):
        pairs = [[d, d | 1 << bit] for d in range(self.devices) if not d >> bit & 1]
        return lax.all_to_all(value, AXES, 0, 0, axis_index_groups=pairs, tiled=True)

    def swap(self, value, bit):
        return lax.ppermute(value, AXES, [(d, d ^ bit) for d in range(self.devices)])


def gather_weights(net, first, second, beside):
    half = net.nd // 2
    other_first = net.swap(first, WIDE)
    other_second = net.swap(after(second, other_first), WIDE)
    own = [jnp.stack([first, other_first]), jnp.stack([second, other_second])]
    offsets = [(0,)] + [(-s, s) for s in range(1, half)] + [(half,)]
    parts = [[], []]
    ahead, back = list(own), list(own)
    sent = None
    for s in range(half + 1):
        for k in (0, 1):
            if k == 0 and s == half - 1:
                ahead[k], back[k] = after((ahead[k], back[k]), beside)
            elif sent is not None:
                ahead[k], back[k] = after((ahead[k], back[k]), sent)
            sent = (ahead[k], back[k])
            if s in (0, half):
                parts[k].append((ahead[k] if s == 0 else jnp.stack([ahead[k], back[k]]))[None])
            else:
                parts[k].append(jnp.stack([ahead[k], back[k]]))
            if s + 1 < half:
                ahead[k] = net.step(ahead[k], 1)
                back[k] = net.step(back[k], -1)
            elif s + 1 == half:
                ahead[k] = net.step(ahead[k][0], 1)
                back[k] = net.step(back[k][1], -1)
    core, wide = net.e % 2, net.e // 2

    def assemble(pieces):
        rows, columns = pieces[0][1].shape[-2:]
        full = jnp.zeros((net.nd, net.ne, rows, columns), BF16)
        for places, mine, other in pieces:
            low = jnp.where(core == 0, mine, other)
            high = jnp.where(core == 0, other, mine)
            both = jnp.stack([low, high], axis=2)
            both = jnp.where(wide == 0, both, both[:, ::-1]).reshape(-1, net.ne, rows, columns)
            for i, offset in enumerate(places):
                at = (net.dp_of(net.r + offset), 0, 0, 0)
                full = lax.dynamic_update_slice(full, both[i : i + 1], at)
        return full.reshape(net.nd * net.ne * rows, columns)

    first_full = assemble(
        [(offsets[i], mine, net.swap(mine, CORE)) for i, mine in enumerate(parts[0])]
    )
    mine = jnp.concatenate(parts[1])
    places = [o for group in offsets for o in group]
    second_full = assemble([(places, mine, net.swap(mine, CORE))])
    return first_full, second_full


def weight_product_kernel(left, extra, right, out):
    columns = right.shape[1]
    out[0, :, :columns] = dot(left[0], right[...]).astype(BF16)
    out[0, :, columns:] = extra[0].astype(BF16)


def weight_product(left, extra, right):
    parts, depth = left.shape[:2]
    columns = right.shape[1] + extra.shape[2]
    return pl.pallas_call(
        weight_product_kernel,
        out_shape=jax.ShapeDtypeStruct((parts, depth, columns), BF16),
        grid=(parts,),
        in_specs=[
            pl.BlockSpec((1,) + left.shape[1:], lambda i: (i, 0, 0)),
            pl.BlockSpec((1,) + extra.shape[1:], lambda i: (i, 0, 0)),
            pl.BlockSpec(right.shape, lambda i: (0, 0)),
        ],
        out_specs=pl.BlockSpec((1, depth, columns), lambda i: (i, 0, 0)),
        compiler_params=pltpu.CompilerParams(vmem_limit_bytes=20 * 2**20),
        cost_estimate=pl.CostEstimate(flops=1024, bytes_accessed=1024, transcendentals=0),
        name="weight_product",
    )(left, extra, right)


def parts_by(array, parts, rows):
    blocks = array.reshape(-1, parts, rows, array.shape[1])
    return jnp.swapaxes(blocks, 0, 1).reshape(parts, -1, array.shape[1])


def halve_kernel(mine, kept, came, out):
    for i in range(2):
        out[i, 0] = (kept[0, i].astype(F32) + came[0, i].astype(F32)).astype(BF16)


def halve(kept, came, rows):
    columns = kept.shape[1]
    kept, came = (a.reshape(-1, 2, rows, columns) for a in (kept, came))
    count = kept.shape[0]
    piece = pl.BlockSpec((1, 2, rows, columns), lambda i: (i, 0, 0, 0))
    return pl.pallas_call(
        functools.partial(halve_kernel, None),
        out_shape=jax.ShapeDtypeStruct((2, count, rows, columns), BF16),
        grid=(count,),
        in_specs=[piece, piece],
        out_specs=pl.BlockSpec((2, 1, rows, columns), lambda i: (0, i, 0, 0)),
        compiler_params=pltpu.CompilerParams(vmem_limit_bytes=12 * 2**20),
        cost_estimate=pl.CostEstimate(flops=1024, bytes_accessed=1024, transcendentals=0),
        name="halve",
    )(kept, came).reshape(2, count * rows, columns)


class BlockSum:
    def __init__(self, net, halves, bit, rows):
        self.net, self.halves, self.bit, self.rows = net, halves, bit, rows
        self.count = net.devices.bit_length() - 1
        self.number = net.p * net.ne + net.e

    def send(self, *earlier):
        mine = self.number // (1 << self.bit) % 2
        halves = after(self.halves, *earlier) if earlier else self.halves
        self.kept = lax.dynamic_index_in_dim(halves, mine, 0, keepdims=False)
        sent = lax.dynamic_index_in_dim(halves, 1 - mine, 0, keepdims=False)
        self.came = self.net.swap(sent, 1 << self.bit)
        self.bit += 1

    def add(self, *earlier):
        came = after(self.came, *earlier) if earlier else self.came
        if self.bit == self.count:
            return self.kept.astype(F32) + came.astype(F32)
        self.halves = halve(self.kept, came, self.rows)
        return self.halves


def in_kernel(places, rows_a, rows_b, grad_pre, *refs):
    came, out = (refs[:2], refs[2:]) if len(refs) > 2 else (None, refs)
    for i, rows in enumerate((rows_a, rows_b)):
        at = slice(i * FE, (i + 1) * FE)
        share = dot(rows[...], grad_pre[0, :, at])
        if came is not None:
            share += came[i][0].astype(F32)
        if len(out) == 2:
            out[i][0] = share.astype(BF16)
        else:
            out[0][0, :, at] = share


def in_share(places, turned_rows, grad_pre, came, last=False):
    local, tokens_all, wide = grad_pre.shape
    depth = turned_rows.shape[0] // lax.axis_size("dp")
    piece = pl.BlockSpec((1, depth, FE), lambda i, place: (i, 0, 0))
    in_specs = [
        pl.BlockSpec((depth, tokens_all), lambda i, place: (place[0], 0)),
        pl.BlockSpec((depth, tokens_all), lambda i, place: (place[1], 0)),
        pl.BlockSpec((1, tokens_all, wide), lambda i, place: (i, 0, 0)),
    ] + [piece] * len(came)
    if last:
        out_shape = [jax.ShapeDtypeStruct((local, depth, wide), F32)]
        out_specs = [pl.BlockSpec((1, depth, wide), lambda i, place: (i, 0, 0))]
    else:
        out_shape = [jax.ShapeDtypeStruct((local, depth, FE), BF16)] * 2
        out_specs = [piece] * 2
    return pl.pallas_call(
        in_kernel,
        out_shape=out_shape,
        grid_spec=pltpu.PrefetchScalarGridSpec(
            num_scalar_prefetch=1, grid=(local,), in_specs=in_specs, out_specs=out_specs
        ),
        compiler_params=pltpu.CompilerParams(vmem_limit_bytes=14 * 2**20),
        cost_estimate=pl.CostEstimate(
            flops=10**13, bytes_accessed=10**9, transcendentals=0
        ),
        name="in_share",
    )(places, turned_rows, turned_rows, grad_pre, *came)


def out_kernel(places, act_a, act_b, up_a, up_b, *refs):
    came, out = (refs[:2], refs[2:]) if len(refs) > 2 else (None, refs)
    local, depth, tokens_all = act_a.shape
    for i, (act, up) in enumerate(((act_a, up_a), (act_b, up_b))):
        share = jnp.dot(
            act[...].reshape(local * depth, tokens_all), up[...], preferred_element_type=F32
        )
        if came is not None:
            share += came[i][...].astype(F32)
        out[i][...] = share.astype(out[i].dtype)


def out_share(places, turned_act, upstream_all, came, last=False):
    local, hidden, tokens_all = turned_act.shape
    width = upstream_all.shape[1]
    depth = hidden // lax.axis_size("dp")
    tile = 2 * LANES
    count = width // (2 * tile)
    piece = pl.BlockSpec((local * depth, tile), lambda i, place: (0, i))
    in_specs = [
        pl.BlockSpec((local, depth, tokens_all), lambda i, place: (0, place[0], 0)),
        pl.BlockSpec((local, depth, tokens_all), lambda i, place: (0, place[1], 0)),
        pl.BlockSpec((tokens_all, tile), lambda i, place: (0, i)),
        pl.BlockSpec((tokens_all, tile), lambda i, place: (0, i + count)),
    ] + [piece] * len(came)
    kind = F32 if last else BF16
    return pl.pallas_call(
        out_kernel,
        out_shape=[jax.ShapeDtypeStruct((local * depth, width // 2), kind)] * 2,
        grid_spec=pltpu.PrefetchScalarGridSpec(
            num_scalar_prefetch=1, grid=(count,), in_specs=in_specs, out_specs=[piece] * 2
        ),
        compiler_params=pltpu.CompilerParams(vmem_limit_bytes=12 * 2**20),
        cost_estimate=pl.CostEstimate(
            flops=10**13, bytes_accessed=10**9, transcendentals=0
        ),
        name="out_share",
    )(places, turned_act, turned_act, upstream_all, upstream_all, *came)


def expert_kernel(
    scalars,
    rows_a,
    rows_b,
    grad_plain,
    weight,
    *refs,
):
    activated, turned_act, grad_pre, gate_grad, turned_rows = refs[-5:]
    expert = pl.program_id(0)
    width = weight.shape[1]
    count = rows_a.shape[0]
    lanes = lax.broadcasted_iota(jnp.int32, (count, LANES), 1)
    here = lanes == scalars[0] + expert
    starts = [pl.multiple_of(scalars[2] * count, count), pl.multiple_of((1 - scalars[2]) * count, count)]

    @pl.when(expert == 0)
    def _():
        gate_grad[...] = jnp.zeros_like(gate_grad)
        for start, rows in zip(starts, (rows_a, rows_b)):
            turned_rows[:, pl.ds(start, count)] = rows[:, :width].T

    for start, rows in zip(starts, (rows_a, rows_b)):
        at = pl.ds(start, count)
        gate = jnp.sum(
            jnp.where(here, rows[:, width:].astype(F32), 0.0), axis=1, keepdims=True
        )
        x = rows[:, :width]
        g = jnp.dot(x, weight[0, :, :FE], preferred_element_type=F32)
        u = jnp.dot(x, weight[0, :, FE:], preferred_element_type=F32)
        s = jax.nn.sigmoid(g)
        silu = g * s
        act = silu * u
        plain = grad_plain[0, at, :]
        gate_grad[at, :] += jnp.where(here, jnp.sum(act * plain, axis=1, keepdims=True), 0.0)
        low = (act * gate).astype(BF16)
        activated[0, at, :] = low
        turned_act[0, :, at] = low.T
        da = plain * gate
        grad_pre[0, at, :FE] = (da * u * s * (1.0 + g * (1.0 - s))).astype(BF16)
        grad_pre[0, at, FE:] = (da * silu).astype(BF16)


def expert_half(scalars, rows_a, rows_b, grad_plain, weight, earlier):
    count = 2 * rows_a.shape[0]
    local, width, wide = weight.shape
    total = 2 * count
    whole = lambda i, sc: (0, 0)
    out_shape = [
        jax.ShapeDtypeStruct((local, total, FE), BF16),
        jax.ShapeDtypeStruct((local, FE, total), BF16),
        jax.ShapeDtypeStruct((local, total, wide), BF16),
        jax.ShapeDtypeStruct((total, LANES), F32),
        jax.ShapeDtypeStruct((width, total), BF16),
    ]
    out_specs = [
        pl.BlockSpec((1, count, FE), lambda i, sc: (i, sc[1], 0)),
        pl.BlockSpec((1, FE, count), lambda i, sc: (i, 0, sc[1])),
        pl.BlockSpec((1, count, wide), lambda i, sc: (i, sc[1], 0)),
        pl.BlockSpec((count, LANES), lambda i, sc: (sc[1], 0)),
        pl.BlockSpec((width, count), lambda i, sc: (0, sc[1])),
    ]
    in_specs = [
        pl.BlockSpec(rows_a.shape, whole),
        pl.BlockSpec(rows_b.shape, whole),
        pl.BlockSpec((1, count, FE), lambda i, sc: (i, sc[1], 0)),
        pl.BlockSpec((1, width, wide), lambda i, sc: (i, 0, 0)),
    ] + [pl.BlockSpec(memory_space=pl.ANY)] * len(earlier)
    flops = 2 * local * count * width * wide
    return pl.pallas_call(
        expert_kernel,
        out_shape=out_shape,
        grid_spec=pltpu.PrefetchScalarGridSpec(
            num_scalar_prefetch=1, grid=(local,), in_specs=in_specs, out_specs=out_specs
        ),
        input_output_aliases={5 + k: k for k in range(len(earlier))},
        compiler_params=pltpu.CompilerParams(
            dimension_semantics=("arbitrary",), vmem_limit_bytes=50 * 2**20
        ),
        cost_estimate=pl.CostEstimate(flops=flops, bytes_accessed=30 * 2**20, transcendentals=0),
        name="expert_half",
    )(scalars, rows_a, rows_b, grad_plain, weight, *earlier)


def on_device(
    tokens,
    cotangent,
    routes,
    segments,
    w_qkv,
    w_out,
    router,
    gain_attn,
    gain_mlp,
    expert_in,
    expert_out,
):
    net = Net()
    length, width = tokens.shape
    local_count = expert_in.shape[0]
    experts_all = local_count * net.ne
    wide_qkv = w_qkv.shape[1]

    small = jnp.concatenate([router, gain_attn[:, None], gain_mlp[:, None]], axis=1)
    small = jnp.pad(small, ((0, 0), (0, LANES - small.shape[1])))
    first_block = jnp.concatenate([w_qkv, small], axis=1)
    upstream_all = lax.all_gather(cotangent, "expert", axis=0, tiled=True)
    grad_act_plain = jnp.einsum("td,efd->etf", upstream_all, expert_out, preferred_element_type=F32)
    first_full, out_full = gather_weights(net, first_block, w_out, grad_act_plain)
    small_full = first_full[:, wide_qkv:]
    gain_row = experts_all % 8

    cos, sin = rope_tables(length)
    places_row = jnp.arange(length)
    bias = (
        (places_row[:, None] <= places_row[None, :])
        & (segments[0][:, None] == segments[0][None, :])
    ).astype(F32)
    normed, normed_turned, queries, key_rows, values, mixed_heads, gains = attend(
        experts_all, tokens, bias, cos, sin, first_full
    )
    hidden_state, sent, normed_two_turned, gate_float = branch(
        gain_row + 1, tokens, mixed_heads, out_full, small_full, gains, routes
    )
    across_rows = net.swap(sent, WIDE)
    own_rows, beside_rows = sent, net.swap(sent, CORE)
    core, wide = net.e % 2, net.e // 2
    scalars = lambda half: jnp.stack([net.e * local_count, half, core]).astype(jnp.int32)
    early = expert_half(scalars(wide), own_rows, beside_rows, grad_act_plain, expert_in, ())
    across_rows = after(across_rows, early)
    corner_rows = net.swap(across_rows, CORE)
    activated, turned_act, grad_pre, gate_grads, turned_rows = expert_half(
        scalars(1 - wide), across_rows, corner_rows, grad_act_plain, expert_in, early
    )

    def places(s):
        return jnp.stack([net.dp_of(net.r - 1 - s), net.dp_of(net.r + 1 + s)]).astype(jnp.int32)

    def advance(shares):
        return [net.step(shares[0], 1), net.step(shares[1], -1)]

    came_in, came_out = (), ()

    def ring_in(s, *earlier):
        nonlocal came_in
        if earlier:
            came_in = after(came_in, *earlier)
        shares = in_share(places(s), turned_rows, grad_pre, came_in)
        came_in = advance(shares)
        return shares

    def ring_out(s, *earlier):
        nonlocal came_out
        if earlier:
            came_out = after(came_out, *earlier)
        shares = out_share(places(s), turned_act, upstream_all, came_out)
        came_out = advance(shares)
        return shares

    def devices(*bits):
        return jnp.stack([net.e ^ bit for bit in bits])

    sent_out = ring_out(0)
    sent_in = ring_in(0, sent_out)
    beside = owner_rows(devices(1, 3), after(grad_pre, sent_in), expert_in, gate_grads)
    sent_out = ring_out(1, beside)
    beside_came = net.swap(after(beside, sent_out), CORE)
    kept = owner_rows(devices(0, 2), after(grad_pre, sent_out), expert_in, gate_grads)
    sent_in = ring_in(1, kept)
    onward = after(kept, sent_in)[length:].astype(F32) + beside_came[length:].astype(F32)
    onward = onward.astype(BF16)
    came = net.swap(onward, WIDE)
    mix = owner_rows(jnp.arange(4), after(activated, onward), expert_out)
    sent_out = ring_out(2, mix)
    grad_hidden, grad_branch, grad_mixed, extra = middle(
        experts_all,
        gain_row + 1,
        kept,
        beside_came,
        after(came, sent_out),
        cotangent,
        hidden_state,
        gate_float,
        normed_two_turned,
        gains,
        small_full,
        out_full,
    )
    block = width // net.devices
    d_out_local = weight_product(
        parts_by(mixed_heads.T, net.ne, block), parts_by(extra, net.ne, block), grad_branch
    )
    sent_in = ring_in(2, d_out_local)
    d_out_some = lax.psum_scatter(
        after(d_out_local, sent_in).reshape(-1, d_out_local.shape[2]),
        "expert",
        scatter_dimension=0,
        tiled=True,
    )
    grad_project, grad_tokens, extra_first = attend_back(
        gain_row,
        tokens,
        queries,
        key_rows,
        values,
        after(grad_mixed, sent_in),
        bias,
        cos,
        sin,
        gains,
        grad_hidden,
        first_full,
    )
    sent_out = ring_out(3, grad_project)
    d_qkv_local = weight_product(
        parts_by(after(normed_turned, sent_out), 2, block), parts_by(extra_first, 2, block), grad_project
    )
    sent_in = ring_in(3, d_qkv_local)
    qkv_sum = BlockSum(net, d_qkv_local, 0, block)
    qkv_sum.send(sent_in)
    sent_out = ring_out(4, sent_in)
    qkv_sum.add(sent_out)
    qkv_sum.send()
    sent_in = ring_in(4, qkv_sum.halves)

    def over_dp(value):
        return lax.all_to_all(value, "dp", 0, 0, tiled=True)

    def total(value):
        return jnp.sum(value.reshape(net.nd, block, -1).astype(F32), axis=0)

    d_out_some = over_dp(after(d_out_some, sent_in))
    sent_out = ring_out(5, sent_in)
    sent_in = ring_in(5, sent_out)
    d_qkv_some = qkv_sum.kept.astype(F32) + after(qkv_sum.came, sent_in).astype(F32)
    d_qkv_some = over_dp(d_qkv_some.astype(BF16))
    mixture = lax.psum_scatter(
        after(mix, qkv_sum.came), "expert", scatter_dimension=0, tiled=True
    )
    sent_out = ring_out(6, sent_in)
    sent_in = ring_in(6, sent_out)
    d_out = total(after(d_out_some, sent_in))
    here = jnp.stack([net.p, net.p]).astype(jnp.int32)
    d_expert_out = jnp.concatenate(
        out_share(here, turned_act, upstream_all, after(came_out, d_out), last=True), axis=1
    ).reshape(local_count, FE // net.nd, width)
    (d_expert_in,) = in_share(here, turned_rows, grad_pre, after(came_in, d_expert_out), last=True)
    activations = (hidden_state + after(mixture, d_expert_out).astype(F32)).astype(BF16)
    d_qkv = total(after(d_qkv_some, d_expert_out))
    return (
        activations,
        grad_tokens,
        d_qkv[:, :wide_qkv],
        d_out[:, :width],
        d_out[:, width : width + experts_all],
        d_qkv[:, wide_qkv],
        d_out[:, width + experts_all],
        d_expert_in,
        d_expert_out,
    )


def solution(mesh):
    rows = P(AXES, None)
    return jax.shard_map(
        on_device,
        mesh=mesh,
        in_specs=(rows,) * 7
        + (P(AXES), P(AXES), P("expert", None, None), P("expert", None, None)),
        out_specs=(rows,) * 5
        + (P(AXES), P(AXES), P("expert", "dp", None), P("expert", "dp", None)),
        check_vma=False,
    )
```

time: 745 us -> 539 us (0.72)
  Pallas kernels: 0 us -> 207 us
  waiting for transfers between devices: 332 us -> 126 us
  matrix products: 202 us -> 14.2 us
  starting transfers between devices: 90.4 us -> 62.8 us
  local copies, waits for them, and re-layouts: 48.5 us -> 75.9 us
  other arithmetic: 46.9 us -> 27.9 us
    pallas_call x0 -> x28, Pallas kernels: none -> 207 us  [the longest x8 52.2 us: in_share(): pl.pallas_call(in_kernel, out_shape=out_shape, grid_spec=pltpu.PrefetchSc...]
    dot_general x52 -> x0, matrix products: 173 us -> none  [the longest x16 48.5 us: make(): jnp.einsum('dt,etf->edf', some, grad_pre[..., low:high], preferred_elemen...]
    ppermute x72 -> x44, waiting for transfers between devices: 203 us -> 63.5 us  [step(): return lax.ppermute(value, AXES, self.ring[way])]
    unnamed x2 -> x3, waiting for transfers between devices: 80.5 us -> 0.05 us
    all_to_all x0 -> x2, waiting for transfers between devices: none -> 50.8 us  [over_dp(): return lax.all_to_all(value, 'dp', 0, 0, tiled=True)]
    ppermute x32 -> x15, waiting for transfers between devices: 48.5 us -> 11.8 us  [swap(): lax.ppermute(value, AXES, [(d, d ^ bit) for d in range(self.devices)])]
    ppermute x72 -> x44, starting transfers between devices: 77.6 us -> 45.6 us  [step(): return lax.ppermute(value, AXES, self.ring[way])]
    unnamed x208 -> x144, local copies, waits for them, and re-layouts: 18.9 us -> 46.9 us
  transfers between devices with their start and end apart: 105 -> 64, of which waited for: 52 -> 24; matrix products, arithmetic and copies ran while one was open for 28% -> 13% of each run, Pallas kernels for 0% -> 34%
where the time goes in v2:
time: 539 us; the launch traced here: 530 us
  Pallas kernels  207 us (38%)
  waiting for transfers between devices  126 us (23%)
  local copies, waits for them, and re-layouts  75.9 us (14%)
  starting transfers between devices  62.8 us (12%)
  other arithmetic  27.9 us (5%)
  between operations  15.7 us (3%)
  matrix products  14.2 us (3%)
    ppermute x44, waiting for transfers between devices, step(): return lax.ppermute(value, AXES, self.ring[way])  63.5 us
    pallas_call x8, Pallas kernels, in_share(): pl.pallas_call(in_kernel, out_shape=out_shape, grid_spec=pltpu.PrefetchSc...  52.2 us
    all_to_all x2, waiting for transfers between devices, over_dp(): return lax.all_to_all(value, 'dp', 0, 0, tiled=True)  50.8 us
    unnamed x144, local copies, waits for them, and re-layouts  46.9 us
    ppermute x44, starting transfers between devices, step(): return lax.ppermute(value, AXES, self.ring[way])  45.6 us
    pallas_call x3, Pallas kernels, owner_rows(): pl.pallas_call(functools.partial(owner_rows_kernel, extra is not None, bl...  41.8 us
    pallas_call x2, Pallas kernels, expert_half(): pl.pallas_call(expert_kernel, out_shape=out_shape, grid_spec=pltpu.Prefet...  36.2 us
    pallas_call x8, Pallas kernels, out_share(): pl.pallas_call(out_kernel, out_shape=[jax.ShapeDtypeStruct((local * depth...  34.9 us
  transfers between devices with their start and end apart: 64, of which 24 were waited for; matrix products, arithmetic and copies ran while one was open for 13% of the time, Pallas kernels for 34%

profile of v2, /device:TPU:0, one launch (start us, length us, event | category | flops | bytes accessed | tf_op | source)
XLA Modules:
  0.0 529.9 jit_solution(17381636061344625452)
XLA Ops:
  10.6 3.0 collective-permute-start
  15.8 4.1 collective-permute-done
  23.8 3.3 collective-permute-done.4
  29.2 7.2 %collective-permute-done.2 = bf16[2,48,2688]{2,1,0:T(8,128)(2,1)S(1)} collective-permute-done((bf16[2,48,2688]{2,1,0:T(8,128)(2,1)S(1)}, bf16[2,48,2688]{2,1,0:T(8,128)(2,1)S(1)}, u32[]{:S(2)}, u32[]{:S(2)}) %collective-permute-start.2) | collective-permute-done | bytes 516128 | tf_op jit(solution)/shard_map/ppermute | solution.py:463
  40.1 2.7 collective-permute-done.8
  47.0 4.0 broadcast_in_dim.28
  57.5 2.7 collective-permute-done.16
  72.7 14.2 %convolution_bitcast_fusion.grad_plain = f32[5,1024,512]{2,1,0:T(8,128)} fusion(bf16[5,512,1536]{2,1,0:T(8,128)(2,1)} %refs_5_.1, bf16[1024,1536]{1,0:T(8,128)(2,1)} %all-gather.2.cloned.1.call-done.up_a.up_b), kind=kOutput, calls=%fused_computation.6 | convolution fusion | flops 8053063680 | bytes 21495808 | tf_op jit(solution)/shard_map/td,efd->etf/dot_general | solution.py:786
  95.2 4.6 collective-permute-done.14
  114.3 10.1 %attend.1 = (bf16[256,1536]{1,0:T(8,128)(2,1)}, bf16[1536,256]{1,0:T(8,128)(2,1)S(1)}, bf16[256,1536]{1,0:T(8,128)(2,1)S(1)}, bf16[256,512]{1,0:T(8,128)(2,1)S(1...) custom-call(bf16[256,1536]{1,0:T(8,128)(2,1)S(1)} %copy-done.14, ...), custom_call_target="tpu_custom_call" | custom-call | flops 1024 | bytes 1024 | tf_op jit(solution)/shard_map/attend/pallas_call | solution.py:175
  129.4 3.0 branch.1
  136.7 18.0 %expert_half.2 = (bf16[5,1024,512]{2,1,0:T(8,128)(2,1)}, bf16[5,512,1024]{2,1,0:T(8,128)(2,1)}, bf16[5,1024,1024]{2,1,0:T(8,128)(2,1)}, f32[1024,128]{1,0:T(8,128)S(1)}, bf16[1536,1024]{1,0:T(8,128)(2,1)}) custom-call(s32[3]{0:T(128)S(1)} %add_add_fusion.1.scalars, bf16[256,1664]{1,0:T(8,128)(2,1)} %get-tuple-element.153.rows_a, ...), custom_call_target="tpu_custom_call" | custom-call | flops 8053063680 | bytes 31457280 | tf_op jit(solution)/shard_map/expert_half/pallas_call | solution.py:748
  158.6 18.2 %expert_half.3 = (bf16[5,1024,512]{2,1,0:T(8,128)(2,1)}, bf16[5,512,1024]{2,1,0:T(8,128)(2,1)}, bf16[5,1024,1024]{2,1,0:T(8,128)(2,1)}, f32[1024,128]{1,0:T(8,128)S(1)}, bf16[1536,1024]{1,0:T(8,128)(2,1)}) custom-call(s32[3]{0:T(128)S(1)} %add_add_fusion.scalars, ...), custom_call_target="tpu_custom_call", output_to_operand_aliasing={{0}: (5, {}), {1}: (6, {}), {2}: (7, {}), {3}: (8, {}), {4}... | custom-call | flops 8053063680 | bytes 31457280 | tf_op jit(solution)/shard_map/expert_half/pallas_call | solution.py:748
  179.3 3.3 out_share.8
  184.6 4.4 in_share.8
  191.2 14.4 %owner_rows.3 = bf16[512,1664]{1,0:T(8,128)(2,1)} custom-call(s32[2]{0:T(128)S(1)} %pad_add_fusion.3.refs_0_, bf16[5,1024,1024]{2,1,0:T(8,128)(2,1)S(1)} %copy-done, bf16[5,1024,1024]{2,1,0:T(8,128)(2,1)S(1)} %copy-done, bf16[5,1536,1024]{2,1,0:T(8,128)(2,1)} %refs_3_.3, f32[1024,128]{1,0:T(8,128)S(1)} %get-tuple-element.169.refs_4_.refs_5_, ...), custom_call_target="tpu_custom_call" | custom-call | flops 1024 | bytes 1024 | tf_op jit(solution)/shard_map/owner_rows/pallas_call | solution.py:276
  205.6 4.5 out_share.9
  212.2 13.2 %owner_rows.4.kept = bf16[512,1664]{1,0:T(8,128)(2,1)S(1)} custom-call(s32[2]{0:T(128)S(1)} %pad_add_fusion.refs_0_, bf16[5,1024,1024]{2,1,0:T(8,128)(2,1)S(1)} %copy-done, bf16[5,1024,1024]{2,1,0:T(8,128)(2,1)S(1)} %copy-done, bf16[5,1536,1024]{2,1,0:T(8,128)(2,1)} %refs_3_.3, f32[1024,128]{1,0:T(8,128)S(1)} %get-tuple-element.169.refs_4_.refs_5_, ...), custom_call_target="tpu_custom_call" | custom-call | flops 1024 | bytes 1024 | tf_op jit(solution)/shard_map/owner_rows/pallas_call | solution.py:276
  225.4 6.3 %in_share.9 = (bf16[5,192,512]{2,1,0:T(8,128)(2,1)}, bf16[5,192,512]{2,1,0:T(8,128)(2,1)}) custom-call(s32[2]{0:T(128)S(1)} %get-tuple-element.326.places, bf16[1536,1024]{1,0:T(8,128)(2,1)S(1)} %copy-done.29, bf16[1536,1024]{1,0:T(8,128)(2,1)S(1)} %copy-done.29, bf16[5,1024,1024]{2,1,0:T(8,128)(2,1)S(1)} %copy-done, ...), custom_call_target="tpu_custom_call" | custom-call | flops 9999999827968 | bytes 1000000000 | tf_op jit(solution)/shard_map/in_share/pallas_call | solution.py:625
  239.1 3.2 copy-done.13
  242.3 14.3 %owner_rows.5 = bf16[1024,1536]{1,0:T(8,128)(2,1)} custom-call(s32[4]{0:T(128)S(1)} %iota.34.refs_0_, bf16[5,1024,512]{2,1,0:T(8,128)(2,1)S(1)} %copy-done.6, bf16[5,1024,512]{2,1,0:T(8,128)(2,1)S(1)} %copy-done.6, bf16[5,1024,512]{2,1,0:T(8,128)(2,1)S(1)} %copy-done.6, bf16[5,1024,512]{2,1,0:T(8,128)(2,1)S(1)} %copy-done.6, bf16[5,512,1536]{2,1,0:T(8,128)(2,1)S(1)} %copy-done.13), custom_call_target="tpu_custom_call" | custom-call | flops 1024 | bytes 1024 | tf_op jit(solution)/shard_map/owner_rows/pallas_call | solution.py:276
  261.0 4.9 out_share.10
  270.3 4.4 middle.1
  276.8 8.1 %in_share.10 = (bf16[5,192,512]{2,1,0:T(8,128)(2,1)}, bf16[5,192,512]{2,1,0:T(8,128)(2,1)}) custom-call(s32[2]{0:T(128)S(1)} %get-tuple-element.329.places, bf16[1536,1024]{1,0:T(8,128)(2,1)S(1)} %copy-done.30, bf16[1536,1024]{1,0:T(8,128)(2,1)S(1)} %copy-done.30, bf16[5,1024,1024]{2,1,0:T(8,128)(2,1)S(1)} %copy-done.1, ...), custom_call_target="tpu_custom_call" | custom-call | flops 9999999827968 | bytes 1000000000 | tf_op jit(solution)/shard_map/in_share/pallas_call | solution.py:625
  287.2 14.6 %attend_back.1 = (bf16[256,2560]{1,0:T(8,128)(2,1)S(1)}, f32[256,1536]{1,0:T(8,128)}, f32[1536,128]{1,0:T(8,128)S(1)}) custom-call(bf16[256,1536]{1,0:T(8,128)(2,1)S(1)} %copy-done.15, bf16[256,1536]{1,0:T(8,128)(2,1)S(1)} %copy-done.47, bf16[256,512]{1,0:T(8,128)(2,1)S(1)} %get-tuple-element.188.key_rows, bf16[256,512]{1,0:T(8,128)(2,1)S(1)} %get-tuple-element.189.values, ...), custom_call_target="tpu_custom_call" | custom-call | flops 1024 | bytes 1024 | tf_op jit(solution)/shard_map/attend_back/pallas_call | solution.py:414
  301.8 4.5 out_share.11
  315.4 6.5 %in_share.11 = (bf16[5,192,512]{2,1,0:T(8,128)(2,1)}, bf16[5,192,512]{2,1,0:T(8,128)(2,1)}) custom-call(s32[2]{0:T(128)S(1)} %get-tuple-element.328.places, bf16[1536,1024]{1,0:T(8,128)(2,1)S(1)} %copy-done.31, bf16[1536,1024]{1,0:T(8,128)(2,1)S(1)} %copy-done.31, bf16[5,1024,1024]{2,1,0:T(8,128)(2,1)S(1)} %copy-done.2, ...), custom_call_target="tpu_custom_call" | custom-call | flops 9999999827968 | bytes 1000000000 | tf_op jit(solution)/shard_map/in_share/pallas_call | solution.py:625
  324.2 2.6 dynamic-slice_bitcast_fusion
  326.8 3.3 copy-done.22
  332.0 4.5 out_share.12
  338.6 5.8 %halve.1 = bf16[2,8,48,2688]{3,2,1,0:T(8,128)(2,1)S(1)} custom-call(bf16[8,2,48,2688]{3,2,1,0:T(8,128)(2,1)S(1)} %bitcast.171, bf16[8,2,48,2688]{3,2,1,0:T(8,128)(2,1)} %bitcast.98.came), custom_call_target="tpu_custom_call" | custom-call | flops 1024 | bytes 1024 | tf_op jit(solution)/shard_map/halve/pallas_call | solution.py:563
  344.4 2.8 collective-permute-done.47.refs_0_
  350.9 7.2 %in_share.12 = (bf16[5,192,512]{2,1,0:T(8,128)(2,1)}, bf16[5,192,512]{2,1,0:T(8,128)(2,1)}) custom-call(s32[2]{0:T(128)S(1)} %get-tuple-element.330.places, bf16[1536,1024]{1,0:T(8,128)(2,1)S(1)} %copy-done.32, bf16[1536,1024]{1,0:T(8,128)(2,1)S(1)} %copy-done.32, bf16[5,1024,1024]{2,1,0:T(8,128)(2,1)S(1)} %copy-done.3, ...), custom_call_target="tpu_custom_call" | custom-call | flops 9999999827968 | bytes 1000000000 | tf_op jit(solution)/shard_map/in_share/pallas_call | solution.py:625
  360.2 4.5 out_share.13
  369.5 13.6 %collective-permute-done.51.refs_0_ = bf16[5,192,512]{2,1,0:T(8,128)(2,1)} collective-permute-done((bf16[5,192,512]{2,1,0:T(8,128)(2,1)}, bf16[5,192,512]{2,1,0:T(8,128)(2,1)}, u32[]{:S(2)}, u32[]{:S(2)}) %collective-permute-start.51) | collective-permute-done | bytes 983072 | tf_op jit(solution)/shard_map/ppermute | solution.py:463
  384.6 6.5 %in_share.13 = (bf16[5,192,512]{2,1,0:T(8,128)(2,1)}, bf16[5,192,512]{2,1,0:T(8,128)(2,1)}) custom-call(s32[2]{0:T(128)S(1)} %get-tuple-element.333.places, bf16[1536,1024]{1,0:T(8,128)(2,1)S(1)} %copy-done.33, bf16[1536,1024]{1,0:T(8,128)(2,1)S(1)} %copy-done.33, bf16[5,1024,1024]{2,1,0:T(8,128)(2,1)S(1)} %copy-done.3, ...), custom_call_target="tpu_custom_call" | custom-call | flops 9999999827968 | bytes 1000000000 | tf_op jit(solution)/shard_map/in_share/pallas_call | solution.py:625
  393.6 4.8 out_share.14
  400.5 15.7 %collective-permute-done.55.refs_0_ = bf16[5,192,512]{2,1,0:T(8,128)(2,1)} collective-permute-done((bf16[5,192,512]{2,1,0:T(8,128)(2,1)}, bf16[5,192,512]{2,1,0:T(8,128)(2,1)}, u32[]{:S(2)}, u32[]{:S(2)}) %collective-permute-start.55) | collective-permute-done | bytes 983072 | tf_op jit(solution)/shard_map/ppermute | solution.py:463
  416.4 4.3 all-to-all-start
  420.8 4.0 copy-done.4
  424.7 6.2 %in_share.14 = (bf16[5,192,512]{2,1,0:T(8,128)(2,1)}, bf16[5,192,512]{2,1,0:T(8,128)(2,1)}) custom-call(s32[2]{0:T(128)S(1)} %get-tuple-element.332.places, bf16[1536,1024]{1,0:T(8,128)(2,1)S(1)} %copy-done.34, bf16[1536,1024]{1,0:T(8,128)(2,1)S(1)} %copy-done.34, bf16[5,1024,1024]{2,1,0:T(8,128)(2,1)S(1)} %copy-done.4, ...), custom_call_target="tpu_custom_call" | custom-call | flops 9999999827968 | bytes 1000000000 | tf_op jit(solution)/shard_map/in_share/pallas_call | solution.py:625
  433.0 4.0 fusion
  437.1 17.0 %all-to-all-done = bf16[8,48,1664]{2,1,0:T(8,128)(2,1)} async-done(((bf16[8,48,1664]{2,1,0:T(8,128)(2,1)}), bf16[8,48,1664]{2,1,0:T(8,128)(2,1)}, u32[]{:S(2)}, u32[]{:S(2)}) %all-to-all-start) | async-done | bytes 1277984 | tf_op jit(solution)/shard_map/all_to_all | solution.py:905
  454.1 4.3 all-to-all-start.1
  465.1 3.9 out_share.15
  470.5 4.0 copy-done.5
  474.6 6.9 %in_share.15 = f32[5,192,1024]{2,1,0:T(8,128)} custom-call(s32[2]{0:T(128)S(1)} %get-tuple-element.331.places, bf16[1536,1024]{1,0:T(8,128)(2,1)S(1)} %copy-done.34, bf16[1536,1024]{1,0:T(8,128)(2,1)S(1)} %copy-done.34, bf16[5,1024,1024]{2,1,0:T(8,128)(2,1)S(1)} %copy-done.5, bf16[5,192,512]{2,1,0:T(8,128)(2,1)} %collective-permute-done.57.refs_0_, ...), custom_call_target="tpu_custom_call" | custom-call | flops 9999999827968 | bytes 1000000000 | tf_op jit(solution)/shard_map/in_share/pallas_call | solution.py:625
  482.2 33.8 %all-to-all-done.1 = bf16[8,48,2688]{2,1,0:T(8,128)(2,1)} async-done(((bf16[8,48,2688]{2,1,0:T(8,128)(2,1)}), bf16[8,48,2688]{2,1,0:T(8,128)(2,1)}, u32[]{:S(2)}, u32[]{:S(2)}) %all-to-all-start.1) | async-done | bytes 2064416 | tf_op jit(solution)/shard_map/all_to_all | solution.py:905
  (350 shorter events, 152.8 us)
Async XLA Ops:
  7.2 65.5 %all-gather.2.cloned.1.call-start = ((), (), s32[]{:S(2)}) async-start(), calls=%async_computation.4 | async-start | bytes 3932160 | tf_op jit(solution)/shard_map/all_gather | solution.py:785
  13.7 402.7 %reduce-scatter.5.cloned.1.call-start = ((), (), s32[]{:S(2)}) async-start(), calls=%async_computation.6 | async-start | bytes 6389760 | tf_op jit(solution)/shard_map/reduce_scatter | solution.py:872
  23.8 22.8 %collective-permute-start.1 = (bf16[1,2,48,2688]{3,2,1,0:T(8,128)(2,1)S(1)}, bf16[1,2,48,2688]{3,2,1,0:T(8,128)(2,1)S(1)}, u32[]{:S(2)}, u32[]{:S(2)}) collective-permute-start(bf16[1,2,48,2688]{3,2,1,0:T(8,128)(2,1)S(1)} %get-tuple-element.318), channel_id=1, source_target_pairs={{0,1},{1,0},{2,3},{3,2},{4,5},{5,4},{6,7},{7,6},{8,9},{9,8},{10,11... | collective-permute-start | bytes 1548296 | tf_op jit(solution)/shard_map/ppermute | solution.py:470
  38.0 15.9 %collective-permute-start.6 = (bf16[2,48,2688]{2,1,0:T(8,128)(2,1)S(1)}, bf16[2,48,2688]{2,1,0:T(8,128)(2,1)}, u32[]{:S(2)}, u32[]{:S(2)}) collective-permute-start(bf16[2,48,2688]{2,1,0:T(8,128)(2,1)S(1)} %collective-permute-done.2), channel_id=1, source_target_pairs={{0,8},{1,9},{2,10},{3,11},{8,16},{9,17},{10,18},{11,19},{16,24},{1... | collective-permute-start | bytes 1548296 | tf_op jit(solution)/shard_map/ppermute | solution.py:463
  39.6 15.9 %collective-permute-start.7 = (bf16[2,48,2688]{2,1,0:T(8,128)(2,1)S(1)}, bf16[2,48,2688]{2,1,0:T(8,128)(2,1)}, u32[]{:S(2)}, u32[]{:S(2)}) collective-permute-start(bf16[2,48,2688]{2,1,0:T(8,128)(2,1)S(1)} %collective-permute-done.3), channel_id=1, source_target_pairs={{0,4},{1,5},{2,6},{3,7},{8,0},{9,1},{10,2},{11,3},{16,8},{17,9},{1... | collective-permute-start | bytes 1548296 | tf_op jit(solution)/shard_map/ppermute | solution.py:463
  44.3 15.9 %collective-permute-start.16 = (bf16[2,48,1536]{2,1,0:T(8,128)(2,1)S(1)}, bf16[2,48,1536]{2,1,0:T(8,128)(2,1)}, u32[]{:S(2)}, u32[]{:S(2)}) collective-permute-start(bf16[2,48,1536]{2,1,0:T(8,128)(2,1)S(1)} %collective-permute-done.8), channel_id=1, source_target_pairs={{0,8},{1,9},{2,10},{3,11},{8,16},{9,17},{10,18},{11,19},{16,24},{1... | collective-permute-start | bytes 884744 | tf_op jit(solution)/shard_map/ppermute | solution.py:463
  46.6 21.0 %collective-permute-start.5 = (bf16[2,2,48,2688]{3,2,1,0:T(8,128)(2,1)S(1)}, bf16[2,2,48,2688]{3,2,1,0:T(8,128)(2,1)S(1)}, u32[]{:S(2)}, u32[]{:S(2)}) collective-permute-start(bf16[2,2,48,2688]{3,2,1,0:T(8,128)(2,1)S(1)} %pad_maximum_fusion.6), channel_id=1, source_target_pairs={{0,1},{1,0},{2,3},{3,2},{4,5},{5,4},{6,7},{7,6},{8,9},{9,8},{10,11... | collective-permute-start | bytes 3096584 | tf_op jit(solution)/shard_map/ppermute | solution.py:470
  55.5 31.4 %collective-permute-start.11 = (bf16[2,48,2688]{2,1,0:T(8,128)(2,1)}, bf16[2,48,2688]{2,1,0:T(8,128)(2,1)S(1)}, u32[]{:S(2)}, u32[]{:S(2)}) collective-permute-start(bf16[2,48,2688]{2,1,0:T(8,128)(2,1)} %collective-permute-done.6), channel_id=1, source_target_pairs={{0,8},{1,9},{2,10},{3,11},{8,16},{9,17},{10,18},{11,19},{16,24},{1... | collective-permute-start | bytes 1548296 | tf_op jit(solution)/shard_map/ppermute | solution.py:463
  57.1 29.8 %collective-permute-start.12 = (bf16[2,48,2688]{2,1,0:T(8,128)(2,1)}, bf16[2,48,2688]{2,1,0:T(8,128)(2,1)}, u32[]{:S(2)}, u32[]{:S(2)}) collective-permute-start(bf16[2,48,2688]{2,1,0:T(8,128)(2,1)} %collective-permute-done.7), channel_id=1, source_target_pairs={{0,4},{1,5},{2,6},{3,7},{8,0},{9,1},{10,2},{11,3},{16,8},{17,9},{1... | collective-permute-start | bytes 1548296 | tf_op jit(solution)/shard_map/ppermute | solution.py:463
  61.5 26.4 %collective-permute-start.18 = (bf16[2,48,1536]{2,1,0:T(8,128)(2,1)}, bf16[2,48,1536]{2,1,0:T(8,128)(2,1)S(1)}, u32[]{:S(2)}, u32[]{:S(2)}) collective-permute-start(bf16[2,48,1536]{2,1,0:T(8,128)(2,1)} %collective-permute-done.16), channel_id=1, source_target_pairs={{0,8},{1,9},{2,10},{3,11},{8,16},{9,17},{10,18},{11,19},{16,24},{1... | collective-permute-start | bytes 884744 | tf_op jit(solution)/shard_map/ppermute | solution.py:463
  63.1 24.8 %collective-permute-start.19 = (bf16[2,48,1536]{2,1,0:T(8,128)(2,1)}, bf16[2,48,1536]{2,1,0:T(8,128)(2,1)}, u32[]{:S(2)}, u32[]{:S(2)}) collective-permute-start(bf16[2,48,1536]{2,1,0:T(8,128)(2,1)} %collective-permute-done.17), channel_id=1, source_target_pairs={{0,4},{1,5},{2,6},{3,7},{8,0},{9,1},{10,2},{11,3},{16,8},{17,9},{1... | collective-permute-start | bytes 884744 | tf_op jit(solution)/shard_map/ppermute | solution.py:463
  88.0 15.9 %collective-permute-start.21 = (bf16[48,1536]{1,0:T(8,128)(2,1)S(1)}, bf16[48,1536]{1,0:T(8,128)(2,1)S(1)}, u32[]{:S(2)}, u32[]{:S(2)}) collective-permute-start(bf16[48,1536]{1,0:T(8,128)(2,1)S(1)} %slice_bitcast_fusion.3), channel_id=1, source_target_pairs={{0,8},{1,9},{2,10},{3,11},{8,16},{9,17},{10,18},{11,19},{16,24},{1... | collective-permute-start | bytes 442376 | tf_op jit(solution)/shard_map/ppermute | solution.py:463
  103.8 21.9 %collective-permute-start.23 = (bf16[8,2,48,1536]{3,2,1,0:T(8,128)(2,1)S(1)}, bf16[8,2,48,1536]{3,2,1,0:T(8,128)(2,1)S(1)}, u32[]{:S(2)}, u32[]{:S(2)}) collective-permute-start(bf16[8,2,48,1536]{3,2,1,0:T(8,128)(2,1)S(1)} %fusion.2), channel_id=1, source_target_pairs={{0,1},{1,0},{2,3},{3,2},{4,5},{5,4},{6,7},{7,6},{8,9},{9,8},{10,11... | collective-permute-start | bytes 7077896 | tf_op jit(solution)/shard_map/ppermute | solution.py:470
  134.3 21.3 %collective-permute-start.24 = (bf16[256,1664]{1,0:T(8,128)(2,1)}, bf16[256,1664]{1,0:T(8,128)(2,1)}, u32[]{:S(2)}, u32[]{:S(2)}) collective-permute-start(bf16[256,1664]{1,0:T(8,128)(2,1)} %get-tuple-element.153.rows_a), channel_id=1, source_target_pairs={{0,2},{1,3},{2,0},{3,1},{4,6},{5,7},{6,4},{7,5},{8,10},{9,11},{10,... | collective-permute-start | bytes 2555912 | tf_op jit(solution)/shard_map/ppermute | solution.py:470
  182.6 23.0 %collective-permute-start.27 = (bf16[320,768]{1,0:T(8,128)(2,1)}, bf16[320,768]{1,0:T(8,128)(2,1)}, u32[]{:S(2)}, u32[]{:S(2)}) collective-permute-start(bf16[320,768]{1,0:T(8,128)(2,1)} %get-tuple-element.163), channel_id=1, source_target_pairs={{0,8},{1,9},{2,10},{3,11},{8,16},{9,17},{10,18},{11,19},{16,24},{1... | collective-permute-start | bytes 1474568 | tf_op jit(solution)/shard_map/ppermute | solution.py:463
  184.4 21.2 %collective-permute-start.28 = (bf16[320,768]{1,0:T(8,128)(2,1)}, bf16[320,768]{1,0:T(8,128)(2,1)}, u32[]{:S(2)}, u32[]{:S(2)}) collective-permute-start(bf16[320,768]{1,0:T(8,128)(2,1)} %get-tuple-element.164), channel_id=1, source_target_pairs={{0,4},{1,5},{2,6},{3,7},{8,0},{9,1},{10,2},{11,3},{16,8},{17,9},{1... | collective-permute-start | bytes 1474568 | tf_op jit(solution)/shard_map/ppermute | solution.py:463
  189.1 36.3 %collective-permute-start.29 = (bf16[5,192,512]{2,1,0:T(8,128)(2,1)}, bf16[5,192,512]{2,1,0:T(8,128)(2,1)}, u32[]{:S(2)}, u32[]{:S(2)}) collective-permute-start(bf16[5,192,512]{2,1,0:T(8,128)(2,1)} %get-tuple-element.166), channel_id=1, source_target_pairs={{0,8},{1,9},{2,10},{3,11},{8,16},{9,17},{10,18},{11,19},{16,24},{1... | collective-permute-start | bytes 2949128 | tf_op jit(solution)/shard_map/ppermute | solution.py:463
  190.9 34.5 %collective-permute-start.30 = (bf16[5,192,512]{2,1,0:T(8,128)(2,1)}, bf16[5,192,512]{2,1,0:T(8,128)(2,1)}, u32[]{:S(2)}, u32[]{:S(2)}) collective-permute-start(bf16[5,192,512]{2,1,0:T(8,128)(2,1)} %get-tuple-element.167), channel_id=1, source_target_pairs={{0,4},{1,5},{2,6},{3,7},{8,0},{9,1},{10,2},{11,3},{16,8},{17,9},{1... | collective-permute-start | bytes 2949128 | tf_op jit(solution)/shard_map/ppermute | solution.py:463
  210.2 46.4 %collective-permute-start.32 = (bf16[320,768]{1,0:T(8,128)(2,1)}, bf16[320,768]{1,0:T(8,128)(2,1)}, u32[]{:S(2)}, u32[]{:S(2)}) collective-permute-start(bf16[320,768]{1,0:T(8,128)(2,1)} %get-tuple-element.172), channel_id=1, source_target_pairs={{0,8},{1,9},{2,10},{3,11},{8,16},{9,17},{10,18},{11,19},{16,24},{1... | collective-permute-start | bytes 1474568 | tf_op jit(solution)/shard_map/ppermute | solution.py:463
  212.0 44.6 %collective-permute-start.33 = (bf16[320,768]{1,0:T(8,128)(2,1)}, bf16[320,768]{1,0:T(8,128)(2,1)}, u32[]{:S(2)}, u32[]{:S(2)}) collective-permute-start(bf16[320,768]{1,0:T(8,128)(2,1)} %get-tuple-element.173), channel_id=1, source_target_pairs={{0,4},{1,5},{2,6},{3,7},{8,0},{9,1},{10,2},{11,3},{16,8},{17,9},{1... | collective-permute-start | bytes 1474568 | tf_op jit(solution)/shard_map/ppermute | solution.py:463
  212.2 21.6 %collective-permute-start.31 = (bf16[512,1664]{1,0:T(8,128)(2,1)}, bf16[512,1664]{1,0:T(8,128)(2,1)}, u32[]{:S(2)}, u32[]{:S(2)}) collective-permute-start(bf16[512,1664]{1,0:T(8,128)(2,1)} %owner_rows.3), channel_id=1, source_target_pairs={{0,1},{1,0},{2,3},{3,2},{4,5},{5,4},{6,7},{7,6},{8,9},{9,8},{10,11... | collective-permute-start | bytes 5111816 | tf_op jit(solution)/shard_map/ppermute | solution.py:470
  231.8 44.9 %collective-permute-start.37 = (bf16[5,192,512]{2,1,0:T(8,128)(2,1)}, bf16[5,192,512]{2,1,0:T(8,128)(2,1)}, u32[]{:S(2)}, u32[]{:S(2)}) collective-permute-start(bf16[5,192,512]{2,1,0:T(8,128)(2,1)} %get-tuple-element.177), channel_id=1, source_target_pairs={{0,8},{1,9},{2,10},{3,11},{8,16},{9,17},{10,18},{11,19},{16,24},{1... | collective-permute-start | bytes 2949128 | tf_op jit(solution)/shard_map/ppermute | solution.py:463
  233.6 43.0 %collective-permute-start.38 = (bf16[5,192,512]{2,1,0:T(8,128)(2,1)}, bf16[5,192,512]{2,1,0:T(8,128)(2,1)}, u32[]{:S(2)}, u32[]{:S(2)}) collective-permute-start(bf16[5,192,512]{2,1,0:T(8,128)(2,1)} %get-tuple-element.178), channel_id=1, source_target_pairs={{0,4},{1,5},{2,6},{3,7},{8,0},{9,1},{10,2},{11,3},{16,8},{17,9},{1... | collective-permute-start | bytes 2949128 | tf_op jit(solution)/shard_map/ppermute | solution.py:463
  236.0 31.8 %collective-permute-start.36 = (bf16[256,1664]{1,0:T(8,128)(2,1)}, bf16[256,1664]{1,0:T(8,128)(2,1)}, u32[]{:S(2)}, u32[]{:S(2)}) collective-permute-start(bf16[256,1664]{1,0:T(8,128)(2,1)} %add_convert_fusion), channel_id=1, source_target_pairs={{0,2},{1,3},{2,0},{3,1},{4,6},{5,7},{6,4},{7,5},{8,10},{9,11},{10,... | collective-permute-start | bytes 2555912 | tf_op jit(solution)/shard_map/ppermute | solution.py:470
  265.9 35.9 %collective-permute-start.34 = (bf16[320,768]{1,0:T(8,128)(2,1)}, bf16[320,768]{1,0:T(8,128)(2,1)}, u32[]{:S(2)}, u32[]{:S(2)}) collective-permute-start(bf16[320,768]{1,0:T(8,128)(2,1)} %get-tuple-element.185), channel_id=1, source_target_pairs={{0,8},{1,9},{2,10},{3,11},{8,16},{9,17},{10,18},{11,19},{16,24},{1... | collective-permute-start | bytes 1474568 | tf_op jit(solution)/shard_map/ppermute | solution.py:463
  267.7 34.1 %collective-permute-start.35 = (bf16[320,768]{1,0:T(8,128)(2,1)}, bf16[320,768]{1,0:T(8,128)(2,1)}, u32[]{:S(2)}, u32[]{:S(2)}) collective-permute-start(bf16[320,768]{1,0:T(8,128)(2,1)} %get-tuple-element.186), channel_id=1, source_target_pairs={{0,4},{1,5},{2,6},{3,7},{8,0},{9,1},{10,2},{11,3},{16,8},{17,9},{1... | collective-permute-start | bytes 1474568 | tf_op jit(solution)/shard_map/ppermute | solution.py:463
  284.9 27.5 %collective-permute-start.39 = (bf16[5,192,512]{2,1,0:T(8,128)(2,1)}, bf16[5,192,512]{2,1,0:T(8,128)(2,1)}, u32[]{:S(2)}, u32[]{:S(2)}) collective-permute-start(bf16[5,192,512]{2,1,0:T(8,128)(2,1)} %get-tuple-element.198), channel_id=1, source_target_pairs={{0,8},{1,9},{2,10},{3,11},{8,16},{9,17},{10,18},{11,19},{16,24},{1... | collective-permute-start | bytes 2949128 | tf_op jit(solution)/shard_map/ppermute | solution.py:463
  286.8 25.7 %collective-permute-start.40 = (bf16[5,192,512]{2,1,0:T(8,128)(2,1)}, bf16[5,192,512]{2,1,0:T(8,128)(2,1)}, u32[]{:S(2)}, u32[]{:S(2)}) collective-permute-start(bf16[5,192,512]{2,1,0:T(8,128)(2,1)} %get-tuple-element.199), channel_id=1, source_target_pairs={{0,4},{1,5},{2,6},{3,7},{8,0},{9,1},{10,2},{11,3},{16,8},{17,9},{1... | collective-permute-start | bytes 2949128 | tf_op jit(solution)/shard_map/ppermute | solution.py:463
  306.4 17.8 %collective-permute-start.42 = (bf16[320,768]{1,0:T(8,128)(2,1)}, bf16[320,768]{1,0:T(8,128)(2,1)}, u32[]{:S(2)}, u32[]{:S(2)}) collective-permute-start(bf16[320,768]{1,0:T(8,128)(2,1)} %get-tuple-element.205), channel_id=1, source_target_pairs={{0,8},{1,9},{2,10},{3,11},{8,16},{9,17},{10,18},{11,19},{16,24},{1... | collective-permute-start | bytes 1474568 | tf_op jit(solution)/shard_map/ppermute | solution.py:463
  308.2 16.0 %collective-permute-start.43 = (bf16[320,768]{1,0:T(8,128)(2,1)}, bf16[320,768]{1,0:T(8,128)(2,1)}, u32[]{:S(2)}, u32[]{:S(2)}) collective-permute-start(bf16[320,768]{1,0:T(8,128)(2,1)} %get-tuple-element.206), channel_id=1, source_target_pairs={{0,4},{1,5},{2,6},{3,7},{8,0},{9,1},{10,2},{11,3},{16,8},{17,9},{1... | collective-permute-start | bytes 1474568 | tf_op jit(solution)/shard_map/ppermute | solution.py:463
  321.9 25.3 %collective-permute-start.47 = (bf16[5,192,512]{2,1,0:T(8,128)(2,1)}, bf16[5,192,512]{2,1,0:T(8,128)(2,1)}, u32[]{:S(2)}, u32[]{:S(2)}) collective-permute-start(bf16[5,192,512]{2,1,0:T(8,128)(2,1)} %get-tuple-element.211), channel_id=1, source_target_pairs={{0,8},{1,9},{2,10},{3,11},{8,16},{9,17},{10,18},{11,19},{16,24},{1... | collective-permute-start | bytes 2949128 | tf_op jit(solution)/shard_map/ppermute | solution.py:463
  324.0 25.0 %collective-permute-start.48 = (bf16[5,192,512]{2,1,0:T(8,128)(2,1)}, bf16[5,192,512]{2,1,0:T(8,128)(2,1)}, u32[]{:S(2)}, u32[]{:S(2)}) collective-permute-start(bf16[5,192,512]{2,1,0:T(8,128)(2,1)} %get-tuple-element.212), channel_id=1, source_target_pairs={{0,4},{1,5},{2,6},{3,7},{8,0},{9,1},{10,2},{11,3},{16,8},{17,9},{1... | collective-permute-start | bytes 2949128 | tf_op jit(solution)/shard_map/ppermute | solution.py:463
  336.5 23.6 %collective-permute-start.45 = (bf16[320,768]{1,0:T(8,128)(2,1)}, bf16[320,768]{1,0:T(8,128)(2,1)}, u32[]{:S(2)}, u32[]{:S(2)}) collective-permute-start(bf16[320,768]{1,0:T(8,128)(2,1)} %get-tuple-element.216), channel_id=1, source_target_pairs={{0,8},{1,9},{2,10},{3,11},{8,16},{9,17},{10,18},{11,19},{16,24},{1... | collective-permute-start | bytes 1474568 | tf_op jit(solution)/shard_map/ppermute | solution.py:463
  338.4 21.8 %collective-permute-start.46 = (bf16[320,768]{1,0:T(8,128)(2,1)}, bf16[320,768]{1,0:T(8,128)(2,1)}, u32[]{:S(2)}, u32[]{:S(2)}) collective-permute-start(bf16[320,768]{1,0:T(8,128)(2,1)} %get-tuple-element.217), channel_id=1, source_target_pairs={{0,4},{1,5},{2,6},{3,7},{8,0},{9,1},{10,2},{11,3},{16,8},{17,9},{1... | collective-permute-start | bytes 1474568 | tf_op jit(solution)/shard_map/ppermute | solution.py:463
  358.1 25.0 %collective-permute-start.51 = (bf16[5,192,512]{2,1,0:T(8,128)(2,1)}, bf16[5,192,512]{2,1,0:T(8,128)(2,1)}, u32[]{:S(2)}, u32[]{:S(2)}) collective-permute-start(bf16[5,192,512]{2,1,0:T(8,128)(2,1)} %get-tuple-element.222), channel_id=1, source_target_pairs={{0,8},{1,9},{2,10},{3,11},{8,16},{9,17},{10,18},{11,19},{16,24},{1... | collective-permute-start | bytes 2949128 | tf_op jit(solution)/shard_map/ppermute | solution.py:463
  359.6 25.0 %collective-permute-start.52 = (bf16[5,192,512]{2,1,0:T(8,128)(2,1)}, bf16[5,192,512]{2,1,0:T(8,128)(2,1)}, u32[]{:S(2)}, u32[]{:S(2)}) collective-permute-start(bf16[5,192,512]{2,1,0:T(8,128)(2,1)} %get-tuple-element.223), channel_id=1, source_target_pairs={{0,4},{1,5},{2,6},{3,7},{8,0},{9,1},{10,2},{11,3},{16,8},{17,9},{1... | collective-permute-start | bytes 2949128 | tf_op jit(solution)/shard_map/ppermute | solution.py:463
  364.7 28.5 %collective-permute-start.49 = (bf16[320,768]{1,0:T(8,128)(2,1)}, bf16[320,768]{1,0:T(8,128)(2,1)}, u32[]{:S(2)}, u32[]{:S(2)}) collective-permute-start(bf16[320,768]{1,0:T(8,128)(2,1)} %get-tuple-element.226), channel_id=1, source_target_pairs={{0,8},{1,9},{2,10},{3,11},{8,16},{9,17},{10,18},{11,19},{16,24},{1... | collective-permute-start | bytes 1474568 | tf_op jit(solution)/shard_map/ppermute | solution.py:463
  366.2 27.5 %collective-permute-start.50 = (bf16[320,768]{1,0:T(8,128)(2,1)}, bf16[320,768]{1,0:T(8,128)(2,1)}, u32[]{:S(2)}, u32[]{:S(2)}) collective-permute-start(bf16[320,768]{1,0:T(8,128)(2,1)} %get-tuple-element.227), channel_id=1, source_target_pairs={{0,4},{1,5},{2,6},{3,7},{8,0},{9,1},{10,2},{11,3},{16,8},{17,9},{1... | collective-permute-start | bytes 1474568 | tf_op jit(solution)/shard_map/ppermute | solution.py:463
  368.1 64.9 %collective-permute-start.44 = (bf16[384,2688]{1,0:T(8,128)(2,1)}, bf16[384,2688]{1,0:T(8,128)(2,1)}, u32[]{:S(2)}, u32[]{:S(2)}) collective-permute-start(bf16[384,2688]{1,0:T(8,128)(2,1)} %dynamic-slice_bitcast_fusion.1), channel_id=1, source_target_pairs={{0,2},{1,3},{2,0},{3,1},{4,6},{5,7},{6,4},{7,5},{8,10},{9,11},{10,... | collective-permute-start | bytes 6193160 | tf_op jit(solution)/shard_map/ppermute | solution.py:470
  391.1 25.0 %collective-permute-start.55 = (bf16[5,192,512]{2,1,0:T(8,128)(2,1)}, bf16[5,192,512]{2,1,0:T(8,128)(2,1)}, u32[]{:S(2)}, u32[]{:S(2)}) collective-permute-start(bf16[5,192,512]{2,1,0:T(8,128)(2,1)} %get-tuple-element.230), channel_id=1, source_target_pairs={{0,8},{1,9},{2,10},{3,11},{8,16},{9,17},{10,18},{11,19},{16,24},{1... | collective-permute-start | bytes 2949128 | tf_op jit(solution)/shard_map/ppermute | solution.py:463
  391.4 25.0 %collective-permute-start.56 = (bf16[5,192,512]{2,1,0:T(8,128)(2,1)}, bf16[5,192,512]{2,1,0:T(8,128)(2,1)}, u32[]{:S(2)}, u32[]{:S(2)}) collective-permute-start(bf16[5,192,512]{2,1,0:T(8,128)(2,1)} %get-tuple-element.231), channel_id=1, source_target_pairs={{0,4},{1,5},{2,6},{3,7},{8,0},{9,1},{10,2},{11,3},{16,8},{17,9},{1... | collective-permute-start | bytes 2949128 | tf_op jit(solution)/shard_map/ppermute | solution.py:463
  398.4 62.2 %collective-permute-start.53 = (bf16[320,768]{1,0:T(8,128)(2,1)}, bf16[320,768]{1,0:T(8,128)(2,1)}, u32[]{:S(2)}, u32[]{:S(2)}) collective-permute-start(bf16[320,768]{1,0:T(8,128)(2,1)} %get-tuple-element.234), channel_id=1, source_target_pairs={{0,8},{1,9},{2,10},{3,11},{8,16},{9,17},{10,18},{11,19},{16,24},{1... | collective-permute-start | bytes 1474568 | tf_op jit(solution)/shard_map/ppermute | solution.py:463
  400.2 60.4 %collective-permute-start.54 = (bf16[320,768]{1,0:T(8,128)(2,1)}, bf16[320,768]{1,0:T(8,128)(2,1)}, u32[]{:S(2)}, u32[]{:S(2)}) collective-permute-start(bf16[320,768]{1,0:T(8,128)(2,1)} %get-tuple-element.235), channel_id=1, source_target_pairs={{0,4},{1,5},{2,6},{3,7},{8,0},{9,1},{10,2},{11,3},{16,8},{17,9},{1... | collective-permute-start | bytes 1474568 | tf_op jit(solution)/shard_map/ppermute | solution.py:463
  416.4 37.7 %all-to-all-start = ((bf16[8,48,1664]{2,1,0:T(8,128)(2,1)}), bf16[8,48,1664]{2,1,0:T(8,128)(2,1)}, u32[]{:S(2)}, u32[]{:S(2)}) async-start(bf16[8,48,1664]{2,1,0:T(8,128)(2,1)} %bitcast.205), calls=%async_computation.2 | async-start | bytes 2555904 | tf_op jit(solution)/shard_map/all_to_all | solution.py:905
  420.7 100.0 %reduce-scatter.3.cloned.1.call-start = ((), (), s32[]{:S(2)}) async-start(), calls=%async_computation.5 | async-start | bytes 3932160 | tf_op jit(solution)/shard_map/reduce_scatter | solution.py:915
  431.0 39.6 %collective-permute-start.57 = (bf16[5,192,512]{2,1,0:T(8,128)(2,1)}, bf16[5,192,512]{2,1,0:T(8,128)(2,1)}, u32[]{:S(2)}, u32[]{:S(2)}) collective-permute-start(bf16[5,192,512]{2,1,0:T(8,128)(2,1)} %get-tuple-element.240), channel_id=1, source_target_pairs={{0,8},{1,9},{2,10},{3,11},{8,16},{9,17},{10,18},{11,19},{16,24},{1... | collective-permute-start | bytes 2949128 | tf_op jit(solution)/shard_map/ppermute | solution.py:463
  432.8 37.7 %collective-permute-start.58 = (bf16[5,192,512]{2,1,0:T(8,128)(2,1)}, bf16[5,192,512]{2,1,0:T(8,128)(2,1)}, u32[]{:S(2)}, u32[]{:S(2)}) collective-permute-start(bf16[5,192,512]{2,1,0:T(8,128)(2,1)} %get-tuple-element.241), channel_id=1, source_target_pairs={{0,4},{1,5},{2,6},{3,7},{8,0},{9,1},{10,2},{11,3},{16,8},{17,9},{1... | collective-permute-start | bytes 2949128 | tf_op jit(solution)/shard_map/ppermute | solution.py:463
  454.1 61.9 %all-to-all-start.1 = ((bf16[8,48,2688]{2,1,0:T(8,128)(2,1)}), bf16[8,48,2688]{2,1,0:T(8,128)(2,1)}, u32[]{:S(2)}, u32[]{:S(2)}) async-start(bf16[8,48,2688]{2,1,0:T(8,128)(2,1)} %bitcast.180), calls=%async_computation.3 | async-start | bytes 4128768 | tf_op jit(solution)/shard_map/all_to_all | solution.py:905
  (84 other events, 1118.6 us)
Sparse Core Ops, SparseCore 0:
  13.8 29.5 all-gather.1
  308.7 50.0 reduce-scatter.4
  433.2 39.1 reduce-scatter.2

commit v3 on v2

v3 whole, which is shorter than its diff:
```python
import functools

import jax
import jax.numpy as jnp
from jax import lax
from jax.experimental import pallas as pl
from jax.experimental.pallas import tpu as pltpu
from jax.sharding import PartitionSpec as P

H = 24
KV = 8
HD = 64
FE = 512
TOP = 8

EPSILON = 1e-06
THETA = 10000.0
NEGATIVE = -1e30
AXES = ("dp", "expert")
CORE, WIDE = 1, 2
LANES = 128

F32 = jnp.float32
BF16 = jnp.bfloat16


def rope_tables(length):
    half_size = HD // 2
    frequency = THETA ** (-(jnp.arange(half_size, dtype=F32) * 2.0) / HD)
    angles = jnp.arange(length, dtype=F32)[:, None] * frequency[None, :]
    cos, sin = jnp.cos(angles), jnp.sin(angles)
    return (
        jnp.concatenate([cos] * (LANES // half_size), axis=1),
        jnp.concatenate([-sin, sin] * (LANES // HD), axis=1),
    )


def rotate_tile(tile, cos, sin):
    half_size = HD // 2
    lane = lax.broadcasted_iota(jnp.int32, tile.shape, 1)
    ahead = pltpu.roll(tile, LANES - half_size, 1)
    back = pltpu.roll(tile, half_size, 1)
    return tile * cos + jnp.where(lane % HD < half_size, ahead, back) * sin


def dot(left, right, dims=((1,), (0,))):
    return lax.dot_general(left, right, (dims, ((), ())), preferred_element_type=F32)


NT = ((1,), (1,))


def spread_row(row, lane, count):
    at = lax.broadcasted_iota(jnp.int32, (count, row.shape[1]), 0) == lane
    return jnp.where(at, jnp.broadcast_to(row, at.shape), 0.0).T


def call(kernel, out_shape, scratch=(), limit=40, name=None, specs=None, aliases=None):
    vmem = pl.BlockSpec(memory_space=pltpu.VMEM)
    return pl.pallas_call(
        kernel,
        out_shape=out_shape,
        in_specs=specs,
        out_specs=jax.tree.map(lambda _: vmem, out_shape),
        scratch_shapes=scratch,
        compiler_params=pltpu.CompilerParams(vmem_limit_bytes=limit * 2**20),
        cost_estimate=pl.CostEstimate(flops=1024, bytes_accessed=1024, transcendentals=0),
        name=name,
    )


VMEM_SPEC = pl.BlockSpec(memory_space=pltpu.VMEM)
SMEM_SPEC = pl.BlockSpec(memory_space=pltpu.SMEM)
ANY_SPEC = pl.BlockSpec(memory_space=pl.ANY)
HBM_SPEC = pl.BlockSpec(memory_space=pltpu.HBM)


def fetch(numbers, pieces, held, sems):
    columns = held.shape[1]
    copies = []
    for piece in pieces:
        places, wides, rows, wide = piece.shape
        for j in range(places):
            for w in range(wides):
                k = len(copies)
                source = piece.at[j, w]
                if columns < wide:
                    source = source.at[:, pl.ds(0, columns)]
                at = pl.ds(pl.multiple_of(numbers[k] * rows, 16), rows)
                copies.append(pltpu.make_async_copy(source, held.at[at], sems.at[k]))
    for copy in copies:
        copy.start()
    return copies


def wait_all(copies):
    for copy in copies:
        copy.wait()


def heads_of(array, group):
    size = H // KV
    first = group * size
    return jnp.concatenate(
        [array[:, h * HD : (h + 1) * HD] for h in range(first, first + size)], axis=0
    )


def group_softmax(queries, keys, bias):
    scores = dot(keys, queries, NT) * HD ** (-0.5)
    scores = jnp.where(bias > 0.0, scores, NEGATIVE)
    exponent = jnp.exp(scores - jnp.max(scores, axis=0, keepdims=True))
    return exponent * (1.0 / jnp.sum(exponent, axis=0, keepdims=True))


def attend_kernel(experts_all, count, numbers, tokens, bias, cos, sin, *refs):
    pieces = refs[:count]
    normed, turned_both, queries, key_rows, values, mixed, gains, small = refs[count : count + 8]
    project, held, sems = refs[count + 8 :]
    copies = fetch(numbers, pieces, held, sems)
    columns = held.shape[1]
    wide = columns - LANES
    x = tokens[...].astype(F32)
    plain = x * lax.rsqrt(jnp.mean(x * x, axis=-1, keepdims=True) + EPSILON)
    wait_all(copies)
    small[...] = held[:, wide:]
    turned = held[:, wide:].astype(F32).T
    gains[...] = turned[experts_all // 8 * 8 : experts_all // 8 * 8 + 16]
    row = experts_all
    low = (plain * turned[row : row + 1]).astype(BF16)
    normed[...] = low
    width = tokens.shape[1]
    turned_both[:width, :] = low.T
    tile = 4 * LANES
    for start in range(0, wide, tile):
        at = slice(start, min(start + tile, wide))
        project[:, at] = dot(low, held[:, at])
    c, s = cos[...], sin[...]
    for t in range(H * HD // LANES):
        at = slice(t * LANES, (t + 1) * LANES)
        queries[:, at] = rotate_tile(project[:, at], c, s).astype(BF16)
    for t in range(KV * HD // LANES):
        at = slice(t * LANES, (t + 1) * LANES)
        from_ = slice(H * HD + t * LANES, H * HD + (t + 1) * LANES)
        key_rows[:, at] = rotate_tile(project[:, from_], c, s).astype(BF16)
    values[...] = project[:, (H + KV) * HD : (H + 2 * KV) * HD].astype(BF16)
    size = H // KV
    length = tokens.shape[0]
    wide_bias = jnp.concatenate([bias[...]] * size, axis=1)
    for g in range(KV):
        at = slice(g * HD, (g + 1) * HD)
        probs = group_softmax(heads_of(queries, g), key_rows[:, at], wide_bias).astype(BF16)
        out = dot(values[:, at].T, probs)
        for j in range(size):
            h = g * size + j
            head = out[:, j * length : (j + 1) * length]
            mixed[:, h * HD : (h + 1) * HD] = head.T.astype(BF16)
            turned_both[width + h * HD : width + (h + 1) * HD, :] = head.astype(BF16)


def attend(experts_all, tokens, bias, cos, sin, weight):
    pieces, numbers = weight
    length, width = tokens.shape
    columns = pieces[0].shape[3]
    shape = lambda *dims, kind=BF16: jax.ShapeDtypeStruct(dims, kind)
    out_shape = [
        shape(length, width),
        shape(width + H * HD, length),
        shape(length, H * HD),
        shape(length, KV * HD),
        shape(length, KV * HD),
        shape(length, H * HD),
        shape(16, width, kind=F32),
        shape(width, LANES),
    ]
    scratch = [
        pltpu.VMEM((length, columns - LANES), F32),
        pltpu.VMEM((width, columns), BF16),
        pltpu.SemaphoreType.DMA(numbers.shape),
    ]
    return call(
        functools.partial(attend_kernel, experts_all, len(pieces)),
        out_shape,
        scratch,
        limit=58,
        name="attend",
        specs=[SMEM_SPEC] + [VMEM_SPEC] * 4 + [HBM_SPEC] * len(pieces),
    )(numbers, tokens, bias, cos, sin, *pieces)


def branch_kernel(gain_row, count, numbers, tokens, mixed, small, gains, routes, *refs):
    pieces = refs[:count]
    hidden, sent, gate_float = refs[count : count + 3]
    held, sems = refs[count + 3 :]
    copies = fetch(numbers, pieces, held, sems)
    width = tokens.shape[1]
    wait_all(copies)
    state = tokens[...].astype(F32) + dot(mixed[...], held[...])
    hidden[...] = state
    recip = lax.rsqrt(jnp.mean(state * state, axis=-1, keepdims=True) + EPSILON)
    low = (state * recip * gains[gain_row : gain_row + 1, :]).astype(BF16)
    sent[:, :width] = low
    logits = dot(low, small[...])
    lanes = lax.broadcasted_iota(jnp.int32, logits.shape, 1)
    chosen = lanes < 0
    for j in range(routes.shape[1]):
        chosen = chosen | (lanes == routes[:, j : j + 1])
    picked = jnp.where(chosen, logits, NEGATIVE)
    exponent = jnp.where(chosen, jnp.exp(picked - jnp.max(picked, axis=-1, keepdims=True)), 0.0)
    gate = exponent / jnp.sum(exponent, axis=-1, keepdims=True)
    gate_float[...] = gate
    sent[:, width:] = gate.astype(BF16)


def branch(gain_row, tokens, mixed, weight, small, gains, routes):
    pieces, numbers = weight
    length, width = tokens.shape
    shape = lambda *dims, kind=BF16: jax.ShapeDtypeStruct(dims, kind)
    return call(
        functools.partial(branch_kernel, gain_row, len(pieces)),
        [
            shape(length, width, kind=F32),
            shape(length, width + LANES),
            shape(length, LANES, kind=F32),
        ],
        [pltpu.VMEM((mixed.shape[1], width), BF16), pltpu.SemaphoreType.DMA(numbers.shape)],
        limit=58,
        name="branch",
        specs=[SMEM_SPEC] + [VMEM_SPEC] * 5 + [HBM_SPEC] * len(pieces),
    )(numbers, tokens, mixed, small, gains, routes, *pieces)


def owner_rows_kernel(extra_given, blocks, *refs):
    refs = refs[1:]
    left, weight = refs[:blocks], refs[blocks]
    extra = refs[blocks + 1 : 2 * blocks + 1] if extra_given else None
    out, total = refs[-2:]
    expert = pl.program_id(0)
    count = left[0].shape[1]
    width = total.shape[1]
    dims = NT if extra_given else ((1,), (0,))
    share = dot(jnp.concatenate([a[0] for a in left], axis=0), weight[0], dims)

    @pl.when(expert == 0)
    def _():
        total[...] = share

    @pl.when(expert > 0)
    def _():
        total[...] += share

    @pl.when(expert == pl.num_programs(0) - 1)
    def _():
        out[:, :width] = total[...].astype(BF16)
        if extra_given:
            for i in range(blocks):
                out[i * count : (i + 1) * count, width:] = extra[i][...].astype(BF16)


def owner_rows(devices, left, weight, extra=None):
    blocks = devices.shape[0]
    local, rows, inner = left.shape
    width = weight.shape[1] if extra is not None else weight.shape[2]
    columns = width if extra is None else width + LANES
    count = rows // 4
    out_shape = jax.ShapeDtypeStruct((blocks * count, columns), BF16)
    piece = lambda k: pl.BlockSpec((1, count, inner), lambda i, d: (i, d[k], 0))
    in_specs = [piece(k) for k in range(blocks)]
    in_specs.append(pl.BlockSpec((1,) + weight.shape[1:], lambda i, d: (i, 0, 0)))
    operands = [left] * blocks + [weight]
    if extra is not None:
        more = lambda k: pl.BlockSpec((count, LANES), lambda i, d: (d[k], 0))
        in_specs += [more(k) for k in range(blocks)]
        operands += [extra] * blocks
    return pl.pallas_call(
        functools.partial(owner_rows_kernel, extra is not None, blocks),
        out_shape=out_shape,
        grid_spec=pltpu.PrefetchScalarGridSpec(
            num_scalar_prefetch=1,
            grid=(local,),
            in_specs=in_specs,
            out_specs=pl.BlockSpec(out_shape.shape, lambda i, d: (0, 0)),
            scratch_shapes=[pltpu.VMEM((blocks * count, width), F32)],
        ),
        compiler_params=pltpu.CompilerParams(vmem_limit_bytes=58 * 2**20),
        cost_estimate=pl.CostEstimate(flops=1024, bytes_accessed=1024, transcendentals=0),
        name="owner_rows",
    )(devices.astype(jnp.int32), *operands)


def middle_kernel(
    experts_all,
    gain_row,
    parts,
    numbers,
    came,
    cotangent,
    hidden,
    gate_float,
    gains,
    small,
    *refs,
):
    pieces = refs[:parts]
    grad_hidden, pack, grad_mixed, held, sems = refs[parts:]
    copies = fetch(numbers, pieces, held, sems)
    count, width = cotangent.shape
    total = came[0].astype(F32) + came[1].astype(F32)
    gate = gate_float[...]
    gate_grad = total[:, width:].astype(BF16).astype(F32)
    centered = gate_grad - jnp.sum(gate * gate_grad, axis=-1, keepdims=True)
    logit_grad = (gate * centered).astype(BF16)
    grad_normed = total[:, :width] + dot(logit_grad, small[...], NT)
    state = hidden[...]
    recip = lax.rsqrt(jnp.mean(state * state, axis=-1, keepdims=True) + EPSILON)
    plain = state * recip
    scaled = grad_normed * gains[gain_row : gain_row + 1, :]
    gain_grad = jnp.sum(grad_normed * plain, axis=0, keepdims=True)
    back = recip * (scaled - plain * jnp.mean(scaled * plain, axis=-1, keepdims=True))
    grad = cotangent[...].astype(F32) + back
    grad_hidden[...] = grad
    low = grad.astype(BF16)
    first = lax.broadcasted_iota(jnp.int32, (16, width), 0) == 0
    high = gain_grad.astype(BF16).astype(F32)
    for k in range(2):
        pack[k, :count, :width] = low
        pack[k, :count, width:] = logit_grad
        pack[k, count:, :width] = jnp.where(first, high, gain_grad - high).astype(BF16)
        pack[k, count:, width:] = jnp.zeros((16, LANES), BF16)
    wait_all(copies)
    grad_mixed[...] = dot(low, held[...], NT).astype(BF16)


def attend_back_kernel(
    queries, key_rows, values, grad_mixed, bias, cos, sin, grad_project, project
):
    columns = grad_project.shape[2]
    size = H // KV
    length = queries.shape[0]
    scale = HD ** (-0.5)
    wide_bias = jnp.concatenate([bias[...]] * size, axis=1)
    for g in range(KV):
        at = slice(g * HD, (g + 1) * HD)
        q, k, v = heads_of(queries, g), key_rows[:, at], values[:, at]
        upstream = heads_of(grad_mixed, g)
        weights = group_softmax(q, k, wide_bias)
        grad_values = dot(weights.astype(BF16), upstream)
        grad_probs = dot(v, upstream, NT)
        delta = jnp.sum(weights * grad_probs, axis=0, keepdims=True)
        grad_scores = (weights * (grad_probs - delta)).astype(BF16)
        grad_keys = dot(grad_scores, q) * scale
        grad_queries = dot(k.T, grad_scores) * scale
        for j in range(size):
            h = g * size + j
            project[:, h * HD : (h + 1) * HD] = grad_queries[:, j * length : (j + 1) * length].T
        project[:, (H + g) * HD : (H + g + 1) * HD] = grad_keys
        project[:, (H + KV + g) * HD : (H + KV + g + 1) * HD] = grad_values
    c, s = cos[...], -sin[...]
    turns = (H + KV) * HD // LANES
    for t in range(turns):
        at = slice(t * LANES, (t + 1) * LANES)
        tile = rotate_tile(project[:, at], c, s).astype(BF16)
        grad_project[0, :, at] = tile
        grad_project[1, :, at] = tile
    rest = slice(turns * LANES, columns)
    tile = project[:, rest].astype(BF16)
    grad_project[0, :, rest] = tile
    grad_project[1, :, rest] = tile


def attend_back(*operands):
    length = operands[0].shape[0]
    columns = (H + 2 * KV) * HD
    return call(
        attend_back_kernel,
        jax.ShapeDtypeStruct((2, length, columns), BF16),
        [pltpu.VMEM((length, columns), F32)],
        limit=58,
        name="attend_back",
        specs=[VMEM_SPEC] * 7,
    )(*operands)


def input_back_kernel(
    gain_row, parts, numbers, tokens, grad_project, gains, grad_hidden, *refs
):
    pieces = refs[:parts]
    grad_tokens, held, sems = refs[parts:]
    copies = fetch(numbers, pieces, held, sems)
    wait_all(copies)
    grad_normed = dot(grad_project[0], held[...], NT)
    x = tokens[...].astype(F32)
    recip = lax.rsqrt(jnp.mean(x * x, axis=-1, keepdims=True) + EPSILON)
    plain = x * recip
    scaled = grad_normed * gains[gain_row : gain_row + 1, :]
    back = recip * (scaled - plain * jnp.mean(scaled * plain, axis=-1, keepdims=True))
    grad_tokens[...] = grad_hidden[...] + back


def middle(experts_all, gain_row, weight, *operands):
    pieces, numbers = weight
    count, width = operands[1].shape
    shape = lambda *dims, kind=BF16: jax.ShapeDtypeStruct(dims, kind)
    return call(
        functools.partial(middle_kernel, experts_all, gain_row, len(pieces)),
        [
            shape(count, width, kind=F32),
            shape(2, count + 16, width + LANES),
            shape(count, H * HD),
        ],
        [pltpu.VMEM((H * HD, width), BF16), pltpu.SemaphoreType.DMA(numbers.shape)],
        limit=58,
        name="middle",
        specs=[SMEM_SPEC] + [VMEM_SPEC] * 6 + [HBM_SPEC] * len(pieces),
    )(numbers, *operands, *pieces)


def input_back(gain_row, weight, *operands):
    pieces, numbers = weight
    length, width = operands[0].shape
    columns = operands[1].shape[2]
    return call(
        functools.partial(input_back_kernel, gain_row, len(pieces)),
        jax.ShapeDtypeStruct((length, width), F32),
        [pltpu.VMEM((width, columns), BF16), pltpu.SemaphoreType.DMA(numbers.shape)],
        limit=58,
        name="input_back",
        specs=[SMEM_SPEC] + [VMEM_SPEC] * 4 + [HBM_SPEC] * len(pieces),
    )(numbers, *operands, *pieces)


def after(value, *earlier):
    return lax.optimization_barrier((value, earlier))[0]


class Net:
    def __init__(self):
        self.nd = lax.axis_size("dp")
        self.ne = lax.axis_size("expert")
        self.p = lax.axis_index("dp")
        self.e = lax.axis_index("expert")
        self.r = self.place_of(self.p)
        order = list(range(0, self.nd, 2)) + list(range(1, self.nd, 2))[::-1]
        nd, ne = self.nd, self.ne
        self.ring = {
            way: [
                (order[i] * ne + e, order[(i + way) % nd] * ne + e)
                for i in range(nd)
                for e in range(ne)
            ]
            for way in (1, -1)
        }
        self.devices = nd * ne

    def place_of(self, p):
        return jnp.where(p % 2 == 0, p // 2, self.nd - 1 - p // 2)

    def dp_of(self, r):
        r = r % self.nd
        return jnp.where(r < self.nd // 2, 2 * r, 2 * (self.nd - 1 - r) + 1)

    def step(self, value, way):
        return lax.ppermute(value, AXES, self.ring[way])

    def exchange(self, value, bit):
        pairs = [[d, d | 1 << bit] for d in range(self.devices) if not d >> bit & 1]
        return lax.all_to_all(value, AXES, 0, 0, axis_index_groups=pairs, tiled=True)

    def swap(self, value, bit):
        return lax.ppermute(value, AXES, [(d, d ^ bit) for d in range(self.devices)])


def gather_weights(net, first, second, beside):
    half = net.nd // 2
    other_first = net.swap(first, WIDE)
    other_second = net.swap(after(second, other_first), WIDE)
    own = [jnp.stack([first, other_first]), jnp.stack([second, other_second])]
    offsets = [(0,)] + [(-s, s) for s in range(1, half)] + [(half,)]
    parts = [[], []]
    ahead, back = list(own), list(own)
    sent = None
    for s in range(half + 1):
        for k in (0, 1):
            if k == 0 and s == half - 2:
                ahead[k], back[k] = after((ahead[k], back[k]), beside)
            elif sent is not None:
                ahead[k], back[k] = after((ahead[k], back[k]), sent)
            sent = (ahead[k], back[k])
            if s in (0, half):
                parts[k].append((ahead[k] if s == 0 else jnp.stack([ahead[k], back[k]]))[None])
            else:
                parts[k].append(jnp.stack([ahead[k], back[k]]))
            if s + 1 < half:
                ahead[k] = net.step(ahead[k], 1)
                back[k] = net.step(back[k], -1)
            elif s + 1 == half:
                ahead[k] = net.step(ahead[k][0], 1)
                back[k] = net.step(back[k][1], -1)
    def numbers(groups):
        return [
            net.dp_of(net.r + offset) * net.ne + (net.e ^ bits)
            for group in groups
            for bits_of_core in (0, CORE)
            for offset in group
            for bits in (bits_of_core, bits_of_core ^ WIDE)
        ]

    first_pieces = [piece for mine in parts[0] for piece in (mine, net.swap(mine, CORE))]
    mine = jnp.concatenate(parts[1])
    second_pieces = [mine, net.swap(mine, CORE)]
    return (
        as_weight(first_pieces, numbers(offsets)),
        as_weight(second_pieces, numbers([[o for group in offsets for o in group]])),
    )


def as_weight(pieces, numbers):
    rows, columns = pieces[0].shape[2:]
    if rows % 16:
        blocks = jnp.concatenate([piece.reshape(-1, rows, columns) for piece in pieces])
        full = jnp.zeros_like(blocks).at[jnp.stack(numbers)].set(blocks)
        pieces, numbers = [full.reshape(1, 1, -1, columns)], [jnp.zeros((), jnp.int32)]
    return pieces, jnp.stack(numbers).astype(jnp.int32)


def weight_products_kernel(place, left, normed_two, gain, *refs):
    projects, packs, out = refs[:2], refs[2:4], refs[4]
    depth, count = out.shape[0], projects[0].shape[1]
    columns = projects[0].shape[2]
    width = packs[0].shape[2] - LANES
    core = place[0] % 2
    order = [2 * wide + c for c in (core, 1 - core) for wide in (0, 1)]

    def below(arrays, at):
        return jnp.concatenate([r[wide, :count, at] for r in arrays for wide in (0, 1)], axis=0)

    first = jnp.concatenate([left[i, :depth, :] for i in order], axis=1)
    second = jnp.concatenate([left[i, depth:, :] for i in order], axis=1)
    third = jnp.concatenate([normed_two[i] for i in order], axis=1)
    tile = 4 * LANES
    for start in range(0, columns, tile):
        at = slice(start, start + tile)
        out[:, at] = dot(first, below(projects, at)).astype(BF16)
    for start in range(0, width, tile):
        at = slice(start, start + tile)
        to = slice(columns + start, columns + start + tile)
        out[:, to] = dot(second, below(packs, at)).astype(BF16)
    rest = dot(third, below(packs, slice(width, width + LANES)))
    out[:, columns + width :] = (rest + gain[...]).astype(BF16)


def weight_products(place, left, normed_two, gain, projects, packs):
    depth = left.shape[1] // 2
    return call(
        weight_products_kernel,
        jax.ShapeDtypeStruct((depth, projects[0].shape[2] + packs[0].shape[2]), BF16),
        limit=58,
        name="weight_products",
        specs=[SMEM_SPEC] + [VMEM_SPEC] * 7,
    )(place, left, normed_two, gain, *projects, *packs)


def gain_column_kernel(lane, *refs):
    packs, out = refs[:2], refs[2]
    width = out.shape[0]
    count = packs[0].shape[1] - 16
    rows = sum(r[wide, count : count + 2, :width].astype(F32) for r in packs for wide in (0, 1))
    out[...] = spread_row(jnp.sum(rows, axis=0, keepdims=True), lane, LANES)


def gain_column(lane, packs):
    return call(
        functools.partial(gain_column_kernel, lane),
        jax.ShapeDtypeStruct((packs[0].shape[2] - LANES, LANES), F32),
        limit=58,
        name="gain_column",
        specs=[VMEM_SPEC] * 2,
    )(*packs)


def fold_kernel(came, out):
    for i in range(2):
        out[i, 0] = (came[0, 0, i].astype(F32) + came[1, 0, i].astype(F32)).astype(BF16)


def fold(came, rows):
    columns = came.shape[2]
    came = came.reshape(2, -1, 2, rows, columns)
    count = came.shape[1]
    return pl.pallas_call(
        fold_kernel,
        out_shape=jax.ShapeDtypeStruct((2, count, rows, columns), BF16),
        grid=(count,),
        in_specs=[pl.BlockSpec((2, 1, 2, rows, columns), lambda i: (0, i, 0, 0, 0))],
        out_specs=pl.BlockSpec((2, 1, rows, columns), lambda i: (0, i, 0, 0)),
        compiler_params=pltpu.CompilerParams(vmem_limit_bytes=58 * 2**20),
        cost_estimate=pl.CostEstimate(flops=1024, bytes_accessed=1024, transcendentals=0),
        name="fold",
    )(came).reshape(2, count * rows, columns)


class BlockSum:
    def __init__(self, net, halves, rows):
        self.net, self.halves, self.bit, self.rows = net, halves, 0, rows
        self.count = net.devices.bit_length() - 1

    def send(self, *earlier):
        halves = after(self.halves, *earlier) if earlier else self.halves
        self.came = self.net.exchange(halves, self.bit)
        self.bit += 1

    def add(self, *earlier):
        came = after(self.came, *earlier) if earlier else self.came
        if self.bit == self.count:
            return jnp.sum(came.astype(F32), axis=0)
        self.halves = fold(came, self.rows)
        return self.halves


def in_kernel(last, places, turned_rows, grad_pre, *refs):
    came, refs = (refs[:2], refs[2:]) if len(refs) > 10 - last else (None, refs)
    outs, (rows, grads, added, shares, rows_sems, grad_sems, came_sems, out_sems) = (
        refs[: 2 - last],
        refs[2 - last :],
    )
    local = grads.shape[0]
    depth = rows.shape[1]

    def rows_copy(i):
        at = pl.ds(pl.multiple_of(places[i] * depth, 16), depth)
        return pltpu.make_async_copy(turned_rows.at[at], rows.at[i], rows_sems.at[i])

    def grad_copy(e):
        return pltpu.make_async_copy(grad_pre.at[e], grads.at[e], grad_sems.at[e])

    def came_copy(i, e):
        return pltpu.make_async_copy(came[i].at[e], added.at[i, e], came_sems.at[i, e])

    def out_copy(i, e):
        if last:
            target = outs[0].at[e, :, pl.ds(i * FE, FE)]
        else:
            target = outs[i].at[e]
        return pltpu.make_async_copy(shares.at[i, e], target, out_sems.at[i, e])

    def begin(e):
        grad_copy(e).start()
        if came is not None:
            for i in range(2):
                came_copy(i, e).start()

    for i in range(2):
        rows_copy(i).start()
    begin(0)
    begin(1)
    for i in range(2):
        rows_copy(i).wait()

    @pl.loop(0, local)
    def _(e):
        @pl.when(e + 2 < local)
        def _():
            begin(e + 2)

        grad_copy(e).wait()
        if came is not None:
            for i in range(2):
                came_copy(i, e).wait()
        for i in range(2):
            share = dot(rows[i], grads[e, :, i * FE : (i + 1) * FE])
            if came is not None:
                share += added[i, e].astype(F32)
            shares[i, e] = share.astype(shares.dtype)
            out_copy(i, e).start()

    @pl.loop(0, local)
    def _(e):
        for i in range(2):
            out_copy(i, e).wait()


def in_share(places, turned_rows, grad_pre, came, cost, last=False):
    local, tokens_all, wide = grad_pre.shape
    depth = turned_rows.shape[0] // lax.axis_size("dp")
    kind = F32 if last else BF16
    if last:
        out_shape = [jax.ShapeDtypeStruct((local, depth, wide), kind)]
    else:
        out_shape = [jax.ShapeDtypeStruct((local, depth, FE), kind)] * 2
    return pl.pallas_call(
        functools.partial(in_kernel, int(last)),
        out_shape=out_shape,
        in_specs=[SMEM_SPEC] + [ANY_SPEC] * (2 + len(came)),
        out_specs=[ANY_SPEC] * len(out_shape),
        scratch_shapes=[
            pltpu.VMEM((2, depth, tokens_all), BF16),
            pltpu.VMEM((local, tokens_all, wide), BF16),
            pltpu.VMEM((2, local, depth, FE), BF16),
            pltpu.VMEM((2, local, depth, FE), kind),
            pltpu.SemaphoreType.DMA((2,)),
            pltpu.SemaphoreType.DMA((local,)),
            pltpu.SemaphoreType.DMA((2, local)),
            pltpu.SemaphoreType.DMA((2, local)),
        ],
        compiler_params=pltpu.CompilerParams(vmem_limit_bytes=58 * 2**20),
        cost_estimate=pl.CostEstimate(flops=cost, bytes_accessed=1024, transcendentals=0),
        name="in_share",
    )(places, turned_rows, grad_pre, *came)


def out_kernel(last, places, turned_act, upstream, *refs):
    came, refs = (refs[:2], refs[2:]) if len(refs) > 10 else (None, refs)
    outs, (rows, ups, added, shares, rows_sems, up_sems, came_sems, out_sems) = refs[:2], refs[2:]
    local, depth, tokens_all = rows.shape[1:]
    half = ups.shape[2]

    def copies(i):
        at = pl.ds(pl.multiple_of(places[i] * depth, 16), depth)
        some = [
            pltpu.make_async_copy(turned_act.at[:, at], rows.at[i], rows_sems.at[i]),
            pltpu.make_async_copy(upstream.at[:, pl.ds(i * half, half)], ups.at[i], up_sems.at[i]),
        ]
        if came is not None:
            some.append(pltpu.make_async_copy(came[i], added.at[i], came_sems.at[i]))
        return some

    def out_copy(i):
        return pltpu.make_async_copy(shares.at[i], outs[i], out_sems.at[i])

    for i in range(2):
        for copy in copies(i):
            copy.start()
    for i in range(2):
        for copy in copies(i):
            copy.wait()
        share = dot(rows[i].reshape(local * depth, tokens_all), ups[i])
        if came is not None:
            share += added[i].astype(F32)
        shares[i] = share.astype(shares.dtype)
        out_copy(i).start()
    for i in range(2):
        out_copy(i).wait()


def out_share(places, turned_act, upstream_all, came, cost, last=False):
    local, hidden, tokens_all = turned_act.shape
    half = upstream_all.shape[1] // 2
    depth = hidden // lax.axis_size("dp")
    kind = F32 if last else BF16
    return pl.pallas_call(
        functools.partial(out_kernel, int(last)),
        out_shape=[jax.ShapeDtypeStruct((local * depth, half), kind)] * 2,
        in_specs=[SMEM_SPEC] + [ANY_SPEC] * (2 + len(came)),
        out_specs=[ANY_SPEC] * 2,
        scratch_shapes=[
            pltpu.VMEM((2, local, depth, tokens_all), BF16),
            pltpu.VMEM((2, tokens_all, half), BF16),
            pltpu.VMEM((2, local * depth, half), BF16),
            pltpu.VMEM((2, local * depth, half), kind),
        ]
        + [pltpu.SemaphoreType.DMA((2,))] * 4,
        compiler_params=pltpu.CompilerParams(vmem_limit_bytes=58 * 2**20),
        cost_estimate=pl.CostEstimate(flops=cost, bytes_accessed=1024, transcendentals=0),
        name="out_share",
    )(places, turned_act, upstream_all, *came)


def owner_grads_kernel(upstream, weight, out):
    out[0] = dot(upstream[...], weight[0], NT).astype(BF16)


def owner_grads(upstream, weight):
    local, hidden, width = weight.shape
    rows = upstream.shape[0]
    return pl.pallas_call(
        owner_grads_kernel,
        out_shape=jax.ShapeDtypeStruct((local, rows, hidden), BF16),
        grid=(local,),
        in_specs=[
            pl.BlockSpec(upstream.shape, lambda i: (0, 0)),
            pl.BlockSpec((1, hidden, width), lambda i: (i, 0, 0)),
        ],
        out_specs=pl.BlockSpec((1, rows, hidden), lambda i: (i, 0, 0)),
        compiler_params=pltpu.CompilerParams(vmem_limit_bytes=58 * 2**20),
        cost_estimate=pl.CostEstimate(
            flops=2 * local * rows * hidden * width, bytes_accessed=16 * 2**20, transcendentals=0
        ),
        name="owner_grads",
    )(upstream, weight)


def expert_kernel(later, scalars, rows_a, rows_b, grad_plain, weight, *refs):
    refs = refs[5 if later else 0 :]
    outs, bufs, (weights, plains, weight_sems, plain_sems, out_sems) = refs[:5], refs[5:10], refs[10:]
    activated, turned_act, grad_pre, gate_grad, turned_rows = bufs
    local, width = weights.shape[:2]
    count = rows_a.shape[0]
    half = pl.ds(pl.multiple_of(scalars[1] * 2 * count, 2 * count), 2 * count)

    def weight_copy(e):
        return pltpu.make_async_copy(weight.at[e], weights.at[e], weight_sems.at[e])

    def plain_copy(e):
        return pltpu.make_async_copy(grad_plain.at[e, half], plains.at[e], plain_sems.at[e])

    def out_copies(e):
        return [
            pltpu.make_async_copy(activated.at[e], outs[0].at[e, half], out_sems.at[0, e]),
            pltpu.make_async_copy(turned_act.at[e], outs[1].at[e, :, half], out_sems.at[1, e]),
            pltpu.make_async_copy(grad_pre.at[e], outs[2].at[e, half], out_sems.at[2, e]),
        ]

    rows_copy = pltpu.make_async_copy(turned_rows, outs[4].at[:, half], out_sems.at[3, 0])
    gate_copy = pltpu.make_async_copy(gate_grad, outs[3].at[half], out_sems.at[3, 1])
    for e in range(2):
        weight_copy(e).start()
        plain_copy(e).start()
    both = (rows_a, rows_b)
    starts = [pl.multiple_of(scalars[2] * count, count), pl.multiple_of((1 - scalars[2]) * count, count)]
    gate_grad[...] = jnp.zeros_like(gate_grad)
    for start, rows in zip(starts, both):
        turned_rows[:, pl.ds(start, count)] = rows[:, :width].T
    rows_copy.start()
    lanes = lax.broadcasted_iota(jnp.int32, (count, LANES), 1)
    tile = 2 * LANES

    @pl.loop(0, local)
    def _(e):
        here = lanes == scalars[0] + e

        @pl.when(e + 2 < local)
        def _():
            weight_copy(e + 2).start()
            plain_copy(e + 2).start()

        weight_copy(e).wait()
        plain_copy(e).wait()
        gates = [
            jnp.sum(jnp.where(here, rows[:, width:].astype(F32), 0.0), axis=1, keepdims=True)
            for rows in both
        ]
        x = jnp.concatenate([rows[:, :width] for rows in both], axis=0)
        sums = [0.0, 0.0]
        for f in range(0, FE, tile):
            g_both = dot(x, weights[e, :, f : f + tile])
            u_both = dot(x, weights[e, :, FE + f : FE + f + tile])
            for i in range(2):
                at = pl.ds(starts[i], count)
                part = slice(i * count, (i + 1) * count)
                g, u, gate = g_both[part], u_both[part], gates[i]
                s = jax.nn.sigmoid(g)
                silu = g * s
                act = silu * u
                plain = plains[e, at, f : f + tile].astype(F32)
                sums[i] += jnp.sum(act * plain, axis=1, keepdims=True)
                low = (act * gate).astype(BF16)
                activated[e, at, f : f + tile] = low
                turned_act[e, f : f + tile, at] = low.T
                da = plain * gate
                grad_pre[e, at, f : f + tile] = (da * u * s * (1.0 + g * (1.0 - s))).astype(BF16)
                grad_pre[e, at, FE + f : FE + f + tile] = (da * silu).astype(BF16)
        for copy in out_copies(e):
            copy.start()
        for i in range(2):
            gate_grad[pl.ds(starts[i], count), :] += jnp.where(here, sums[i], 0.0)

    gate_copy.start()
    rows_copy.wait()
    gate_copy.wait()

    @pl.loop(0, local)
    def _(e):
        for copy in out_copies(e):
            copy.wait()


def expert_half(scalars, rows_a, rows_b, grad_plain, weight, earlier):
    count = 2 * rows_a.shape[0]
    local, width, wide = weight.shape
    total = 2 * count
    out_shape = [
        jax.ShapeDtypeStruct((local, total, FE), BF16),
        jax.ShapeDtypeStruct((local, FE, total), BF16),
        jax.ShapeDtypeStruct((local, total, wide), BF16),
        jax.ShapeDtypeStruct((total, LANES), F32),
        jax.ShapeDtypeStruct((width, total), BF16),
    ]
    return pl.pallas_call(
        functools.partial(expert_kernel, bool(earlier)),
        out_shape=out_shape,
        in_specs=[SMEM_SPEC, VMEM_SPEC, VMEM_SPEC, ANY_SPEC, ANY_SPEC] + [ANY_SPEC] * len(earlier),
        out_specs=[ANY_SPEC] * 5,
        scratch_shapes=[
            pltpu.VMEM((local, count, FE), BF16),
            pltpu.VMEM((local, FE, count), BF16),
            pltpu.VMEM((local, count, wide), BF16),
            pltpu.VMEM((count, LANES), F32),
            pltpu.VMEM((width, count), BF16),
            pltpu.VMEM(weight.shape, BF16),
            pltpu.VMEM((local, count, FE), BF16),
            pltpu.SemaphoreType.DMA((local,)),
            pltpu.SemaphoreType.DMA((local,)),
            pltpu.SemaphoreType.DMA((4, max(local, 2))),
        ],
        input_output_aliases={5 + k: k for k in range(len(earlier))},
        compiler_params=pltpu.CompilerParams(vmem_limit_bytes=58 * 2**20),
        cost_estimate=pl.CostEstimate(
            flops=2 * local * count * width * wide, bytes_accessed=30 * 2**20, transcendentals=0
        ),
        name="expert_half",
    )(scalars, rows_a, rows_b, grad_plain, weight, *earlier)


def on_device(
    tokens,
    cotangent,
    routes,
    segments,
    w_qkv,
    w_out,
    router,
    gain_attn,
    gain_mlp,
    expert_in,
    expert_out,
):
    net = Net()
    length, width = tokens.shape
    local_count = expert_in.shape[0]
    experts_all = local_count * net.ne
    wide_qkv = w_qkv.shape[1]

    small = jnp.concatenate([router, gain_attn[:, None], gain_mlp[:, None]], axis=1)
    small = jnp.pad(small, ((0, 0), (0, LANES - small.shape[1])))
    first_block = jnp.concatenate([w_qkv, small], axis=1)
    upstream_all = lax.all_gather(cotangent, "expert", axis=0, tiled=True)
    grad_act_plain = owner_grads(upstream_all, expert_out)
    qkv_weight, out_weight = gather_weights(net, first_block, w_out, grad_act_plain)
    gain_row = experts_all % 8

    cos, sin = rope_tables(length)
    places_row = jnp.arange(length)
    bias = (
        (places_row[:, None] <= places_row[None, :])
        & (segments[0][:, None] == segments[0][None, :])
    ).astype(F32)
    normed, turned_both, queries, key_rows, values, mixed_heads, gains, small_full = attend(
        experts_all, tokens, bias, cos, sin, qkv_weight
    )
    hidden_state, sent, gate_float = branch(
        gain_row + 1, tokens, mixed_heads, out_weight, small_full, gains, routes
    )
    across_rows = net.swap(sent, WIDE)
    own_rows, beside_rows = sent, net.swap(sent, CORE)
    core, wide = net.e % 2, net.e // 2
    scalars = lambda half: jnp.stack([net.e * local_count, half, core]).astype(jnp.int32)
    early = expert_half(scalars(wide), own_rows, beside_rows, grad_act_plain, expert_in, ())
    across_rows = after(across_rows, early)
    corner_rows = net.swap(across_rows, CORE)
    activated, turned_act, grad_pre, gate_grads, turned_rows = expert_half(
        scalars(1 - wide), across_rows, corner_rows, grad_act_plain, expert_in, early
    )

    def places(s):
        return jnp.stack([net.dp_of(net.r - 1 - s), net.dp_of(net.r + 1 + s)]).astype(jnp.int32)

    def cost(s):
        return 10**10 if s == 4 else 3 * 10**10

    def advance(shares):
        return [net.step(shares[0], 1), net.step(shares[1], -1)]

    came_in, came_out = (), ()

    def ring_in(s, *earlier, beside=None):
        nonlocal came_in
        if earlier:
            came_in = after(came_in, *earlier)
        shares = in_share(places(s), turned_rows, grad_pre, came_in, cost(s))
        if beside is not None:
            shares = after(shares, beside)
        came_in = advance(shares)
        return shares

    def ring_out(s, *earlier, beside=None):
        nonlocal came_out
        if earlier:
            came_out = after(came_out, *earlier)
        shares = out_share(places(s), turned_act, upstream_all, came_out, cost(s))
        if beside is not None:
            shares = after(shares, beside)
        came_out = advance(shares)
        return shares

    def devices(*bits):
        return jnp.stack([net.e ^ bit for bit in bits])

    sent_out = ring_out(0)
    sent_in = ring_in(0, sent_out)
    block = width // net.devices
    lefts = turned_both.reshape(2, net.nd, net.ne, block, length).transpose(2, 0, 1, 3, 4)
    lefts = lax.all_to_all(
        lefts.reshape(net.ne, -1, length), "expert", 0, 0, tiled=True
    )
    beside = owner_rows(devices(1, 3), after(grad_pre, sent_in, lefts), expert_in, gate_grads)
    beside_came = net.swap(beside, CORE)
    sent_out = ring_out(1, beside, beside=beside_came)
    kept = owner_rows(devices(0, 2), after(grad_pre, sent_out), expert_in, gate_grads)
    both = (kept.astype(F32) + beside_came.astype(F32)).astype(BF16)
    both = both.reshape(2, length, -1)
    came = net.exchange(jnp.where(wide == 0, both, both[::-1]), 1)
    sent_in = ring_in(1, both)
    mix = owner_rows(jnp.arange(4), after(activated, sent_in), expert_out)
    sent_out = ring_out(2, mix)
    grad_hidden, pack, grad_mixed = middle(
        experts_all,
        gain_row + 1,
        out_weight,
        after(came, sent_out),
        cotangent,
        hidden_state,
        gate_float,
        gains,
        small_full,
    )
    packs = net.exchange(pack, 1)
    sent_in = ring_in(2, grad_mixed)
    grad_project = attend_back(
        queries, key_rows, values, after(grad_mixed, sent_in), bias, cos, sin
    )
    projects = net.exchange(grad_project, 1)
    sent_out = ring_out(3, grad_project)
    sent_in = ring_in(3, sent_out)
    sent_out = ring_out(4, sent_in)
    projects, packs = after((projects, packs), sent_out, came_in)
    projects_beside, packs_beside = net.swap(projects, CORE), net.swap(packs, CORE)
    sent_in = ring_in(4, projects, packs, beside=(projects_beside, packs_beside))
    mine = lambda rows: lax.dynamic_index_in_dim(
        rows.reshape(net.nd, net.ne, block, -1), net.e, 1, keepdims=False
    ).reshape(net.nd * block, -1)
    normed_two = mine(turned_rows).reshape(-1, net.ne, length).transpose(1, 0, 2)
    packs = (packs, packs_beside)
    products = weight_products(
        net.e.astype(jnp.int32).reshape(1),
        after(lefts, sent_in),
        normed_two,
        mine(gain_column(experts_all, packs)),
        (projects, projects_beside),
        packs,
    )
    sent_out = ring_out(5, products)
    d_all = lax.psum_scatter(after(products, sent_out), "dp", scatter_dimension=0, tiled=True)
    sent_in = ring_in(5, sent_out)
    mix_all = lax.all_to_all(after(mix, sent_in), "expert", 0, 0, tiled=True)
    for s in range(6, net.nd - 1):
        sent_out = ring_out(s, sent_in)
        sent_in = ring_in(s, sent_out)
    grad_tokens = input_back(
        gain_row, qkv_weight, tokens, after(grad_project, sent_in), gains, grad_hidden
    )
    mixture = jnp.sum(mix_all.reshape(net.ne, length, width).astype(F32), axis=0)
    activations = (hidden_state + mixture).astype(BF16)
    here = jnp.stack([net.p, net.p]).astype(jnp.int32)
    d_expert_out = jnp.concatenate(
        out_share(
            here, turned_act, upstream_all, after(came_out, grad_tokens), cost(net.nd), last=True
        ),
        axis=1,
    ).reshape(local_count, FE // net.nd, width)
    d_all = after(d_all, d_expert_out).astype(F32)
    d_qkv = d_all[:, :wide_qkv]
    d_small = d_all[:, wide_qkv + width :]
    d_gain_first = jnp.sum(d_qkv * w_qkv.astype(F32), axis=1) / gain_attn.astype(F32)
    (d_expert_in,) = in_share(
        here, turned_rows, grad_pre, after(came_in, d_gain_first), cost(net.nd), last=True
    )
    return (
        activations,
        grad_tokens,
        d_qkv,
        d_all[:, wide_qkv : wide_qkv + width],
        d_small[:, :experts_all],
        d_gain_first,
        d_small[:, experts_all],
        d_expert_in,
        d_expert_out,
    )


def solution(mesh):
    rows = P(AXES, None)
    return jax.shard_map(
        on_device,
        mesh=mesh,
        in_specs=(rows,) * 7
        + (P(AXES), P(AXES), P("expert", None, None), P("expert", None, None)),
        out_specs=(rows,) * 5
        + (P(AXES), P(AXES), P("expert", "dp", None), P("expert", "dp", None)),
        check_vma=False,
    )
```

time: 539 us -> 525 us (0.974)
  Pallas kernels: 207 us -> 259 us
  local copies, waits for them, and re-layouts: 75.9 us -> 30 us
  matrix products: 14.2 us -> 0 us
  starting transfers between devices: 62.8 us -> 73.6 us
  waiting for transfers between devices: 126 us -> 117 us
    pallas_call x25 -> x26, Pallas kernels: 165 us -> 212 us  [the longest x8 64.8 us: in_share(): pl.pallas_call(functools.partial(in_kernel, int(last)), out_shape=out_sha...]
    all_to_all x2 -> x5, waiting for transfers between devices: 50.8 us -> 9.2 us  [the longest x3 9.19 us: exchange(): lax.all_to_all(value, AXES, 0, 0, axis_index_groups=pairs, tiled=True)]
    unnamed x144 -> x101, local copies, waits for them, and re-layouts: 46.9 us -> 18.9 us
    ppermute x44, waiting for transfers between devices: 63.5 us -> 80.7 us  [step(): return lax.ppermute(value, AXES, self.ring[way])]
    dot_general x1 -> x0, matrix products: 14.2 us -> none  [on_device(): jnp.einsum('td,efd->etf', upstream_all, expert_out, preferred_element_typ...]
    reduce_scatter x2 -> x1, waiting for transfers between devices: 0.01 us -> 11.6 us  [on_device(): lax.psum_scatter(after(products, sent_out), 'dp', scatter_dimension=0, ti...]
    all_to_all x2 -> x5, starting transfers between devices: 8.6 us -> 19.7 us  [the longest x3 12.4 us: exchange(): lax.all_to_all(value, AXES, 0, 0, axis_index_groups=pairs, tiled=True)]
    dynamic_update_slice x16 -> x0, local copies, waits for them, and re-layouts: 8.94 us -> none  [assemble(): full = lax.dynamic_update_slice(full, both[i:i + 1], at)]
  transfers between devices with their start and end apart: 64 -> 65, of which waited for: 24 -> 27; matrix products, arithmetic and copies ran while one was open for 13% -> 8% of each run, Pallas kernels for 34% -> 47%
where the time goes in v3:
time: 525 us; the launch traced here: 521 us
  Pallas kernels  259 us (49%)
  waiting for transfers between devices  117 us (22%)
  starting transfers between devices  73.6 us (14%)
  local copies, waits for them, and re-layouts  30 us (6%)
  other arithmetic  25.6 us (5%)
  between operations  15.1 us (3%)
    ppermute x44, waiting for transfers between devices, step(): return lax.ppermute(value, AXES, self.ring[way])  80.7 us
    pallas_call x8, Pallas kernels, in_share(): pl.pallas_call(functools.partial(in_kernel, int(last)), out_shape=out_sha...  64.8 us
    pallas_call x3, Pallas kernels, owner_rows(): pl.pallas_call(functools.partial(owner_rows_kernel, extra is not None, bl...  47.1 us
    ppermute x44, starting transfers between devices, step(): return lax.ppermute(value, AXES, self.ring[way])  46.1 us
    pallas_call x8, Pallas kernels, out_share(): pl.pallas_call(functools.partial(out_kernel, int(last)), out_shape=[jax.S...  39.7 us
    pallas_call x2, Pallas kernels, expert_half(): pl.pallas_call(functools.partial(expert_kernel, bool(earlier)), out_shape...  34 us
    unnamed x101, local copies, waits for them, and re-layouts  18.9 us
    ppermute x14, waiting for transfers between devices, swap(): lax.ppermute(value, AXES, [(d, d ^ bit) for d in range(self.devices)])  14.6 us
  transfers between devices with their start and end apart: 65, of which 27 were waited for; matrix products, arithmetic and copies ran while one was open for 8% of the time, Pallas kernels for 47%

profile of v3, /device:TPU:0, one launch (start us, length us, event | category | flops | bytes accessed | tf_op | source)
XLA Modules:
  0.0 520.5 jit_solution(7209712592681771477)
XLA Ops:
  11.3 3.0 collective-permute-start
  14.3 6.2 %collective-permute-done = bf16[48,2688]{1,0:T(8,128)(2,1)S(1)} collective-permute-done((bf16[48,2688]{1,0:T(8,128)(2,1)S(1)}, bf16[48,2688]{1,0:T(8,128)(2,1)S(1)}, u32[]{:S(2)}, u32[]{:S(2)}) %collective-permute-start) | collective-permute-done | bytes 258080 | tf_op jit(solution)/shard_map/ppermute | solution.py:470
  25.2 4.7 collective-permute-done.4
  32.1 5.8 %collective-permute-done.3 = bf16[2,48,2688]{2,1,0:T(8,128)(2,1)S(1)} collective-permute-done((bf16[2,48,2688]{2,1,0:T(8,128)(2,1)S(1)}, bf16[2,48,2688]{2,1,0:T(8,128)(2,1)S(1)}, u32[]{:S(2)}, u32[]{:S(2)}) %collective-permute-start.3) | collective-permute-done | bytes 516128 | tf_op jit(solution)/shard_map/ppermute | solution.py:463
  49.8 12.5 %owner_grads.1.grad_plain = bf16[5,1024,512]{2,1,0:T(8,128)(2,1)} custom-call(bf16[1024,1536]{1,0:T(8,128)(2,1)} %all-gather.2.cloned.1.call-done.upstream, bf16[5,512,1536]{2,1,0:T(8,128)(2,1)} %refs_5_.1), custom_call_target="tpu_custom_call" | custom-call | flops 8053063680 | bytes 16777216 | tf_op jit(solution)/shard_map/owner_grads/pallas_call | solution.py:775
  68.5 6.1 %collective-permute-done.9 = bf16[2,48,2688]{2,1,0:T(8,128)(2,1)S(1)} collective-permute-done((bf16[2,48,2688]{2,1,0:T(8,128)(2,1)}, bf16[2,48,2688]{2,1,0:T(8,128)(2,1)S(1)}, u32[]{:S(2)}, u32[]{:S(2)}) %collective-permute-start.9) | collective-permute-done | bytes 516128 | tf_op jit(solution)/shard_map/ppermute | solution.py:463
  75.1 4.3 collective-permute-done.18
  85.6 4.1 collective-permute-done.17
  102.4 13.2 %attend.1 = (bf16[256,1536]{1,0:T(8,128)(2,1)}, bf16[3072,256]{1,0:T(8,128)(2,1)}, bf16[256,1536]{1,0:T(8,128)(2,1)}, bf16[256,512]{1,0:T(8,128)(2,1)}, bf16[256...) custom-call(s32[32]{0:T(128)} %stack.377.numbers, ...), custom_call_target="tpu_custom_call" | custom-call | flops 1024 | bytes 1024 | tf_op jit(solution)/shard_map/attend/pallas_call | solution.py:181
  115.7 7.2 %branch.1 = (f32[256,1536]{1,0:T(8,128)}, bf16[256,1664]{1,0:T(8,128)(2,1)}, f32[256,128]{1,0:T(8,128)}) custom-call(s32[32]{0:T(128)} %stack.376.numbers, bf16[256,1536]{1,0:T(8,128)(2,1)} %tokens.5, bf16[256,1536]{1,0:T(8,128)(2,1)} %get-tuple-element.143.mixed, bf16[1536,128]{1,0:T(8,128)(2,1)} %get-tuple-element.144.small, ...), custom_call_target="tpu_custom_call" | custom-call | flops 1024 | bytes 1024 | tf_op jit(solution)/shard_map/branch/pallas_call | solution.py:219
  126.4 17.0 %expert_half.2 = (bf16[5,1024,512]{2,1,0:T(8,128)(2,1)}, bf16[5,512,1024]{2,1,0:T(8,128)(2,1)}, bf16[5,1024,1024]{2,1,0:T(8,128)(2,1)}, f32[1024,128]{1,0:T(8,128)}, bf16[1536,1024]{1,0:T(8,128)(2,1)}) custom-call(s32[3]{0:T(128)} %add_add_fusion.1.scalars, bf16[256,1664]{1,0:T(8,128)(2,1)} %get-tuple-element.149.rows_a, bf16[256,1664]{1,0:T(8,128)(2,1)} %copy-done.37, ...), custom_call_target="tpu_custom_call" | custom-call | flops 8053063680 | bytes 31457280 | tf_op jit(solution)/shard_map/expert_half/pallas_call | solution.py:888
  150.0 3.6 all-to-all-start
  154.5 17.0 %expert_half.3 = (bf16[5,1024,512]{2,1,0:T(8,128)(2,1)}, bf16[5,512,1024]{2,1,0:T(8,128)(2,1)}, bf16[5,1024,1024]{2,1,0:T(8,128)(2,1)}, f32[1024,128]{1,0:T(8,128)}, bf16[1536,1024]{1,0:T(8,128)(2,1)}) custom-call(s32[3]{0:T(128)} %add_add_fusion.scalars, ...), custom_call_target="tpu_custom_call", output_to_operand_aliasing={{0}: (5, {}), {1}: (6, {}), {2}: (7, {}), {3}: (8, {}), {4}... | custom-call | flops 8053063680 | bytes 31457280 | tf_op jit(solution)/shard_map/expert_half/pallas_call | solution.py:888
  171.6 4.9 out_share.8
  178.5 7.9 %in_share.8 = (bf16[5,192,512]{2,1,0:T(8,128)(2,1)}, bf16[5,192,512]{2,1,0:T(8,128)(2,1)}) custom-call(s32[2]{0:T(128)} %pad_add_fusion.1.places, bf16[1536,1024]{1,0:T(8,128)(2,1)} %get-tuple-element.157.turned_rows, bf16[5,1024,1024]{2,1,0:T(8,128)(2,1)} %get-tuple-element.173.grad_pre.refs_1_.refs_2_), custom_call_target="tpu_custom_call" | custom-call | flops 30000001024 | bytes 1024 | tf_op jit(solution)/shard_map/in_share/pallas_call | solution.py:690
  188.5 15.2 %owner_rows.3 = bf16[512,1664]{1,0:T(8,128)(2,1)} custom-call(s32[2]{0:T(128)} %pad_add_fusion.3.refs_0_, bf16[5,1024,1024]{2,1,0:T(8,128)(2,1)} %get-tuple-element.173.grad_pre.refs_1_.refs_2_, bf16[5,1024,1024]{2,1,0:T(8,128)(2,1)} %get-tuple-element.173.grad_pre.refs_1_.refs_2_, bf16[5,1536,1024]{2,1,0:T(8,128)(2,1)} %refs_3_.3, ...), custom_call_target="tpu_custom_call" | custom-call | flops 1024 | bytes 1024 | tf_op jit(solution)/shard_map/owner_rows/pallas_call | solution.py:275
  203.8 4.9 out_share.9
  210.8 15.6 %owner_rows.4 = bf16[512,1664]{1,0:T(8,128)(2,1)} custom-call(s32[2]{0:T(128)} %pad_add_fusion.2.refs_0_, bf16[5,1024,1024]{2,1,0:T(8,128)(2,1)} %get-tuple-element.173.grad_pre.refs_1_.refs_2_, bf16[5,1024,1024]{2,1,0:T(8,128)(2,1)} %get-tuple-element.173.grad_pre.refs_1_.refs_2_, bf16[5,1536,1024]{2,1,0:T(8,128)(2,1)} %refs_3_.3, ...), custom_call_target="tpu_custom_call" | custom-call | flops 1024 | bytes 1024 | tf_op jit(solution)/shard_map/owner_rows/pallas_call | solution.py:275
  228.2 7.9 %in_share.9 = (bf16[5,192,512]{2,1,0:T(8,128)(2,1)}, bf16[5,192,512]{2,1,0:T(8,128)(2,1)}) custom-call(s32[2]{0:T(128)} %pad_add_fusion.places, bf16[1536,1024]{1,0:T(8,128)(2,1)} %get-tuple-element.157.turned_rows, bf16[5,1024,1024]{2,1,0:T(8,128)(2,1)} %get-tuple-element.173.grad_pre.refs_1_.refs_2_, bf16[5,192,512]{2,1,0:T(8,128)(2,1)} %collective-permute-done.27.refs_0_, ...), custom_call_target="tpu_custom_call" | custom-call | flops 30000001024 | bytes 1024 | tf_op jit(solution)/shard_map/in_share/pallas_call | solution.py:690
  239.7 3.7 all-to-all-start.1
  243.9 16.3 %owner_rows.5 = bf16[1024,1536]{1,0:T(8,128)(2,1)} custom-call(s32[4]{0:T(128)} %iota.34.refs_0_, bf16[5,1024,512]{2,1,0:T(8,128)(2,1)} %get-tuple-element.178.refs_1_.refs_2_.refs_3_.refs_4_, bf16[5,1024,512]{2,1,0:T(8,128)(2,1)} %get-tuple-element.178.refs_1_.refs_2_.refs_3_.refs_4_, ...), custom_call_target="tpu_custom_call" | custom-call | flops 1024 | bytes 1024 | tf_op jit(solution)/shard_map/owner_rows/pallas_call | solution.py:275
  260.2 4.9 out_share.10
  268.4 7.3 %middle.1 = (f32[256,1536]{1,0:T(8,128)}, bf16[2,272,1664]{2,1,0:T(8,128)(2,1)}, bf16[256,1536]{1,0:T(8,128)(2,1)}) custom-call(s32[32]{0:T(128)} %stack.376.numbers, bf16[2,256,1664]{2,1,0:T(8,128)(2,1)} %copy-done.5, bf16[256,1536]{1,0:T(8,128)(2,1)} %cotangent.1, f32[256,1536]{1,0:T(8,128)} %get-tuple-element.148.hidden, ...), custom_call_target="tpu_custom_call" | custom-call | flops 1024 | bytes 1024 | tf_op jit(solution)/shard_map/middle/pallas_call | solution.py:404
  275.7 3.7 all-to-all-start.3
  280.4 7.8 %in_share.10 = (bf16[5,192,512]{2,1,0:T(8,128)(2,1)}, bf16[5,192,512]{2,1,0:T(8,128)(2,1)}) custom-call(s32[2]{0:T(128)} %pad_add_fusion.7.places, bf16[1536,1024]{1,0:T(8,128)(2,1)} %get-tuple-element.157.turned_rows, bf16[5,1024,1024]{2,1,0:T(8,128)(2,1)} %get-tuple-element.173.grad_pre.refs_1_.refs_2_, bf16[5,192,512]{2,1,0:T(8,128)(2,1)} %copy-done.33, ...), custom_call_target="tpu_custom_call" | custom-call | flops 30000001024 | bytes 1024 | tf_op jit(solution)/shard_map/in_share/pallas_call | solution.py:690
  290.5 10.8 %attend_back.1.grad_project = bf16[2,256,2560]{2,1,0:T(8,128)(2,1)} custom-call(bf16[256,1536]{1,0:T(8,128)(2,1)} %get-tuple-element.190.queries, bf16[256,512]{1,0:T(8,128)(2,1)} %get-tuple-element.191.key_rows, bf16[256,512]{1,0:T(8,128)(2,1)} %get-tuple-element.192.values, bf16[256,1536]{1,0:T(8,128)(2,1)} %get-tuple-element.193.grad_mixed, ...), custom_call_target="tpu_custom_call" | custom-call | flops 1024 | bytes 1024 | tf_op jit(solution)/shard_map/attend_back/pallas_call | solution.py:374
  302.0 4.9 out_share.11
  309.0 4.1 collective-permute-done.36.refs_0_
  315.2 5.0 all-to-all-start.2
  320.3 8.5 %in_share.11 = (bf16[5,192,512]{2,1,0:T(8,128)(2,1)}, bf16[5,192,512]{2,1,0:T(8,128)(2,1)}) custom-call(s32[2]{0:T(128)} %pad_add_fusion.6.places, bf16[1536,1024]{1,0:T(8,128)(2,1)} %get-tuple-element.157.turned_rows, bf16[5,1024,1024]{2,1,0:T(8,128)(2,1)} %get-tuple-element.173.grad_pre.refs_1_.refs_2_, bf16[5,192,512]{2,1,0:T(8,128)(2,1)} %copy-done.35, ...), custom_call_target="tpu_custom_call" | custom-call | flops 30000001024 | bytes 1024 | tf_op jit(solution)/shard_map/in_share/pallas_call | solution.py:690
  332.4 5.0 out_share.12
  337.4 9.2 %all-to-all-done.2.refs_0_ = bf16[2,256,2560]{2,1,0:T(8,128)(2,1)} async-done(((bf16[2,256,2560]{2,1,0:T(8,128)(2,1)}), bf16[2,256,2560]{2,1,0:T(8,128)(2,1)}, u32[]{:S(2)}, u32[]{:S(2)}) %all-to-all-start.2) | async-done | bytes 2621472 | tf_op jit(solution)/shard_map/all_to_all | solution.py:467
  356.5 7.8 %in_share.12 = (bf16[5,192,512]{2,1,0:T(8,128)(2,1)}, bf16[5,192,512]{2,1,0:T(8,128)(2,1)}) custom-call(s32[2]{0:T(128)} %pad_add_fusion.5.places, bf16[1536,1024]{1,0:T(8,128)(2,1)} %get-tuple-element.157.turned_rows, bf16[5,1024,1024]{2,1,0:T(8,128)(2,1)} %get-tuple-element.173.grad_pre.refs_1_.refs_2_, bf16[5,192,512]{2,1,0:T(8,128)(2,1)} %copy-done.32, ...), custom_call_target="tpu_custom_call" | custom-call | flops 10000000000 | bytes 1024 | tf_op jit(solution)/shard_map/in_share/pallas_call | solution.py:690
  364.4 3.3 gain_column.1
  371.3 9.6 %weight_products.1 = bf16[384,4224]{1,0:T(8,128)(2,1)} custom-call(s32[1]{0:T(128)} %bitcast.71.place, bf16[4,768,256]{2,1,0:T(8,128)(2,1)} %copy-done.7, bf16[4,384,256]{2,1,0:T(8,128)(2,1)} %bitcast.126, f32[384,128]{1,0:T(8,128)} %bitcast.132, bf16[2,256,2560]{2,1,0:T(8,128)(2,1)} %all-to-all-done.2.refs_0_, ...), custom_call_target="tpu_custom_call" | custom-call | flops 1024 | bytes 1024 | tf_op jit(solution)/shard_map/weight_products/pallas_call | solution.py:554
  381.7 5.0 out_share.13
  388.8 5.4 %collective-permute-done.46.refs_0_ = bf16[5,192,512]{2,1,0:T(8,128)(2,1)S(1)} collective-permute-done((bf16[5,192,512]{2,1,0:T(8,128)(2,1)}, bf16[5,192,512]{2,1,0:T(8,128)(2,1)S(1)}, u32[]{:S(2)}, u32[]{:S(2)}) %collective-permute-start.46) | collective-permute-done | bytes 983072 | tf_op jit(solution)/shard_map/ppermute | solution.py:463
  395.6 7.9 %in_share.13 = (bf16[5,192,512]{2,1,0:T(8,128)(2,1)}, bf16[5,192,512]{2,1,0:T(8,128)(2,1)}) custom-call(s32[2]{0:T(128)} %pad_add_fusion.4.places, bf16[1536,1024]{1,0:T(8,128)(2,1)} %get-tuple-element.157.turned_rows, bf16[5,1024,1024]{2,1,0:T(8,128)(2,1)} %get-tuple-element.173.grad_pre.refs_1_.refs_2_, bf16[5,192,512]{2,1,0:T(8,128)(2,1)} %copy-done.36, ...), custom_call_target="tpu_custom_call" | custom-call | flops 30000001024 | bytes 1024 | tf_op jit(solution)/shard_map/in_share/pallas_call | solution.py:690
  405.6 5.7 %collective-permute-done.52.refs_0_ = bf16[320,768]{1,0:T(8,128)(2,1)S(1)} collective-permute-done((bf16[320,768]{1,0:T(8,128)(2,1)}, bf16[320,768]{1,0:T(8,128)(2,1)S(1)}, u32[]{:S(2)}, u32[]{:S(2)}) %collective-permute-start.52) | collective-permute-done | bytes 491552 | tf_op jit(solution)/shard_map/ppermute | solution.py:463
  411.3 5.5 %collective-permute-done.53.refs_1_ = bf16[320,768]{1,0:T(8,128)(2,1)S(1)} collective-permute-done((bf16[320,768]{1,0:T(8,128)(2,1)}, bf16[320,768]{1,0:T(8,128)(2,1)S(1)}, u32[]{:S(2)}, u32[]{:S(2)}) %collective-permute-start.53) | collective-permute-done | bytes 491552 | tf_op jit(solution)/shard_map/ppermute | solution.py:463
  417.6 3.7 all-to-all-start.4
  421.3 5.0 out_share.14
  428.4 22.6 %collective-permute-done.50.refs_0_ = bf16[5,192,512]{2,1,0:T(8,128)(2,1)} collective-permute-done((bf16[5,192,512]{2,1,0:T(8,128)(2,1)}, bf16[5,192,512]{2,1,0:T(8,128)(2,1)}, u32[]{:S(2)}, u32[]{:S(2)}) %collective-permute-start.50) | collective-permute-done | bytes 983072 | tf_op jit(solution)/shard_map/ppermute | solution.py:463
  453.3 8.0 %in_share.14 = (bf16[5,192,512]{2,1,0:T(8,128)(2,1)}, bf16[5,192,512]{2,1,0:T(8,128)(2,1)}) custom-call(s32[2]{0:T(128)} %pad_add_fusion.8.places, bf16[1536,1024]{1,0:T(8,128)(2,1)} %get-tuple-element.157.turned_rows, bf16[5,1024,1024]{2,1,0:T(8,128)(2,1)} %get-tuple-element.173.grad_pre.refs_1_.refs_2_, ...), custom_call_target="tpu_custom_call" | custom-call | flops 30000001024 | bytes 1024 | tf_op jit(solution)/shard_map/in_share/pallas_call | solution.py:690
  463.6 9.9 %input_back.1 = f32[256,1536]{1,0:T(8,128)} custom-call(s32[32]{0:T(128)} %stack.377.numbers, bf16[256,1536]{1,0:T(8,128)(2,1)} %tokens.5, bf16[2,256,2560]{2,1,0:T(8,128)(2,1)} %attend_back.1.grad_project, f32[16,1536]{1,0:T(8,128)} %get-tuple-element.145.gains, f32[256,1536]{1,0:T(8,128)} %get-tuple-element.234.grad_hidden, ...), custom_call_target="tpu_custom_call" | custom-call | flops 1024 | bytes 1024 | tf_op jit(solution)/shard_map/input_back/pallas_call | solution.py:422
  475.1 5.1 out_share.15
  485.7 11.6 %reduce-scatter.2.cloned.1.call-done = bf16[48,4224]{1,0:T(8,128)(2,1)} async-done(((bf16[384,4224]{1,0:T(8,128)(2,1)}), bf16[48,4224]{1,0:T(8,128)(2,1)}) %reduce-scatter.2.cloned.1.call-update) | async-done | bytes 405520 | tf_op jit(solution)/shard_map/reduce_scatter | solution.py:1052
  504.4 8.9 %in_share.15 = f32[5,192,1024]{2,1,0:T(8,128)} custom-call(s32[2]{0:T(128)} %pad_add_fusion.9.places, bf16[1536,1024]{1,0:T(8,128)(2,1)} %get-tuple-element.157.turned_rows, bf16[5,1024,1024]{2,1,0:T(8,128)(2,1)} %get-tuple-element.173.grad_pre.refs_1_.refs_2_, bf16[5,192,512]{2,1,0:T(8,128)(2,1)} %collective-permute-done.56.refs_0_, ...), custom_call_target="tpu_custom_call" | custom-call | flops 30000001024 | bytes 1024 | tf_op jit(solution)/shard_map/in_share/pallas_call | solution.py:690
  (263 shorter events, 127.9 us)
Async XLA Ops:
  7.2 42.6 %all-gather.2.cloned.1.call-start = ((), (), s32[]{:S(2)}) async-start(), calls=%async_computation.6 | async-start | bytes 3932160 | tf_op jit(solution)/shard_map/all_gather | solution.py:936
  23.2 14.7 %collective-permute-start.3 = (bf16[2,48,2688]{2,1,0:T(8,128)(2,1)S(1)}, bf16[2,48,2688]{2,1,0:T(8,128)(2,1)S(1)}, u32[]{:S(2)}, u32[]{:S(2)}) collective-permute-start(bf16[2,48,2688]{2,1,0:T(8,128)(2,1)S(1)} %get-tuple-element.263), channel_id=1, source_target_pairs={{0,4},{1,5},{2,6},{3,7},{8,0},{9,1},{10,2},{11,3},{16,8},{17,9},{1... | collective-permute-start | bytes 1548296 | tf_op jit(solution)/shard_map/ppermute | solution.py:463
  24.7 14.7 %collective-permute-start.2 = (bf16[2,48,2688]{2,1,0:T(8,128)(2,1)S(1)}, bf16[2,48,2688]{2,1,0:T(8,128)(2,1)S(1)}, u32[]{:S(2)}, u32[]{:S(2)}) collective-permute-start(bf16[2,48,2688]{2,1,0:T(8,128)(2,1)S(1)} %get-tuple-element.263), channel_id=1, source_target_pairs={{0,8},{1,9},{2,10},{3,11},{8,16},{9,17},{10,18},{11,19},{16,24},{1... | collective-permute-start | bytes 1548296 | tf_op jit(solution)/shard_map/ppermute | solution.py:463
  30.0 14.3 %collective-permute-start.12 = (bf16[2,48,1536]{2,1,0:T(8,128)(2,1)S(1)}, bf16[2,48,1536]{2,1,0:T(8,128)(2,1)}, u32[]{:S(2)}, u32[]{:S(2)}) collective-permute-start(bf16[2,48,1536]{2,1,0:T(8,128)(2,1)S(1)} %pad_maximum_fusion.5), channel_id=1, source_target_pairs={{0,4},{1,5},{2,6},{3,7},{8,0},{9,1},{10,2},{11,3},{16,8},{17,9},{1... | collective-permute-start | bytes 884744 | tf_op jit(solution)/shard_map/ppermute | solution.py:463
  39.3 23.0 %collective-permute-start.6 = (bf16[2,48,2688]{2,1,0:T(8,128)(2,1)S(1)}, bf16[2,48,2688]{2,1,0:T(8,128)(2,1)}, u32[]{:S(2)}, u32[]{:S(2)}) collective-permute-start(bf16[2,48,2688]{2,1,0:T(8,128)(2,1)S(1)} %collective-permute-done.2), channel_id=1, source_target_pairs={{0,8},{1,9},{2,10},{3,11},{8,16},{9,17},{10,18},{11,19},{16,24},{1... | collective-permute-start | bytes 1548296 | tf_op jit(solution)/shard_map/ppermute | solution.py:463
  39.9 22.4 %collective-permute-start.7 = (bf16[2,48,2688]{2,1,0:T(8,128)(2,1)S(1)}, bf16[2,48,2688]{2,1,0:T(8,128)(2,1)}, u32[]{:S(2)}, u32[]{:S(2)}) collective-permute-start(bf16[2,48,2688]{2,1,0:T(8,128)(2,1)S(1)} %collective-permute-done.3), channel_id=1, source_target_pairs={{0,4},{1,5},{2,6},{3,7},{8,0},{9,1},{10,2},{11,3},{16,8},{17,9},{1... | collective-permute-start | bytes 1548296 | tf_op jit(solution)/shard_map/ppermute | solution.py:463
  45.8 18.6 %collective-permute-start.13 = (bf16[2,48,1536]{2,1,0:T(8,128)(2,1)}, bf16[2,48,1536]{2,1,0:T(8,128)(2,1)}, u32[]{:S(2)}, u32[]{:S(2)}) collective-permute-start(bf16[2,48,1536]{2,1,0:T(8,128)(2,1)} %collective-permute-done.11), channel_id=1, source_target_pairs={{0,8},{1,9},{2,10},{3,11},{8,16},{9,17},{10,18},{11,19},{16,24},{1... | collective-permute-start | bytes 884744 | tf_op jit(solution)/shard_map/ppermute | solution.py:463
  46.3 18.1 %collective-permute-start.14 = (bf16[2,48,1536]{2,1,0:T(8,128)(2,1)}, bf16[2,48,1536]{2,1,0:T(8,128)(2,1)}, u32[]{:S(2)}, u32[]{:S(2)}) collective-permute-start(bf16[2,48,1536]{2,1,0:T(8,128)(2,1)} %collective-permute-done.12), channel_id=1, source_target_pairs={{0,4},{1,5},{2,6},{3,7},{8,0},{9,1},{10,2},{11,3},{16,8},{17,9},{1... | collective-permute-start | bytes 884744 | tf_op jit(solution)/shard_map/ppermute | solution.py:463
  64.4 15.0 %collective-permute-start.18 = (bf16[2,48,1536]{2,1,0:T(8,128)(2,1)}, bf16[2,48,1536]{2,1,0:T(8,128)(2,1)S(1)}, u32[]{:S(2)}, u32[]{:S(2)}) collective-permute-start(bf16[2,48,1536]{2,1,0:T(8,128)(2,1)} %collective-permute-done.13), channel_id=1, source_target_pairs={{0,8},{1,9},{2,10},{3,11},{8,16},{9,17},{10,18},{11,19},{16,24},{1... | collective-permute-start | bytes 884744 | tf_op jit(solution)/shard_map/ppermute | solution.py:463
  66.0 15.3 %collective-permute-start.19 = (bf16[2,48,1536]{2,1,0:T(8,128)(2,1)}, bf16[2,48,1536]{2,1,0:T(8,128)(2,1)S(1)}, u32[]{:S(2)}, u32[]{:S(2)}) collective-permute-start(bf16[2,48,1536]{2,1,0:T(8,128)(2,1)} %collective-permute-done.14), channel_id=1, source_target_pairs={{0,4},{1,5},{2,6},{3,7},{8,0},{9,1},{10,2},{11,3},{16,8},{17,9},{1... | collective-permute-start | bytes 884744 | tf_op jit(solution)/shard_map/ppermute | solution.py:463
  90.4 25.2 %collective-permute-start.23 = (bf16[8,2,48,1536]{3,2,1,0:T(8,128)(2,1)S(1)}, bf16[8,2,48,1536]{3,2,1,0:T(8,128)(2,1)}, u32[]{:S(2)}, u32[]{:S(2)}) collective-permute-start(bf16[8,2,48,1536]{3,2,1,0:T(8,128)(2,1)S(1)} %fusion.refs_0_), channel_id=1, source_target_pairs={{0,1},{1,0},{2,3},{3,2},{4,5},{5,4},{6,7},{7,6},{8,9},{9,8},{10,11... | collective-permute-start | bytes 7077896 | tf_op jit(solution)/shard_map/ppermute | solution.py:470
  123.3 21.2 %collective-permute-start.24 = (bf16[256,1664]{1,0:T(8,128)(2,1)}, bf16[256,1664]{1,0:T(8,128)(2,1)S(1)}, u32[]{:S(2)}, u32[]{:S(2)}) collective-permute-start(bf16[256,1664]{1,0:T(8,128)(2,1)} %get-tuple-element.149.rows_a), channel_id=1, source_target_pairs={{0,2},{1,3},{2,0},{3,1},{4,6},{5,7},{6,4},{7,5},{8,10},{9,11},{10,... | collective-permute-start | bytes 2555912 | tf_op jit(solution)/shard_map/ppermute | solution.py:470
  150.0 38.5 %all-to-all-start = ((bf16[4,768,256]{2,1,0:T(8,128)(2,1)}), bf16[4,768,256]{2,1,0:T(8,128)(2,1)S(1)}, u32[]{:S(2)}, u32[]{:S(2)}) async-start(bf16[4,768,256]{2,1,0:T(8,128)(2,1)} %bitcast.77), calls=%async_computation | async-start | bytes 3145728 | tf_op jit(solution)/shard_map/all_to_all | solution.py:1002
  176.4 27.3 %collective-permute-start.29 = (bf16[320,768]{1,0:T(8,128)(2,1)}, bf16[320,768]{1,0:T(8,128)(2,1)}, u32[]{:S(2)}, u32[]{:S(2)}) collective-permute-start(bf16[320,768]{1,0:T(8,128)(2,1)} %get-tuple-element.162), channel_id=1, source_target_pairs={{0,8},{1,9},{2,10},{3,11},{8,16},{9,17},{10,18},{11,19},{16,24},{1... | collective-permute-start | bytes 1474568 | tf_op jit(solution)/shard_map/ppermute | solution.py:463
  178.2 25.5 %collective-permute-start.30 = (bf16[320,768]{1,0:T(8,128)(2,1)}, bf16[320,768]{1,0:T(8,128)(2,1)}, u32[]{:S(2)}, u32[]{:S(2)}) collective-permute-start(bf16[320,768]{1,0:T(8,128)(2,1)} %get-tuple-element.163), channel_id=1, source_target_pairs={{0,4},{1,5},{2,6},{3,7},{8,0},{9,1},{10,2},{11,3},{16,8},{17,9},{1... | collective-permute-start | bytes 1474568 | tf_op jit(solution)/shard_map/ppermute | solution.py:463
  186.4 41.8 %collective-permute-start.27 = (bf16[5,192,512]{2,1,0:T(8,128)(2,1)}, bf16[5,192,512]{2,1,0:T(8,128)(2,1)}, u32[]{:S(2)}, u32[]{:S(2)}) collective-permute-start(bf16[5,192,512]{2,1,0:T(8,128)(2,1)} %get-tuple-element.159), channel_id=1, source_target_pairs={{0,8},{1,9},{2,10},{3,11},{8,16},{9,17},{10,18},{11,19},{16,24},{1... | collective-permute-start | bytes 2949128 | tf_op jit(solution)/shard_map/ppermute | solution.py:463
  188.2 40.0 %collective-permute-start.28 = (bf16[5,192,512]{2,1,0:T(8,128)(2,1)}, bf16[5,192,512]{2,1,0:T(8,128)(2,1)}, u32[]{:S(2)}, u32[]{:S(2)}) collective-permute-start(bf16[5,192,512]{2,1,0:T(8,128)(2,1)} %get-tuple-element.160), channel_id=1, source_target_pairs={{0,4},{1,5},{2,6},{3,7},{8,0},{9,1},{10,2},{11,3},{16,8},{17,9},{1... | collective-permute-start | bytes 2949128 | tf_op jit(solution)/shard_map/ppermute | solution.py:463
  208.7 51.5 %collective-permute-start.34 = (bf16[320,768]{1,0:T(8,128)(2,1)}, bf16[320,768]{1,0:T(8,128)(2,1)}, u32[]{:S(2)}, u32[]{:S(2)}) collective-permute-start(bf16[320,768]{1,0:T(8,128)(2,1)} %get-tuple-element.171), channel_id=1, source_target_pairs={{0,8},{1,9},{2,10},{3,11},{8,16},{9,17},{10,18},{11,19},{16,24},{1... | collective-permute-start | bytes 1474568 | tf_op jit(solution)/shard_map/ppermute | solution.py:463
  210.5 49.7 %collective-permute-start.35 = (bf16[320,768]{1,0:T(8,128)(2,1)}, bf16[320,768]{1,0:T(8,128)(2,1)}, u32[]{:S(2)}, u32[]{:S(2)}) collective-permute-start(bf16[320,768]{1,0:T(8,128)(2,1)} %get-tuple-element.172), channel_id=1, source_target_pairs={{0,4},{1,5},{2,6},{3,7},{8,0},{9,1},{10,2},{11,3},{16,8},{17,9},{1... | collective-permute-start | bytes 1474568 | tf_op jit(solution)/shard_map/ppermute | solution.py:463
  236.1 43.3 %collective-permute-start.32 = (bf16[5,192,512]{2,1,0:T(8,128)(2,1)}, bf16[5,192,512]{2,1,0:T(8,128)(2,1)S(1)}, u32[]{:S(2)}, u32[]{:S(2)}) collective-permute-start(bf16[5,192,512]{2,1,0:T(8,128)(2,1)} %get-tuple-element.176), channel_id=1, source_target_pairs={{0,8},{1,9},{2,10},{3,11},{8,16},{9,17},{10,18},{11,19},{16,24},{1... | collective-permute-start | bytes 2949128 | tf_op jit(solution)/shard_map/ppermute | solution.py:463
  237.9 41.5 %collective-permute-start.33 = (bf16[5,192,512]{2,1,0:T(8,128)(2,1)}, bf16[5,192,512]{2,1,0:T(8,128)(2,1)}, u32[]{:S(2)}, u32[]{:S(2)}) collective-permute-start(bf16[5,192,512]{2,1,0:T(8,128)(2,1)} %get-tuple-element.177), channel_id=1, source_target_pairs={{0,4},{1,5},{2,6},{3,7},{8,0},{9,1},{10,2},{11,3},{16,8},{17,9},{1... | collective-permute-start | bytes 2949128 | tf_op jit(solution)/shard_map/ppermute | solution.py:463
  239.7 27.5 %all-to-all-start.1 = ((bf16[2,256,1664]{2,1,0:T(8,128)(2,1)}), bf16[2,256,1664]{2,1,0:T(8,128)(2,1)S(1)}, u32[]{:S(2)}, u32[]{:S(2)}) async-start(bf16[2,256,1664]{2,1,0:T(8,128)(2,1)} %reverse_select_fusion), calls=%async_computation.1 | async-start | bytes 3407872 | tf_op jit(solution)/shard_map/all_to_all | solution.py:467
  265.1 36.1 %collective-permute-start.38 = (bf16[320,768]{1,0:T(8,128)(2,1)}, bf16[320,768]{1,0:T(8,128)(2,1)S(1)}, u32[]{:S(2)}, u32[]{:S(2)}) collective-permute-start(bf16[320,768]{1,0:T(8,128)(2,1)} %get-tuple-element.181), channel_id=1, source_target_pairs={{0,8},{1,9},{2,10},{3,11},{8,16},{9,17},{10,18},{11,19},{16,24},{1... | collective-permute-start | bytes 1474568 | tf_op jit(solution)/shard_map/ppermute | solution.py:463
  266.9 34.3 %collective-permute-start.39 = (bf16[320,768]{1,0:T(8,128)(2,1)}, bf16[320,768]{1,0:T(8,128)(2,1)}, u32[]{:S(2)}, u32[]{:S(2)}) collective-permute-start(bf16[320,768]{1,0:T(8,128)(2,1)} %get-tuple-element.182), channel_id=1, source_target_pairs={{0,4},{1,5},{2,6},{3,7},{8,0},{9,1},{10,2},{11,3},{16,8},{17,9},{1... | collective-permute-start | bytes 1474568 | tf_op jit(solution)/shard_map/ppermute | solution.py:463
  275.7 39.5 %all-to-all-start.3 = ((bf16[2,272,1664]{2,1,0:T(8,128)(2,1)}), bf16[2,272,1664]{2,1,0:T(8,128)(2,1)S(1)}, u32[]{:S(2)}, u32[]{:S(2)}) async-start(bf16[2,272,1664]{2,1,0:T(8,128)(2,1)} %get-tuple-element.202), calls=%async_computation.3 | async-start | bytes 3620864 | tf_op jit(solution)/shard_map/all_to_all | solution.py:467
  288.2 25.0 %collective-permute-start.36 = (bf16[5,192,512]{2,1,0:T(8,128)(2,1)}, bf16[5,192,512]{2,1,0:T(8,128)(2,1)S(1)}, u32[]{:S(2)}, u32[]{:S(2)}) collective-permute-start(bf16[5,192,512]{2,1,0:T(8,128)(2,1)} %get-tuple-element.188), channel_id=1, source_target_pairs={{0,8},{1,9},{2,10},{3,11},{8,16},{9,17},{10,18},{11,19},{16,24},{1... | collective-permute-start | bytes 2949128 | tf_op jit(solution)/shard_map/ppermute | solution.py:463
  290.0 25.2 %collective-permute-start.37 = (bf16[5,192,512]{2,1,0:T(8,128)(2,1)}, bf16[5,192,512]{2,1,0:T(8,128)(2,1)}, u32[]{:S(2)}, u32[]{:S(2)}) collective-permute-start(bf16[5,192,512]{2,1,0:T(8,128)(2,1)} %get-tuple-element.189), channel_id=1, source_target_pairs={{0,4},{1,5},{2,6},{3,7},{8,0},{9,1},{10,2},{11,3},{16,8},{17,9},{1... | collective-permute-start | bytes 2949128 | tf_op jit(solution)/shard_map/ppermute | solution.py:463
  307.0 24.7 %collective-permute-start.42 = (bf16[320,768]{1,0:T(8,128)(2,1)}, bf16[320,768]{1,0:T(8,128)(2,1)S(1)}, u32[]{:S(2)}, u32[]{:S(2)}) collective-permute-start(bf16[320,768]{1,0:T(8,128)(2,1)} %get-tuple-element.196), channel_id=1, source_target_pairs={{0,8},{1,9},{2,10},{3,11},{8,16},{9,17},{10,18},{11,19},{16,24},{1... | collective-permute-start | bytes 1474568 | tf_op jit(solution)/shard_map/ppermute | solution.py:463
  308.8 22.9 %collective-permute-start.43 = (bf16[320,768]{1,0:T(8,128)(2,1)}, bf16[320,768]{1,0:T(8,128)(2,1)}, u32[]{:S(2)}, u32[]{:S(2)}) collective-permute-start(bf16[320,768]{1,0:T(8,128)(2,1)} %get-tuple-element.197), channel_id=1, source_target_pairs={{0,4},{1,5},{2,6},{3,7},{8,0},{9,1},{10,2},{11,3},{16,8},{17,9},{1... | collective-permute-start | bytes 1474568 | tf_op jit(solution)/shard_map/ppermute | solution.py:463
  315.2 31.4 %all-to-all-start.2 = ((bf16[2,256,2560]{2,1,0:T(8,128)(2,1)}), bf16[2,256,2560]{2,1,0:T(8,128)(2,1)}, u32[]{:S(2)}, u32[]{:S(2)}) async-start(bf16[2,256,2560]{2,1,0:T(8,128)(2,1)} %attend_back.1.grad_project), calls=%async_computation.2 | async-start | bytes 5242880 | tf_op jit(solution)/shard_map/all_to_all | solution.py:467
  320.2 177.0 %reduce-scatter.2.cloned.1.call-start = ((), (), s32[]{:S(2)}) async-start(), calls=%async_computation.7 | async-start | bytes 3649536 | tf_op jit(solution)/shard_map/reduce_scatter | solution.py:1052
  328.8 19.3 %collective-permute-start.40 = (bf16[5,192,512]{2,1,0:T(8,128)(2,1)}, bf16[5,192,512]{2,1,0:T(8,128)(2,1)S(1)}, u32[]{:S(2)}, u32[]{:S(2)}) collective-permute-start(bf16[5,192,512]{2,1,0:T(8,128)(2,1)} %get-tuple-element.200), channel_id=1, source_target_pairs={{0,8},{1,9},{2,10},{3,11},{8,16},{9,17},{10,18},{11,19},{16,24},{1... | collective-permute-start | bytes 2949128 | tf_op jit(solution)/shard_map/ppermute | solution.py:463
  330.3 19.1 %collective-permute-start.41 = (bf16[5,192,512]{2,1,0:T(8,128)(2,1)}, bf16[5,192,512]{2,1,0:T(8,128)(2,1)}, u32[]{:S(2)}, u32[]{:S(2)}) collective-permute-start(bf16[5,192,512]{2,1,0:T(8,128)(2,1)} %get-tuple-element.201), channel_id=1, source_target_pairs={{0,4},{1,5},{2,6},{3,7},{8,0},{9,1},{10,2},{11,3},{16,8},{17,9},{1... | collective-permute-start | bytes 2949128 | tf_op jit(solution)/shard_map/ppermute | solution.py:463
  349.4 19.8 %collective-permute-start.44 = (bf16[2,256,2560]{2,1,0:T(8,128)(2,1)}, bf16[2,256,2560]{2,1,0:T(8,128)(2,1)}, u32[]{:S(2)}, u32[]{:S(2)}) collective-permute-start(bf16[2,256,2560]{2,1,0:T(8,128)(2,1)} %all-to-all-done.2.refs_0_), channel_id=1, source_target_pairs={{0,1},{1,0},{2,3},{3,2},{4,5},{5,4},{6,7},{7,6},{8,9},{9,8},{10,11... | collective-permute-start | bytes 7864328 | tf_op jit(solution)/shard_map/ppermute | solution.py:470
  349.4 14.9 %collective-permute-start.45 = (bf16[2,272,1664]{2,1,0:T(8,128)(2,1)S(1)}, bf16[2,272,1664]{2,1,0:T(8,128)(2,1)}, u32[]{:S(2)}, u32[]{:S(2)}) collective-permute-start(bf16[2,272,1664]{2,1,0:T(8,128)(2,1)S(1)} %all-to-all-done.3.refs_0_.refs_2_), channel_id=1, source_target_pairs={{0,1},{1,0},{2,3},{3,2},{4,5},{5,4},{6,7},{7,6},{8,9},{9,8},{10,11... | collective-permute-start | bytes 5431304 | tf_op jit(solution)/shard_map/ppermute | solution.py:470
  354.5 26.5 %collective-permute-start.48 = (bf16[320,768]{1,0:T(8,128)(2,1)}, bf16[320,768]{1,0:T(8,128)(2,1)S(1)}, u32[]{:S(2)}, u32[]{:S(2)}) collective-permute-start(bf16[320,768]{1,0:T(8,128)(2,1)} %get-tuple-element.205), channel_id=1, source_target_pairs={{0,8},{1,9},{2,10},{3,11},{8,16},{9,17},{10,18},{11,19},{16,24},{1... | collective-permute-start | bytes 1474568 | tf_op jit(solution)/shard_map/ppermute | solution.py:463
  356.0 24.9 %collective-permute-start.49 = (bf16[320,768]{1,0:T(8,128)(2,1)}, bf16[320,768]{1,0:T(8,128)(2,1)}, u32[]{:S(2)}, u32[]{:S(2)}) collective-permute-start(bf16[320,768]{1,0:T(8,128)(2,1)} %get-tuple-element.206), channel_id=1, source_target_pairs={{0,4},{1,5},{2,6},{3,7},{8,0},{9,1},{10,2},{11,3},{16,8},{17,9},{1... | collective-permute-start | bytes 1474568 | tf_op jit(solution)/shard_map/ppermute | solution.py:463
  369.3 24.9 %collective-permute-start.46 = (bf16[5,192,512]{2,1,0:T(8,128)(2,1)}, bf16[5,192,512]{2,1,0:T(8,128)(2,1)S(1)}, u32[]{:S(2)}, u32[]{:S(2)}) collective-permute-start(bf16[5,192,512]{2,1,0:T(8,128)(2,1)} %get-tuple-element.213), channel_id=1, source_target_pairs={{0,8},{1,9},{2,10},{3,11},{8,16},{9,17},{10,18},{11,19},{16,24},{1... | collective-permute-start | bytes 2949128 | tf_op jit(solution)/shard_map/ppermute | solution.py:463
  370.8 24.8 %collective-permute-start.47 = (bf16[5,192,512]{2,1,0:T(8,128)(2,1)S(1)}, bf16[5,192,512]{2,1,0:T(8,128)(2,1)}, u32[]{:S(2)}, u32[]{:S(2)}) collective-permute-start(bf16[5,192,512]{2,1,0:T(8,128)(2,1)S(1)} %copy-done.34), channel_id=1, source_target_pairs={{0,4},{1,5},{2,6},{3,7},{8,0},{9,1},{10,2},{11,3},{16,8},{17,9},{1... | collective-permute-start | bytes 2949128 | tf_op jit(solution)/shard_map/ppermute | solution.py:463
  386.7 24.7 %collective-permute-start.52 = (bf16[320,768]{1,0:T(8,128)(2,1)}, bf16[320,768]{1,0:T(8,128)(2,1)S(1)}, u32[]{:S(2)}, u32[]{:S(2)}) collective-permute-start(bf16[320,768]{1,0:T(8,128)(2,1)} %get-tuple-element.218), channel_id=1, source_target_pairs={{0,8},{1,9},{2,10},{3,11},{8,16},{9,17},{10,18},{11,19},{16,24},{1... | collective-permute-start | bytes 1474568 | tf_op jit(solution)/shard_map/ppermute | solution.py:463
  388.3 28.5 %collective-permute-start.53 = (bf16[320,768]{1,0:T(8,128)(2,1)}, bf16[320,768]{1,0:T(8,128)(2,1)S(1)}, u32[]{:S(2)}, u32[]{:S(2)}) collective-permute-start(bf16[320,768]{1,0:T(8,128)(2,1)} %get-tuple-element.219), channel_id=1, source_target_pairs={{0,4},{1,5},{2,6},{3,7},{8,0},{9,1},{10,2},{11,3},{16,8},{17,9},{1... | collective-permute-start | bytes 1474568 | tf_op jit(solution)/shard_map/ppermute | solution.py:463
  403.5 47.5 %collective-permute-start.50 = (bf16[5,192,512]{2,1,0:T(8,128)(2,1)}, bf16[5,192,512]{2,1,0:T(8,128)(2,1)}, u32[]{:S(2)}, u32[]{:S(2)}) collective-permute-start(bf16[5,192,512]{2,1,0:T(8,128)(2,1)} %get-tuple-element.222), channel_id=1, source_target_pairs={{0,8},{1,9},{2,10},{3,11},{8,16},{9,17},{10,18},{11,19},{16,24},{1... | collective-permute-start | bytes 2949128 | tf_op jit(solution)/shard_map/ppermute | solution.py:463
  405.1 48.2 %collective-permute-start.51 = (bf16[5,192,512]{2,1,0:T(8,128)(2,1)}, bf16[5,192,512]{2,1,0:T(8,128)(2,1)}, u32[]{:S(2)}, u32[]{:S(2)}) collective-permute-start(bf16[5,192,512]{2,1,0:T(8,128)(2,1)} %get-tuple-element.223), channel_id=1, source_target_pairs={{0,4},{1,5},{2,6},{3,7},{8,0},{9,1},{10,2},{11,3},{16,8},{17,9},{1... | collective-permute-start | bytes 2949128 | tf_op jit(solution)/shard_map/ppermute | solution.py:463
  417.6 65.6 %all-to-all-start.4 = ((bf16[4,256,1536]{2,1,0:T(8,128)(2,1)}), bf16[4,256,1536]{2,1,0:T(8,128)(2,1)S(1)}, u32[]{:S(2)}, u32[]{:S(2)}) async-start(bf16[4,256,1536]{2,1,0:T(8,128)(2,1)} %bitcast.91), calls=%async_computation.4 | async-start | bytes 6291456 | tf_op jit(solution)/shard_map/all_to_all | solution.py:1054
  426.3 47.2 %collective-permute-start.54 = (bf16[320,768]{1,0:T(8,128)(2,1)}, bf16[320,768]{1,0:T(8,128)(2,1)S(1)}, u32[]{:S(2)}, u32[]{:S(2)}) collective-permute-start(bf16[320,768]{1,0:T(8,128)(2,1)} %get-tuple-element.227), channel_id=1, source_target_pairs={{0,8},{1,9},{2,10},{3,11},{8,16},{9,17},{10,18},{11,19},{16,24},{1... | collective-permute-start | bytes 1474568 | tf_op jit(solution)/shard_map/ppermute | solution.py:463
  426.6 47.0 %collective-permute-start.55 = (bf16[320,768]{1,0:T(8,128)(2,1)}, bf16[320,768]{1,0:T(8,128)(2,1)S(1)}, u32[]{:S(2)}, u32[]{:S(2)}) collective-permute-start(bf16[320,768]{1,0:T(8,128)(2,1)} %get-tuple-element.228), channel_id=1, source_target_pairs={{0,4},{1,5},{2,6},{3,7},{8,0},{9,1},{10,2},{11,3},{16,8},{17,9},{1... | collective-permute-start | bytes 1474568 | tf_op jit(solution)/shard_map/ppermute | solution.py:463
  461.3 43.1 %collective-permute-start.56 = (bf16[5,192,512]{2,1,0:T(8,128)(2,1)}, bf16[5,192,512]{2,1,0:T(8,128)(2,1)}, u32[]{:S(2)}, u32[]{:S(2)}) collective-permute-start(bf16[5,192,512]{2,1,0:T(8,128)(2,1)} %get-tuple-element.231), channel_id=1, source_target_pairs={{0,8},{1,9},{2,10},{3,11},{8,16},{9,17},{10,18},{11,19},{16,24},{1... | collective-permute-start | bytes 2949128 | tf_op jit(solution)/shard_map/ppermute | solution.py:463
  462.8 41.6 %collective-permute-start.57 = (bf16[5,192,512]{2,1,0:T(8,128)(2,1)}, bf16[5,192,512]{2,1,0:T(8,128)(2,1)}, u32[]{:S(2)}, u32[]{:S(2)}) collective-permute-start(bf16[5,192,512]{2,1,0:T(8,128)(2,1)} %get-tuple-element.232), channel_id=1, source_target_pairs={{0,4},{1,5},{2,6},{3,7},{8,0},{9,1},{10,2},{11,3},{16,8},{17,9},{1... | collective-permute-start | bytes 2949128 | tf_op jit(solution)/shard_map/ppermute | solution.py:463
  (62 other events, 453.4 us)
Sparse Core Ops, SparseCore 0:
  9.6 34.3 all-gather.1
  388.9 108.3 reduce-scatter.1

commit v4 on v3

--- a/solution.py
+++ b/solution.py
@@ -523,41 +523,72 @@
     return pieces, jnp.stack(numbers).astype(jnp.int32)
 
 
-def weight_products_kernel(place, left, normed_two, gain, *refs):
-    projects, packs, out = refs[:2], refs[2:4], refs[4]
-    depth, count = out.shape[0], projects[0].shape[1]
-    columns = projects[0].shape[2]
-    width = packs[0].shape[2] - LANES
-    core = place[0] % 2
+def below(arrays, rows, at):
+    return jnp.concatenate([r[wide, :rows, at] for r in arrays for wide in (0, 1)], axis=0)
+
+
+def beside_each_other(left, core, rows):
     order = [2 * wide + c for c in (core, 1 - core) for wide in (0, 1)]
-
-    def below(arrays, at):
-        return jnp.concatenate([r[wide, :count, at] for r in arrays for wide in (0, 1)], axis=0)
-
-    first = jnp.concatenate([left[i, :depth, :] for i in order], axis=1)
-    second = jnp.concatenate([left[i, depth:, :] for i in order], axis=1)
-    third = jnp.concatenate([normed_two[i] for i in order], axis=1)
+    return jnp.concatenate([left[i, rows, :] for i in order], axis=1)
+
+
+def project_products_kernel(place, left, earlier, own, other, out):
+    depth = out.shape[0]
+    first = beside_each_other(left, place[0] % 2, slice(0, depth))
+    columns = own.shape[2]
     tile = 4 * LANES
     for start in range(0, columns, tile):
         at = slice(start, start + tile)
-        out[:, at] = dot(first, below(projects, at)).astype(BF16)
+        out[:, at] = dot(first, below((own, other), own.shape[1], at)).astype(BF16)
+    out[:, columns:] = earlier[...]
+
+
+def pack_products_kernel(place, left, normed_two, gain, own, other, out):
+    depth = out.shape[0]
+    count, width = own.shape[1] - 16, own.shape[2] - LANES
+    core = place[0] % 2
+    second = beside_each_other(left, core, slice(depth, 2 * depth))
+    third = beside_each_other(normed_two, core, slice(0, depth))
+    tile = 4 * LANES
     for start in range(0, width, tile):
         at = slice(start, start + tile)
-        to = slice(columns + start, columns + start + tile)
-        out[:, to] = dot(second, below(packs, at)).astype(BF16)
-    rest = dot(third, below(packs, slice(width, width + LANES)))
-    out[:, columns + width :] = (rest + gain[...]).astype(BF16)
-
-
-def weight_products(place, left, normed_two, gain, projects, packs):
-    depth = left.shape[1] // 2
+        out[:, at] = dot(second, below((own, other), count, at)).astype(BF16)
+    rest = dot(third, below((own, other), count, slice(width, width + LANES)))
+    out[:, width:] = (rest + gain[...]).astype(BF16)
+
+
+def weight_products(place, left, pieces, *more):
+    columns = pieces[0].shape[2] + (more[0].shape[1] if len(more) == 1 else 0)
     return call(
-        weight_products_kernel,
-        jax.ShapeDtypeStruct((depth, projects[0].shape[2] + packs[0].shape[2]), BF16),
+        pack_products_kernel if len(more) > 1 else project_products_kernel,
+        jax.ShapeDtypeStruct((left.shape[1] // 2, columns), BF16),
         limit=58,
         name="weight_products",
-        specs=[SMEM_SPEC] + [VMEM_SPEC] * 7,
-    )(place, left, normed_two, gain, *projects, *packs)
+        specs=[SMEM_SPEC] + [VMEM_SPEC] * (3 + len(more)),
+    )(place, left, *more, *pieces)
+
+
+def finish_kernel(total, weight, d_qkv, d_out, d_small):
+    columns, width = d_qkv.shape[1], d_out.shape[1]
+    first = total[:, :columns].astype(F32)
+    d_qkv[...] = first
+    d_out[...] = total[:, columns : columns + width].astype(F32)
+    small = total[:, columns + width :].astype(F32)
+    lanes = lax.broadcasted_iota(jnp.int32, small.shape, 1)
+    row_sum = jnp.sum(first * weight[...].astype(F32), axis=1, keepdims=True)
+    d_small[...] = jnp.where(lanes == LANES - 1, row_sum, small)
+
+
+def finish(total, weight):
+    rows, columns = weight.shape
+    shape = lambda n: jax.ShapeDtypeStruct((rows, n), F32)
+    return call(
+        finish_kernel,
+        [shape(columns), shape(total.shape[1] - columns - LANES), shape(LANES)],
+        limit=40,
+        name="finish",
+        specs=[VMEM_SPEC] * 2,
+    )(total, weight)
 
 
 def gain_column_kernel(lane, *refs):
@@ -617,7 +648,7 @@
         return self.halves
 
 
-def in_kernel(last, places, turned_rows, grad_pre, *refs):
+def in_kernel(last, step, places, turned_rows, grad_pre, *refs):
     came, refs = (refs[:2], refs[2:]) if len(refs) > 10 - last else (None, refs)
     outs, (rows, grads, added, shares, rows_sems, grad_sems, came_sems, out_sems) = (
         refs[: 2 - last],
@@ -627,7 +658,7 @@
     depth = rows.shape[1]
 
     def rows_copy(i):
-        at = pl.ds(pl.multiple_of(places[i] * depth, 16), depth)
+        at = pl.ds(pl.multiple_of(places[step, i] * depth, 16), depth)
         return pltpu.make_async_copy(turned_rows.at[at], rows.at[i], rows_sems.at[i])
 
     def grad_copy(e):
@@ -679,7 +710,7 @@
             out_copy(i, e).wait()
 
 
-def in_share(places, turned_rows, grad_pre, came, cost, last=False):
+def in_share(step, places, turned_rows, grad_pre, came, cost, last=False):
     local, tokens_all, wide = grad_pre.shape
     depth = turned_rows.shape[0] // lax.axis_size("dp")
     kind = F32 if last else BF16
@@ -688,7 +719,7 @@
     else:
         out_shape = [jax.ShapeDtypeStruct((local, depth, FE), kind)] * 2
     return pl.pallas_call(
-        functools.partial(in_kernel, int(last)),
+        functools.partial(in_kernel, int(last), step),
         out_shape=out_shape,
         in_specs=[SMEM_SPEC] + [ANY_SPEC] * (2 + len(came)),
         out_specs=[ANY_SPEC] * len(out_shape),
@@ -708,14 +739,14 @@
     )(places, turned_rows, grad_pre, *came)
 
 
-def out_kernel(last, places, turned_act, upstream, *refs):
+def out_kernel(step, places, turned_act, upstream, *refs):
     came, refs = (refs[:2], refs[2:]) if len(refs) > 10 else (None, refs)
     outs, (rows, ups, added, shares, rows_sems, up_sems, came_sems, out_sems) = refs[:2], refs[2:]
     local, depth, tokens_all = rows.shape[1:]
     half = ups.shape[2]
 
     def copies(i):
-        at = pl.ds(pl.multiple_of(places[i] * depth, 16), depth)
+        at = pl.ds(pl.multiple_of(places[step, i] * depth, 16), depth)
         some = [
             pltpu.make_async_copy(turned_act.at[:, at], rows.at[i], rows_sems.at[i]),
             pltpu.make_async_copy(upstream.at[:, pl.ds(i * half, half)], ups.at[i], up_sems.at[i]),
@@ -742,13 +773,13 @@
         out_copy(i).wait()
 
 
-def out_share(places, turned_act, upstream_all, came, cost, last=False):
+def out_share(step, places, turned_act, upstream_all, came, cost, last=False):
     local, hidden, tokens_all = turned_act.shape
     half = upstream_all.shape[1] // 2
     depth = hidden // lax.axis_size("dp")
     kind = F32 if last else BF16
     return pl.pallas_call(
-        functools.partial(out_kernel, int(last)),
+        functools.partial(out_kernel, step),
         out_shape=[jax.ShapeDtypeStruct((local * depth, half), kind)] * 2,
         in_specs=[SMEM_SPEC] + [ANY_SPEC] * (2 + len(came)),
         out_specs=[ANY_SPEC] * 2,
@@ -789,7 +820,8 @@
     )(upstream, weight)
 
 
-def expert_kernel(later, scalars, rows_a, rows_b, grad_plain, weight, *refs):
+def expert_kernel(later, both_scalars, rows_a, rows_b, grad_plain, weight, *refs):
+    scalars = [both_scalars[int(later), i] for i in range(3)]
     refs = refs[5 if later else 0 :]
     outs, bufs, (weights, plains, weight_sems, plain_sems, out_sems) = refs[:5], refs[5:10], refs[10:]
     activated, turned_act, grad_pre, gate_grad, turned_rows = bufs
@@ -953,16 +985,19 @@
     across_rows = net.swap(sent, WIDE)
     own_rows, beside_rows = sent, net.swap(sent, CORE)
     core, wide = net.e % 2, net.e // 2
-    scalars = lambda half: jnp.stack([net.e * local_count, half, core]).astype(jnp.int32)
-    early = expert_half(scalars(wide), own_rows, beside_rows, grad_act_plain, expert_in, ())
+    first_expert = net.e * local_count
+    scalars = jnp.stack([first_expert, wide, core, first_expert, 1 - wide, core])
+    scalars = scalars.reshape(2, 3).astype(jnp.int32)
+    early = expert_half(scalars, own_rows, beside_rows, grad_act_plain, expert_in, ())
     across_rows = after(across_rows, early)
     corner_rows = net.swap(across_rows, CORE)
     activated, turned_act, grad_pre, gate_grads, turned_rows = expert_half(
-        scalars(1 - wide), across_rows, corner_rows, grad_act_plain, expert_in, early
-    )
-
-    def places(s):
-        return jnp.stack([net.dp_of(net.r - 1 - s), net.dp_of(net.r + 1 + s)]).astype(jnp.int32)
+        scalars, across_rows, corner_rows, grad_act_plain, expert_in, early
+    )
+
+    steps = jnp.arange(net.nd, dtype=jnp.int32)
+    ways = jnp.stack([net.r - 1 - steps, net.r + 1 + steps], axis=1)
+    places = jnp.where(steps[:, None] < net.nd - 1, net.dp_of(ways), net.p).astype(jnp.int32)
 
     def cost(s):
         return 10**10 if s == 4 else 3 * 10**10
@@ -976,7 +1011,7 @@
         nonlocal came_in
         if earlier:
             came_in = after(came_in, *earlier)
-        shares = in_share(places(s), turned_rows, grad_pre, came_in, cost(s))
+        shares = in_share(s, places, turned_rows, grad_pre, came_in, cost(s))
         if beside is not None:
             shares = after(shares, beside)
         came_in = advance(shares)
@@ -986,7 +1021,7 @@
         nonlocal came_out
         if earlier:
             came_out = after(came_out, *earlier)
-        shares = out_share(places(s), turned_act, upstream_all, came_out, cost(s))
+        shares = out_share(s, places, turned_act, upstream_all, came_out, cost(s))
         if beside is not None:
             shares = after(shares, beside)
         came_out = advance(shares)
@@ -1030,24 +1065,26 @@
     )
     projects = net.exchange(grad_project, 1)
     sent_out = ring_out(3, grad_project)
-    sent_in = ring_in(3, sent_out)
-    sent_out = ring_out(4, sent_in)
-    projects, packs = after((projects, packs), sent_out, came_in)
-    projects_beside, packs_beside = net.swap(projects, CORE), net.swap(packs, CORE)
-    sent_in = ring_in(4, projects, packs, beside=(projects_beside, packs_beside))
+    packs = after(packs, sent_out, came_in)
+    packs = (packs, net.swap(packs, CORE))
+    sent_in = ring_in(3, sent_out, packs[0], beside=packs[1])
     mine = lambda rows: lax.dynamic_index_in_dim(
         rows.reshape(net.nd, net.ne, block, -1), net.e, 1, keepdims=False
     ).reshape(net.nd * block, -1)
     normed_two = mine(turned_rows).reshape(-1, net.ne, length).transpose(1, 0, 2)
-    packs = (packs, packs_beside)
-    products = weight_products(
-        net.e.astype(jnp.int32).reshape(1),
+    place = net.e.astype(jnp.int32).reshape(1)
+    out_products = weight_products(
+        place,
         after(lefts, sent_in),
+        packs,
         normed_two,
         mine(gain_column(experts_all, packs)),
-        (projects, projects_beside),
-        packs,
-    )
+    )
+    sent_out = ring_out(4, out_products)
+    projects = after(projects, sent_out, came_in)
+    projects = (projects, net.swap(projects, CORE))
+    sent_in = ring_in(4, projects[0], beside=projects[1])
+    products = weight_products(place, after(lefts, sent_in), projects, out_products)
     sent_out = ring_out(5, products)
     d_all = lax.psum_scatter(after(products, sent_out), "dp", scatter_dimension=0, tiled=True)
     sent_in = ring_in(5, sent_out)
@@ -1060,25 +1097,22 @@
     )
     mixture = jnp.sum(mix_all.reshape(net.ne, length, width).astype(F32), axis=0)
     activations = (hidden_state + mixture).astype(BF16)
-    here = jnp.stack([net.p, net.p]).astype(jnp.int32)
     d_expert_out = jnp.concatenate(
         out_share(
-            here, turned_act, upstream_all, after(came_out, grad_tokens), cost(net.nd), last=True
+            net.nd - 1, places, turned_act, upstream_all, after(came_out, grad_tokens), cost(net.nd), last=True
         ),
         axis=1,
     ).reshape(local_count, FE // net.nd, width)
-    d_all = after(d_all, d_expert_out).astype(F32)
-    d_qkv = d_all[:, :wide_qkv]
-    d_small = d_all[:, wide_qkv + width :]
-    d_gain_first = jnp.sum(d_qkv * w_qkv.astype(F32), axis=1) / gain_attn.astype(F32)
     (d_expert_in,) = in_share(
-        here, turned_rows, grad_pre, after(came_in, d_gain_first), cost(net.nd), last=True
-    )
+        net.nd - 1, places, turned_rows, grad_pre, after(came_in, d_expert_out, activations), cost(net.nd), last=True
+    )
+    d_qkv, d_out, d_small = finish(after(d_all, d_expert_in), w_qkv)
+    d_gain_first = d_small[:, LANES - 1] / gain_attn.astype(F32)
     return (
         activations,
         grad_tokens,
         d_qkv,
-        d_all[:, wide_qkv : wide_qkv + width],
+        d_out,
         d_small[:, :experts_all],
         d_gain_first,
         d_small[:, experts_all],

time: 525 us -> 516 us (0.983)
  other arithmetic: 25.6 us -> 17.5 us
  waiting for transfers between devices: 117 us -> 111 us
    ppermute x44, waiting for transfers between devices: 80.7 us -> 94.7 us  [step(): return lax.ppermute(value, AXES, self.ring[way])]
    reduce_scatter x1, waiting for transfers between devices: 11.6 us -> 0.02 us  [on_device(): lax.psum_scatter(after(products, sent_out), 'dp', scatter_dimension=0, ti...]
    all_to_all x3, waiting for transfers between devices: 9.19 us -> 1.09 us  [exchange(): lax.all_to_all(value, AXES, 0, 0, axis_index_groups=pairs, tiled=True)]
    another operation x10 -> x1, other arithmetic: 6 us -> 0.01 us  [on_device(): ways = jnp.stack([net.r - 1 - steps, net.r + 1 + steps], axis=1)]
    pallas_call x17 -> x19, Pallas kernels: 114 us -> 119 us  [the longest x8 65.3 us: in_share(): pl.pallas_call(functools.partial(in_kernel, int(last), step), out_shape=o...]
    unnamed x101 -> x107, local copies, waits for them, and re-layouts: 18.9 us -> 20.1 us
  transfers between devices with their start and end apart: 65 -> 65, of which waited for: 27 -> 26; matrix products, arithmetic and copies ran while one was open for 8% -> 6% of each run, Pallas kernels for 47% -> 50%
where the time goes in v4:
time: 516 us; the launch traced here: 511 us
  Pallas kernels  264 us (51%)
  waiting for transfers between devices  111 us (22%)
  starting transfers between devices  73.7 us (14%)
  local copies, waits for them, and re-layouts  29.7 us (6%)
  other arithmetic  17.5 us (3%)
  between operations  15.3 us (3%)
    ppermute x44, waiting for transfers between devices, step(): return lax.ppermute(value, AXES, self.ring[way])  94.7 us
    pallas_call x8, Pallas kernels, in_share(): pl.pallas_call(functools.partial(in_kernel, int(last), step), out_shape=o...  65.3 us
    pallas_call x3, Pallas kernels, owner_rows(): pl.pallas_call(functools.partial(owner_rows_kernel, extra is not None, bl...  46.8 us
    ppermute x44, starting transfers between devices, step(): return lax.ppermute(value, AXES, self.ring[way])  46.3 us
    pallas_call x8, Pallas kernels, out_share(): pl.pallas_call(functools.partial(out_kernel, step), out_shape=[jax.ShapeD...  40.2 us
    pallas_call x2, Pallas kernels, expert_half(): pl.pallas_call(functools.partial(expert_kernel, bool(earlier)), out_shape...  34.1 us
    unnamed x107, local copies, waits for them, and re-layouts  20.1 us
    ppermute x14, waiting for transfers between devices, swap(): lax.ppermute(value, AXES, [(d, d ^ bit) for d in range(self.devices)])  14.3 us
  transfers between devices with their start and end apart: 65, of which 26 were waited for; matrix products, arithmetic and copies ran while one was open for 6% of the time, Pallas kernels for 50%

profile of v4, /device:TPU:0, one launch (start us, length us, event | category | flops | bytes accessed | tf_op | source)
XLA Modules:
  0.0 511.1 jit_solution(8104061238230357125)
XLA Ops:
  11.3 3.0 collective-permute-start
  14.3 6.2 %collective-permute-done = bf16[48,2688]{1,0:T(8,128)(2,1)S(1)} collective-permute-done((bf16[48,2688]{1,0:T(8,128)(2,1)S(1)}, bf16[48,2688]{1,0:T(8,128)(2,1)S(1)}, u32[]{:S(2)}, u32[]{:S(2)}) %collective-permute-start) | collective-permute-done | bytes 258080 | tf_op jit(solution)/shard_map/ppermute | solution.py:470
  25.2 4.7 collective-permute-done.4
  32.1 5.8 %collective-permute-done.2 = bf16[2,48,2688]{2,1,0:T(8,128)(2,1)S(1)} collective-permute-done((bf16[2,48,2688]{2,1,0:T(8,128)(2,1)S(1)}, bf16[2,48,2688]{2,1,0:T(8,128)(2,1)S(1)}, u32[]{:S(2)}, u32[]{:S(2)}) %collective-permute-start.2) | collective-permute-done | bytes 516128 | tf_op jit(solution)/shard_map/ppermute | solution.py:463
  49.9 12.6 %owner_grads.1.grad_plain = bf16[5,1024,512]{2,1,0:T(8,128)(2,1)} custom-call(bf16[1024,1536]{1,0:T(8,128)(2,1)} %all-gather.2.cloned.1.call-done.upstream, bf16[5,512,1536]{2,1,0:T(8,128)(2,1)} %refs_5_.1), custom_call_target="tpu_custom_call" | custom-call | flops 8053063680 | bytes 16777216 | tf_op jit(solution)/shard_map/owner_grads/pallas_call | solution.py:806
  68.6 6.2 %collective-permute-done.10 = bf16[2,48,2688]{2,1,0:T(8,128)(2,1)S(1)} collective-permute-done((bf16[2,48,2688]{2,1,0:T(8,128)(2,1)}, bf16[2,48,2688]{2,1,0:T(8,128)(2,1)S(1)}, u32[]{:S(2)}, u32[]{:S(2)}) %collective-permute-start.10) | collective-permute-done | bytes 516128 | tf_op jit(solution)/shard_map/ppermute | solution.py:463
  75.1 6.2 %collective-permute-done.18 = bf16[2,48,1536]{2,1,0:T(8,128)(2,1)S(1)} collective-permute-done((bf16[2,48,1536]{2,1,0:T(8,128)(2,1)}, bf16[2,48,1536]{2,1,0:T(8,128)(2,1)S(1)}, u32[]{:S(2)}, u32[]{:S(2)}) %collective-permute-start.18) | collective-permute-done | bytes 294944 | tf_op jit(solution)/shard_map/ppermute | solution.py:463
  85.8 4.1 collective-permute-done.16
  102.5 13.3 %attend.1 = (bf16[256,1536]{1,0:T(8,128)(2,1)}, bf16[3072,256]{1,0:T(8,128)(2,1)}, bf16[256,1536]{1,0:T(8,128)(2,1)}, bf16[256,512]{1,0:T(8,128)(2,1)}, bf16[256...) custom-call(s32[32]{0:T(128)} %stack.288.numbers, ...), custom_call_target="tpu_custom_call" | custom-call | flops 1024 | bytes 1024 | tf_op jit(solution)/shard_map/attend/pallas_call | solution.py:181
  115.8 7.2 %branch.1 = (f32[256,1536]{1,0:T(8,128)}, bf16[256,1664]{1,0:T(8,128)(2,1)}, f32[256,128]{1,0:T(8,128)}) custom-call(s32[32]{0:T(128)} %stack.287.numbers, bf16[256,1536]{1,0:T(8,128)(2,1)} %tokens.5, bf16[256,1536]{1,0:T(8,128)(2,1)} %get-tuple-element.149.mixed, bf16[1536,128]{1,0:T(8,128)(2,1)} %get-tuple-element.150.small, ...), custom_call_target="tpu_custom_call" | custom-call | flops 1024 | bytes 1024 | tf_op jit(solution)/shard_map/branch/pallas_call | solution.py:219
  126.5 17.0 %expert_half.2 = (bf16[5,1024,512]{2,1,0:T(8,128)(2,1)}, bf16[5,512,1024]{2,1,0:T(8,128)(2,1)}, bf16[5,1024,1024]{2,1,0:T(8,128)(2,1)}, f32[1024,128]{1,0:T(8,128)}, bf16[1536,1024]{1,0:T(8,128)(2,1)}) custom-call(s32[2,3]{1,0:T(2,128)} %reshape.76.both_scalars, bf16[256,1664]{1,0:T(8,128)(2,1)} %get-tuple-element.155.rows_a, bf16[256,1664]{1,0:T(8,128)(2,1)} %copy-done.41, ...), custom_call_target="tpu_custom_call" | custom-call | flops 8053063680 | bytes 31457280 | tf_op jit(solution)/shard_map/expert_half/pallas_call | solution.py:920
  147.9 3.6 all-to-all-start
  152.4 17.0 %expert_half.3 = (bf16[5,1024,512]{2,1,0:T(8,128)(2,1)}, bf16[5,512,1024]{2,1,0:T(8,128)(2,1)}, bf16[5,1024,1024]{2,1,0:T(8,128)(2,1)}, f32[1024,128]{1,0:T(8,128)}, bf16[1536,1024]{1,0:T(8,128)(2,1)}) custom-call(s32[2,3]{1,0:T(2,128)} %reshape.76.both_scalars, ...), custom_call_target="tpu_custom_call", output_to_operand_aliasing={{0}: (5, {}), {1}: (6, {}), {2}: (7, {}), {3}: (8, {}), {4}... | custom-call | flops 8053063680 | bytes 31457280 | tf_op jit(solution)/shard_map/expert_half/pallas_call | solution.py:920
  169.4 4.9 out_share.8
  176.5 7.9 %in_share.8 = (bf16[5,192,512]{2,1,0:T(8,128)(2,1)}, bf16[5,192,512]{2,1,0:T(8,128)(2,1)}) custom-call(s32[8,2]{1,0:T(8,128)} %select_select_fusion.places, bf16[1536,1024]{1,0:T(8,128)(2,1)} %get-tuple-element.163.turned_rows, bf16[5,1024,1024]{2,1,0:T(8,128)(2,1)} %get-tuple-element.179.grad_pre.refs_1_.refs_2_), custom_call_target="tpu_custom_call" | custom-call | flops 30000001024 | bytes 1024 | tf_op jit(solution)/shard_map/in_share/pallas_call | solution.py:721
  186.5 15.2 %owner_rows.3 = bf16[512,1664]{1,0:T(8,128)(2,1)} custom-call(s32[2]{0:T(128)} %pad_add_fusion.2.refs_0_, bf16[5,1024,1024]{2,1,0:T(8,128)(2,1)} %get-tuple-element.179.grad_pre.refs_1_.refs_2_, bf16[5,1024,1024]{2,1,0:T(8,128)(2,1)} %get-tuple-element.179.grad_pre.refs_1_.refs_2_, bf16[5,1536,1024]{2,1,0:T(8,128)(2,1)} %refs_3_.3, ...), custom_call_target="tpu_custom_call" | custom-call | flops 1024 | bytes 1024 | tf_op jit(solution)/shard_map/owner_rows/pallas_call | solution.py:275
  204.5 5.0 out_share.9
  211.6 15.3 %owner_rows.4 = bf16[512,1664]{1,0:T(8,128)(2,1)} custom-call(s32[2]{0:T(128)} %pad_add_fusion.1.refs_0_, bf16[5,1024,1024]{2,1,0:T(8,128)(2,1)} %get-tuple-element.179.grad_pre.refs_1_.refs_2_, bf16[5,1024,1024]{2,1,0:T(8,128)(2,1)} %get-tuple-element.179.grad_pre.refs_1_.refs_2_, bf16[5,1536,1024]{2,1,0:T(8,128)(2,1)} %refs_3_.3, ...), custom_call_target="tpu_custom_call" | custom-call | flops 1024 | bytes 1024 | tf_op jit(solution)/shard_map/owner_rows/pallas_call | solution.py:275
  228.8 7.9 %in_share.9 = (bf16[5,192,512]{2,1,0:T(8,128)(2,1)}, bf16[5,192,512]{2,1,0:T(8,128)(2,1)}) custom-call(s32[8,2]{1,0:T(8,128)} %select_select_fusion.places, bf16[1536,1024]{1,0:T(8,128)(2,1)} %get-tuple-element.163.turned_rows, bf16[5,1024,1024]{2,1,0:T(8,128)(2,1)} %get-tuple-element.179.grad_pre.refs_1_.refs_2_, ...), custom_call_target="tpu_custom_call" | custom-call | flops 30000001024 | bytes 1024 | tf_op jit(solution)/shard_map/in_share/pallas_call | solution.py:721
  240.3 3.7 all-to-all-start.1
  244.5 16.3 %owner_rows.5 = bf16[1024,1536]{1,0:T(8,128)(2,1)} custom-call(s32[4]{0:T(128)} %iota.45.refs_0_, bf16[5,1024,512]{2,1,0:T(8,128)(2,1)} %get-tuple-element.184.refs_1_.refs_2_.refs_3_.refs_4_, bf16[5,1024,512]{2,1,0:T(8,128)(2,1)} %get-tuple-element.184.refs_1_.refs_2_.refs_3_.refs_4_, ...), custom_call_target="tpu_custom_call" | custom-call | flops 1024 | bytes 1024 | tf_op jit(solution)/shard_map/owner_rows/pallas_call | solution.py:275
  260.8 5.0 out_share.10
  269.1 7.3 %middle.1 = (f32[256,1536]{1,0:T(8,128)}, bf16[2,272,1664]{2,1,0:T(8,128)(2,1)}, bf16[256,1536]{1,0:T(8,128)(2,1)}) custom-call(s32[32]{0:T(128)} %stack.287.numbers, bf16[2,256,1664]{2,1,0:T(8,128)(2,1)} %copy-done.9, bf16[256,1536]{1,0:T(8,128)(2,1)} %cotangent.1, f32[256,1536]{1,0:T(8,128)} %get-tuple-element.154.hidden, ...), custom_call_target="tpu_custom_call" | custom-call | flops 1024 | bytes 1024 | tf_op jit(solution)/shard_map/middle/pallas_call | solution.py:404
  276.4 3.7 all-to-all-start.2
  281.1 7.9 %in_share.10 = (bf16[5,192,512]{2,1,0:T(8,128)(2,1)}, bf16[5,192,512]{2,1,0:T(8,128)(2,1)}) custom-call(s32[8,2]{1,0:T(8,128)} %select_select_fusion.places, bf16[1536,1024]{1,0:T(8,128)(2,1)} %get-tuple-element.163.turned_rows, bf16[5,1024,1024]{2,1,0:T(8,128)(2,1)} %get-tuple-element.179.grad_pre.refs_1_.refs_2_, bf16[5,192,512]{2,1,0:T(8,128)(2,1)} %copy-done.35, ...), custom_call_target="tpu_custom_call" | custom-call | flops 30000001024 | bytes 1024 | tf_op jit(solution)/shard_map/in_share/pallas_call | solution.py:721
  291.3 10.8 %attend_back.1.grad_project = bf16[2,256,2560]{2,1,0:T(8,128)(2,1)} custom-call(bf16[256,1536]{1,0:T(8,128)(2,1)} %get-tuple-element.196.queries, bf16[256,512]{1,0:T(8,128)(2,1)} %get-tuple-element.197.key_rows, bf16[256,512]{1,0:T(8,128)(2,1)} %get-tuple-element.198.values, bf16[256,1536]{1,0:T(8,128)(2,1)} %get-tuple-element.199.grad_mixed, ...), custom_call_target="tpu_custom_call" | custom-call | flops 1024 | bytes 1024 | tf_op jit(solution)/shard_map/attend_back/pallas_call | solution.py:374
  302.9 5.0 out_share.11
  310.0 5.0 all-to-all-start.3
  316.1 8.6 %in_share.11 = (bf16[5,192,512]{2,1,0:T(8,128)(2,1)}, bf16[5,192,512]{2,1,0:T(8,128)(2,1)}) custom-call(s32[8,2]{1,0:T(8,128)} %select_select_fusion.places, bf16[1536,1024]{1,0:T(8,128)(2,1)} %get-tuple-element.163.turned_rows, bf16[5,1024,1024]{2,1,0:T(8,128)(2,1)} %get-tuple-element.179.grad_pre.refs_1_.refs_2_, bf16[5,192,512]{2,1,0:T(8,128)(2,1)} %copy-done.36, ...), custom_call_target="tpu_custom_call" | custom-call | flops 30000001024 | bytes 1024 | tf_op jit(solution)/shard_map/in_share/pallas_call | solution.py:721
  327.0 3.2 gain_column.1
  331.9 5.5 %weight_products.2.earlier = bf16[384,1664]{1,0:T(8,128)(2,1)} custom-call(s32[1]{0:T(128)} %bitcast.67.place, bf16[4,768,256]{2,1,0:T(8,128)(2,1)} %copy-done.3, bf16[4,384,256]{2,1,0:T(8,128)(2,1)} %bitcast.113, f32[384,128]{1,0:T(8,128)} %bitcast.119, bf16[2,272,1664]{2,1,0:T(8,128)(2,1)} %copy-done.2, bf16[2,272,1664]{2,1,0:T(8,128)(2,1)} %copy-done.8), custom_call_target="tpu_custom_call" | custom-call | flops 1024 | bytes 1024 | tf_op jit(solution)/shard_map/weight_products/pallas_call | solution.py:562
  338.1 5.0 out_share.12
  344.2 5.0 collective-permute-done.41.refs_0_
  353.1 7.9 %in_share.12 = (bf16[5,192,512]{2,1,0:T(8,128)(2,1)}, bf16[5,192,512]{2,1,0:T(8,128)(2,1)}) custom-call(s32[8,2]{1,0:T(8,128)} %select_select_fusion.places, bf16[1536,1024]{1,0:T(8,128)(2,1)} %get-tuple-element.163.turned_rows, bf16[5,1024,1024]{2,1,0:T(8,128)(2,1)} %get-tuple-element.179.grad_pre.refs_1_.refs_2_, bf16[5,192,512]{2,1,0:T(8,128)(2,1)} %copy-done.37, ...), custom_call_target="tpu_custom_call" | custom-call | flops 10000000000 | bytes 1024 | tf_op jit(solution)/shard_map/in_share/pallas_call | solution.py:721
  363.1 7.3 %weight_products.3 = bf16[384,4224]{1,0:T(8,128)(2,1)} custom-call(s32[1]{0:T(128)} %bitcast.67.place, bf16[4,768,256]{2,1,0:T(8,128)(2,1)} %copy-done.3, bf16[384,1664]{1,0:T(8,128)(2,1)} %weight_products.2.earlier, bf16[2,256,2560]{2,1,0:T(8,128)(2,1)} %all-to-all-done.3.own, bf16[2,256,2560]{2,1,0:T(8,128)(2,1)} %copy-done.15), custom_call_target="tpu_custom_call" | custom-call | flops 1024 | bytes 1024 | tf_op jit(solution)/shard_map/weight_products/pallas_call | solution.py:562
  371.9 5.0 out_share.13
  379.0 7.3 %collective-permute-done.46.refs_0_ = bf16[5,192,512]{2,1,0:T(8,128)(2,1)S(1)} collective-permute-done((bf16[5,192,512]{2,1,0:T(8,128)(2,1)}, bf16[5,192,512]{2,1,0:T(8,128)(2,1)S(1)}, u32[]{:S(2)}, u32[]{:S(2)}) %collective-permute-start.46) | collective-permute-done | bytes 983072 | tf_op jit(solution)/shard_map/ppermute | solution.py:463
  388.8 7.9 %in_share.13 = (bf16[5,192,512]{2,1,0:T(8,128)(2,1)}, bf16[5,192,512]{2,1,0:T(8,128)(2,1)}) custom-call(s32[8,2]{1,0:T(8,128)} %select_select_fusion.places, bf16[1536,1024]{1,0:T(8,128)(2,1)} %get-tuple-element.163.turned_rows, bf16[5,1024,1024]{2,1,0:T(8,128)(2,1)} %get-tuple-element.179.grad_pre.refs_1_.refs_2_, bf16[5,192,512]{2,1,0:T(8,128)(2,1)} %copy-done.39, ...), custom_call_target="tpu_custom_call" | custom-call | flops 30000001024 | bytes 1024 | tf_op jit(solution)/shard_map/in_share/pallas_call | solution.py:721
  398.8 7.0 %collective-permute-done.52.refs_0_ = bf16[320,768]{1,0:T(8,128)(2,1)S(1)} collective-permute-done((bf16[320,768]{1,0:T(8,128)(2,1)}, bf16[320,768]{1,0:T(8,128)(2,1)S(1)}, u32[]{:S(2)}, u32[]{:S(2)}) %collective-permute-start.52) | collective-permute-done | bytes 491552 | tf_op jit(solution)/shard_map/ppermute | solution.py:463
  405.8 5.6 %collective-permute-done.53.refs_1_ = bf16[320,768]{1,0:T(8,128)(2,1)S(1)} collective-permute-done((bf16[320,768]{1,0:T(8,128)(2,1)}, bf16[320,768]{1,0:T(8,128)(2,1)S(1)}, u32[]{:S(2)}, u32[]{:S(2)}) %collective-permute-start.53) | collective-permute-done | bytes 491552 | tf_op jit(solution)/shard_map/ppermute | solution.py:463
  412.2 5.1 out_share.14
  419.4 3.9 all-to-all-start.4
  423.3 19.7 %collective-permute-done.50.refs_0_ = bf16[5,192,512]{2,1,0:T(8,128)(2,1)} collective-permute-done((bf16[5,192,512]{2,1,0:T(8,128)(2,1)}, bf16[5,192,512]{2,1,0:T(8,128)(2,1)}, u32[]{:S(2)}, u32[]{:S(2)}) %collective-permute-start.50) | collective-permute-done | bytes 983072 | tf_op jit(solution)/shard_map/ppermute | solution.py:463
  445.6 8.0 %in_share.14 = (bf16[5,192,512]{2,1,0:T(8,128)(2,1)}, bf16[5,192,512]{2,1,0:T(8,128)(2,1)}) custom-call(s32[8,2]{1,0:T(8,128)} %select_select_fusion.places, bf16[1536,1024]{1,0:T(8,128)(2,1)} %get-tuple-element.163.turned_rows, bf16[5,1024,1024]{2,1,0:T(8,128)(2,1)} %get-tuple-element.179.grad_pre.refs_1_.refs_2_, ...), custom_call_target="tpu_custom_call" | custom-call | flops 30000001024 | bytes 1024 | tf_op jit(solution)/shard_map/in_share/pallas_call | solution.py:721
  456.0 9.8 %input_back.1 = f32[256,1536]{1,0:T(8,128)} custom-call(s32[32]{0:T(128)} %stack.288.numbers, bf16[256,1536]{1,0:T(8,128)(2,1)} %tokens.5, bf16[2,256,2560]{2,1,0:T(8,128)(2,1)} %attend_back.1.grad_project, f32[16,1536]{1,0:T(8,128)} %get-tuple-element.151.gains, f32[256,1536]{1,0:T(8,128)} %get-tuple-element.243.grad_hidden, ...), custom_call_target="tpu_custom_call" | custom-call | flops 1024 | bytes 1024 | tf_op jit(solution)/shard_map/input_back/pallas_call | solution.py:422
  465.8 5.2 %out_share.15 = (f32[320,768]{1,0:T(8,128)}, f32[320,768]{1,0:T(8,128)}) custom-call(s32[8,2]{1,0:T(8,128)} %select_select_fusion.places, bf16[5,512,1024]{2,1,0:T(8,128)(2,1)} %get-tuple-element.167.turned_act, bf16[1024,1536]{1,0:T(8,128)(2,1)} %all-gather.2.cloned.1.call-done.upstream, bf16[320,768]{1,0:T(8,128)(2,1)} %collective-permute-done.56.refs_0_, ...), custom_call_target="tpu_custom_call" | custom-call | flops 30000001024 | bytes 1024 | tf_op jit(solution)/shard_map/out_share/pallas_call | solution.py:781
  476.5 11.8 %collective-permute-done.54.refs_0_ = bf16[5,192,512]{2,1,0:T(8,128)(2,1)} collective-permute-done((bf16[5,192,512]{2,1,0:T(8,128)(2,1)}, bf16[5,192,512]{2,1,0:T(8,128)(2,1)}, u32[]{:S(2)}, u32[]{:S(2)}) %collective-permute-start.54) | collective-permute-done | bytes 983072 | tf_op jit(solution)/shard_map/ppermute | solution.py:463
  490.8 9.1 %in_share.15 = f32[5,192,1024]{2,1,0:T(8,128)} custom-call(s32[8,2]{1,0:T(8,128)} %select_select_fusion.places, bf16[1536,1024]{1,0:T(8,128)(2,1)} %get-tuple-element.163.turned_rows, bf16[5,1024,1024]{2,1,0:T(8,128)(2,1)} %get-tuple-element.179.grad_pre.refs_1_.refs_2_, bf16[5,192,512]{2,1,0:T(8,128)(2,1)} %collective-permute-done.54.refs_0_, ...), custom_call_target="tpu_custom_call" | custom-call | flops 30000001024 | bytes 1024 | tf_op jit(solution)/shard_map/in_share/pallas_call | solution.py:721
  (264 shorter events, 119.9 us)
Async XLA Ops:
  7.2 42.7 %all-gather.2.cloned.1.call-start = ((), (), s32[]{:S(2)}) async-start(), calls=%async_computation.6 | async-start | bytes 3932160 | tf_op jit(solution)/shard_map/all_gather | solution.py:968
  23.2 14.7 %collective-permute-start.2 = (bf16[2,48,2688]{2,1,0:T(8,128)(2,1)S(1)}, bf16[2,48,2688]{2,1,0:T(8,128)(2,1)S(1)}, u32[]{:S(2)}, u32[]{:S(2)}) collective-permute-start(bf16[2,48,2688]{2,1,0:T(8,128)(2,1)S(1)} %get-tuple-element.284), channel_id=1, source_target_pairs={{0,8},{1,9},{2,10},{3,11},{8,16},{9,17},{10,18},{11,19},{16,24},{1... | collective-permute-start | bytes 1548296 | tf_op jit(solution)/shard_map/ppermute | solution.py:463
  24.8 14.7 %collective-permute-start.3 = (bf16[2,48,2688]{2,1,0:T(8,128)(2,1)S(1)}, bf16[2,48,2688]{2,1,0:T(8,128)(2,1)S(1)}, u32[]{:S(2)}, u32[]{:S(2)}) collective-permute-start(bf16[2,48,2688]{2,1,0:T(8,128)(2,1)S(1)} %get-tuple-element.284), channel_id=1, source_target_pairs={{0,4},{1,5},{2,6},{3,7},{8,0},{9,1},{10,2},{11,3},{16,8},{17,9},{1... | collective-permute-start | bytes 1548296 | tf_op jit(solution)/shard_map/ppermute | solution.py:463
  30.0 14.3 %collective-permute-start.11 = (bf16[2,48,1536]{2,1,0:T(8,128)(2,1)S(1)}, bf16[2,48,1536]{2,1,0:T(8,128)(2,1)}, u32[]{:S(2)}, u32[]{:S(2)}) collective-permute-start(bf16[2,48,1536]{2,1,0:T(8,128)(2,1)S(1)} %pad_maximum_fusion.5), channel_id=1, source_target_pairs={{0,8},{1,9},{2,10},{3,11},{8,16},{9,17},{10,18},{11,19},{16,24},{1... | collective-permute-start | bytes 884744 | tf_op jit(solution)/shard_map/ppermute | solution.py:463
  31.8 14.1 %collective-permute-start.12 = (bf16[2,48,1536]{2,1,0:T(8,128)(2,1)S(1)}, bf16[2,48,1536]{2,1,0:T(8,128)(2,1)}, u32[]{:S(2)}, u32[]{:S(2)}) collective-permute-start(bf16[2,48,1536]{2,1,0:T(8,128)(2,1)S(1)} %pad_maximum_fusion.5), channel_id=1, source_target_pairs={{0,4},{1,5},{2,6},{3,7},{8,0},{9,1},{10,2},{11,3},{16,8},{17,9},{1... | collective-permute-start | bytes 884744 | tf_op jit(solution)/shard_map/ppermute | solution.py:463
  39.4 23.0 %collective-permute-start.6 = (bf16[2,48,2688]{2,1,0:T(8,128)(2,1)S(1)}, bf16[2,48,2688]{2,1,0:T(8,128)(2,1)}, u32[]{:S(2)}, u32[]{:S(2)}) collective-permute-start(bf16[2,48,2688]{2,1,0:T(8,128)(2,1)S(1)} %collective-permute-done.2), channel_id=1, source_target_pairs={{0,8},{1,9},{2,10},{3,11},{8,16},{9,17},{10,18},{11,19},{16,24},{1... | collective-permute-start | bytes 1548296 | tf_op jit(solution)/shard_map/ppermute | solution.py:463
  41.0 21.5 %collective-permute-start.7 = (bf16[2,48,2688]{2,1,0:T(8,128)(2,1)S(1)}, bf16[2,48,2688]{2,1,0:T(8,128)(2,1)}, u32[]{:S(2)}, u32[]{:S(2)}) collective-permute-start(bf16[2,48,2688]{2,1,0:T(8,128)(2,1)S(1)} %collective-permute-done.3), channel_id=1, source_target_pairs={{0,4},{1,5},{2,6},{3,7},{8,0},{9,1},{10,2},{11,3},{16,8},{17,9},{1... | collective-permute-start | bytes 1548296 | tf_op jit(solution)/shard_map/ppermute | solution.py:463
  45.9 18.7 %collective-permute-start.13 = (bf16[2,48,1536]{2,1,0:T(8,128)(2,1)}, bf16[2,48,1536]{2,1,0:T(8,128)(2,1)}, u32[]{:S(2)}, u32[]{:S(2)}) collective-permute-start(bf16[2,48,1536]{2,1,0:T(8,128)(2,1)} %collective-permute-done.11), channel_id=1, source_target_pairs={{0,8},{1,9},{2,10},{3,11},{8,16},{9,17},{10,18},{11,19},{16,24},{1... | collective-permute-start | bytes 884744 | tf_op jit(solution)/shard_map/ppermute | solution.py:463
  47.4 17.1 %collective-permute-start.14 = (bf16[2,48,1536]{2,1,0:T(8,128)(2,1)}, bf16[2,48,1536]{2,1,0:T(8,128)(2,1)}, u32[]{:S(2)}, u32[]{:S(2)}) collective-permute-start(bf16[2,48,1536]{2,1,0:T(8,128)(2,1)} %collective-permute-done.12), channel_id=1, source_target_pairs={{0,4},{1,5},{2,6},{3,7},{8,0},{9,1},{10,2},{11,3},{16,8},{17,9},{1... | collective-permute-start | bytes 884744 | tf_op jit(solution)/shard_map/ppermute | solution.py:463
  62.5 12.3 %collective-permute-start.10 = (bf16[2,48,2688]{2,1,0:T(8,128)(2,1)}, bf16[2,48,2688]{2,1,0:T(8,128)(2,1)S(1)}, u32[]{:S(2)}, u32[]{:S(2)}) collective-permute-start(bf16[2,48,2688]{2,1,0:T(8,128)(2,1)} %collective-permute-done.7), channel_id=1, source_target_pairs={{0,4},{1,5},{2,6},{3,7},{8,0},{9,1},{10,2},{11,3},{16,8},{17,9},{1... | collective-permute-start | bytes 1548296 | tf_op jit(solution)/shard_map/ppermute | solution.py:463
  64.6 16.8 %collective-permute-start.18 = (bf16[2,48,1536]{2,1,0:T(8,128)(2,1)}, bf16[2,48,1536]{2,1,0:T(8,128)(2,1)S(1)}, u32[]{:S(2)}, u32[]{:S(2)}) collective-permute-start(bf16[2,48,1536]{2,1,0:T(8,128)(2,1)} %collective-permute-done.13), channel_id=1, source_target_pairs={{0,8},{1,9},{2,10},{3,11},{8,16},{9,17},{10,18},{11,19},{16,24},{1... | collective-permute-start | bytes 884744 | tf_op jit(solution)/shard_map/ppermute | solution.py:463
  66.1 15.2 %collective-permute-start.19 = (bf16[2,48,1536]{2,1,0:T(8,128)(2,1)}, bf16[2,48,1536]{2,1,0:T(8,128)(2,1)S(1)}, u32[]{:S(2)}, u32[]{:S(2)}) collective-permute-start(bf16[2,48,1536]{2,1,0:T(8,128)(2,1)} %collective-permute-done.14), channel_id=1, source_target_pairs={{0,4},{1,5},{2,6},{3,7},{8,0},{9,1},{10,2},{11,3},{16,8},{17,9},{1... | collective-permute-start | bytes 884744 | tf_op jit(solution)/shard_map/ppermute | solution.py:463
  90.6 25.2 %collective-permute-start.23 = (bf16[8,2,48,1536]{3,2,1,0:T(8,128)(2,1)S(1)}, bf16[8,2,48,1536]{3,2,1,0:T(8,128)(2,1)}, u32[]{:S(2)}, u32[]{:S(2)}) collective-permute-start(bf16[8,2,48,1536]{3,2,1,0:T(8,128)(2,1)S(1)} %fusion.refs_0_), channel_id=1, source_target_pairs={{0,1},{1,0},{2,3},{3,2},{4,5},{5,4},{6,7},{7,6},{8,9},{9,8},{10,11... | collective-permute-start | bytes 7077896 | tf_op jit(solution)/shard_map/ppermute | solution.py:470
  123.4 21.2 %collective-permute-start.24 = (bf16[256,1664]{1,0:T(8,128)(2,1)}, bf16[256,1664]{1,0:T(8,128)(2,1)S(1)}, u32[]{:S(2)}, u32[]{:S(2)}) collective-permute-start(bf16[256,1664]{1,0:T(8,128)(2,1)} %get-tuple-element.155.rows_a), channel_id=1, source_target_pairs={{0,2},{1,3},{2,0},{3,1},{4,6},{5,7},{6,4},{7,5},{8,10},{9,11},{10,... | collective-permute-start | bytes 2555912 | tf_op jit(solution)/shard_map/ppermute | solution.py:470
  147.9 38.6 %all-to-all-start = ((bf16[4,768,256]{2,1,0:T(8,128)(2,1)}), bf16[4,768,256]{2,1,0:T(8,128)(2,1)S(1)}, u32[]{:S(2)}, u32[]{:S(2)}) async-start(bf16[4,768,256]{2,1,0:T(8,128)(2,1)} %bitcast.73), calls=%async_computation | async-start | bytes 3145728 | tf_op jit(solution)/shard_map/all_to_all | solution.py:1037
  174.4 30.1 %collective-permute-start.29 = (bf16[320,768]{1,0:T(8,128)(2,1)}, bf16[320,768]{1,0:T(8,128)(2,1)}, u32[]{:S(2)}, u32[]{:S(2)}) collective-permute-start(bf16[320,768]{1,0:T(8,128)(2,1)} %get-tuple-element.168), channel_id=1, source_target_pairs={{0,8},{1,9},{2,10},{3,11},{8,16},{9,17},{10,18},{11,19},{16,24},{1... | collective-permute-start | bytes 1474568 | tf_op jit(solution)/shard_map/ppermute | solution.py:463
  176.2 28.3 %collective-permute-start.30 = (bf16[320,768]{1,0:T(8,128)(2,1)}, bf16[320,768]{1,0:T(8,128)(2,1)}, u32[]{:S(2)}, u32[]{:S(2)}) collective-permute-start(bf16[320,768]{1,0:T(8,128)(2,1)} %get-tuple-element.169), channel_id=1, source_target_pairs={{0,4},{1,5},{2,6},{3,7},{8,0},{9,1},{10,2},{11,3},{16,8},{17,9},{1... | collective-permute-start | bytes 1474568 | tf_op jit(solution)/shard_map/ppermute | solution.py:463
  184.4 44.4 %collective-permute-start.27 = (bf16[5,192,512]{2,1,0:T(8,128)(2,1)}, bf16[5,192,512]{2,1,0:T(8,128)(2,1)}, u32[]{:S(2)}, u32[]{:S(2)}) collective-permute-start(bf16[5,192,512]{2,1,0:T(8,128)(2,1)} %get-tuple-element.165), channel_id=1, source_target_pairs={{0,8},{1,9},{2,10},{3,11},{8,16},{9,17},{10,18},{11,19},{16,24},{1... | collective-permute-start | bytes 2949128 | tf_op jit(solution)/shard_map/ppermute | solution.py:463
  186.2 42.6 %collective-permute-start.28 = (bf16[5,192,512]{2,1,0:T(8,128)(2,1)}, bf16[5,192,512]{2,1,0:T(8,128)(2,1)}, u32[]{:S(2)}, u32[]{:S(2)}) collective-permute-start(bf16[5,192,512]{2,1,0:T(8,128)(2,1)} %get-tuple-element.166), channel_id=1, source_target_pairs={{0,4},{1,5},{2,6},{3,7},{8,0},{9,1},{10,2},{11,3},{16,8},{17,9},{1... | collective-permute-start | bytes 2949128 | tf_op jit(solution)/shard_map/ppermute | solution.py:463
  209.5 51.3 %collective-permute-start.34 = (bf16[320,768]{1,0:T(8,128)(2,1)}, bf16[320,768]{1,0:T(8,128)(2,1)}, u32[]{:S(2)}, u32[]{:S(2)}) collective-permute-start(bf16[320,768]{1,0:T(8,128)(2,1)} %get-tuple-element.177), channel_id=1, source_target_pairs={{0,8},{1,9},{2,10},{3,11},{8,16},{9,17},{10,18},{11,19},{16,24},{1... | collective-permute-start | bytes 1474568 | tf_op jit(solution)/shard_map/ppermute | solution.py:463
  211.4 49.4 %collective-permute-start.35 = (bf16[320,768]{1,0:T(8,128)(2,1)}, bf16[320,768]{1,0:T(8,128)(2,1)}, u32[]{:S(2)}, u32[]{:S(2)}) collective-permute-start(bf16[320,768]{1,0:T(8,128)(2,1)} %get-tuple-element.178), channel_id=1, source_target_pairs={{0,4},{1,5},{2,6},{3,7},{8,0},{9,1},{10,2},{11,3},{16,8},{17,9},{1... | collective-permute-start | bytes 1474568 | tf_op jit(solution)/shard_map/ppermute | solution.py:463
  236.7 43.4 %collective-permute-start.32 = (bf16[5,192,512]{2,1,0:T(8,128)(2,1)}, bf16[5,192,512]{2,1,0:T(8,128)(2,1)S(1)}, u32[]{:S(2)}, u32[]{:S(2)}) collective-permute-start(bf16[5,192,512]{2,1,0:T(8,128)(2,1)} %get-tuple-element.182), channel_id=1, source_target_pairs={{0,8},{1,9},{2,10},{3,11},{8,16},{9,17},{10,18},{11,19},{16,24},{1... | collective-permute-start | bytes 2949128 | tf_op jit(solution)/shard_map/ppermute | solution.py:463
  238.6 41.6 %collective-permute-start.33 = (bf16[5,192,512]{2,1,0:T(8,128)(2,1)}, bf16[5,192,512]{2,1,0:T(8,128)(2,1)}, u32[]{:S(2)}, u32[]{:S(2)}) collective-permute-start(bf16[5,192,512]{2,1,0:T(8,128)(2,1)} %get-tuple-element.183), channel_id=1, source_target_pairs={{0,4},{1,5},{2,6},{3,7},{8,0},{9,1},{10,2},{11,3},{16,8},{17,9},{1... | collective-permute-start | bytes 2949128 | tf_op jit(solution)/shard_map/ppermute | solution.py:463
  240.3 27.6 %all-to-all-start.1 = ((bf16[2,256,1664]{2,1,0:T(8,128)(2,1)}), bf16[2,256,1664]{2,1,0:T(8,128)(2,1)S(1)}, u32[]{:S(2)}, u32[]{:S(2)}) async-start(bf16[2,256,1664]{2,1,0:T(8,128)(2,1)} %reverse_select_fusion), calls=%async_computation.1 | async-start | bytes 3407872 | tf_op jit(solution)/shard_map/all_to_all | solution.py:467
  265.8 36.3 %collective-permute-start.38 = (bf16[320,768]{1,0:T(8,128)(2,1)}, bf16[320,768]{1,0:T(8,128)(2,1)S(1)}, u32[]{:S(2)}, u32[]{:S(2)}) collective-permute-start(bf16[320,768]{1,0:T(8,128)(2,1)} %get-tuple-element.187), channel_id=1, source_target_pairs={{0,8},{1,9},{2,10},{3,11},{8,16},{9,17},{10,18},{11,19},{16,24},{1... | collective-permute-start | bytes 1474568 | tf_op jit(solution)/shard_map/ppermute | solution.py:463
  267.7 34.5 %collective-permute-start.39 = (bf16[320,768]{1,0:T(8,128)(2,1)}, bf16[320,768]{1,0:T(8,128)(2,1)}, u32[]{:S(2)}, u32[]{:S(2)}) collective-permute-start(bf16[320,768]{1,0:T(8,128)(2,1)} %get-tuple-element.188), channel_id=1, source_target_pairs={{0,4},{1,5},{2,6},{3,7},{8,0},{9,1},{10,2},{11,3},{16,8},{17,9},{1... | collective-permute-start | bytes 1474568 | tf_op jit(solution)/shard_map/ppermute | solution.py:463
  276.4 33.5 %all-to-all-start.2 = ((bf16[2,272,1664]{2,1,0:T(8,128)(2,1)}), bf16[2,272,1664]{2,1,0:T(8,128)(2,1)S(1)}, u32[]{:S(2)}, u32[]{:S(2)}) async-start(bf16[2,272,1664]{2,1,0:T(8,128)(2,1)} %get-tuple-element.204), calls=%async_computation.2 | async-start | bytes 3620864 | tf_op jit(solution)/shard_map/all_to_all | solution.py:467
  289.0 26.0 %collective-permute-start.36 = (bf16[5,192,512]{2,1,0:T(8,128)(2,1)}, bf16[5,192,512]{2,1,0:T(8,128)(2,1)S(1)}, u32[]{:S(2)}, u32[]{:S(2)}) collective-permute-start(bf16[5,192,512]{2,1,0:T(8,128)(2,1)} %get-tuple-element.194), channel_id=1, source_target_pairs={{0,8},{1,9},{2,10},{3,11},{8,16},{9,17},{10,18},{11,19},{16,24},{1... | collective-permute-start | bytes 2949128 | tf_op jit(solution)/shard_map/ppermute | solution.py:463
  290.9 25.2 %collective-permute-start.37 = (bf16[5,192,512]{2,1,0:T(8,128)(2,1)}, bf16[5,192,512]{2,1,0:T(8,128)(2,1)}, u32[]{:S(2)}, u32[]{:S(2)}) collective-permute-start(bf16[5,192,512]{2,1,0:T(8,128)(2,1)} %get-tuple-element.195), channel_id=1, source_target_pairs={{0,4},{1,5},{2,6},{3,7},{8,0},{9,1},{10,2},{11,3},{16,8},{17,9},{1... | collective-permute-start | bytes 2949128 | tf_op jit(solution)/shard_map/ppermute | solution.py:463
  307.9 29.4 %collective-permute-start.43 = (bf16[320,768]{1,0:T(8,128)(2,1)}, bf16[320,768]{1,0:T(8,128)(2,1)S(1)}, u32[]{:S(2)}, u32[]{:S(2)}) collective-permute-start(bf16[320,768]{1,0:T(8,128)(2,1)} %get-tuple-element.202), channel_id=1, source_target_pairs={{0,8},{1,9},{2,10},{3,11},{8,16},{9,17},{10,18},{11,19},{16,24},{1... | collective-permute-start | bytes 1474568 | tf_op jit(solution)/shard_map/ppermute | solution.py:463
  309.7 27.6 %collective-permute-start.44 = (bf16[320,768]{1,0:T(8,128)(2,1)}, bf16[320,768]{1,0:T(8,128)(2,1)}, u32[]{:S(2)}, u32[]{:S(2)}) collective-permute-start(bf16[320,768]{1,0:T(8,128)(2,1)} %get-tuple-element.203), channel_id=1, source_target_pairs={{0,4},{1,5},{2,6},{3,7},{8,0},{9,1},{10,2},{11,3},{16,8},{17,9},{1... | collective-permute-start | bytes 1474568 | tf_op jit(solution)/shard_map/ppermute | solution.py:463
  310.0 34.2 %all-to-all-start.3 = ((bf16[2,256,2560]{2,1,0:T(8,128)(2,1)}), bf16[2,256,2560]{2,1,0:T(8,128)(2,1)}, u32[]{:S(2)}, u32[]{:S(2)}) async-start(bf16[2,256,2560]{2,1,0:T(8,128)(2,1)} %attend_back.1.grad_project), calls=%async_computation.3 | async-start | bytes 5242880 | tf_op jit(solution)/shard_map/all_to_all | solution.py:467
  315.0 184.9 %reduce-scatter.2.cloned.1.call-start = ((), (), s32[]{:S(2)}) async-start(), calls=%async_computation.7 | async-start | bytes 3649536 | tf_op jit(solution)/shard_map/reduce_scatter | solution.py:1089
  324.7 24.4 %collective-permute-start.41 = (bf16[5,192,512]{2,1,0:T(8,128)(2,1)}, bf16[5,192,512]{2,1,0:T(8,128)(2,1)S(1)}, u32[]{:S(2)}, u32[]{:S(2)}) collective-permute-start(bf16[5,192,512]{2,1,0:T(8,128)(2,1)} %get-tuple-element.210), channel_id=1, source_target_pairs={{0,8},{1,9},{2,10},{3,11},{8,16},{9,17},{10,18},{11,19},{16,24},{1... | collective-permute-start | bytes 2949128 | tf_op jit(solution)/shard_map/ppermute | solution.py:463
  326.7 24.3 %collective-permute-start.42 = (bf16[5,192,512]{2,1,0:T(8,128)(2,1)}, bf16[5,192,512]{2,1,0:T(8,128)(2,1)S(1)}, u32[]{:S(2)}, u32[]{:S(2)}) collective-permute-start(bf16[5,192,512]{2,1,0:T(8,128)(2,1)} %get-tuple-element.211), channel_id=1, source_target_pairs={{0,4},{1,5},{2,6},{3,7},{8,0},{9,1},{10,2},{11,3},{16,8},{17,9},{1... | collective-permute-start | bytes 2949128 | tf_op jit(solution)/shard_map/ppermute | solution.py:463
  351.0 19.4 %collective-permute-start.48 = (bf16[320,768]{1,0:T(8,128)(2,1)}, bf16[320,768]{1,0:T(8,128)(2,1)S(1)}, u32[]{:S(2)}, u32[]{:S(2)}) collective-permute-start(bf16[320,768]{1,0:T(8,128)(2,1)} %get-tuple-element.215), channel_id=1, source_target_pairs={{0,8},{1,9},{2,10},{3,11},{8,16},{9,17},{10,18},{11,19},{16,24},{1... | collective-permute-start | bytes 1474568 | tf_op jit(solution)/shard_map/ppermute | solution.py:463
  352.5 17.9 %collective-permute-start.49 = (bf16[320,768]{1,0:T(8,128)(2,1)}, bf16[320,768]{1,0:T(8,128)(2,1)S(1)}, u32[]{:S(2)}, u32[]{:S(2)}) collective-permute-start(bf16[320,768]{1,0:T(8,128)(2,1)} %get-tuple-element.216), channel_id=1, source_target_pairs={{0,4},{1,5},{2,6},{3,7},{8,0},{9,1},{10,2},{11,3},{16,8},{17,9},{1... | collective-permute-start | bytes 1474568 | tf_op jit(solution)/shard_map/ppermute | solution.py:463
  361.0 25.3 %collective-permute-start.46 = (bf16[5,192,512]{2,1,0:T(8,128)(2,1)}, bf16[5,192,512]{2,1,0:T(8,128)(2,1)S(1)}, u32[]{:S(2)}, u32[]{:S(2)}) collective-permute-start(bf16[5,192,512]{2,1,0:T(8,128)(2,1)} %get-tuple-element.222), channel_id=1, source_target_pairs={{0,8},{1,9},{2,10},{3,11},{8,16},{9,17},{10,18},{11,19},{16,24},{1... | collective-permute-start | bytes 2949128 | tf_op jit(solution)/shard_map/ppermute | solution.py:463
  362.5 25.3 %collective-permute-start.47 = (bf16[5,192,512]{2,1,0:T(8,128)(2,1)}, bf16[5,192,512]{2,1,0:T(8,128)(2,1)S(1)}, u32[]{:S(2)}, u32[]{:S(2)}) collective-permute-start(bf16[5,192,512]{2,1,0:T(8,128)(2,1)} %get-tuple-element.223), channel_id=1, source_target_pairs={{0,4},{1,5},{2,6},{3,7},{8,0},{9,1},{10,2},{11,3},{16,8},{17,9},{1... | collective-permute-start | bytes 2949128 | tf_op jit(solution)/shard_map/ppermute | solution.py:463
  376.9 28.9 %collective-permute-start.52 = (bf16[320,768]{1,0:T(8,128)(2,1)}, bf16[320,768]{1,0:T(8,128)(2,1)S(1)}, u32[]{:S(2)}, u32[]{:S(2)}) collective-permute-start(bf16[320,768]{1,0:T(8,128)(2,1)} %get-tuple-element.227), channel_id=1, source_target_pairs={{0,8},{1,9},{2,10},{3,11},{8,16},{9,17},{10,18},{11,19},{16,24},{1... | collective-permute-start | bytes 1474568 | tf_op jit(solution)/shard_map/ppermute | solution.py:463
  378.4 33.0 %collective-permute-start.53 = (bf16[320,768]{1,0:T(8,128)(2,1)}, bf16[320,768]{1,0:T(8,128)(2,1)S(1)}, u32[]{:S(2)}, u32[]{:S(2)}) collective-permute-start(bf16[320,768]{1,0:T(8,128)(2,1)} %get-tuple-element.228), channel_id=1, source_target_pairs={{0,4},{1,5},{2,6},{3,7},{8,0},{9,1},{10,2},{11,3},{16,8},{17,9},{1... | collective-permute-start | bytes 1474568 | tf_op jit(solution)/shard_map/ppermute | solution.py:463
  396.7 46.4 %collective-permute-start.50 = (bf16[5,192,512]{2,1,0:T(8,128)(2,1)}, bf16[5,192,512]{2,1,0:T(8,128)(2,1)}, u32[]{:S(2)}, u32[]{:S(2)}) collective-permute-start(bf16[5,192,512]{2,1,0:T(8,128)(2,1)} %get-tuple-element.231), channel_id=1, source_target_pairs={{0,8},{1,9},{2,10},{3,11},{8,16},{9,17},{10,18},{11,19},{16,24},{1... | collective-permute-start | bytes 2949128 | tf_op jit(solution)/shard_map/ppermute | solution.py:463
  398.1 47.5 %collective-permute-start.51 = (bf16[5,192,512]{2,1,0:T(8,128)(2,1)}, bf16[5,192,512]{2,1,0:T(8,128)(2,1)}, u32[]{:S(2)}, u32[]{:S(2)}) collective-permute-start(bf16[5,192,512]{2,1,0:T(8,128)(2,1)} %get-tuple-element.232), channel_id=1, source_target_pairs={{0,4},{1,5},{2,6},{3,7},{8,0},{9,1},{10,2},{11,3},{16,8},{17,9},{1... | collective-permute-start | bytes 2949128 | tf_op jit(solution)/shard_map/ppermute | solution.py:463
  417.3 48.4 %collective-permute-start.56 = (bf16[320,768]{1,0:T(8,128)(2,1)}, bf16[320,768]{1,0:T(8,128)(2,1)}, u32[]{:S(2)}, u32[]{:S(2)}) collective-permute-start(bf16[320,768]{1,0:T(8,128)(2,1)} %get-tuple-element.236), channel_id=1, source_target_pairs={{0,8},{1,9},{2,10},{3,11},{8,16},{9,17},{10,18},{11,19},{16,24},{1... | collective-permute-start | bytes 1474568 | tf_op jit(solution)/shard_map/ppermute | solution.py:463
  417.4 48.4 %collective-permute-start.57 = (bf16[320,768]{1,0:T(8,128)(2,1)}, bf16[320,768]{1,0:T(8,128)(2,1)}, u32[]{:S(2)}, u32[]{:S(2)}) collective-permute-start(bf16[320,768]{1,0:T(8,128)(2,1)} %get-tuple-element.237), channel_id=1, source_target_pairs={{0,4},{1,5},{2,6},{3,7},{8,0},{9,1},{10,2},{11,3},{16,8},{17,9},{1... | collective-permute-start | bytes 1474568 | tf_op jit(solution)/shard_map/ppermute | solution.py:463
  419.4 54.6 %all-to-all-start.4 = ((bf16[4,256,1536]{2,1,0:T(8,128)(2,1)}), bf16[4,256,1536]{2,1,0:T(8,128)(2,1)S(1)}, u32[]{:S(2)}, u32[]{:S(2)}) async-start(bf16[4,256,1536]{2,1,0:T(8,128)(2,1)} %bitcast.79), calls=%async_computation.4 | async-start | bytes 6291456 | tf_op jit(solution)/shard_map/all_to_all | solution.py:1091
  453.6 34.7 %collective-permute-start.54 = (bf16[5,192,512]{2,1,0:T(8,128)(2,1)}, bf16[5,192,512]{2,1,0:T(8,128)(2,1)}, u32[]{:S(2)}, u32[]{:S(2)}) collective-permute-start(bf16[5,192,512]{2,1,0:T(8,128)(2,1)} %get-tuple-element.240), channel_id=1, source_target_pairs={{0,8},{1,9},{2,10},{3,11},{8,16},{9,17},{10,18},{11,19},{16,24},{1... | collective-permute-start | bytes 2949128 | tf_op jit(solution)/shard_map/ppermute | solution.py:463
  455.0 35.8 %collective-permute-start.55 = (bf16[5,192,512]{2,1,0:T(8,128)(2,1)}, bf16[5,192,512]{2,1,0:T(8,128)(2,1)}, u32[]{:S(2)}, u32[]{:S(2)}) collective-permute-start(bf16[5,192,512]{2,1,0:T(8,128)(2,1)} %get-tuple-element.241), channel_id=1, source_target_pairs={{0,4},{1,5},{2,6},{3,7},{8,0},{9,1},{10,2},{11,3},{16,8},{17,9},{1... | collective-permute-start | bytes 2949128 | tf_op jit(solution)/shard_map/ppermute | solution.py:463
  (65 other events, 398.4 us)
Sparse Core Ops, SparseCore 0:
  9.6 34.3 all-gather.1
  379.2 109.6 reduce-scatter.1

commit v5 on v4

--- a/solution.py
+++ b/solution.py
@@ -234,7 +234,7 @@
     refs = refs[1:]
     left, weight = refs[:blocks], refs[blocks]
     extra = refs[blocks + 1 : 2 * blocks + 1] if extra_given else None
-    out, total = refs[-2:]
+    outs, total = refs[-1 - (2 if extra_given else 1) : -1], refs[-1]
     expert = pl.program_id(0)
     count = left[0].shape[1]
     width = total.shape[1]
@@ -251,10 +251,12 @@
 
     @pl.when(expert == pl.num_programs(0) - 1)
     def _():
-        out[:, :width] = total[...].astype(BF16)
-        if extra_given:
-            for i in range(blocks):
-                out[i * count : (i + 1) * count, width:] = extra[i][...].astype(BF16)
+        each = blocks // len(outs)
+        for i in range(blocks):
+            out, at = outs[i // each], slice(i % each * count, (i % each + 1) * count)
+            out[at, :width] = total[i * count : (i + 1) * count].astype(BF16)
+            if extra_given:
+                out[at, width:] = extra[i][...].astype(BF16)
 
 
 def owner_rows(devices, left, weight, extra=None):
@@ -263,7 +265,8 @@
     width = weight.shape[1] if extra is not None else weight.shape[2]
     columns = width if extra is None else width + LANES
     count = rows // 4
-    out_shape = jax.ShapeDtypeStruct((blocks * count, columns), BF16)
+    parts = 1 if extra is None else 2
+    out_shape = [jax.ShapeDtypeStruct((blocks // parts * count, columns), BF16)] * parts
     piece = lambda k: pl.BlockSpec((1, count, inner), lambda i, d: (i, d[k], 0))
     in_specs = [piece(k) for k in range(blocks)]
     in_specs.append(pl.BlockSpec((1,) + weight.shape[1:], lambda i, d: (i, 0, 0)))
@@ -279,7 +282,7 @@
             num_scalar_prefetch=1,
             grid=(local,),
             in_specs=in_specs,
-            out_specs=pl.BlockSpec(out_shape.shape, lambda i, d: (0, 0)),
+            out_specs=[pl.BlockSpec(o.shape, lambda i, d: (0, 0)) for o in out_shape],
             scratch_shapes=[pltpu.VMEM((blocks * count, width), F32)],
         ),
         compiler_params=pltpu.CompilerParams(vmem_limit_bytes=58 * 2**20),
@@ -1030,23 +1033,25 @@
     def devices(*bits):
         return jnp.stack([net.e ^ bit for bit in bits])
 
-    sent_out = ring_out(0)
-    sent_in = ring_in(0, sent_out)
+    sent_in = ring_in(0)
+    sent_out = ring_out(0, sent_in)
     block = width // net.devices
     lefts = turned_both.reshape(2, net.nd, net.ne, block, length).transpose(2, 0, 1, 3, 4)
     lefts = lax.all_to_all(
         lefts.reshape(net.ne, -1, length), "expert", 0, 0, tiled=True
     )
-    beside = owner_rows(devices(1, 3), after(grad_pre, sent_in, lefts), expert_in, gate_grads)
+    beside, kept = owner_rows(
+        devices(1, 3, 0, 2), after(grad_pre, sent_out, lefts), expert_in, gate_grads
+    )
     beside_came = net.swap(beside, CORE)
-    sent_out = ring_out(1, beside, beside=beside_came)
-    kept = owner_rows(devices(0, 2), after(grad_pre, sent_out), expert_in, gate_grads)
-    both = (kept.astype(F32) + beside_came.astype(F32)).astype(BF16)
+    sent_in = ring_in(1, kept, beside=beside_came)
+    both = (kept.astype(F32) + after(beside_came, sent_in).astype(F32)).astype(BF16)
     both = both.reshape(2, length, -1)
-    came = net.exchange(jnp.where(wide == 0, both, both[::-1]), 1)
-    sent_in = ring_in(1, both)
-    mix = owner_rows(jnp.arange(4), after(activated, sent_in), expert_out)
-    sent_out = ring_out(2, mix)
+    both = jnp.where(wide == 0, both, both[::-1])
+    came = net.exchange(both, 1)
+    sent_out = ring_out(1, both)
+    (mix,) = owner_rows(jnp.arange(4), after(activated, sent_out), expert_out)
+    sent_out = mix
     grad_hidden, pack, grad_mixed = middle(
         experts_all,
         gain_row + 1,
@@ -1060,8 +1065,9 @@
     )
     packs = net.exchange(pack, 1)
     sent_in = ring_in(2, grad_mixed)
+    sent_out = ring_out(2, sent_in)
     grad_project = attend_back(
-        queries, key_rows, values, after(grad_mixed, sent_in), bias, cos, sin
+        queries, key_rows, values, after(grad_mixed, sent_out), bias, cos, sin
     )
     projects = net.exchange(grad_project, 1)
     sent_out = ring_out(3, grad_project)

time: 516 us -> 513 us (level)
    pallas_call x3 -> x2, Pallas kernels: 46.8 us -> 42.5 us  [owner_rows(): pl.pallas_call(functools.partial(owner_rows_kernel, extra is not None, bl...]
    unnamed x107 -> x113, local copies, waits for them, and re-layouts: 20.1 us -> 21.8 us
  transfers between devices with their start and end apart: 65 -> 65, of which waited for: 26 -> 28; matrix products, arithmetic and copies ran while one was open for 6% -> 6% of each run, Pallas kernels for 50% -> 49%
where the time goes in v5:
time: 513 us; the launch traced here: 508 us
  Pallas kernels  260 us (51%)
  waiting for transfers between devices  113 us (22%)
  starting transfers between devices  73.5 us (14%)
  local copies, waits for them, and re-layouts  31.4 us (6%)
  other arithmetic  15.5 us (3%)
  between operations  15.2 us (3%)
    ppermute x44, waiting for transfers between devices, step(): return lax.ppermute(value, AXES, self.ring[way])  97.1 us
    pallas_call x8, Pallas kernels, in_share(): pl.pallas_call(functools.partial(in_kernel, int(last), step), out_shape=o...  65.4 us
    ppermute x44, starting transfers between devices, step(): return lax.ppermute(value, AXES, self.ring[way])  46.5 us
    pallas_call x2, Pallas kernels, owner_rows(): pl.pallas_call(functools.partial(owner_rows_kernel, extra is not None, bl...  42.5 us
    pallas_call x8, Pallas kernels, out_share(): pl.pallas_call(functools.partial(out_kernel, step), out_shape=[jax.ShapeD...  40.1 us
    pallas_call x2, Pallas kernels, expert_half(): pl.pallas_call(functools.partial(expert_kernel, bool(earlier)), out_shape...  34 us
    unnamed x113, local copies, waits for them, and re-layouts  21.8 us
    ppermute x14, waiting for transfers between devices, swap(): lax.ppermute(value, AXES, [(d, d ^ bit) for d in range(self.devices)])  14.5 us
  transfers between devices with their start and end apart: 65, of which 28 were waited for; matrix products, arithmetic and copies ran while one was open for 6% of the time, Pallas kernels for 49%

profile of v5, /device:TPU:0, one launch (start us, length us, event | category | flops | bytes accessed | tf_op | source)
XLA Modules:
  0.0 508.3 jit_solution(13510373814195386520)
XLA Ops:
  11.3 3.0 collective-permute-start
  14.3 6.2 %collective-permute-done = bf16[48,2688]{1,0:T(8,128)(2,1)S(1)} collective-permute-done((bf16[48,2688]{1,0:T(8,128)(2,1)S(1)}, bf16[48,2688]{1,0:T(8,128)(2,1)S(1)}, u32[]{:S(2)}, u32[]{:S(2)}) %collective-permute-start) | collective-permute-done | bytes 258080 | tf_op jit(solution)/shard_map/ppermute | solution.py:473
  25.2 4.7 collective-permute-done.4
  32.1 5.8 %collective-permute-done.2 = bf16[2,48,2688]{2,1,0:T(8,128)(2,1)S(1)} collective-permute-done((bf16[2,48,2688]{2,1,0:T(8,128)(2,1)S(1)}, bf16[2,48,2688]{2,1,0:T(8,128)(2,1)S(1)}, u32[]{:S(2)}, u32[]{:S(2)}) %collective-permute-start.2) | collective-permute-done | bytes 516128 | tf_op jit(solution)/shard_map/ppermute | solution.py:466
  49.9 12.6 %owner_grads.1.grad_plain = bf16[5,1024,512]{2,1,0:T(8,128)(2,1)} custom-call(bf16[1024,1536]{1,0:T(8,128)(2,1)} %all-gather.2.cloned.1.call-done.upstream, bf16[5,512,1536]{2,1,0:T(8,128)(2,1)} %refs_5_.3), custom_call_target="tpu_custom_call" | custom-call | flops 8053063680 | bytes 16777216 | tf_op jit(solution)/shard_map/owner_grads/pallas_call | solution.py:809
  68.6 6.1 %collective-permute-done.10 = bf16[2,48,2688]{2,1,0:T(8,128)(2,1)S(1)} collective-permute-done((bf16[2,48,2688]{2,1,0:T(8,128)(2,1)}, bf16[2,48,2688]{2,1,0:T(8,128)(2,1)S(1)}, u32[]{:S(2)}, u32[]{:S(2)}) %collective-permute-start.10) | collective-permute-done | bytes 516128 | tf_op jit(solution)/shard_map/ppermute | solution.py:466
  75.2 6.2 %collective-permute-done.18 = bf16[2,48,1536]{2,1,0:T(8,128)(2,1)S(1)} collective-permute-done((bf16[2,48,1536]{2,1,0:T(8,128)(2,1)}, bf16[2,48,1536]{2,1,0:T(8,128)(2,1)S(1)}, u32[]{:S(2)}, u32[]{:S(2)}) %collective-permute-start.18) | collective-permute-done | bytes 294944 | tf_op jit(solution)/shard_map/ppermute | solution.py:466
  85.8 4.1 collective-permute-done.16
  102.5 13.3 %attend.1 = (bf16[256,1536]{1,0:T(8,128)(2,1)}, bf16[3072,256]{1,0:T(8,128)(2,1)}, bf16[256,1536]{1,0:T(8,128)(2,1)}, bf16[256,512]{1,0:T(8,128)(2,1)}, bf16[256...) custom-call(s32[32]{0:T(128)} %stack.285.numbers, ...), custom_call_target="tpu_custom_call" | custom-call | flops 1024 | bytes 1024 | tf_op jit(solution)/shard_map/attend/pallas_call | solution.py:181
  115.8 7.2 %branch.1 = (f32[256,1536]{1,0:T(8,128)}, bf16[256,1664]{1,0:T(8,128)(2,1)}, f32[256,128]{1,0:T(8,128)}) custom-call(s32[32]{0:T(128)} %stack.284.numbers, bf16[256,1536]{1,0:T(8,128)(2,1)} %tokens.5, bf16[256,1536]{1,0:T(8,128)(2,1)} %get-tuple-element.151.mixed, bf16[1536,128]{1,0:T(8,128)(2,1)} %get-tuple-element.152.small, ...), custom_call_target="tpu_custom_call" | custom-call | flops 1024 | bytes 1024 | tf_op jit(solution)/shard_map/branch/pallas_call | solution.py:219
  126.6 17.0 %expert_half.2 = (bf16[5,1024,512]{2,1,0:T(8,128)(2,1)}, bf16[5,512,1024]{2,1,0:T(8,128)(2,1)}, bf16[5,1024,1024]{2,1,0:T(8,128)(2,1)}, f32[1024,128]{1,0:T(8,128)}, bf16[1536,1024]{1,0:T(8,128)(2,1)}) custom-call(s32[2,3]{1,0:T(2,128)} %reshape.76.both_scalars, bf16[256,1664]{1,0:T(8,128)(2,1)} %get-tuple-element.157.rows_a, bf16[256,1664]{1,0:T(8,128)(2,1)} %copy-done.43, ...), custom_call_target="tpu_custom_call" | custom-call | flops 8053063680 | bytes 31457280 | tf_op jit(solution)/shard_map/expert_half/pallas_call | solution.py:923
  147.4 3.6 all-to-all-start
  151.9 17.0 %expert_half.3 = (bf16[5,1024,512]{2,1,0:T(8,128)(2,1)}, bf16[5,512,1024]{2,1,0:T(8,128)(2,1)}, bf16[5,1024,1024]{2,1,0:T(8,128)(2,1)}, f32[1024,128]{1,0:T(8,128)}, bf16[1536,1024]{1,0:T(8,128)(2,1)}) custom-call(s32[2,3]{1,0:T(2,128)} %reshape.76.both_scalars, ...), custom_call_target="tpu_custom_call", output_to_operand_aliasing={{0}: (5, {}), {1}: (6, {}), {2}: (7, {}), {3}: (8, {}), {4}... | custom-call | flops 8053063680 | bytes 31457280 | tf_op jit(solution)/shard_map/expert_half/pallas_call | solution.py:923
  168.9 8.0 %in_share.8 = (bf16[5,192,512]{2,1,0:T(8,128)(2,1)}, bf16[5,192,512]{2,1,0:T(8,128)(2,1)}) custom-call(s32[8,2]{1,0:T(8,128)} %select_select_fusion.places, bf16[1536,1024]{1,0:T(8,128)(2,1)} %get-tuple-element.174.turned_rows, bf16[5,1024,1024]{2,1,0:T(8,128)(2,1)} %get-tuple-element.170.refs_1_.refs_2_.refs_3_.refs_4_.grad_pre), custom_call_target="tpu_custom_call" | custom-call | flops 30000001024 | bytes 1024 | tf_op jit(solution)/shard_map/in_share/pallas_call | solution.py:724
  178.9 4.9 out_share.8
  185.9 26.1 %owner_rows.2 = (bf16[512,1664]{1,0:T(8,128)(2,1)}, bf16[512,1664]{1,0:T(8,128)(2,1)}) custom-call(s32[4]{0:T(128)} %pad_add_fusion.1.refs_0_, bf16[5,1024,1024]{2,1,0:T(8,128)(2,1)} %get-tuple-element.170.refs_1_.refs_2_.refs_3_.refs_4_.grad_pre, bf16[5,1024,1024]{2,1,0:T(8,128)(2,1)} %get-tuple-element.170.refs_1_.refs_2_.refs_3_.refs_4_.grad_pre, ...), custom_call_target="tpu_custom_call" | custom-call | flops 1024 | bytes 1024 | tf_op jit(solution)/shard_map/owner_rows/pallas_call | solution.py:278
  213.1 8.0 %in_share.9 = (bf16[5,192,512]{2,1,0:T(8,128)(2,1)}, bf16[5,192,512]{2,1,0:T(8,128)(2,1)}) custom-call(s32[8,2]{1,0:T(8,128)} %select_select_fusion.places, bf16[1536,1024]{1,0:T(8,128)(2,1)} %get-tuple-element.174.turned_rows, bf16[5,1024,1024]{2,1,0:T(8,128)(2,1)} %get-tuple-element.170.refs_1_.refs_2_.refs_3_.refs_4_.grad_pre, ...), custom_call_target="tpu_custom_call" | custom-call | flops 30000001024 | bytes 1024 | tf_op jit(solution)/shard_map/in_share/pallas_call | solution.py:724
  225.5 3.7 all-to-all-start.1
  229.3 5.0 out_share.9
  236.8 16.3 %owner_rows.3 = bf16[1024,1536]{1,0:T(8,128)(2,1)} custom-call(s32[4]{0:T(128)} %iota.45.refs_0_, bf16[5,1024,512]{2,1,0:T(8,128)(2,1)} %get-tuple-element.188.refs_1_.refs_2_.refs_3_.refs_4_, bf16[5,1024,512]{2,1,0:T(8,128)(2,1)} %get-tuple-element.188.refs_1_.refs_2_.refs_3_.refs_4_, ...), custom_call_target="tpu_custom_call" | custom-call | flops 1024 | bytes 1024 | tf_op jit(solution)/shard_map/owner_rows/pallas_call | solution.py:278
  254.4 7.3 %middle.1 = (f32[256,1536]{1,0:T(8,128)}, bf16[2,272,1664]{2,1,0:T(8,128)(2,1)}, bf16[256,1536]{1,0:T(8,128)(2,1)}) custom-call(s32[32]{0:T(128)} %stack.284.numbers, bf16[2,256,1664]{2,1,0:T(8,128)(2,1)} %copy-done.9, bf16[256,1536]{1,0:T(8,128)(2,1)} %cotangent.1, f32[256,1536]{1,0:T(8,128)} %get-tuple-element.156.hidden, ...), custom_call_target="tpu_custom_call" | custom-call | flops 1024 | bytes 1024 | tf_op jit(solution)/shard_map/middle/pallas_call | solution.py:407
  262.7 7.9 %in_share.10 = (bf16[5,192,512]{2,1,0:T(8,128)(2,1)}, bf16[5,192,512]{2,1,0:T(8,128)(2,1)}) custom-call(s32[8,2]{1,0:T(8,128)} %select_select_fusion.places, bf16[1536,1024]{1,0:T(8,128)(2,1)} %get-tuple-element.174.turned_rows, bf16[5,1024,1024]{2,1,0:T(8,128)(2,1)} %get-tuple-element.170.refs_1_.refs_2_.refs_3_.refs_4_.grad_pre, ...), custom_call_target="tpu_custom_call" | custom-call | flops 30000001024 | bytes 1024 | tf_op jit(solution)/shard_map/in_share/pallas_call | solution.py:724
  271.4 5.0 out_share.10
  281.3 3.7 all-to-all-start.2
  287.2 10.8 %attend_back.1.grad_project = bf16[2,256,2560]{2,1,0:T(8,128)(2,1)} custom-call(bf16[256,1536]{1,0:T(8,128)(2,1)} %get-tuple-element.200.queries, bf16[256,512]{1,0:T(8,128)(2,1)} %get-tuple-element.201.key_rows, bf16[256,512]{1,0:T(8,128)(2,1)} %get-tuple-element.202.values, bf16[256,1536]{1,0:T(8,128)(2,1)} %get-tuple-element.203.grad_mixed, ...), custom_call_target="tpu_custom_call" | custom-call | flops 1024 | bytes 1024 | tf_op jit(solution)/shard_map/attend_back/pallas_call | solution.py:377
  298.8 5.0 out_share.11
  306.4 5.0 all-to-all-start.3
  313.7 8.5 %in_share.11 = (bf16[5,192,512]{2,1,0:T(8,128)(2,1)}, bf16[5,192,512]{2,1,0:T(8,128)(2,1)}) custom-call(s32[8,2]{1,0:T(8,128)} %select_select_fusion.places, bf16[1536,1024]{1,0:T(8,128)(2,1)} %get-tuple-element.174.turned_rows, bf16[5,1024,1024]{2,1,0:T(8,128)(2,1)} %get-tuple-element.170.refs_1_.refs_2_.refs_3_.refs_4_.grad_pre, ...), custom_call_target="tpu_custom_call" | custom-call | flops 30000001024 | bytes 1024 | tf_op jit(solution)/shard_map/in_share/pallas_call | solution.py:724
  324.6 3.2 gain_column.1
  329.4 5.5 %weight_products.2.earlier = bf16[384,1664]{1,0:T(8,128)(2,1)} custom-call(s32[1]{0:T(128)} %bitcast.69.place, bf16[4,768,256]{2,1,0:T(8,128)(2,1)} %copy-done.3, bf16[4,384,256]{2,1,0:T(8,128)(2,1)} %bitcast.113, f32[384,128]{1,0:T(8,128)} %bitcast.119, bf16[2,272,1664]{2,1,0:T(8,128)(2,1)} %copy-done.2, bf16[2,272,1664]{2,1,0:T(8,128)(2,1)} %copy-done.8), custom_call_target="tpu_custom_call" | custom-call | flops 1024 | bytes 1024 | tf_op jit(solution)/shard_map/weight_products/pallas_call | solution.py:565
  335.6 5.0 out_share.12
  340.8 5.9 %collective-permute-done.41.refs_0_ = bf16[5,192,512]{2,1,0:T(8,128)(2,1)S(1)} collective-permute-done((bf16[5,192,512]{2,1,0:T(8,128)(2,1)}, bf16[5,192,512]{2,1,0:T(8,128)(2,1)S(1)}, u32[]{:S(2)}, u32[]{:S(2)}) %collective-permute-start.41) | collective-permute-done | bytes 983072 | tf_op jit(solution)/shard_map/ppermute | solution.py:466
  350.6 7.9 %in_share.12 = (bf16[5,192,512]{2,1,0:T(8,128)(2,1)}, bf16[5,192,512]{2,1,0:T(8,128)(2,1)}) custom-call(s32[8,2]{1,0:T(8,128)} %select_select_fusion.places, bf16[1536,1024]{1,0:T(8,128)(2,1)} %get-tuple-element.174.turned_rows, bf16[5,1024,1024]{2,1,0:T(8,128)(2,1)} %get-tuple-element.170.refs_1_.refs_2_.refs_3_.refs_4_.grad_pre, ...), custom_call_target="tpu_custom_call" | custom-call | flops 10000000000 | bytes 1024 | tf_op jit(solution)/shard_map/in_share/pallas_call | solution.py:724
  360.6 7.4 %weight_products.3 = bf16[384,4224]{1,0:T(8,128)(2,1)} custom-call(s32[1]{0:T(128)} %bitcast.69.place, bf16[4,768,256]{2,1,0:T(8,128)(2,1)} %copy-done.3, bf16[384,1664]{1,0:T(8,128)(2,1)} %weight_products.2.earlier, bf16[2,256,2560]{2,1,0:T(8,128)(2,1)} %all-to-all-done.3.own, bf16[2,256,2560]{2,1,0:T(8,128)(2,1)} %copy-done.15), custom_call_target="tpu_custom_call" | custom-call | flops 1024 | bytes 1024 | tf_op jit(solution)/shard_map/weight_products/pallas_call | solution.py:565
  369.5 5.0 out_share.13
  376.6 7.2 %collective-permute-done.46.refs_0_ = bf16[5,192,512]{2,1,0:T(8,128)(2,1)S(1)} collective-permute-done((bf16[5,192,512]{2,1,0:T(8,128)(2,1)}, bf16[5,192,512]{2,1,0:T(8,128)(2,1)S(1)}, u32[]{:S(2)}, u32[]{:S(2)}) %collective-permute-start.46) | collective-permute-done | bytes 983072 | tf_op jit(solution)/shard_map/ppermute | solution.py:466
  386.3 7.9 %in_share.13 = (bf16[5,192,512]{2,1,0:T(8,128)(2,1)}, bf16[5,192,512]{2,1,0:T(8,128)(2,1)}) custom-call(s32[8,2]{1,0:T(8,128)} %select_select_fusion.places, bf16[1536,1024]{1,0:T(8,128)(2,1)} %get-tuple-element.174.turned_rows, bf16[5,1024,1024]{2,1,0:T(8,128)(2,1)} %get-tuple-element.170.refs_1_.refs_2_.refs_3_.refs_4_.grad_pre, ...), custom_call_target="tpu_custom_call" | custom-call | flops 30000001024 | bytes 1024 | tf_op jit(solution)/shard_map/in_share/pallas_call | solution.py:724
  396.4 7.3 %collective-permute-done.52.refs_0_ = bf16[320,768]{1,0:T(8,128)(2,1)S(1)} collective-permute-done((bf16[320,768]{1,0:T(8,128)(2,1)}, bf16[320,768]{1,0:T(8,128)(2,1)S(1)}, u32[]{:S(2)}, u32[]{:S(2)}) %collective-permute-start.52) | collective-permute-done | bytes 491552 | tf_op jit(solution)/shard_map/ppermute | solution.py:466
  403.6 5.7 %collective-permute-done.53.refs_1_ = bf16[320,768]{1,0:T(8,128)(2,1)S(1)} collective-permute-done((bf16[320,768]{1,0:T(8,128)(2,1)}, bf16[320,768]{1,0:T(8,128)(2,1)S(1)}, u32[]{:S(2)}, u32[]{:S(2)}) %collective-permute-start.53) | collective-permute-done | bytes 491552 | tf_op jit(solution)/shard_map/ppermute | solution.py:466
  410.1 5.0 out_share.14
  417.2 3.7 all-to-all-start.4
  420.9 19.7 %collective-permute-done.50.refs_0_ = bf16[5,192,512]{2,1,0:T(8,128)(2,1)} collective-permute-done((bf16[5,192,512]{2,1,0:T(8,128)(2,1)}, bf16[5,192,512]{2,1,0:T(8,128)(2,1)}, u32[]{:S(2)}, u32[]{:S(2)}) %collective-permute-start.50) | collective-permute-done | bytes 983072 | tf_op jit(solution)/shard_map/ppermute | solution.py:466
  443.2 8.0 %in_share.14 = (bf16[5,192,512]{2,1,0:T(8,128)(2,1)}, bf16[5,192,512]{2,1,0:T(8,128)(2,1)}) custom-call(s32[8,2]{1,0:T(8,128)} %select_select_fusion.places, bf16[1536,1024]{1,0:T(8,128)(2,1)} %get-tuple-element.174.turned_rows, bf16[5,1024,1024]{2,1,0:T(8,128)(2,1)} %get-tuple-element.170.refs_1_.refs_2_.refs_3_.refs_4_.grad_pre, ...), custom_call_target="tpu_custom_call" | custom-call | flops 30000001024 | bytes 1024 | tf_op jit(solution)/shard_map/in_share/pallas_call | solution.py:724
  453.4 9.8 %input_back.1 = f32[256,1536]{1,0:T(8,128)} custom-call(s32[32]{0:T(128)} %stack.285.numbers, bf16[256,1536]{1,0:T(8,128)(2,1)} %tokens.5, bf16[2,256,2560]{2,1,0:T(8,128)(2,1)} %attend_back.1.grad_project, f32[16,1536]{1,0:T(8,128)} %get-tuple-element.153.gains, f32[256,1536]{1,0:T(8,128)} %get-tuple-element.247.grad_hidden, ...), custom_call_target="tpu_custom_call" | custom-call | flops 1024 | bytes 1024 | tf_op jit(solution)/shard_map/input_back/pallas_call | solution.py:425
  463.3 5.2 %out_share.15 = (f32[320,768]{1,0:T(8,128)}, f32[320,768]{1,0:T(8,128)}) custom-call(s32[8,2]{1,0:T(8,128)} %select_select_fusion.places, bf16[5,512,1024]{2,1,0:T(8,128)(2,1)} %get-tuple-element.165.turned_act, bf16[1024,1536]{1,0:T(8,128)(2,1)} %all-gather.2.cloned.1.call-done.upstream, bf16[320,768]{1,0:T(8,128)(2,1)} %collective-permute-done.56.refs_0_, ...), custom_call_target="tpu_custom_call" | custom-call | flops 30000001024 | bytes 1024 | tf_op jit(solution)/shard_map/out_share/pallas_call | solution.py:784
  468.4 3.0 pad_maximum_fusion
  473.9 11.8 %collective-permute-done.54.refs_0_ = bf16[5,192,512]{2,1,0:T(8,128)(2,1)} collective-permute-done((bf16[5,192,512]{2,1,0:T(8,128)(2,1)}, bf16[5,192,512]{2,1,0:T(8,128)(2,1)}, u32[]{:S(2)}, u32[]{:S(2)}) %collective-permute-start.54) | collective-permute-done | bytes 983072 | tf_op jit(solution)/shard_map/ppermute | solution.py:466
  488.2 9.1 %in_share.15 = f32[5,192,1024]{2,1,0:T(8,128)} custom-call(s32[8,2]{1,0:T(8,128)} %select_select_fusion.places, bf16[1536,1024]{1,0:T(8,128)(2,1)} %get-tuple-element.174.turned_rows, bf16[5,1024,1024]{2,1,0:T(8,128)(2,1)} %get-tuple-element.170.refs_1_.refs_2_.refs_3_.refs_4_.grad_pre, bf16[5,192,512]{2,1,0:T(8,128)(2,1)} %collective-permute-done.54.refs_0_, ...), custom_call_target="tpu_custom_call" | custom-call | flops 30000001024 | bytes 1024 | tf_op jit(solution)/shard_map/in_share/pallas_call | solution.py:724
  (268 shorter events, 117.7 us)
Async XLA Ops:
  7.2 42.7 %all-gather.2.cloned.1.call-start = ((), (), s32[]{:S(2)}) async-start(), calls=%async_computation.6 | async-start | bytes 3932160 | tf_op jit(solution)/shard_map/all_gather | solution.py:971
  23.2 14.7 %collective-permute-start.2 = (bf16[2,48,2688]{2,1,0:T(8,128)(2,1)S(1)}, bf16[2,48,2688]{2,1,0:T(8,128)(2,1)S(1)}, u32[]{:S(2)}, u32[]{:S(2)}) collective-permute-start(bf16[2,48,2688]{2,1,0:T(8,128)(2,1)S(1)} %get-tuple-element.288), channel_id=1, source_target_pairs={{0,8},{1,9},{2,10},{3,11},{8,16},{9,17},{10,18},{11,19},{16,24},{1... | collective-permute-start | bytes 1548296 | tf_op jit(solution)/shard_map/ppermute | solution.py:466
  24.8 14.7 %collective-permute-start.3 = (bf16[2,48,2688]{2,1,0:T(8,128)(2,1)S(1)}, bf16[2,48,2688]{2,1,0:T(8,128)(2,1)S(1)}, u32[]{:S(2)}, u32[]{:S(2)}) collective-permute-start(bf16[2,48,2688]{2,1,0:T(8,128)(2,1)S(1)} %get-tuple-element.288), channel_id=1, source_target_pairs={{0,4},{1,5},{2,6},{3,7},{8,0},{9,1},{10,2},{11,3},{16,8},{17,9},{1... | collective-permute-start | bytes 1548296 | tf_op jit(solution)/shard_map/ppermute | solution.py:466
  30.0 14.3 %collective-permute-start.11 = (bf16[2,48,1536]{2,1,0:T(8,128)(2,1)S(1)}, bf16[2,48,1536]{2,1,0:T(8,128)(2,1)}, u32[]{:S(2)}, u32[]{:S(2)}) collective-permute-start(bf16[2,48,1536]{2,1,0:T(8,128)(2,1)S(1)} %pad_maximum_fusion.5), channel_id=1, source_target_pairs={{0,8},{1,9},{2,10},{3,11},{8,16},{9,17},{10,18},{11,19},{16,24},{1... | collective-permute-start | bytes 884744 | tf_op jit(solution)/shard_map/ppermute | solution.py:466
  31.8 14.1 %collective-permute-start.12 = (bf16[2,48,1536]{2,1,0:T(8,128)(2,1)S(1)}, bf16[2,48,1536]{2,1,0:T(8,128)(2,1)}, u32[]{:S(2)}, u32[]{:S(2)}) collective-permute-start(bf16[2,48,1536]{2,1,0:T(8,128)(2,1)S(1)} %pad_maximum_fusion.5), channel_id=1, source_target_pairs={{0,4},{1,5},{2,6},{3,7},{8,0},{9,1},{10,2},{11,3},{16,8},{17,9},{1... | collective-permute-start | bytes 884744 | tf_op jit(solution)/shard_map/ppermute | solution.py:466
  39.5 23.1 %collective-permute-start.6 = (bf16[2,48,2688]{2,1,0:T(8,128)(2,1)S(1)}, bf16[2,48,2688]{2,1,0:T(8,128)(2,1)}, u32[]{:S(2)}, u32[]{:S(2)}) collective-permute-start(bf16[2,48,2688]{2,1,0:T(8,128)(2,1)S(1)} %collective-permute-done.2), channel_id=1, source_target_pairs={{0,8},{1,9},{2,10},{3,11},{8,16},{9,17},{10,18},{11,19},{16,24},{1... | collective-permute-start | bytes 1548296 | tf_op jit(solution)/shard_map/ppermute | solution.py:466
  41.0 21.5 %collective-permute-start.7 = (bf16[2,48,2688]{2,1,0:T(8,128)(2,1)S(1)}, bf16[2,48,2688]{2,1,0:T(8,128)(2,1)}, u32[]{:S(2)}, u32[]{:S(2)}) collective-permute-start(bf16[2,48,2688]{2,1,0:T(8,128)(2,1)S(1)} %collective-permute-done.3), channel_id=1, source_target_pairs={{0,4},{1,5},{2,6},{3,7},{8,0},{9,1},{10,2},{11,3},{16,8},{17,9},{1... | collective-permute-start | bytes 1548296 | tf_op jit(solution)/shard_map/ppermute | solution.py:466
  45.9 18.7 %collective-permute-start.13 = (bf16[2,48,1536]{2,1,0:T(8,128)(2,1)}, bf16[2,48,1536]{2,1,0:T(8,128)(2,1)}, u32[]{:S(2)}, u32[]{:S(2)}) collective-permute-start(bf16[2,48,1536]{2,1,0:T(8,128)(2,1)} %collective-permute-done.11), channel_id=1, source_target_pairs={{0,8},{1,9},{2,10},{3,11},{8,16},{9,17},{10,18},{11,19},{16,24},{1... | collective-permute-start | bytes 884744 | tf_op jit(solution)/shard_map/ppermute | solution.py:466
  47.5 17.1 %collective-permute-start.14 = (bf16[2,48,1536]{2,1,0:T(8,128)(2,1)}, bf16[2,48,1536]{2,1,0:T(8,128)(2,1)}, u32[]{:S(2)}, u32[]{:S(2)}) collective-permute-start(bf16[2,48,1536]{2,1,0:T(8,128)(2,1)} %collective-permute-done.12), channel_id=1, source_target_pairs={{0,4},{1,5},{2,6},{3,7},{8,0},{9,1},{10,2},{11,3},{16,8},{17,9},{1... | collective-permute-start | bytes 884744 | tf_op jit(solution)/shard_map/ppermute | solution.py:466
  62.5 12.2 %collective-permute-start.10 = (bf16[2,48,2688]{2,1,0:T(8,128)(2,1)}, bf16[2,48,2688]{2,1,0:T(8,128)(2,1)S(1)}, u32[]{:S(2)}, u32[]{:S(2)}) collective-permute-start(bf16[2,48,2688]{2,1,0:T(8,128)(2,1)} %collective-permute-done.7), channel_id=1, source_target_pairs={{0,4},{1,5},{2,6},{3,7},{8,0},{9,1},{10,2},{11,3},{16,8},{17,9},{1... | collective-permute-start | bytes 1548296 | tf_op jit(solution)/shard_map/ppermute | solution.py:466
  64.6 16.8 %collective-permute-start.18 = (bf16[2,48,1536]{2,1,0:T(8,128)(2,1)}, bf16[2,48,1536]{2,1,0:T(8,128)(2,1)S(1)}, u32[]{:S(2)}, u32[]{:S(2)}) collective-permute-start(bf16[2,48,1536]{2,1,0:T(8,128)(2,1)} %collective-permute-done.13), channel_id=1, source_target_pairs={{0,8},{1,9},{2,10},{3,11},{8,16},{9,17},{10,18},{11,19},{16,24},{1... | collective-permute-start | bytes 884744 | tf_op jit(solution)/shard_map/ppermute | solution.py:466
  66.2 15.2 %collective-permute-start.19 = (bf16[2,48,1536]{2,1,0:T(8,128)(2,1)}, bf16[2,48,1536]{2,1,0:T(8,128)(2,1)S(1)}, u32[]{:S(2)}, u32[]{:S(2)}) collective-permute-start(bf16[2,48,1536]{2,1,0:T(8,128)(2,1)} %collective-permute-done.14), channel_id=1, source_target_pairs={{0,4},{1,5},{2,6},{3,7},{8,0},{9,1},{10,2},{11,3},{16,8},{17,9},{1... | collective-permute-start | bytes 884744 | tf_op jit(solution)/shard_map/ppermute | solution.py:466
  90.6 25.2 %collective-permute-start.23 = (bf16[8,2,48,1536]{3,2,1,0:T(8,128)(2,1)S(1)}, bf16[8,2,48,1536]{3,2,1,0:T(8,128)(2,1)}, u32[]{:S(2)}, u32[]{:S(2)}) collective-permute-start(bf16[8,2,48,1536]{3,2,1,0:T(8,128)(2,1)S(1)} %fusion.refs_0_), channel_id=1, source_target_pairs={{0,1},{1,0},{2,3},{3,2},{4,5},{5,4},{6,7},{7,6},{8,9},{9,8},{10,11... | collective-permute-start | bytes 7077896 | tf_op jit(solution)/shard_map/ppermute | solution.py:473
  123.4 21.2 %collective-permute-start.24 = (bf16[256,1664]{1,0:T(8,128)(2,1)}, bf16[256,1664]{1,0:T(8,128)(2,1)S(1)}, u32[]{:S(2)}, u32[]{:S(2)}) collective-permute-start(bf16[256,1664]{1,0:T(8,128)(2,1)} %get-tuple-element.157.rows_a), channel_id=1, source_target_pairs={{0,2},{1,3},{2,0},{3,1},{4,6},{5,7},{6,4},{7,5},{8,10},{9,11},{10,... | collective-permute-start | bytes 2555912 | tf_op jit(solution)/shard_map/ppermute | solution.py:473
  147.4 38.5 %all-to-all-start = ((bf16[4,768,256]{2,1,0:T(8,128)(2,1)}), bf16[4,768,256]{2,1,0:T(8,128)(2,1)S(1)}, u32[]{:S(2)}, u32[]{:S(2)}) async-start(bf16[4,768,256]{2,1,0:T(8,128)(2,1)} %bitcast.73), calls=%async_computation | async-start | bytes 3145728 | tf_op jit(solution)/shard_map/all_to_all | solution.py:1040
  176.9 35.3 %collective-permute-start.30 = (bf16[5,192,512]{2,1,0:T(8,128)(2,1)}, bf16[5,192,512]{2,1,0:T(8,128)(2,1)S(1)}, u32[]{:S(2)}, u32[]{:S(2)}) collective-permute-start(bf16[5,192,512]{2,1,0:T(8,128)(2,1)} %get-tuple-element.175), channel_id=1, source_target_pairs={{0,8},{1,9},{2,10},{3,11},{8,16},{9,17},{10,18},{11,19},{16,24},{1... | collective-permute-start | bytes 2949128 | tf_op jit(solution)/shard_map/ppermute | solution.py:466
  178.7 33.5 %collective-permute-start.31 = (bf16[5,192,512]{2,1,0:T(8,128)(2,1)}, bf16[5,192,512]{2,1,0:T(8,128)(2,1)}, u32[]{:S(2)}, u32[]{:S(2)}) collective-permute-start(bf16[5,192,512]{2,1,0:T(8,128)(2,1)} %get-tuple-element.176), channel_id=1, source_target_pairs={{0,4},{1,5},{2,6},{3,7},{8,0},{9,1},{10,2},{11,3},{16,8},{17,9},{1... | collective-permute-start | bytes 2949128 | tf_op jit(solution)/shard_map/ppermute | solution.py:466
  183.8 45.4 %collective-permute-start.27 = (bf16[320,768]{1,0:T(8,128)(2,1)}, bf16[320,768]{1,0:T(8,128)(2,1)}, u32[]{:S(2)}, u32[]{:S(2)}) collective-permute-start(bf16[320,768]{1,0:T(8,128)(2,1)} %get-tuple-element.166), channel_id=1, source_target_pairs={{0,8},{1,9},{2,10},{3,11},{8,16},{9,17},{10,18},{11,19},{16,24},{1... | collective-permute-start | bytes 1474568 | tf_op jit(solution)/shard_map/ppermute | solution.py:466
  185.7 43.6 %collective-permute-start.28 = (bf16[320,768]{1,0:T(8,128)(2,1)}, bf16[320,768]{1,0:T(8,128)(2,1)}, u32[]{:S(2)}, u32[]{:S(2)}) collective-permute-start(bf16[320,768]{1,0:T(8,128)(2,1)} %get-tuple-element.167), channel_id=1, source_target_pairs={{0,4},{1,5},{2,6},{3,7},{8,0},{9,1},{10,2},{11,3},{16,8},{17,9},{1... | collective-permute-start | bytes 1474568 | tf_op jit(solution)/shard_map/ppermute | solution.py:466
  221.2 40.5 %collective-permute-start.32 = (bf16[5,192,512]{2,1,0:T(8,128)(2,1)}, bf16[5,192,512]{2,1,0:T(8,128)(2,1)S(1)}, u32[]{:S(2)}, u32[]{:S(2)}) collective-permute-start(bf16[5,192,512]{2,1,0:T(8,128)(2,1)} %get-tuple-element.181), channel_id=1, source_target_pairs={{0,8},{1,9},{2,10},{3,11},{8,16},{9,17},{10,18},{11,19},{16,24},{1... | collective-permute-start | bytes 2949128 | tf_op jit(solution)/shard_map/ppermute | solution.py:466
  223.0 38.7 %collective-permute-start.33 = (bf16[5,192,512]{2,1,0:T(8,128)(2,1)}, bf16[5,192,512]{2,1,0:T(8,128)(2,1)}, u32[]{:S(2)}, u32[]{:S(2)}) collective-permute-start(bf16[5,192,512]{2,1,0:T(8,128)(2,1)} %get-tuple-element.182), channel_id=1, source_target_pairs={{0,4},{1,5},{2,6},{3,7},{8,0},{9,1},{10,2},{11,3},{16,8},{17,9},{1... | collective-permute-start | bytes 2949128 | tf_op jit(solution)/shard_map/ppermute | solution.py:466
  225.5 27.6 %all-to-all-start.1 = ((bf16[2,256,1664]{2,1,0:T(8,128)(2,1)}), bf16[2,256,1664]{2,1,0:T(8,128)(2,1)S(1)}, u32[]{:S(2)}, u32[]{:S(2)}) async-start(bf16[2,256,1664]{2,1,0:T(8,128)(2,1)} %reverse_select_fusion), calls=%async_computation.1 | async-start | bytes 3407872 | tf_op jit(solution)/shard_map/all_to_all | solution.py:470
  234.2 36.4 %collective-permute-start.36 = (bf16[320,768]{1,0:T(8,128)(2,1)}, bf16[320,768]{1,0:T(8,128)(2,1)S(1)}, u32[]{:S(2)}, u32[]{:S(2)}) collective-permute-start(bf16[320,768]{1,0:T(8,128)(2,1)} %get-tuple-element.186), channel_id=1, source_target_pairs={{0,8},{1,9},{2,10},{3,11},{8,16},{9,17},{10,18},{11,19},{16,24},{1... | collective-permute-start | bytes 1474568 | tf_op jit(solution)/shard_map/ppermute | solution.py:466
  236.1 34.6 %collective-permute-start.37 = (bf16[320,768]{1,0:T(8,128)(2,1)}, bf16[320,768]{1,0:T(8,128)(2,1)}, u32[]{:S(2)}, u32[]{:S(2)}) collective-permute-start(bf16[320,768]{1,0:T(8,128)(2,1)} %get-tuple-element.187), channel_id=1, source_target_pairs={{0,4},{1,5},{2,6},{3,7},{8,0},{9,1},{10,2},{11,3},{16,8},{17,9},{1... | collective-permute-start | bytes 1474568 | tf_op jit(solution)/shard_map/ppermute | solution.py:466
  276.4 21.7 %collective-permute-start.38 = (bf16[320,768]{1,0:T(8,128)(2,1)}, bf16[320,768]{1,0:T(8,128)(2,1)S(1)}, u32[]{:S(2)}, u32[]{:S(2)}) collective-permute-start(bf16[320,768]{1,0:T(8,128)(2,1)} %get-tuple-element.198), channel_id=1, source_target_pairs={{0,8},{1,9},{2,10},{3,11},{8,16},{9,17},{10,18},{11,19},{16,24},{1... | collective-permute-start | bytes 1474568 | tf_op jit(solution)/shard_map/ppermute | solution.py:466
  278.2 19.9 %collective-permute-start.39 = (bf16[320,768]{1,0:T(8,128)(2,1)}, bf16[320,768]{1,0:T(8,128)(2,1)}, u32[]{:S(2)}, u32[]{:S(2)}) collective-permute-start(bf16[320,768]{1,0:T(8,128)(2,1)} %get-tuple-element.199), channel_id=1, source_target_pairs={{0,4},{1,5},{2,6},{3,7},{8,0},{9,1},{10,2},{11,3},{16,8},{17,9},{1... | collective-permute-start | bytes 1474568 | tf_op jit(solution)/shard_map/ppermute | solution.py:466
  281.3 25.1 %all-to-all-start.2 = ((bf16[2,272,1664]{2,1,0:T(8,128)(2,1)}), bf16[2,272,1664]{2,1,0:T(8,128)(2,1)S(1)}, u32[]{:S(2)}, u32[]{:S(2)}) async-start(bf16[2,272,1664]{2,1,0:T(8,128)(2,1)} %get-tuple-element.208), calls=%async_computation.2 | async-start | bytes 3620864 | tf_op jit(solution)/shard_map/all_to_all | solution.py:470
  285.0 27.0 %collective-permute-start.34 = (bf16[5,192,512]{2,1,0:T(8,128)(2,1)}, bf16[5,192,512]{2,1,0:T(8,128)(2,1)}, u32[]{:S(2)}, u32[]{:S(2)}) collective-permute-start(bf16[5,192,512]{2,1,0:T(8,128)(2,1)} %get-tuple-element.194), channel_id=1, source_target_pairs={{0,8},{1,9},{2,10},{3,11},{8,16},{9,17},{10,18},{11,19},{16,24},{1... | collective-permute-start | bytes 2949128 | tf_op jit(solution)/shard_map/ppermute | solution.py:466
  286.8 26.9 %collective-permute-start.35 = (bf16[5,192,512]{2,1,0:T(8,128)(2,1)S(1)}, bf16[5,192,512]{2,1,0:T(8,128)(2,1)}, u32[]{:S(2)}, u32[]{:S(2)}) collective-permute-start(bf16[5,192,512]{2,1,0:T(8,128)(2,1)S(1)} %copy-done.36), channel_id=1, source_target_pairs={{0,4},{1,5},{2,6},{3,7},{8,0},{9,1},{10,2},{11,3},{16,8},{17,9},{1... | collective-permute-start | bytes 2949128 | tf_op jit(solution)/shard_map/ppermute | solution.py:466
  303.8 31.0 %collective-permute-start.43 = (bf16[320,768]{1,0:T(8,128)(2,1)}, bf16[320,768]{1,0:T(8,128)(2,1)S(1)}, u32[]{:S(2)}, u32[]{:S(2)}) collective-permute-start(bf16[320,768]{1,0:T(8,128)(2,1)} %get-tuple-element.206), channel_id=1, source_target_pairs={{0,8},{1,9},{2,10},{3,11},{8,16},{9,17},{10,18},{11,19},{16,24},{1... | collective-permute-start | bytes 1474568 | tf_op jit(solution)/shard_map/ppermute | solution.py:466
  305.6 29.2 %collective-permute-start.44 = (bf16[320,768]{1,0:T(8,128)(2,1)}, bf16[320,768]{1,0:T(8,128)(2,1)}, u32[]{:S(2)}, u32[]{:S(2)}) collective-permute-start(bf16[320,768]{1,0:T(8,128)(2,1)} %get-tuple-element.207), channel_id=1, source_target_pairs={{0,4},{1,5},{2,6},{3,7},{8,0},{9,1},{10,2},{11,3},{16,8},{17,9},{1... | collective-permute-start | bytes 1474568 | tf_op jit(solution)/shard_map/ppermute | solution.py:466
  306.4 34.4 %all-to-all-start.3 = ((bf16[2,256,2560]{2,1,0:T(8,128)(2,1)}), bf16[2,256,2560]{2,1,0:T(8,128)(2,1)}, u32[]{:S(2)}, u32[]{:S(2)}) async-start(bf16[2,256,2560]{2,1,0:T(8,128)(2,1)} %attend_back.1.grad_project), calls=%async_computation.3 | async-start | bytes 5242880 | tf_op jit(solution)/shard_map/all_to_all | solution.py:470
  311.4 186.0 %reduce-scatter.2.cloned.1.call-start = ((), (), s32[]{:S(2)}) async-start(), calls=%async_computation.7 | async-start | bytes 3649536 | tf_op jit(solution)/shard_map/reduce_scatter | solution.py:1095
  322.3 24.4 %collective-permute-start.41 = (bf16[5,192,512]{2,1,0:T(8,128)(2,1)}, bf16[5,192,512]{2,1,0:T(8,128)(2,1)S(1)}, u32[]{:S(2)}, u32[]{:S(2)}) collective-permute-start(bf16[5,192,512]{2,1,0:T(8,128)(2,1)} %get-tuple-element.214), channel_id=1, source_target_pairs={{0,8},{1,9},{2,10},{3,11},{8,16},{9,17},{10,18},{11,19},{16,24},{1... | collective-permute-start | bytes 2949128 | tf_op jit(solution)/shard_map/ppermute | solution.py:466
  324.2 24.3 %collective-permute-start.42 = (bf16[5,192,512]{2,1,0:T(8,128)(2,1)}, bf16[5,192,512]{2,1,0:T(8,128)(2,1)S(1)}, u32[]{:S(2)}, u32[]{:S(2)}) collective-permute-start(bf16[5,192,512]{2,1,0:T(8,128)(2,1)} %get-tuple-element.215), channel_id=1, source_target_pairs={{0,4},{1,5},{2,6},{3,7},{8,0},{9,1},{10,2},{11,3},{16,8},{17,9},{1... | collective-permute-start | bytes 2949128 | tf_op jit(solution)/shard_map/ppermute | solution.py:466
  348.5 19.4 %collective-permute-start.48 = (bf16[320,768]{1,0:T(8,128)(2,1)}, bf16[320,768]{1,0:T(8,128)(2,1)S(1)}, u32[]{:S(2)}, u32[]{:S(2)}) collective-permute-start(bf16[320,768]{1,0:T(8,128)(2,1)} %get-tuple-element.219), channel_id=1, source_target_pairs={{0,8},{1,9},{2,10},{3,11},{8,16},{9,17},{10,18},{11,19},{16,24},{1... | collective-permute-start | bytes 1474568 | tf_op jit(solution)/shard_map/ppermute | solution.py:466
  350.1 17.9 %collective-permute-start.49 = (bf16[320,768]{1,0:T(8,128)(2,1)}, bf16[320,768]{1,0:T(8,128)(2,1)S(1)}, u32[]{:S(2)}, u32[]{:S(2)}) collective-permute-start(bf16[320,768]{1,0:T(8,128)(2,1)} %get-tuple-element.220), channel_id=1, source_target_pairs={{0,4},{1,5},{2,6},{3,7},{8,0},{9,1},{10,2},{11,3},{16,8},{17,9},{1... | collective-permute-start | bytes 1474568 | tf_op jit(solution)/shard_map/ppermute | solution.py:466
  358.5 25.3 %collective-permute-start.46 = (bf16[5,192,512]{2,1,0:T(8,128)(2,1)}, bf16[5,192,512]{2,1,0:T(8,128)(2,1)S(1)}, u32[]{:S(2)}, u32[]{:S(2)}) collective-permute-start(bf16[5,192,512]{2,1,0:T(8,128)(2,1)} %get-tuple-element.226), channel_id=1, source_target_pairs={{0,8},{1,9},{2,10},{3,11},{8,16},{9,17},{10,18},{11,19},{16,24},{1... | collective-permute-start | bytes 2949128 | tf_op jit(solution)/shard_map/ppermute | solution.py:466
  360.1 25.3 %collective-permute-start.47 = (bf16[5,192,512]{2,1,0:T(8,128)(2,1)}, bf16[5,192,512]{2,1,0:T(8,128)(2,1)S(1)}, u32[]{:S(2)}, u32[]{:S(2)}) collective-permute-start(bf16[5,192,512]{2,1,0:T(8,128)(2,1)} %get-tuple-element.227), channel_id=1, source_target_pairs={{0,4},{1,5},{2,6},{3,7},{8,0},{9,1},{10,2},{11,3},{16,8},{17,9},{1... | collective-permute-start | bytes 2949128 | tf_op jit(solution)/shard_map/ppermute | solution.py:466
  374.5 29.1 %collective-permute-start.52 = (bf16[320,768]{1,0:T(8,128)(2,1)}, bf16[320,768]{1,0:T(8,128)(2,1)S(1)}, u32[]{:S(2)}, u32[]{:S(2)}) collective-permute-start(bf16[320,768]{1,0:T(8,128)(2,1)} %get-tuple-element.231), channel_id=1, source_target_pairs={{0,8},{1,9},{2,10},{3,11},{8,16},{9,17},{10,18},{11,19},{16,24},{1... | collective-permute-start | bytes 1474568 | tf_op jit(solution)/shard_map/ppermute | solution.py:466
  376.1 33.3 %collective-permute-start.53 = (bf16[320,768]{1,0:T(8,128)(2,1)}, bf16[320,768]{1,0:T(8,128)(2,1)S(1)}, u32[]{:S(2)}, u32[]{:S(2)}) collective-permute-start(bf16[320,768]{1,0:T(8,128)(2,1)} %get-tuple-element.232), channel_id=1, source_target_pairs={{0,4},{1,5},{2,6},{3,7},{8,0},{9,1},{10,2},{11,3},{16,8},{17,9},{1... | collective-permute-start | bytes 1474568 | tf_op jit(solution)/shard_map/ppermute | solution.py:466
  394.3 46.4 %collective-permute-start.50 = (bf16[5,192,512]{2,1,0:T(8,128)(2,1)}, bf16[5,192,512]{2,1,0:T(8,128)(2,1)}, u32[]{:S(2)}, u32[]{:S(2)}) collective-permute-start(bf16[5,192,512]{2,1,0:T(8,128)(2,1)} %get-tuple-element.235), channel_id=1, source_target_pairs={{0,8},{1,9},{2,10},{3,11},{8,16},{9,17},{10,18},{11,19},{16,24},{1... | collective-permute-start | bytes 2949128 | tf_op jit(solution)/shard_map/ppermute | solution.py:466
  395.6 47.6 %collective-permute-start.51 = (bf16[5,192,512]{2,1,0:T(8,128)(2,1)}, bf16[5,192,512]{2,1,0:T(8,128)(2,1)}, u32[]{:S(2)}, u32[]{:S(2)}) collective-permute-start(bf16[5,192,512]{2,1,0:T(8,128)(2,1)} %get-tuple-element.236), channel_id=1, source_target_pairs={{0,4},{1,5},{2,6},{3,7},{8,0},{9,1},{10,2},{11,3},{16,8},{17,9},{1... | collective-permute-start | bytes 2949128 | tf_op jit(solution)/shard_map/ppermute | solution.py:466
  415.1 48.1 %collective-permute-start.56 = (bf16[320,768]{1,0:T(8,128)(2,1)}, bf16[320,768]{1,0:T(8,128)(2,1)}, u32[]{:S(2)}, u32[]{:S(2)}) collective-permute-start(bf16[320,768]{1,0:T(8,128)(2,1)} %get-tuple-element.240), channel_id=1, source_target_pairs={{0,8},{1,9},{2,10},{3,11},{8,16},{9,17},{10,18},{11,19},{16,24},{1... | collective-permute-start | bytes 1474568 | tf_op jit(solution)/shard_map/ppermute | solution.py:466
  415.2 48.0 %collective-permute-start.57 = (bf16[320,768]{1,0:T(8,128)(2,1)}, bf16[320,768]{1,0:T(8,128)(2,1)}, u32[]{:S(2)}, u32[]{:S(2)}) collective-permute-start(bf16[320,768]{1,0:T(8,128)(2,1)} %get-tuple-element.241), channel_id=1, source_target_pairs={{0,4},{1,5},{2,6},{3,7},{8,0},{9,1},{10,2},{11,3},{16,8},{17,9},{1... | collective-permute-start | bytes 1474568 | tf_op jit(solution)/shard_map/ppermute | solution.py:466
  417.2 54.2 %all-to-all-start.4 = ((bf16[4,256,1536]{2,1,0:T(8,128)(2,1)}), bf16[4,256,1536]{2,1,0:T(8,128)(2,1)S(1)}, u32[]{:S(2)}, u32[]{:S(2)}) async-start(bf16[4,256,1536]{2,1,0:T(8,128)(2,1)} %bitcast.79), calls=%async_computation.4 | async-start | bytes 6291456 | tf_op jit(solution)/shard_map/all_to_all | solution.py:1097
  451.1 34.6 %collective-permute-start.54 = (bf16[5,192,512]{2,1,0:T(8,128)(2,1)}, bf16[5,192,512]{2,1,0:T(8,128)(2,1)}, u32[]{:S(2)}, u32[]{:S(2)}) collective-permute-start(bf16[5,192,512]{2,1,0:T(8,128)(2,1)} %get-tuple-element.244), channel_id=1, source_target_pairs={{0,8},{1,9},{2,10},{3,11},{8,16},{9,17},{10,18},{11,19},{16,24},{1... | collective-permute-start | bytes 2949128 | tf_op jit(solution)/shard_map/ppermute | solution.py:466
  452.5 35.7 %collective-permute-start.55 = (bf16[5,192,512]{2,1,0:T(8,128)(2,1)}, bf16[5,192,512]{2,1,0:T(8,128)(2,1)}, u32[]{:S(2)}, u32[]{:S(2)}) collective-permute-start(bf16[5,192,512]{2,1,0:T(8,128)(2,1)} %get-tuple-element.245), channel_id=1, source_target_pairs={{0,4},{1,5},{2,6},{3,7},{8,0},{9,1},{10,2},{11,3},{16,8},{17,9},{1... | collective-permute-start | bytes 2949128 | tf_op jit(solution)/shard_map/ppermute | solution.py:466
  (68 other events, 428.0 us)
Sparse Core Ops, SparseCore 0:
  9.6 34.3 all-gather.1
  376.7 109.5 reduce-scatter.1
